TPU v7x, 32 devices: a whole 2x2x4 slice. The times are simulated.
32 devices in a mesh: dp: 8 (over z, x), rep: 4 (over y, core).
Axes of the slice: x: 2, y: 2, z: 4, core: 2. Of those that a mesh axis runs over, the one named last changes fastest.
Arguments:
- tokens: bfloat16 [512, 256, 384], P(('dp', 'rep')), may hold values from -6 to 6
- conditioning: float32 [512, 384], P(('dp', 'rep')), may hold values from -6 to 6
- ada_weight: bfloat16 [384, 2304], P(None, 'dp'), may hold values from -0.3125 to 0.3125
- ada_bias: bfloat16 [2304], P('dp'), may hold values from -3 to 3
- qkv_weight: bfloat16 [384, 1152], P(None, 'dp'), may hold values from -0.3125 to 0.3125
- qv_bias: bfloat16 [768], P('dp'), may hold values from -3 to 3
- out_weight: bfloat16 [384, 384], P(None, 'dp'), may hold values from -1.25 to 1.25
- out_bias: bfloat16 [384], P('dp'), may hold values from -2 to 2
- up_weight: bfloat16 [384, 1536], P(None, 'dp'), may hold values from -0.3125 to 0.3125
- up_bias: bfloat16 [1536], P('dp'), may hold values from -3 to 3
- down_weight: bfloat16 [1536, 384], P(None, 'dp'), may hold values from -0.15625 to 0.15625
- down_bias: bfloat16 [384], P('dp'), may hold values from -2 to 2
- cotangent: bfloat16 [512, 256, 384], P(('dp', 'rep')), may hold values from -6 to 6
Outputs:
- output: bfloat16 [512, 256, 384], P(('dp', 'rep'))
- tokens_grad: bfloat16 [512, 256, 384], P(('dp', 'rep'))
- conditioning_grad: float32 [512, 384], P(('dp', 'rep'))
- ada_weight_grad: float32 [384, 2304], P(None, 'dp')
- ada_bias_grad: float32 [2304], P('dp')
- qkv_weight_grad: float32 [384, 1152], P(None, 'dp')
- qv_bias_grad: float32 [768], P('dp')
- out_weight_grad: float32 [384, 384], P(None, 'dp')
- out_bias_grad: float32 [384], P('dp')
- up_weight_grad: float32 [384, 1536], P(None, 'dp')
- up_bias_grad: float32 [1536], P('dp')
- down_weight_grad: float32 [1536, 384], P(None, 'dp')
- down_bias_grad: float32 [384], P('dp')
All inputs are finite; a program needn't handle non-finite values.
Results may differ from a plain program's by a relative error of at most 0.014.
The roundings to bfloat16 on the way count: a program that leaves them out, or rounds other values in their place, can miss the bound.
Values may be sent and summed in bfloat16 or wider, within the bound.
No kernel may reach another device: no remote copies, remote signals or barrier semaphores. Data moves between devices by JAX's collectives and lax.ppermute only.
A program may use at most 256 MiB of HBM per device.

v0:
```python
import jax
import jax.numpy as jnp
from jax import lax
from jax.sharding import PartitionSpec as P

HEAD_DIM = 64
MICRO = 4


def modulate(values, shift, scale):
    average = jnp.mean(values, axis=-1, keepdims=True)
    centred = values - average
    spread = jnp.mean(centred * centred, axis=-1, keepdims=True)
    return centred * lax.rsqrt(spread + 1e-06) * (1.0 + scale[:, None, :]) + shift[:, None, :]


def fetch_forward(shards):
    return (
        lax.all_gather(shards[0], "dp", axis=1, tiled=True),
        lax.all_gather(shards[1], "dp", axis=0, tiled=True),
        lax.all_gather(shards[2], "dp", axis=1, tiled=True),
        lax.all_gather(shards[3], "dp", axis=0, tiled=True),
        lax.all_gather(shards[4], "dp", axis=1, tiled=True),
        lax.all_gather(shards[5], "dp", axis=0, tiled=True),
        lax.all_gather(shards[6], "dp", axis=1, tiled=True),
        lax.all_gather(shards[7], "dp", axis=0, tiled=True),
        lax.all_gather(shards[8], "dp", axis=1, tiled=True),
        lax.all_gather(shards[9], "dp", axis=0, tiled=True),
    )


def fetch_backward(shards):
    return (
        lax.all_gather(shards[0], "dp", axis=1, tiled=True),
        lax.all_gather(shards[1], "dp", axis=0, tiled=True),
        lax.all_gather(shards[2], "dp", axis=1, tiled=True),
        lax.all_gather(shards[3], "dp", axis=0, tiled=True),
        lax.all_gather(shards[4], "dp", axis=1, tiled=True),
        lax.all_gather(shards[5], "dp", axis=0, tiled=True),
        lax.all_gather(shards[6], "dp", axis=1, tiled=True),
        lax.all_gather(shards[7], "dp", axis=0, tiled=True),
        lax.all_gather(shards[8], "dp", axis=1, tiled=True),
        lax.all_gather(shards[9], "dp", axis=0, tiled=True),
    )


def attention_scores(queries, keys_in):
    return jnp.einsum(
        "bqhe,bkhe->bhqk", queries, keys_in, preferred_element_type=jnp.float32
    ) * HEAD_DIM ** (-0.5)


def forward_pass(values, condition, weights):
    (
        ada_weight,
        ada_bias,
        qkv_weight,
        qv_bias,
        out_weight,
        out_bias,
        up_weight,
        up_bias,
        down_weight,
        down_bias,
    ) = weights
    batch, length, width = values.shape
    heads = width // HEAD_DIM
    silu_low = jax.nn.silu(condition).astype(jnp.bfloat16)
    modulation = jnp.dot(
        silu_low, ada_weight, preferred_element_type=jnp.float32
    ) + ada_bias.astype(jnp.float32)
    shift_one, scale_one, gate_one, shift_two, scale_two, gate_two = jnp.split(
        modulation, 6, axis=-1
    )
    normed_one = modulate(values, shift_one, scale_one).astype(jnp.bfloat16)
    bias_float = qv_bias.astype(jnp.float32)
    full_bias = jnp.concatenate(
        [bias_float[:width], jnp.zeros((width,), jnp.float32), bias_float[width:]]
    )
    qkv = (
        jnp.einsum("bld,de->ble", normed_one, qkv_weight, preferred_element_type=jnp.float32)
        + full_bias
    ).astype(jnp.bfloat16)
    queries = qkv[..., :width].reshape(batch, length, heads, HEAD_DIM)
    keys_in = qkv[..., width : 2 * width].reshape(batch, length, heads, HEAD_DIM)
    values_in = qkv[..., 2 * width :].reshape(batch, length, heads, HEAD_DIM)
    scores = attention_scores(queries, keys_in)
    highest_score = jnp.max(scores, axis=-1, keepdims=True)
    log_total = highest_score + jnp.log(
        jnp.sum(jnp.exp(scores - highest_score), axis=-1, keepdims=True)
    )
    probs_low = jnp.exp(scores - log_total).astype(jnp.bfloat16)
    attended = jnp.einsum(
        "bhqk,bkhe->bqhe", probs_low, values_in, preferred_element_type=jnp.float32
    )
    attended = attended.astype(jnp.bfloat16).reshape(batch, length, width)
    branch = jnp.einsum(
        "bld,de->ble", attended, out_weight, preferred_element_type=jnp.float32
    ) + out_bias.astype(jnp.float32)
    middle = values + gate_one[:, None, :] * branch
    normed_two = modulate(middle, shift_two, scale_two).astype(jnp.bfloat16)
    hidden = jnp.einsum(
        "bld,di->bli", normed_two, up_weight, preferred_element_type=jnp.float32
    ) + up_bias.astype(jnp.float32)
    active = jax.nn.gelu(hidden, approximate=True).astype(jnp.bfloat16)
    feed = jnp.einsum(
        "bli,id->bld", active, down_weight, preferred_element_type=jnp.float32
    ) + down_bias.astype(jnp.float32)
    result = middle + gate_two[:, None, :] * feed
    kept = (
        values,
        condition,
        silu_low,
        modulation,
        normed_one,
        qkv,
        log_total,
        attended,
        branch,
        middle,
        normed_two,
        hidden,
        active,
        feed,
    )
    return (result, kept)


def backward_pass(incoming, kept, weights):
    (
        ada_weight,
        ada_bias,
        qkv_weight,
        qv_bias,
        out_weight,
        out_bias,
        up_weight,
        up_bias,
        down_weight,
        down_bias,
    ) = weights
    (
        values,
        condition,
        silu_low,
        modulation,
        normed_one,
        qkv,
        log_total,
        attended,
        branch,
        middle,
        normed_two,
        hidden,
        active,
        feed,
    ) = kept
    batch, length, width = values.shape
    heads = width // HEAD_DIM
    shift_one, scale_one, gate_one, shift_two, scale_two, gate_two = jnp.split(
        modulation, 6, axis=-1
    )
    grad_feed = (incoming * gate_two[:, None, :]).astype(jnp.bfloat16)
    grad_gate_two = jnp.sum(incoming * feed, axis=1)
    down_grad = jnp.einsum("bli,bld->id", active, grad_feed, preferred_element_type=jnp.float32)
    down_bias_grad = jnp.sum(grad_feed.astype(jnp.float32), axis=(0, 1))
    grad_active = jnp.einsum(
        "bld,id->bli", grad_feed, down_weight, preferred_element_type=jnp.float32
    )
    gelu_out, gelu_pull = jax.vjp(lambda inner: jax.nn.gelu(inner, approximate=True), hidden)
    grad_hidden = gelu_pull(grad_active)[0].astype(jnp.bfloat16)
    up_grad = jnp.einsum("bld,bli->di", normed_two, grad_hidden, preferred_element_type=jnp.float32)
    up_bias_grad = jnp.sum(grad_hidden.astype(jnp.float32), axis=(0, 1))
    grad_normed_two = jnp.einsum(
        "bli,di->bld", grad_hidden, up_weight, preferred_element_type=jnp.float32
    )
    norm_two_out, norm_two_pull = jax.vjp(modulate, middle, shift_two, scale_two)
    grad_middle_norm, grad_shift_two, grad_scale_two = norm_two_pull(grad_normed_two)
    grad_middle = incoming + grad_middle_norm
    grad_branch = (grad_middle * gate_one[:, None, :]).astype(jnp.bfloat16)
    grad_gate_one = jnp.sum(grad_middle * branch, axis=1)
    out_grad = jnp.einsum("bld,ble->de", attended, grad_branch, preferred_element_type=jnp.float32)
    out_bias_grad = jnp.sum(grad_branch.astype(jnp.float32), axis=(0, 1))
    grad_attended = jnp.einsum(
        "ble,de->bld", grad_branch, out_weight, preferred_element_type=jnp.float32
    )
    grad_attended = grad_attended.astype(jnp.bfloat16).reshape(batch, length, heads, HEAD_DIM)
    queries = qkv[..., :width].reshape(batch, length, heads, HEAD_DIM)
    keys_in = qkv[..., width : 2 * width].reshape(batch, length, heads, HEAD_DIM)
    values_in = qkv[..., 2 * width :].reshape(batch, length, heads, HEAD_DIM)
    probs = jnp.exp(attention_scores(queries, keys_in) - log_total)
    probs_low = probs.astype(jnp.bfloat16)
    grad_probs = jnp.einsum(
        "bqhe,bkhe->bhqk", grad_attended, values_in, preferred_element_type=jnp.float32
    )
    row_terms = jnp.sum(probs * grad_probs, axis=-1, keepdims=True)
    grad_scores = (probs * (grad_probs - row_terms)).astype(jnp.bfloat16)
    grad_queries = jnp.einsum(
        "bhqk,bkhe->bqhe", grad_scores, keys_in, preferred_element_type=jnp.float32
    ) * HEAD_DIM ** (-0.5)
    grad_keys = jnp.einsum(
        "bhqk,bqhe->bkhe", grad_scores, queries, preferred_element_type=jnp.float32
    ) * HEAD_DIM ** (-0.5)
    grad_values = jnp.einsum(
        "bhqk,bqhe->bkhe", probs_low, grad_attended, preferred_element_type=jnp.float32
    )
    grad_qkv = jnp.concatenate(
        [
            grad_queries.reshape(batch, length, width),
            grad_keys.reshape(batch, length, width),
            grad_values.reshape(batch, length, width),
        ],
        axis=-1,
    ).astype(jnp.bfloat16)
    qkv_grad = jnp.einsum("bld,ble->de", normed_one, grad_qkv, preferred_element_type=jnp.float32)
    column_sums = jnp.sum(grad_qkv.astype(jnp.float32), axis=(0, 1))
    qv_bias_grad = jnp.concatenate([column_sums[:width], column_sums[2 * width :]])
    grad_normed_one = jnp.einsum(
        "ble,de->bld", grad_qkv, qkv_weight, preferred_element_type=jnp.float32
    )
    norm_one_out, norm_one_pull = jax.vjp(modulate, values, shift_one, scale_one)
    grad_tokens_norm, grad_shift_one, grad_scale_one = norm_one_pull(grad_normed_one)
    tokens_grad = (grad_middle + grad_tokens_norm).astype(jnp.bfloat16)
    grad_modulation = jnp.concatenate(
        [
            grad_shift_one,
            grad_scale_one,
            grad_gate_one,
            grad_shift_two,
            grad_scale_two,
            grad_gate_two,
        ],
        axis=-1,
    )
    highest = lax.Precision.HIGHEST
    ada_grad = jnp.dot(silu_low.astype(jnp.float32).T, grad_modulation, precision=highest)
    ada_bias_grad = jnp.sum(grad_modulation, axis=0)
    grad_silu = jnp.dot(grad_modulation, ada_weight.astype(jnp.float32).T, precision=highest)
    silu_out, silu_pull = jax.vjp(jax.nn.silu, condition)
    condition_grad = silu_pull(grad_silu)[0]
    grads = (
        ada_grad,
        ada_bias_grad,
        qkv_grad,
        qv_bias_grad,
        out_grad,
        out_bias_grad,
        up_grad,
        up_bias_grad,
        down_grad,
        down_bias_grad,
    )
    return (tokens_grad, condition_grad, grads)


def body(
    tokens,
    conditioning,
    ada_weight,
    ada_bias,
    qkv_weight,
    qv_bias,
    out_weight,
    out_bias,
    up_weight,
    up_bias,
    down_weight,
    down_bias,
    cotangent,
):
    shards = (
        ada_weight,
        ada_bias,
        qkv_weight,
        qv_bias,
        out_weight,
        out_bias,
        up_weight,
        up_bias,
        down_weight,
        down_bias,
    )
    per_micro = tokens.shape[0] // MICRO
    results = []
    token_grads = []
    condition_grads = []
    totals = None
    for micro_index in range(MICRO):
        lower = micro_index * per_micro
        values = tokens[lower : lower + per_micro].astype(jnp.float32)
        condition = conditioning[lower : lower + per_micro]
        incoming = cotangent[lower : lower + per_micro].astype(jnp.float32)
        weights_ahead = fetch_forward(shards)
        result, kept = forward_pass(values, condition, weights_ahead)
        weights_behind = fetch_backward(shards)
        tokens_grad, condition_grad, grads = backward_pass(incoming, kept, weights_behind)
        results.append(result.astype(jnp.bfloat16))
        token_grads.append(tokens_grad)
        condition_grads.append(condition_grad)
        if totals is None:
            totals = tuple(grads)
        else:
            totals = tuple((left + right for left, right in zip(totals, grads)))
    owned = (
        lax.psum_scatter(totals[0], "dp", scatter_dimension=1, tiled=True),
        lax.psum_scatter(totals[1], "dp", scatter_dimension=0, tiled=True),
        lax.psum_scatter(totals[2], "dp", scatter_dimension=1, tiled=True),
        lax.psum_scatter(totals[3], "dp", scatter_dimension=0, tiled=True),
        lax.psum_scatter(totals[4], "dp", scatter_dimension=1, tiled=True),
        lax.psum_scatter(totals[5], "dp", scatter_dimension=0, tiled=True),
        lax.psum_scatter(totals[6], "dp", scatter_dimension=1, tiled=True),
        lax.psum_scatter(totals[7], "dp", scatter_dimension=0, tiled=True),
        lax.psum_scatter(totals[8], "dp", scatter_dimension=1, tiled=True),
        lax.psum_scatter(totals[9], "dp", scatter_dimension=0, tiled=True),
    )
    final = (
        lax.psum(owned[0].astype(jnp.bfloat16), "rep").astype(jnp.float32),
        lax.psum(owned[1].astype(jnp.bfloat16), "rep").astype(jnp.float32),
        lax.psum(owned[2].astype(jnp.bfloat16), "rep").astype(jnp.float32),
        lax.psum(owned[3].astype(jnp.bfloat16), "rep").astype(jnp.float32),
        lax.psum(owned[4].astype(jnp.bfloat16), "rep").astype(jnp.float32),
        lax.psum(owned[5].astype(jnp.bfloat16), "rep").astype(jnp.float32),
        lax.psum(owned[6].astype(jnp.bfloat16), "rep").astype(jnp.float32),
        lax.psum(owned[7].astype(jnp.bfloat16), "rep").astype(jnp.float32),
        lax.psum(owned[8].astype(jnp.bfloat16), "rep").astype(jnp.float32),
        lax.psum(owned[9].astype(jnp.bfloat16), "rep").astype(jnp.float32),
    )
    return (
        jnp.concatenate(results, axis=0),
        jnp.concatenate(token_grads, axis=0),
        jnp.concatenate(condition_grads, axis=0),
        final[0],
        final[1],
        final[2],
        final[3],
        final[4],
        final[5],
        final[6],
        final[7],
        final[8],
        final[9],
    )


def solution(mesh):
    return jax.shard_map(
        body,
        mesh=mesh,
        in_specs=(
            P(("dp", "rep"), None, None),
            P(("dp", "rep"), None),
            P(None, "dp"),
            P("dp"),
            P(None, "dp"),
            P("dp"),
            P(None, "dp"),
            P("dp"),
            P(None, "dp"),
            P("dp"),
            P(None, "dp"),
            P("dp"),
            P(("dp", "rep"), None, None),
        ),
        out_specs=(
            P(("dp", "rep"), None, None),
            P(("dp", "rep"), None, None),
            P(("dp", "rep"), None),
            P(None, "dp"),
            P("dp"),
            P(None, "dp"),
            P("dp"),
            P(None, "dp"),
            P("dp"),
            P(None, "dp"),
            P("dp"),
            P(None, "dp"),
            P("dp"),
        ),
        check_vma=False,
    )
```

profile of v0, /device:TPU:0, one launch (start us, length us, event | category | flops | bytes accessed | tf_op | source)
XLA Modules:
  0.0 834.7 jit_solution(18215287013457234597)
XLA Ops:
  20.6 39.3 %all-reduce.11 = (bf16[768]{0:T(1024)(128)(2,1)S(1)}, bf16[2304]{0:T(1024)(128)(2,1)S(1)}, bf16[384]{0:T(512)(128)(2,1)S(1)}, bf16[1536]{0:T(1024)(128)(2,1)S(1)}, bf16[384]{0:T(512)(128)(2,1)S(1)}) all-reduce(bf16[768]{0:T(1024)(128)(2,1)S(1)} %dynamic-update-slice.1, ...), channel_id=1, replica_groups=mesh['dp'=8,'rep'=4] {'dp'}, use_global_device_ids=true, to_apply=%add.1 | all-reduce | flops 5376 | bytes 21504
  61.1 31.3 %all_gather.24 = bf16[384,384]{0,1:T(8,128)(2,1)S(1)} all-gather(bf16[384,48]{0,1:T(8,128)(2,1)} %param.19), channel_id=1, replica_groups=mesh['dp'=8,'rep'=4] {'dp'}, dimensions={1}, use_global_device_ids=true | all-gather | bytes 331776 | tf_op jit(solution)/shard_map/all_gather | solution.py:23
  92.4 33.1 %all_gather.22 = bf16[384,1152]{0,1:T(8,128)(2,1)S(1)} all-gather(bf16[384,144]{0,1:T(8,128)(2,1)S(1)} %copy-done.135), channel_id=1, replica_groups=mesh['dp'=8,'rep'=4] {'dp'}, dimensions={1}, use_global_device_ids=true | all-gather | bytes 995328 | tf_op jit(solution)/shard_map/all_gather | solution.py:21
  141.4 5.8 fusion.126
  150.5 8.6 %convert_reduce_fusion.3 = (f32[1536]{0:T(1024)}, bf16[4,256,1536]{2,1,0:T(8,128)(2,1)S(1)}) fusion(f32[4,256,1536]{2,1,0:T(8,128)} %fusion.126, f32[1536]{0:T(1024)S(1)} %copy-done.239, bf16[1536,384]{0,1:T(8,128)(2,1)} %all-gather.8.cloned.1.call-done, f32[4,384]{1,0:T(4,128)S(1)} %copy-done.195, bf16[16,256,384]{2,1,0:T(8,128)(2,1)} %param.25), kind=kOutput, calls=%fused_computation.39 | convolution fusion | flops 1245313536 | bytes 11421696 | tf_op jit(solution)/shard_map/bld,id->bli/dot_general | solution.py:167
  168.9 5.3 convolution_convert_fusion.3
  193.7 11.5 %fusion.80 = (f32[4,384]{1,0:T(4,128)}, f32[4,256]{1,0:T(4,128)S(1)}, f32[4,256]{1,0:T(4,128)S(1)}, f32[4,256]{1,0:T(4,128)S(1)}, f32[4,256]{1,0:T(4,128)S(1)}, /*index=5*/f32[4,384]{1,0:T(4,128)}) fusion(f32[4,256,384]{2,1,0:T(8,128)S(1)} %get-tuple-element.180, f32[4,256]{1,0:T(4,128)S(1)} %copy-done.168, f32[4,256]{1,0:T(4,128)S(1)} %broadcast_multiply_fusion.7, ...), kind=kLoop, calls=%fused_computation.181 | loop fusion | flops 9430016 | bytes 4777984 | tf_op jit(solution)/shard_map/transpose(jvp())/reduce_sum | solution.py:14
  260.8 6.4 convert_reduce_fusion.1
  282.5 6.9 multiply_convert_fusion.6
  297.4 5.5 convert_reduce_fusion.15
  306.6 5.3 convolution_convert_fusion.1
  319.7 8.4 %convert_reduce_fusion.2 = (f32[1536]{0:T(1024)}, bf16[4,256,1536]{2,1,0:T(8,128)(2,1)S(1)}) fusion(f32[4,256,1536]{2,1,0:T(8,128)} %get-tuple-element.186, f32[1536]{0:T(1024)S(1)} %copy-done.241, bf16[1536,384]{0,1:T(8,128)(2,1)S(1)} %copy-done.124, f32[4,384]{1,0:T(4,128)S(1)} %copy-done.150, bf16[16,256,384]{2,1,0:T(8,128)(2,1)S(1)} %copy-done.25), kind=kOutput, calls=%fused_computation.38 | convolution fusion | flops 1245313536 | bytes 11423744 | tf_op jit(solution)/shard_map/bld,id->bli/dot_general | solution.py:167
  332.3 6.4 convert_reduce_fusion
  358.4 7.1 multiply_reduce_fusion.2
  377.4 5.3 convolution_convert_fusion
  382.7 7.0 multiply_reduce_fusion
  449.2 5.8 fusion.77
  507.3 57.3 %reduce-scatter.14.cloned.1.call-done = f32[1536,48]{0,1:T(8,128)} async-done(((f32[1536,384]{0,1:T(8,128)}), f32[1536,48]{0,1:T(8,128)}) %reduce-scatter.14.cloned.1.call-update) | async-done | bytes 294928 | tf_op jit(solution)/shard_map/reduce_scatter | solution.py:313
  566.3 70.8 %reduce-scatter.12.cloned.1.call-done = f32[384,192]{0,1:T(8,128)} async-done(((f32[384,1536]{0,1:T(8,128)}), f32[384,192]{0,1:T(8,128)}) %reduce-scatter.12.cloned.1.call-update) | async-done | bytes 294928 | tf_op jit(solution)/shard_map/reduce_scatter | solution.py:311
  638.7 80.6 %reduce-scatter.6.cloned.1.call-done = f32[384,288]{0,1:T(8,128)} async-done(((f32[384,2304]{0,1:T(8,128)}), f32[384,288]{0,1:T(8,128)}) %reduce-scatter.6.cloned.1.call-update) | async-done | bytes 442384 | tf_op jit(solution)/shard_map/reduce_scatter | solution.py:305
  721.2 35.9 %all-reduce.10 = (bf16[2304]{0:T(1024)(128)(2,1)S(1)}, bf16[768]{0:T(1024)(128)(2,1)S(1)}, bf16[384]{0:T(512)(128)(2,1)S(1)}, bf16[1536]{0:T(1024)(128)(2,1)S(1)}, bf16[384]{0:T(512)(128)(2,1)S(1)}) all-reduce(f32[2304]{0:T(1024)S(1)} %add_add_fusion.8, f32[768]{0:T(1024)S(1)} %fusion.193, ...), channel_id=3, replica_groups=mesh['dp'=8,'rep'=4] {'dp'}, use_global_device_ids=true, to_apply=%region_74.75.clone | all-reduce | flops 5376 | bytes 32256
  759.4 25.3 %reduce-scatter.10.cloned.1.call-done = f32[384,48]{0,1:T(8,128)} async-done(((f32[384,384]{0,1:T(8,128)}), f32[384,48]{0,1:T(8,128)}) %reduce-scatter.10.cloned.1.call-update) | async-done | bytes 73744 | tf_op jit(solution)/shard_map/reduce_scatter | solution.py:309
  785.6 10.5 %all-reduce.12 = (bf16[288]{0:T(512)(128)(2,1)S(1)}, bf16[96]{0:T(256)(128)(2,1)S(1)}, bf16[384,48]{0,1:T(8,128)(2,1)S(1)}, bf16[48]{0:T(256)(128)(2,1)S(1)}, bf...) all-reduce(bf16[288]{0:T(512)(128)(2,1)S(1)} %dynamic-slice.20, ...), channel_id=1, replica_groups=mesh['dp'=8,'rep'=4] {'rep'}, use_global_device_ids=true, to_apply=%region_75.76 | all-reduce | flops 19104 | bytes 76416 | tf_op jit(solution)/shard_map/psum | solution.py:318
  799.5 21.9 %all-reduce.16.cloned.1.call-done = (bf16[384,288]{0,1:T(8,128)(2,1)}, bf16[384,144]{0,1:T(8,128)(2,1)}, bf16[384,192]{0,1:T(8,128)(2,1)}, bf16[1536,48]{0,1:T(8,128)(2,1)}) async-done(((bf16[384,288]{0,1:T(8,128)(2,1)}, bf16[384,144]{0,1:T(8,128)(2,1)}, bf16[384,192]{0,1:T(8,128)(2,1)}, bf16[1536,48]{0,1:T(8,128)(2,1)}), (bf16[384,288]{0,1:T(8,128)(2,1)}, bf16[384,144]{0,1:T(8,128)(2,1)}, ...) | async-done | bytes 626704 | tf_op jit(solution)/shard_map/psum | solution.py:317
  (863 shorter events, 310.4 us)
Async XLA Ops:
  7.2 85.2 %copy-start.135 = (bf16[384,144]{0,1:T(8,128)(2,1)S(1)}, bf16[384,144]{0,1:T(8,128)(2,1)}, u32[]{:S(2)}) copy-start(bf16[384,144]{0,1:T(8,128)(2,1)} %param.17) | copy-start | bytes 331780
  7.2 118.4 %copy-start.129 = (f32[16,384]{1,0:T(8,128)S(1)}, f32[16,384]{1,0:T(8,128)}, u32[]{:S(2)}) copy-start(f32[16,384]{1,0:T(8,128)} %param.14) | copy-start | bytes 73732
  7.2 118.4 %all-gather.4.cloned.1.call-start = ((), (), s32[]{:S(2)}) async-start(), calls=%async_computation.5 | async-start | bytes 1990656 | tf_op jit(solution)/shard_map/all_gather | solution.py:19
  7.9 133.4 %all-gather.6.cloned.1.call-start = ((), (), s32[]{:S(2)}) async-start(), calls=%async_computation.6 | async-start | bytes 1327104 | tf_op jit(solution)/shard_map/all_gather | solution.py:25
  8.7 141.8 %all-gather.8.cloned.1.call-start = ((), (), s32[]{:S(2)}) async-start(), calls=%async_computation.7 | async-start | bytes 1327104 | tf_op jit(solution)/shard_map/all_gather | solution.py:27
  9.4 496.2 %reduce-scatter.8.cloned.1.call-start = ((), (), s32[]{:S(2)}) async-start(), calls=%async_computation.9 | async-start | bytes 1990656 | tf_op jit(solution)/shard_map/reduce_scatter | solution.py:307
  16.3 115.0 %copy-start.167 = (f32[4,256]{1,0:T(4,128)}, f32[4,256]{1,0:T(4,128)S(1)}, u32[]{:S(2)}) copy-start(f32[4,256]{1,0:T(4,128)S(1)} %fusion.194) | copy-start | bytes 12292
  59.9 77.6 %copy-start.163 = (f32[384]{0:T(512)}, f32[384]{0:T(512)S(1)}, u32[]{:S(2)}) copy-start(f32[384]{0:T(512)S(1)} %convert_element_type.367) | copy-start | bytes 4612
  128.5 65.1 %copy-start.161 = (f32[4,384]{1,0:T(4,128)}, f32[4,384]{1,0:T(4,128)S(1)}, u32[]{:S(2)}) copy-start(f32[4,384]{1,0:T(4,128)S(1)} %get-tuple-element.154) | copy-start | bytes 18436
  256.8 73.9 %copy-start.174 = (f32[4,256]{1,0:T(4,128)}, f32[4,256]{1,0:T(4,128)S(1)}, u32[]{:S(2)}) copy-start(f32[4,256]{1,0:T(4,128)S(1)} %broadcast_multiply_fusion.4) | copy-start | bytes 12292
  428.0 136.6 %reduce-scatter.14.cloned.1.call-start = ((), (), s32[]{:S(2)}) async-start(), calls=%async_computation.12 | async-start | bytes 2654208 | tf_op jit(solution)/shard_map/reduce_scatter | solution.py:313
  442.5 194.6 %reduce-scatter.12.cloned.1.call-start = ((), (), s32[]{:S(2)}) async-start(), calls=%async_computation.11 | async-start | bytes 2654208 | tf_op jit(solution)/shard_map/reduce_scatter | solution.py:311
  465.7 253.6 %reduce-scatter.6.cloned.1.call-start = ((), (), s32[]{:S(2)}) async-start(), calls=%async_computation.8 | async-start | bytes 3981312 | tf_op jit(solution)/shard_map/reduce_scatter | solution.py:305
  479.7 304.9 %reduce-scatter.10.cloned.1.call-start = ((), (), s32[]{:S(2)}) async-start(), calls=%async_computation.10 | async-start | bytes 663552 | tf_op jit(solution)/shard_map/reduce_scatter | solution.py:309
  493.5 327.9 %all-reduce.16.cloned.1.call-start = ((), (), s32[]{:S(2)}) async-start(), calls=%async_computation.13 | async-start | bytes 1253376 | tf_op jit(solution)/shard_map/psum | solution.py:317
  505.5 215.6 %copy-start.243 = (f32[384]{0:T(512)S(1)}, f32[384]{0:T(512)}, u32[]{:S(2)}) copy-start(f32[384]{0:T(512)} %get-tuple-element.162) | copy-start | bytes 4612
  505.5 215.6 %copy-start.244 = (f32[384]{0:T(512)S(1)}, f32[384]{0:T(512)}, u32[]{:S(2)}) copy-start(f32[384]{0:T(512)} %get-tuple-element.163) | copy-start | bytes 4612
  505.5 215.6 %copy-start.245 = (f32[384]{0:T(512)S(1)}, f32[384]{0:T(512)}, u32[]{:S(2)}) copy-start(f32[384]{0:T(512)} %get-tuple-element.164) | copy-start | bytes 4612
  505.5 215.6 %copy-start.246 = (f32[384]{0:T(512)S(1)}, f32[384]{0:T(512)}, u32[]{:S(2)}) copy-start(f32[384]{0:T(512)} %get-tuple-element.165) | copy-start | bytes 4612
  505.5 215.6 %copy-start.247 = (f32[384]{0:T(512)S(1)}, f32[384]{0:T(512)}, u32[]{:S(2)}) copy-start(f32[384]{0:T(512)} %get-tuple-element.160) | copy-start | bytes 4612
  505.5 215.6 %copy-start.248 = (f32[384]{0:T(512)S(1)}, f32[384]{0:T(512)}, u32[]{:S(2)}) copy-start(f32[384]{0:T(512)} %get-tuple-element.161) | copy-start | bytes 4612
  505.5 251.9 %copy-start.91 = (bf16[4,256,384]{2,1,0:T(8,128)(2,1)S(1)}, bf16[4,256,384]{2,1,0:T(8,128)(2,1)}, u32[]{:S(2)}) copy-start(bf16[4,256,384]{2,1,0:T(8,128)(2,1)} %get-tuple-element.113) | copy-start | bytes 2359300
  505.5 251.9 %copy-start.92 = (bf16[4,256,384]{2,1,0:T(8,128)(2,1)S(1)}, bf16[4,256,384]{2,1,0:T(8,128)(2,1)}, u32[]{:S(2)}) copy-start(bf16[4,256,384]{2,1,0:T(8,128)(2,1)} %add_convert_fusion.2) | copy-start | bytes 2359300
  505.6 251.9 %copy-start.93 = (bf16[4,256,384]{2,1,0:T(8,128)(2,1)S(1)}, bf16[4,256,384]{2,1,0:T(8,128)(2,1)}, u32[]{:S(2)}) copy-start(bf16[4,256,384]{2,1,0:T(8,128)(2,1)} %add_convert_fusion.1) | copy-start | bytes 2359300
  (278 other events, 1548.0 us)
Sparse Core Ops, SparseCore 0:
  10.2 48.7 all-gather.3
  61.2 46.3 all-gather.5
  109.7 40.7 all-gather.7
  428.2 64.7 reduce-scatter.7
  496.7 67.9 reduce-scatter.13
  569.0 68.0 reduce-scatter.11
  641.1 78.1 reduce-scatter.5
  723.0 61.6 reduce-scatter.9
  788.4 32.8 all-reduce.15
where the time goes:
time: 841 us; the launch traced here: 835 us
  waiting for transfers between devices  262 us (31%)
  matrix products  228 us (27%)
  blocking collectives  150 us (18%)
  local copies, waits for them, and re-layouts  87.4 us (10%)
  other arithmetic  83.4 us (10%)
  between operations  23.1 us (3%)
    reduce_scatter x1, waiting for transfers between devices, body(): lax.psum_scatter(totals[0], 'dp', scatter_dimension=1, tiled=True)  80.6 us
    unnamed x2, blocking collectives  75.2 us
    reduce_scatter x1, waiting for transfers between devices, body(): lax.psum_scatter(totals[6], 'dp', scatter_dimension=1, tiled=True)  70.8 us
    reduce_scatter x1, waiting for transfers between devices, body(): lax.psum_scatter(totals[8], 'dp', scatter_dimension=1, tiled=True)  57.3 us
    all_gather x1, blocking collectives, fetch_forward(): lax.all_gather(shards[2], 'dp', axis=1, tiled=True)  33.1 us
    all_gather x1, blocking collectives, fetch_forward(): lax.all_gather(shards[4], 'dp', axis=1, tiled=True)  31.3 us
    dot_general x4, matrix products, backward_pass(): jnp.einsum('bld,id->bli', grad_feed, down_weight, preferred_element_type=...  29.8 us
    unnamed x622, local copies, waits for them, and re-layouts  27 us
  transfers between devices with their start and end apart: 9, of which 6 were waited for; matrix products, arithmetic and copies ran while one was open for 13% of the time, Pallas kernels for 0%

commit v1 on v0

v1 whole, which is shorter than its diff:
```python
import functools

import jax
import jax.numpy as jnp
from jax import lax
from jax.experimental import pallas as pl
from jax.experimental.pallas import tpu as pltpu
from jax.sharding import PartitionSpec as P

HEAD_DIM = 64
EPS = 1e-06
GELU_C = 0.7978845608028654
VMEM_LIMIT = 56 * 1024 * 1024
F32 = jnp.float32
BF16 = jnp.bfloat16


def dot_nn(left, right):
    return lax.dot_general(left, right, (((1,), (0,)), ((), ())), preferred_element_type=F32)


def dot_nt(left, right):
    return lax.dot_general(left, right, (((1,), (1,)), ((), ())), preferred_element_type=F32)


def dot_tn(left, right):
    return lax.dot_general(left, right, (((0,), (0,)), ((), ())), preferred_element_type=F32)


def normalise(values):
    average = jnp.mean(values, axis=-1, keepdims=True)
    centred = values - average
    spread = jnp.mean(centred * centred, axis=-1, keepdims=True)
    inverse = lax.rsqrt(spread + EPS)
    return centred * inverse, inverse


def normalise_back(upstream, normal, inverse):
    first = jnp.mean(upstream, axis=-1, keepdims=True)
    second = jnp.mean(upstream * normal, axis=-1, keepdims=True)
    return inverse * (upstream - first - normal * second)


def lane_low(shape):
    return lax.broadcasted_iota(jnp.int32, shape, 1) < HEAD_DIM


def attention_forward_kernel(
    tokens_ref, mod_ref, weight_ref, bias_ref, normed_ref, qkv_ref, lse_ref, attended_ref
):
    latents, length, width = tokens_ref.shape
    pairs = width // (2 * HEAD_DIM)
    mask = lane_low((length, 2 * HEAD_DIM))
    for latent in range(latents):
        normal, _ = normalise(tokens_ref[latent].astype(F32))
        normed = normal * (1.0 + mod_ref[latent, 1:2, :]) + mod_ref[latent, 0:1, :]
        normed = normed.astype(BF16)
        normed_ref[latent] = normed
        qkv = (dot_nt(normed, weight_ref[...]) + bias_ref[...]).astype(BF16)
        qkv_ref[latent] = qkv
        for pair in range(pairs):
            low = pair * 2 * HEAD_DIM
            high = low + 2 * HEAD_DIM
            queries = qkv[:, low:high]
            keys_in = qkv[:, width + low : width + high]
            values_in = qkv[:, 2 * width + low : 2 * width + high]
            halves = []
            for side in range(2):
                keep = mask if side == 0 else jnp.logical_not(mask)
                keys_side = jnp.where(keep, keys_in, jnp.zeros_like(keys_in))
                scores = dot_nt(keys_side, queries) * HEAD_DIM ** (-0.5)
                highest = jnp.max(scores, axis=0, keepdims=True)
                shifted = jnp.exp(scores - highest)
                total = jnp.sum(shifted, axis=0, keepdims=True)
                probs = (shifted * (1.0 / total)).astype(BF16)
                lse_ref[latent, 2 * pair + side : 2 * pair + side + 1, :] = highest + jnp.log(total)
                halves.append(dot_tn(probs, values_in))
            attended_ref[latent, :, low:high] = jnp.where(mask, halves[0], halves[1]).astype(BF16)


def feed_kernel(
    tokens_ref,
    cotangent_ref,
    attended_ref,
    mod_ref,
    out_weight_ref,
    out_bias_ref,
    up_weight_ref,
    up_bias_ref,
    down_weight_ref,
    down_bias_ref,
    output_ref,
    grad_middle_ref,
    grad_attended_ref,
    grad_mod_ref,
    out_grad_ref,
    up_grad_ref,
    down_grad_ref,
    bias_grad_ref,
    out_acc,
    up_acc,
    down_acc,
    bias_acc,
    *,
    chunk,
):
    step = pl.program_id(0)
    length, width = tokens_ref.shape[1:]
    hidden_width = up_weight_ref.shape[0]

    @pl.when(step == 0)
    def _():
        out_acc[...] = jnp.zeros_like(out_acc)
        up_acc[...] = jnp.zeros_like(up_acc)
        down_acc[...] = jnp.zeros_like(down_acc)
        bias_acc[...] = jnp.zeros_like(bias_acc)

    gate_one = mod_ref[0, 2:3, :]
    shift_two = mod_ref[0, 3:4, :]
    scale_two = 1.0 + mod_ref[0, 4:5, :]
    gate_two = mod_ref[0, 5:6, :]
    attended = attended_ref[0]
    branch = dot_nt(attended, out_weight_ref[...]) + out_bias_ref[...]
    middle = tokens_ref[0].astype(F32) + gate_one * branch
    normal, inverse = normalise(middle)
    normed = (normal * scale_two + shift_two).astype(BF16)
    incoming = cotangent_ref[0].astype(F32)
    grad_feed = (incoming * gate_two).astype(BF16)
    bias_acc[0:1, :width] += jnp.sum(grad_feed.astype(F32), axis=0, keepdims=True)

    feed = jnp.zeros((length, width), F32)
    grad_normed = jnp.zeros((length, width), F32)
    for low in range(0, hidden_width, chunk):
        high = low + chunk
        hidden = dot_nt(normed, up_weight_ref[low:high, :]) + up_bias_ref[:, low:high]
        square = hidden * hidden
        bent = jnp.tanh(hidden * (GELU_C + (GELU_C * 0.044715) * square))
        half = 0.5 + 0.5 * bent
        active = (hidden * half).astype(BF16)
        slope = half + hidden * (0.5 - 0.5 * (bent * bent)) * (
            GELU_C + (3.0 * GELU_C * 0.044715) * square
        )
        feed += dot_nt(active, down_weight_ref[:, low:high])
        grad_active = dot_nn(grad_feed, down_weight_ref[:, low:high])
        grad_hidden_wide = grad_active * slope
        grad_hidden = grad_hidden_wide.astype(BF16)
        bias_acc[2:3, low:high] += jnp.sum(grad_hidden.astype(F32), axis=0, keepdims=True)
        grad_normed += dot_nn(grad_hidden, up_weight_ref[low:high, :])
        up_acc[:, low:high] += dot_tn(normed, grad_hidden)
        down_acc[:, low:high] += dot_tn(grad_feed, active)

    feed = feed + down_bias_ref[...]
    output_ref[0] = (middle + gate_two * feed).astype(BF16)
    grad_mod_ref[0, 3:4, :] = jnp.sum(incoming * feed, axis=0, keepdims=True)
    grad_mod_ref[0, 1:2, :] = jnp.sum(grad_normed, axis=0, keepdims=True)
    grad_mod_ref[0, 2:3, :] = jnp.sum(grad_normed * normal, axis=0, keepdims=True)
    grad_middle = incoming + normalise_back(grad_normed * scale_two, normal, inverse)
    grad_middle_ref[0] = grad_middle
    grad_branch = (grad_middle * gate_one).astype(BF16)
    grad_mod_ref[0, 0:1, :] = jnp.sum(grad_middle * branch, axis=0, keepdims=True)
    bias_acc[1:2, :width] += jnp.sum(grad_branch.astype(F32), axis=0, keepdims=True)
    grad_attended_ref[0] = dot_nn(grad_branch, out_weight_ref[...]).astype(BF16)
    out_acc[...] += dot_tn(grad_branch, attended)

    @pl.when(step == pl.num_programs(0) - 1)
    def _():
        out_grad_ref[...] = out_acc[...].astype(BF16)
        up_grad_ref[...] = up_acc[...].T.astype(BF16)
        down_grad_ref[...] = down_acc[...].astype(BF16)
        bias_grad_ref[...] = bias_acc[...]


def attention_backward_kernel(
    qkv_ref,
    lse_ref,
    grad_attended_ref,
    normed_ref,
    grad_qkv_ref,
    weight_grad_ref,
    bias_grad_ref,
    acc,
    bias_acc,
):
    step = pl.program_id(0)
    length, width = grad_attended_ref.shape[1:]
    pairs = width // (2 * HEAD_DIM)
    mask = lane_low((length, 2 * HEAD_DIM))

    @pl.when(step == 0)
    def _():
        acc[...] = jnp.zeros_like(acc)
        bias_acc[...] = jnp.zeros_like(bias_acc)

    for pair in range(pairs):
        low = pair * 2 * HEAD_DIM
        high = low + 2 * HEAD_DIM
        queries = qkv_ref[0, :, low:high]
        keys_in = qkv_ref[0, :, width + low : width + high]
        values_in = qkv_ref[0, :, 2 * width + low : 2 * width + high]
        grad_out = grad_attended_ref[0, :, low:high]
        sides_q = []
        sides_k = []
        sides_v = []
        for side in range(2):
            keep = mask if side == 0 else jnp.logical_not(mask)
            keys_side = jnp.where(keep, keys_in, jnp.zeros_like(keys_in))
            values_side = jnp.where(keep, values_in, jnp.zeros_like(values_in))
            scores = dot_nt(keys_side, queries) * HEAD_DIM ** (-0.5)
            probs = jnp.exp(scores - lse_ref[0, 2 * pair + side : 2 * pair + side + 1, :])
            grad_probs = dot_nt(values_side, grad_out)
            row_terms = jnp.sum(probs * grad_probs, axis=0, keepdims=True)
            grad_scores = (probs * (grad_probs - row_terms)).astype(BF16)
            sides_v.append(dot_nn(probs.astype(BF16), grad_out))
            sides_k.append(dot_nn(grad_scores, queries))
            sides_q.append(dot_tn(grad_scores, keys_in))
        grad_qkv_ref[0, :, low:high] = (
            jnp.where(mask, sides_q[0], sides_q[1]) * HEAD_DIM ** (-0.5)
        ).astype(BF16)
        grad_qkv_ref[0, :, width + low : width + high] = (
            jnp.where(mask, sides_k[0], sides_k[1]) * HEAD_DIM ** (-0.5)
        ).astype(BF16)
        grad_qkv_ref[0, :, 2 * width + low : 2 * width + high] = jnp.where(
            mask, sides_v[0], sides_v[1]
        ).astype(BF16)
    grad_qkv = grad_qkv_ref[0]
    bias_acc[0:1, :] += jnp.sum(grad_qkv.astype(F32), axis=0, keepdims=True)
    acc[...] += dot_tn(normed_ref[0], grad_qkv)

    @pl.when(step == pl.num_programs(0) - 1)
    def _():
        weight_grad_ref[...] = acc[...].T.astype(BF16)
        bias_grad_ref[...] = bias_acc[...]


def first_norm_kernel(
    grad_qkv_ref, tokens_ref, grad_middle_ref, mod_ref, weight_ref, tokens_grad_ref, grad_mod_ref
):
    normal, inverse = normalise(tokens_ref[0].astype(F32))
    grad_normed = dot_nn(grad_qkv_ref[0], weight_ref[...])
    grad_mod_ref[0, 0:1, :] = jnp.sum(grad_normed, axis=0, keepdims=True)
    grad_mod_ref[0, 1:2, :] = jnp.sum(grad_normed * normal, axis=0, keepdims=True)
    upstream = grad_normed * (1.0 + mod_ref[0, 1:2, :])
    tokens_grad_ref[0] = (grad_middle_ref[0] + normalise_back(upstream, normal, inverse)).astype(
        BF16
    )


def each(shape):
    zeros = (0,) * (len(shape) - 1)
    return pl.BlockSpec((1,) + tuple(shape[1:]), lambda step: (step,) + zeros)


def whole(shape):
    zeros = (0,) * len(shape)
    return pl.BlockSpec(tuple(shape), lambda step: zeros)


def run_kernel(kernel, steps, streamed, fixed, streamed_out, fixed_out, scratch, order, cost):
    operands = [item for kind, item in order]
    in_specs = [each(item.shape) if kind == "s" else whole(item.shape) for kind, item in order]
    del streamed, fixed
    outs = list(streamed_out) + list(fixed_out)
    out_specs = [each(item.shape) for item in streamed_out] + [
        whole(item.shape) for item in fixed_out
    ]
    return pl.pallas_call(
        kernel,
        grid=(steps,),
        in_specs=in_specs,
        out_specs=out_specs,
        out_shape=outs,
        scratch_shapes=scratch,
        compiler_params=pltpu.CompilerParams(
            dimension_semantics=("arbitrary",), vmem_limit_bytes=VMEM_LIMIT
        ),
        cost_estimate=cost,
    )(*operands)


def shape_of(dims, kind):
    return jax.ShapeDtypeStruct(tuple(dims), kind)


def pair_shift(n_dp, n_rep, hop):
    return [
        (d * n_rep + r, ((d + hop) % n_dp) * n_rep + r) for d in range(n_dp) for r in range(n_rep)
    ]


def rep_shift(n_dp, n_rep, hop):
    return [(d * n_rep + r, d * n_rep + (r ^ hop)) for d in range(n_dp) for r in range(n_rep)]


AXES = ("dp", "rep")


def by_source(pieces, position):
    count = len(pieces)
    backwards = jnp.stack(pieces[::-1])
    twice = jnp.concatenate([backwards, backwards])
    return lax.dynamic_slice_in_dim(twice, count - 1 - position, count, axis=0)


def gather_halves(shard, n_dp, n_rep, axis):
    position = lax.axis_index("dp")
    core = lax.axis_index("rep") % 2
    half = shard.shape[axis] // 2
    mine = lax.dynamic_slice_in_dim(shard, core * half, half, axis=axis)
    pieces = [mine]
    for hop in range(1, n_dp):
        pieces.append(lax.ppermute(mine, AXES, pair_shift(n_dp, n_rep, hop)))
    stacked = by_source(pieces, position)
    other = lax.ppermute(stacked, AXES, rep_shift(n_dp, n_rep, 1))
    first = jnp.where(core == 0, stacked, other)
    second = jnp.where(core == 0, other, stacked)
    return jnp.concatenate([first, second], axis=axis + 1)


def exchange(blocks, n_dp, n_rep):
    position = lax.axis_index("dp")
    pieces = [lax.dynamic_index_in_dim(blocks, position, keepdims=False)]
    for hop in range(1, n_dp):
        target = (position + hop) % n_dp
        block = lax.dynamic_index_in_dim(blocks, target, keepdims=False)
        pieces.append(lax.ppermute(block, AXES, pair_shift(n_dp, n_rep, hop)))
    return by_source(pieces, position)


def spread_rep(value, n_dp, n_rep):
    place = lax.axis_index("rep")
    pieces = [value]
    for hop in range(1, n_rep):
        pieces.append(lax.ppermute(value, AXES, rep_shift(n_dp, n_rep, hop)))
    return jnp.stack([select_piece(pieces, place ^ r) for r in range(n_rep)])


def select_piece(pieces, index):
    chosen = pieces[0]
    for hop in range(1, len(pieces)):
        chosen = jnp.where(index == hop, pieces[hop], chosen)
    return chosen


def reduce_to_owner(blocks, n_dp, n_rep):
    place = lax.axis_index("rep")
    position = lax.axis_index("dp")
    total = lax.dynamic_index_in_dim(blocks, place, axis=1, keepdims=False).astype(F32)
    for hop in range(1, n_rep):
        block = lax.dynamic_index_in_dim(blocks, place ^ hop, axis=1, keepdims=False)
        total = total + lax.ppermute(block, AXES, rep_shift(n_dp, n_rep, hop)).astype(F32)
    total_low = total.astype(BF16)
    result = lax.dynamic_index_in_dim(total, position, keepdims=False)
    for hop in range(1, n_dp):
        block = lax.dynamic_index_in_dim(total_low, (position + hop) % n_dp, keepdims=False)
        result = result + lax.ppermute(block, AXES, pair_shift(n_dp, n_rep, hop)).astype(F32)
    return result


def quarters(grad, n_dp, n_rep):
    blocks = grad.reshape(n_dp, -1, grad.shape[-1])
    blocks = jnp.pad(blocks, ((0, 0), (0, -blocks.shape[1] % n_rep), (0, 0)))
    return blocks.reshape(n_dp, n_rep, -1, grad.shape[-1])


def body(
    n_dp,
    n_rep,
    tokens,
    conditioning,
    ada_weight,
    ada_bias,
    qkv_weight,
    qv_bias,
    out_weight,
    out_bias,
    up_weight,
    up_bias,
    down_weight,
    down_bias,
    cotangent,
):
    latents, length, width = tokens.shape
    hidden_width = up_weight.shape[1] * n_dp
    heads = width // HEAD_DIM
    rows = latents * length

    silu_low = jax.nn.silu(conditioning).astype(BF16)
    silu_group = exchange(jnp.broadcast_to(silu_low, (n_dp,) + silu_low.shape), n_dp, n_rep)
    mod_columns = jnp.dot(
        silu_group.reshape(n_dp * latents, width), ada_weight, preferred_element_type=F32
    ) + ada_bias.astype(F32)
    mod_parts = exchange(mod_columns.reshape(n_dp, latents, -1), n_dp, n_rep)
    modulation = mod_parts.transpose(1, 0, 2).reshape(latents, 6, width)

    bias_shard = jnp.concatenate([qv_bias, out_bias, up_bias, down_bias])
    bias_all = exchange(
        jnp.broadcast_to(bias_shard, (n_dp,) + bias_shard.shape), n_dp, n_rep
    ).astype(F32)
    cuts = [0]
    for part in (qv_bias, out_bias, up_bias, down_bias):
        cuts.append(cuts[-1] + part.shape[0])
    qv_full, out_full, up_full, down_full = (
        bias_all[:, low:high].reshape(1, -1) for low, high in zip(cuts[:-1], cuts[1:])
    )
    qkv_bias = jnp.concatenate(
        [qv_full[:, :width], jnp.zeros((1, width), F32), qv_full[:, width:]], axis=1
    )

    qkv_full = gather_halves(qkv_weight.T, n_dp, n_rep, 0).reshape(3 * width, width)
    out_wide, up_shard, down_shard, _ = lax.optimization_barrier(
        (out_weight.T, up_weight.T, down_weight.T, qkv_full)
    )
    out_all = gather_halves(out_wide, n_dp, n_rep, 0).reshape(width, width)
    up_all = gather_halves(up_shard, n_dp, n_rep, 0).reshape(hidden_width, width)
    down_all = gather_halves(down_shard, n_dp, n_rep, 1).reshape(width, hidden_width)

    normed, qkv, lse, attended = run_kernel(
        attention_forward_kernel,
        latents,
        None,
        None,
        [
            shape_of((latents, length, width), BF16),
            shape_of((latents, length, 3 * width), BF16),
            shape_of((latents, 8 * ((heads + 7) // 8), length), F32),
            shape_of((latents, length, width), BF16),
        ],
        [],
        [],
        [("s", tokens), ("s", modulation), ("f", qkv_full), ("f", qkv_bias)],
        pl.CostEstimate(
            flops=2 * rows * width * (3 * width + 2 * length),
            bytes_accessed=rows * width * 12,
            transcendentals=rows * heads * length,
        ),
    )

    (
        output,
        grad_middle,
        grad_attended,
        grad_mod_two,
        out_grad,
        up_grad,
        down_grad,
        bias_grad,
    ) = run_kernel(
        functools.partial(feed_kernel, chunk=512),
        latents,
        None,
        None,
        [
            shape_of((latents, length, width), BF16),
            shape_of((latents, length, width), F32),
            shape_of((latents, length, width), BF16),
            shape_of((latents, 4, width), F32),
        ],
        [
            shape_of((width, width), BF16),
            shape_of((hidden_width, width), BF16),
            shape_of((width, hidden_width), BF16),
            shape_of((8, hidden_width), F32),
        ],
        [
            pltpu.VMEM((width, width), F32),
            pltpu.VMEM((width, hidden_width), F32),
            pltpu.VMEM((width, hidden_width), F32),
            pltpu.VMEM((8, hidden_width), F32),
        ],
        [
            ("s", tokens),
            ("s", cotangent),
            ("s", attended),
            ("s", modulation),
            ("f", out_all),
            ("f", out_full),
            ("f", up_all),
            ("f", up_full),
            ("f", down_all),
            ("f", down_full),
        ],
        pl.CostEstimate(
            flops=6 * rows * width * (width + 2 * hidden_width),
            bytes_accessed=rows * width * 14,
            transcendentals=rows * hidden_width,
        ),
    )

    out_rows = width // n_dp
    up_rows = hidden_width // n_dp
    up_quarter = -(-up_rows // n_rep)
    down_quarter = hidden_width // n_rep
    up_blocks = quarters(up_grad, n_dp, n_rep)
    down_blocks = down_grad.reshape(n_dp, out_rows, n_rep, down_quarter).transpose(0, 2, 1, 3)
    out_blocks = quarters(out_grad, n_dp, n_rep)
    up_sum = reduce_to_owner(
        jnp.concatenate([up_blocks, out_blocks], axis=2), n_dp, n_rep
    )
    down_sum = reduce_to_owner(down_blocks, n_dp, n_rep)

    grad_qkv, qkv_grad, qkv_bias_grad = run_kernel(
        attention_backward_kernel,
        latents,
        None,
        None,
        [shape_of((latents, length, 3 * width), BF16)],
        [shape_of((3 * width, width), BF16), shape_of((8, 3 * width), F32)],
        [pltpu.VMEM((width, 3 * width), F32), pltpu.VMEM((8, 3 * width), F32)],
        [("s", qkv), ("s", lse), ("s", grad_attended), ("s", normed)],
        pl.CostEstimate(
            flops=2 * rows * width * (3 * width + 5 * length),
            bytes_accessed=rows * width * 16,
            transcendentals=rows * heads * length,
        ),
    )
    qkv_rows = 3 * width // n_dp
    qkv_sum = reduce_to_owner(quarters(qkv_grad, n_dp, n_rep), n_dp, n_rep)

    tokens_grad, grad_mod_one = run_kernel(
        first_norm_kernel,
        latents,
        None,
        None,
        [shape_of((latents, length, width), BF16), shape_of((latents, 2, width), F32)],
        [],
        [],
        [
            ("s", grad_qkv),
            ("s", tokens),
            ("s", grad_middle),
            ("s", modulation),
            ("f", qkv_full),
        ],
        pl.CostEstimate(
            flops=6 * rows * width * width, bytes_accessed=rows * width * 14, transcendentals=0
        ),
    )

    grad_modulation = jnp.concatenate([grad_mod_one, grad_mod_two], axis=1).reshape(
        latents, 6 * width
    )
    highest = lax.Precision.HIGHEST
    grad_columns = exchange(
        grad_modulation.reshape(latents, n_dp, -1).transpose(1, 0, 2), n_dp, n_rep
    ).reshape(n_dp * latents, -1)
    silu_wide = silu_group.reshape(n_dp * latents, width).astype(F32)
    ada_part = lax.dot_general(
        grad_columns, silu_wide, (((0,), (0,)), ((), ())), precision=highest
    )
    ada_bias_part = jnp.sum(grad_columns, axis=0)
    silu_part = lax.dot_general(
        grad_columns, ada_weight.astype(F32), (((1,), (1,)), ((), ())), precision=highest
    )
    grad_silu = jnp.sum(exchange(silu_part.reshape(n_dp, latents, width), n_dp, n_rep), axis=0)
    _, silu_pull = jax.vjp(jax.nn.silu, conditioning)
    condition_grad = silu_pull(grad_silu)[0]

    qkv_columns = qkv_bias_grad[0]
    qv_columns = jnp.concatenate([qkv_columns[:width], qkv_columns[2 * width :]])
    bias_blocks = jnp.concatenate(
        [
            qv_columns.reshape(n_dp, -1),
            bias_grad[1, :width].reshape(n_dp, -1),
            bias_grad[2].reshape(n_dp, -1),
            bias_grad[0, :width].reshape(n_dp, -1),
        ],
        axis=1,
    )
    bias_part = jnp.sum(exchange(bias_blocks, n_dp, n_rep), axis=0)

    ada_sum = jnp.sum(spread_rep(ada_part.astype(BF16), n_dp, n_rep).astype(F32), axis=0)
    small = jnp.concatenate([bias_part, ada_bias_part])
    small_sum = jnp.sum(spread_rep(small, n_dp, n_rep), axis=0)
    up_out = spread_rep(up_sum.astype(BF16), n_dp, n_rep).astype(F32)
    up_owned = up_out[:, :up_quarter].reshape(-1, width)[:up_rows]
    out_owned = up_out[:, up_quarter:].reshape(-1, width)[:out_rows]
    down_owned = (
        spread_rep(down_sum.astype(BF16), n_dp, n_rep)
        .astype(F32)
        .transpose(1, 0, 2)
        .reshape(out_rows, hidden_width)
    )
    qkv_owned = spread_rep(qkv_sum.astype(BF16), n_dp, n_rep).astype(F32)
    qkv_owned = qkv_owned.reshape(-1, width)[:qkv_rows]
    ends = list(cuts) + [cuts[-1] + ada_bias_part.shape[0]]
    qv_sum, out_bias_sum, up_bias_sum, down_bias_sum, ada_bias_sum = (
        small_sum[low:high] for low, high in zip(ends[:-1], ends[1:])
    )
    return (
        output,
        tokens_grad,
        condition_grad,
        ada_sum.T,
        ada_bias_sum,
        qkv_owned.T,
        qv_sum,
        out_owned.T,
        out_bias_sum,
        up_owned.T,
        up_bias_sum,
        down_owned.T,
        down_bias_sum,
    )


def solution(mesh):
    return jax.shard_map(
        functools.partial(body, mesh.shape["dp"], mesh.shape["rep"]),
        mesh=mesh,
        in_specs=(
            P(("dp", "rep"), None, None),
            P(("dp", "rep"), None),
            P(None, "dp"),
            P("dp"),
            P(None, "dp"),
            P("dp"),
            P(None, "dp"),
            P("dp"),
            P(None, "dp"),
            P("dp"),
            P(None, "dp"),
            P("dp"),
            P(("dp", "rep"), None, None),
        ),
        out_specs=(
            P(("dp", "rep"), None, None),
            P(("dp", "rep"), None, None),
            P(("dp", "rep"), None),
            P(None, "dp"),
            P("dp"),
            P(None, "dp"),
            P("dp"),
            P(None, "dp"),
            P("dp"),
            P(None, "dp"),
            P("dp"),
            P(None, "dp"),
            P("dp"),
        ),
        check_vma=False,
    )
```

time: 841 us -> 507 us (0.60)
  matrix products: 228 us -> 0.98 us
  starting transfers between devices: 1.15 us -> 170 us
  Pallas kernels: 0 us -> 161 us
  blocking collectives: 150 us -> 0 us
  waiting for transfers between devices: 262 us -> 125 us
  other arithmetic: 83.4 us -> 15.2 us
  local copies, waits for them, and re-layouts: 87.4 us -> 31.6 us
  between operations: 23.1 us -> 2.01 us
    reduce_scatter x5 -> x0, waiting for transfers between devices: 234 us -> none  [the longest x1 80.6 us: body(): lax.psum_scatter(totals[0], 'dp', scatter_dimension=1, tiled=True)]
    dot_general x84 -> x3, matrix products: 228 us -> 0.98 us  [the longest x1 0.39 us: body(): lax.dot_general(grad_columns, silu_wide, (((0,), (0,)), ((), ())), precis...]
    ppermute x0 -> x119, starting transfers between devices: none -> 170 us  [the longest x42 80.2 us: exchange(): pieces.append(lax.ppermute(block, AXES, pair_shift(n_dp, n_rep, hop)))]
    pallas_call x0 -> x4, Pallas kernels: none -> 161 us  [run_kernel(): pl.pallas_call(kernel, grid=(steps,), in_specs=in_specs, out_specs=out_sp...]
    ppermute x0 -> x119, waiting for transfers between devices: none -> 125 us  [the longest x42 61 us: exchange(): pieces.append(lax.ppermute(block, AXES, pair_shift(n_dp, n_rep, hop)))]
    unnamed x2 -> x0, blocking collectives: 75.2 us -> none
    all_gather x2 -> x0, blocking collectives: 64.4 us -> none  [the longest x1 33.1 us: fetch_forward(): lax.all_gather(shards[2], 'dp', axis=1, tiled=True)]
    reduce_sum x27 -> x5, other arithmetic: 39.4 us -> 0.99 us  [the longest x1 0.88 us: body(): jnp.sum(spread_rep(ada_part.astype(BF16), n_dp, n_rep).astype(F32), axis=0)]
  transfers between devices with their start and end apart: 9 -> 119, of which waited for: 6 -> 53; matrix products, arithmetic and copies ran while one was open for 13% -> 7% of each run, Pallas kernels for 0% -> 9%
where the time goes in v1:
time: 507 us; the launch traced here: 506 us
  starting transfers between devices  170 us (34%)
  Pallas kernels  161 us (32%)
  waiting for transfers between devices  125 us (25%)
  local copies, waits for them, and re-layouts  31.6 us (6%)
  other arithmetic  15.2 us (3%)
    pallas_call x4, Pallas kernels, run_kernel(): pl.pallas_call(kernel, grid=(steps,), in_specs=in_specs, out_specs=out_sp...  161 us
    ppermute x42, starting transfers between devices, exchange(): pieces.append(lax.ppermute(block, AXES, pair_shift(n_dp, n_rep, hop)))  80.2 us
    ppermute x42, waiting for transfers between devices, exchange(): pieces.append(lax.ppermute(block, AXES, pair_shift(n_dp, n_rep, hop)))  61 us
    ppermute x28, starting transfers between devices, gather_halves(): pieces.append(lax.ppermute(mine, AXES, pair_shift(n_dp, n_rep, hop)))  38.7 us
    ppermute x28, waiting for transfers between devices, gather_halves(): pieces.append(lax.ppermute(mine, AXES, pair_shift(n_dp, n_rep, hop)))  35.8 us
    ppermute x21, starting transfers between devices, reduce_to_owner(): lax.ppermute(block, AXES, pair_shift(n_dp, n_rep, hop)).astype(F32)  34.4 us
    ppermute x9, waiting for transfers between devices, reduce_to_owner(): lax.ppermute(block, AXES, rep_shift(n_dp, n_rep, hop)).astype(F32)  12.6 us
  transfers between devices with their start and end apart: 119, of which 53 were waited for; matrix products, arithmetic and copies ran while one was open for 7% of the time, Pallas kernels for 9%

profile of v1, /device:TPU:0, one launch (start us, length us, event | category | flops | bytes accessed | tf_op | source)
XLA Modules:
  0.0 505.8 jit_solution(3766292838262064179)
XLA Ops:
  1.5 6.0 %collective-permute-start.22 = (bf16[384]{0:T(512)(128)(2,1)S(1)}, bf16[384]{0:T(512)(128)(2,1)S(1)}, u32[]{:S(2)}, u32[]{:S(2)}) collective-permute-start(bf16[384]{0:T(512)(128)(2,1)S(1)} %pad_maximum_fusion.10), channel_id=1, source_target_pairs={{0,28},{1,29},{2,30},{3,31},{4,0},{5,1},{6,2},{7,3},{8,4},{9,5},{1... | collective-permute-start | bytes 2312 | tf_op jit(solution)/shard_map/ppermute | solution.py:325
  16.2 3.6 collective-permute-start.14
  31.5 3.7 collective-permute-start.2
  36.6 3.9 collective-permute-start.3
  42.2 3.8 collective-permute-start.4
  66.0 3.6 collective-permute-done.8
  79.0 3.7 collective-permute-start.11
  87.5 3.7 collective-permute-done.12
  93.7 4.0 collective-permute-done.13
  99.8 3.9 collective-permute-done.18
  116.0 25.9 %shard_map.228 = (bf16[16,256,384]{2,1,0:T(8,128)(2,1)}, bf16[16,256,1152]{2,1,0:T(8,128)(2,1)}, f32[16,8,256]{2,1,0:T(8,128)}, bf16[16,256,384]{2,1,0:T(8,128)(2,1)}) custom-call(bf16[16,256,384]{2,1,0:T(8,128)(2,1)} %tokens_ref.5, f32[16,6,384]{2,1,0:T(8,128)} %reshape.145.mod_ref, bf16[1152,384]{1,0:T(8,128)(2,1)} %bitcast.432, f32[1,1152]{1,0:T(1,128)} %fusion.47.bias_ref), custom_call_target="tpu_custom_call" | custom-call | flops 5234491392 | bytes 18874368 | tf_op jit(solution)/shard_map/pallas_call | solution.py:266
  146.4 4.1 collective-permute-done.31
  151.1 4.0 collective-permute-done.32
  163.9 4.2 collective-permute-done.34
  169.5 5.3 %collective-permute-done.35 = bf16[24,384]{1,0:T(8,128)(2,1)S(1)} collective-permute-done((bf16[24,384]{1,0:T(8,128)(2,1)S(1)}, bf16[24,384]{1,0:T(8,128)(2,1)S(1)}, u32[]{:S(2)}, u32[]{:S(2)}) %collective-permute-start.35) | collective-permute-done | bytes 18464 | tf_op jit(solution)/shard_map/ppermute | solution.py:311
  199.7 72.1 %shard_map.229 = (bf16[16,256,384]{2,1,0:T(8,128)(2,1)}, f32[16,256,384]{2,1,0:T(8,128)}, bf16[16,256,384]{2,1,0:T(8,128)(2,1)}, f32[16,4,384]{2,1,0:T(4,128)}, ...) custom-call(bf16[16,256,384]{2,1,0:T(8,128)(2,1)} %tokens_ref.5, ...), custom_call_target="tpu_custom_call" | custom-call | flops 32614907904 | bytes 22020096 | tf_op jit(solution)/shard_map/pallas_call | solution.py:266
  276.1 44.7 %shard_map.230 = (bf16[16,256,1152]{2,1,0:T(8,128)(2,1)}, bf16[1152,384]{1,0:T(8,128)(2,1)}, f32[8,1152]{1,0:T(8,128)}) custom-call(bf16[16,256,1152]{2,1,0:T(8,128)(2,1)} %get-tuple-element.38.qkv_ref, f32[16,8,256]{2,1,0:T(8,128)} %get-tuple-element.39.lse_ref, bf16[16,256,384]{2,1,0:T(8,128)(2,1)} %get-tuple-element.40.grad_attended_ref, ...), custom_call_target="tpu_custom_call" | custom-call | flops 7650410496 | bytes 25165824 | tf_op jit(solution)/shard_map/pallas_call | solution.py:266
  330.1 18.3 %shard_map.231 = (bf16[16,256,384]{2,1,0:T(8,128)(2,1)}, f32[16,2,384]{2,1,0:T(2,128)}) custom-call(bf16[16,256,1152]{2,1,0:T(8,128)(2,1)} %get-tuple-element.42.grad_qkv_ref, bf16[16,256,384]{2,1,0:T(8,128)(2,1)} %tokens_ref.5, f32[16,256,384]{2,1,0:T(8,128)} %get-tuple-element.43.grad_middle_ref, f32[16,6,384]{2,1,0:T(8,128)} %reshape.145.mod_ref, ...), custom_call_target="tpu_custom_call" | custom-call | flops 3623878656 | bytes 22020096 | tf_op jit(solution)/shard_map/pallas_call | solution.py:266
  383.1 3.6 collective-permute-done.59
  395.5 3.8 collective-permute-done.61
  400.6 3.5 collective-permute-done.62
  422.9 3.7 collective-permute-done.66
  446.0 5.1 %collective-permute-done.108 = bf16[8,48,384]{2,1,0:T(8,128)(2,1)S(1)} collective-permute-done((bf16[8,48,384]{2,1,0:T(8,128)(2,1)S(1)}, bf16[8,48,384]{2,1,0:T(8,128)(2,1)S(1)}, u32[]{:S(2)}, u32[]{:S(2)}) %collective-permute-start.108) | collective-permute-done | bytes 294944 | tf_op jit(solution)/shard_map/ppermute | solution.py:350
  473.0 6.4 %collective-permute-done.95 = bf16[8,60,384]{2,1,0:T(8,128)(2,1)S(1)} collective-permute-done((bf16[8,60,384]{2,1,0:T(8,128)(2,1)S(1)}, bf16[8,60,384]{2,1,0:T(8,128)(2,1)S(1)}, u32[]{:S(2)}, u32[]{:S(2)}) %collective-permute-start.95) | collective-permute-done | bytes 368672 | tf_op jit(solution)/shard_map/ppermute | solution.py:350
  (498 shorter events, 259.4 us)
Async XLA Ops:
  16.2 81.5 %collective-permute-start.14 = (bf16[72,384]{1,0:T(8,128)(2,1)S(1)}, bf16[72,384]{1,0:T(8,128)(2,1)S(1)}, u32[]{:S(2)}, u32[]{:S(2)}) collective-permute-start(bf16[72,384]{1,0:T(8,128)(2,1)S(1)} %dynamic-slice_bitcast_fusion.11), channel_id=1, source_target_pairs={{0,28},{1,29},{2,30},{3,31},{4,0},{5,1},{6,2},{7,3},{8,4},{9,5},{1... | collective-permute-start | bytes 165896 | tf_op jit(solution)/shard_map/ppermute | solution.py:311
  19.9 78.0 %collective-permute-start.15 = (bf16[72,384]{1,0:T(8,128)(2,1)S(1)}, bf16[72,384]{1,0:T(8,128)(2,1)S(1)}, u32[]{:S(2)}, u32[]{:S(2)}) collective-permute-start(bf16[72,384]{1,0:T(8,128)(2,1)S(1)} %dynamic-slice_bitcast_fusion.11), channel_id=1, source_target_pairs={{0,24},{1,25},{2,26},{3,27},{4,28},{5,29},{6,30},{7,31},{8,0},{9,1... | collective-permute-start | bytes 165896 | tf_op jit(solution)/shard_map/ppermute | solution.py:311
  21.1 78.7 %collective-permute-start.16 = (bf16[72,384]{1,0:T(8,128)(2,1)S(1)}, bf16[72,384]{1,0:T(8,128)(2,1)S(1)}, u32[]{:S(2)}, u32[]{:S(2)}) collective-permute-start(bf16[72,384]{1,0:T(8,128)(2,1)S(1)} %dynamic-slice_bitcast_fusion.11), channel_id=1, source_target_pairs={{0,20},{1,21},{2,22},{3,23},{4,24},{5,25},{6,26},{7,27},{8,28},{9,... | collective-permute-start | bytes 165896 | tf_op jit(solution)/shard_map/ppermute | solution.py:311
  21.7 78.1 %collective-permute-start.17 = (bf16[72,384]{1,0:T(8,128)(2,1)S(1)}, bf16[72,384]{1,0:T(8,128)(2,1)S(1)}, u32[]{:S(2)}, u32[]{:S(2)}) collective-permute-start(bf16[72,384]{1,0:T(8,128)(2,1)S(1)} %dynamic-slice_bitcast_fusion.11), channel_id=1, source_target_pairs={{0,16},{1,17},{2,18},{3,19},{4,20},{5,21},{6,22},{7,23},{8,24},{9,... | collective-permute-start | bytes 165896 | tf_op jit(solution)/shard_map/ppermute | solution.py:311
  108.1 66.9 %collective-permute-start.45 = (bf16[48,768]{1,0:T(8,128)(2,1)S(1)}, bf16[48,768]{1,0:T(8,128)(2,1)S(1)}, u32[]{:S(2)}, u32[]{:S(2)}) collective-permute-start(bf16[48,768]{1,0:T(8,128)(2,1)S(1)} %constant_dynamic-slice_fusion.22), channel_id=1, source_target_pairs={{0,28},{1,29},{2,30},{3,31},{4,0},{5,1},{6,2},{7,3},{8,4},{9,5},{1... | collective-permute-start | bytes 221192 | tf_op jit(solution)/shard_map/ppermute | solution.py:311
  108.6 66.4 %collective-permute-start.46 = (bf16[48,768]{1,0:T(8,128)(2,1)S(1)}, bf16[48,768]{1,0:T(8,128)(2,1)S(1)}, u32[]{:S(2)}, u32[]{:S(2)}) collective-permute-start(bf16[48,768]{1,0:T(8,128)(2,1)S(1)} %constant_dynamic-slice_fusion.22), channel_id=1, source_target_pairs={{0,24},{1,25},{2,26},{3,27},{4,28},{5,29},{6,30},{7,31},{8,0},{9,1... | collective-permute-start | bytes 221192 | tf_op jit(solution)/shard_map/ppermute | solution.py:311
  110.7 66.7 %collective-permute-start.47 = (bf16[48,768]{1,0:T(8,128)(2,1)S(1)}, bf16[48,768]{1,0:T(8,128)(2,1)S(1)}, u32[]{:S(2)}, u32[]{:S(2)}) collective-permute-start(bf16[48,768]{1,0:T(8,128)(2,1)S(1)} %constant_dynamic-slice_fusion.22), channel_id=1, source_target_pairs={{0,20},{1,21},{2,22},{3,23},{4,24},{5,25},{6,26},{7,27},{8,28},{9,... | collective-permute-start | bytes 221192 | tf_op jit(solution)/shard_map/ppermute | solution.py:311
  111.4 68.5 %collective-permute-start.48 = (bf16[48,768]{1,0:T(8,128)(2,1)S(1)}, bf16[48,768]{1,0:T(8,128)(2,1)S(1)}, u32[]{:S(2)}, u32[]{:S(2)}) collective-permute-start(bf16[48,768]{1,0:T(8,128)(2,1)S(1)} %constant_dynamic-slice_fusion.22), channel_id=1, source_target_pairs={{0,16},{1,17},{2,18},{3,19},{4,20},{5,21},{6,22},{7,23},{8,24},{9,... | collective-permute-start | bytes 221192 | tf_op jit(solution)/shard_map/ppermute | solution.py:311
  114.5 27.4 %collective-permute-start.29 = (bf16[24,384]{1,0:T(8,128)(2,1)S(1)}, bf16[24,384]{1,0:T(8,128)(2,1)S(1)}, u32[]{:S(2)}, u32[]{:S(2)}) collective-permute-start(bf16[24,384]{1,0:T(8,128)(2,1)S(1)} %constant_dynamic-slice_fusion.26), channel_id=1, source_target_pairs={{0,28},{1,29},{2,30},{3,31},{4,0},{5,1},{6,2},{7,3},{8,4},{9,5},{1... | collective-permute-start | bytes 55304 | tf_op jit(solution)/shard_map/ppermute | solution.py:311
  324.1 32.3 %collective-permute-start.70 = (f32[384]{0:T(512)S(1)}, f32[384]{0:T(512)S(1)}, u32[]{:S(2)}, u32[]{:S(2)}) collective-permute-start(f32[384]{0:T(512)S(1)} %get-tuple-element.63), channel_id=1, source_target_pairs={{0,28},{1,29},{2,30},{3,31},{4,0},{5,1},{6,2},{7,3},{8,4},{9,5},{1... | collective-permute-start | bytes 4616 | tf_op jit(solution)/shard_map/ppermute | solution.py:325
  325.7 31.8 %collective-permute-start.71 = (f32[384]{0:T(512)S(1)}, f32[384]{0:T(512)S(1)}, u32[]{:S(2)}, u32[]{:S(2)}) collective-permute-start(f32[384]{0:T(512)S(1)} %get-tuple-element.62), channel_id=1, source_target_pairs={{0,24},{1,25},{2,26},{3,27},{4,28},{5,29},{6,30},{7,31},{8,0},{9,1... | collective-permute-start | bytes 4616 | tf_op jit(solution)/shard_map/ppermute | solution.py:325
  325.7 33.6 %collective-permute-start.72 = (f32[384]{0:T(512)S(1)}, f32[384]{0:T(512)S(1)}, u32[]{:S(2)}, u32[]{:S(2)}) collective-permute-start(f32[384]{0:T(512)S(1)} %get-tuple-element.61), channel_id=1, source_target_pairs={{0,20},{1,21},{2,22},{3,23},{4,24},{5,25},{6,26},{7,27},{8,28},{9,... | collective-permute-start | bytes 4616 | tf_op jit(solution)/shard_map/ppermute | solution.py:325
  328.2 36.6 %collective-permute-start.73 = (f32[384]{0:T(512)S(1)}, f32[384]{0:T(512)S(1)}, u32[]{:S(2)}, u32[]{:S(2)}) collective-permute-start(f32[384]{0:T(512)S(1)} %get-tuple-element.60), channel_id=1, source_target_pairs={{0,16},{1,17},{2,18},{3,19},{4,20},{5,21},{6,22},{7,23},{8,24},{9,... | collective-permute-start | bytes 4616 | tf_op jit(solution)/shard_map/ppermute | solution.py:325
  349.5 25.4 %collective-permute-start.53 = (f32[16,288]{1,0:T(8,128)S(1)}, f32[16,288]{1,0:T(8,128)S(1)}, u32[]{:S(2)}, u32[]{:S(2)}) collective-permute-start(f32[16,288]{1,0:T(8,128)S(1)} %bitcast.458), channel_id=1, source_target_pairs={{0,28},{1,29},{2,30},{3,31},{4,0},{5,1},{6,2},{7,3},{8,4},{9,5},{1... | collective-permute-start | bytes 55304 | tf_op jit(solution)/shard_map/ppermute | solution.py:325
  364.8 62.5 %collective-permute-start.80 = (bf16[8,36,384]{2,1,0:T(8,128)(2,1)}, bf16[8,36,384]{2,1,0:T(8,128)(2,1)}, u32[]{:S(2)}, u32[]{:S(2)}) collective-permute-start(bf16[8,36,384]{2,1,0:T(8,128)(2,1)} %get-tuple-element.81), channel_id=1, source_target_pairs={{0,1},{1,0},{2,3},{3,2},{4,5},{5,4},{6,7},{7,6},{8,9},{9,8},{10,11... | collective-permute-start | bytes 663560 | tf_op jit(solution)/shard_map/ppermute | solution.py:350
  365.4 61.9 %collective-permute-start.81 = (bf16[8,36,384]{2,1,0:T(8,128)(2,1)}, bf16[8,36,384]{2,1,0:T(8,128)(2,1)}, u32[]{:S(2)}, u32[]{:S(2)}) collective-permute-start(bf16[8,36,384]{2,1,0:T(8,128)(2,1)} %get-tuple-element.83), channel_id=1, source_target_pairs={{0,2},{1,3},{2,0},{3,1},{4,6},{5,7},{6,4},{7,5},{8,10},{9,11},{10,... | collective-permute-start | bytes 663560 | tf_op jit(solution)/shard_map/ppermute | solution.py:350
  389.9 37.4 %collective-permute-start.82 = (bf16[8,36,384]{2,1,0:T(8,128)(2,1)S(1)}, bf16[8,36,384]{2,1,0:T(8,128)(2,1)S(1)}, u32[]{:S(2)}, u32[]{:S(2)}) collective-permute-start(bf16[8,36,384]{2,1,0:T(8,128)(2,1)S(1)} %copy-done.14), channel_id=1, source_target_pairs={{0,3},{1,2},{2,1},{3,0},{4,7},{5,6},{6,5},{7,4},{8,11},{9,10},{10,... | collective-permute-start | bytes 663560 | tf_op jit(solution)/shard_map/ppermute | solution.py:350
  390.6 38.5 %collective-permute-start.67 = (bf16[288,384]{1,0:T(8,128)(2,1)S(1)}, bf16[288,384]{1,0:T(8,128)(2,1)S(1)}, u32[]{:S(2)}, u32[]{:S(2)}) collective-permute-start(bf16[288,384]{1,0:T(8,128)(2,1)S(1)} %fusion), channel_id=1, source_target_pairs={{0,3},{1,2},{2,1},{3,0},{4,7},{5,6},{6,5},{7,4},{8,11},{9,10},{10,... | collective-permute-start | bytes 663560 | tf_op jit(solution)/shard_map/ppermute | solution.py:333
  437.6 13.5 %collective-permute-start.108 = (bf16[8,48,384]{2,1,0:T(8,128)(2,1)S(1)}, bf16[8,48,384]{2,1,0:T(8,128)(2,1)S(1)}, u32[]{:S(2)}, u32[]{:S(2)}) collective-permute-start(bf16[8,48,384]{2,1,0:T(8,128)(2,1)S(1)} %bitcast.448), channel_id=1, source_target_pairs={{0,3},{1,2},{2,1},{3,0},{4,7},{5,6},{6,5},{7,4},{8,11},{9,10},{10,... | collective-permute-start | bytes 884744 | tf_op jit(solution)/shard_map/ppermute | solution.py:350
  446.0 12.8 %collective-permute-start.92 = (bf16[36,384]{1,0:T(8,128)(2,1)S(1)}, bf16[36,384]{1,0:T(8,128)(2,1)S(1)}, u32[]{:S(2)}, u32[]{:S(2)}) collective-permute-start(bf16[36,384]{1,0:T(8,128)(2,1)S(1)} %fusion.40), channel_id=1, source_target_pairs={{0,1},{1,0},{2,3},{3,2},{4,5},{5,4},{6,7},{7,6},{8,9},{9,8},{10,11... | collective-permute-start | bytes 82952 | tf_op jit(solution)/shard_map/ppermute | solution.py:333
  462.4 16.9 %collective-permute-start.95 = (bf16[8,60,384]{2,1,0:T(8,128)(2,1)S(1)}, bf16[8,60,384]{2,1,0:T(8,128)(2,1)S(1)}, u32[]{:S(2)}, u32[]{:S(2)}) collective-permute-start(bf16[8,60,384]{2,1,0:T(8,128)(2,1)S(1)} %get-tuple-element.72), channel_id=1, source_target_pairs={{0,3},{1,2},{2,1},{3,0},{4,7},{5,6},{6,5},{7,4},{8,11},{9,10},{10,... | collective-permute-start | bytes 1105928 | tf_op jit(solution)/shard_map/ppermute | solution.py:350
  469.9 15.7 %collective-permute-start.116 = (bf16[48,384]{1,0:T(8,128)(2,1)S(1)}, bf16[48,384]{1,0:T(8,128)(2,1)S(1)}, u32[]{:S(2)}, u32[]{:S(2)}) collective-permute-start(bf16[48,384]{1,0:T(8,128)(2,1)S(1)} %fusion.33), channel_id=1, source_target_pairs={{0,3},{1,2},{2,1},{3,0},{4,7},{5,6},{6,5},{7,4},{8,11},{9,10},{10,... | collective-permute-start | bytes 110600 | tf_op jit(solution)/shard_map/ppermute | solution.py:333
  470.1 18.1 %collective-permute-start.117 = (bf16[48,384]{1,0:T(8,128)(2,1)S(1)}, bf16[48,384]{1,0:T(8,128)(2,1)S(1)}, u32[]{:S(2)}, u32[]{:S(2)}) collective-permute-start(bf16[48,384]{1,0:T(8,128)(2,1)S(1)} %fusion.33), channel_id=1, source_target_pairs={{0,2},{1,3},{2,0},{3,1},{4,6},{5,7},{6,4},{7,5},{8,10},{9,11},{10,... | collective-permute-start | bytes 110600 | tf_op jit(solution)/shard_map/ppermute | solution.py:333
  471.9 16.4 %collective-permute-start.118 = (bf16[48,384]{1,0:T(8,128)(2,1)S(1)}, bf16[48,384]{1,0:T(8,128)(2,1)S(1)}, u32[]{:S(2)}, u32[]{:S(2)}) collective-permute-start(bf16[48,384]{1,0:T(8,128)(2,1)S(1)} %fusion.33), channel_id=1, source_target_pairs={{0,1},{1,0},{2,3},{3,2},{4,5},{5,4},{6,7},{7,6},{8,9},{9,8},{10,11... | collective-permute-start | bytes 110600 | tf_op jit(solution)/shard_map/ppermute | solution.py:333
  (112 other events, 889.1 us)

commit v2 on v1

v2 whole, which is shorter than its diff:
```python
import functools

import jax
import jax.numpy as jnp
from jax import lax
from jax.experimental import pallas as pl
from jax.experimental.pallas import tpu as pltpu
from jax.sharding import PartitionSpec as P

HEAD_DIM = 64
EPS = 1e-06
GELU_C = 0.7978845608028654
VMEM_LIMIT = 56 * 1024 * 1024
F32 = jnp.float32
BF16 = jnp.bfloat16


def dot_nn(left, right):
    return lax.dot_general(left, right, (((1,), (0,)), ((), ())), preferred_element_type=F32)


def dot_nt(left, right):
    return lax.dot_general(left, right, (((1,), (1,)), ((), ())), preferred_element_type=F32)


def dot_tn(left, right):
    return lax.dot_general(left, right, (((0,), (0,)), ((), ())), preferred_element_type=F32)


def normalise(values):
    average = jnp.mean(values, axis=-1, keepdims=True)
    centred = values - average
    spread = jnp.mean(centred * centred, axis=-1, keepdims=True)
    inverse = lax.rsqrt(spread + EPS)
    return centred * inverse, inverse


def normalise_back(upstream, normal, inverse):
    first = jnp.mean(upstream, axis=-1, keepdims=True)
    second = jnp.mean(upstream * normal, axis=-1, keepdims=True)
    return inverse * (upstream - first - normal * second)


def lane_low(shape):
    return lax.broadcasted_iota(jnp.int32, shape, 1) < HEAD_DIM


def attention_forward_kernel(
    tokens_ref, mod_ref, weight_ref, bias_ref, normed_ref, qkv_ref, lse_ref, attended_ref
):
    latents, length, width = tokens_ref.shape
    pairs = width // (2 * HEAD_DIM)
    mask = lane_low((length, 2 * HEAD_DIM))
    for latent in range(latents):
        normal, _ = normalise(tokens_ref[latent].astype(F32))
        normed = normal * (1.0 + mod_ref[latent, 1:2, :]) + mod_ref[latent, 0:1, :]
        normed = normed.astype(BF16)
        normed_ref[latent] = normed
        qkv = (dot_nt(normed, weight_ref[...]) + bias_ref[...]).astype(BF16)
        qkv_ref[latent] = qkv
        for pair in range(pairs):
            low = pair * 2 * HEAD_DIM
            high = low + 2 * HEAD_DIM
            queries = qkv[:, low:high]
            keys_in = qkv[:, width + low : width + high]
            values_in = qkv[:, 2 * width + low : 2 * width + high]
            halves = []
            for side in range(2):
                keep = mask if side == 0 else jnp.logical_not(mask)
                keys_side = jnp.where(keep, keys_in, jnp.zeros_like(keys_in))
                scores = dot_nt(keys_side, queries) * HEAD_DIM ** (-0.5)
                highest = jnp.max(scores, axis=0, keepdims=True)
                shifted = jnp.exp(scores - highest)
                total = jnp.sum(shifted, axis=0, keepdims=True)
                probs = (shifted * (1.0 / total)).astype(BF16)
                lse_ref[latent, 2 * pair + side : 2 * pair + side + 1, :] = highest + jnp.log(total)
                halves.append(dot_tn(probs, values_in))
            attended_ref[latent, :, low:high] = jnp.where(mask, halves[0], halves[1]).astype(BF16)


def feed_kernel(
    tokens_ref,
    cotangent_ref,
    attended_ref,
    mod_ref,
    out_weight_ref,
    out_bias_ref,
    up_weight_ref,
    up_bias_ref,
    down_weight_ref,
    down_bias_ref,
    output_ref,
    grad_middle_ref,
    grad_attended_ref,
    grad_mod_ref,
    out_grad_ref,
    up_grad_ref,
    down_grad_ref,
    bias_grad_ref,
    out_acc,
    up_acc,
    down_acc,
    bias_acc,
    *,
    chunk,
):
    step = pl.program_id(0)
    latents, length, width = tokens_ref.shape
    rows = latents * length
    hidden_width = up_weight_ref.shape[0]

    @pl.when(step == 0)
    def _():
        out_acc[...] = jnp.zeros_like(out_acc)
        up_acc[...] = jnp.zeros_like(up_acc)
        down_acc[...] = jnp.zeros_like(down_acc)
        bias_acc[...] = jnp.zeros_like(bias_acc)

    def flat(values):
        return values.reshape(rows, width)

    def deep(values):
        return values.reshape(latents, length, width)

    gate_one = mod_ref[:, 2:3, :]
    shift_two = mod_ref[:, 3:4, :]
    scale_two = 1.0 + mod_ref[:, 4:5, :]
    gate_two = mod_ref[:, 5:6, :]
    attended = flat(attended_ref[...])
    branch = deep(dot_nt(attended, out_weight_ref[...]) + out_bias_ref[...])
    middle = tokens_ref[...].astype(F32) + gate_one * branch
    normal, inverse = normalise(middle)
    normed = flat((normal * scale_two + shift_two).astype(BF16))
    incoming = cotangent_ref[...].astype(F32)
    grad_feed = flat((incoming * gate_two).astype(BF16))
    bias_acc[0:1, :width] += jnp.sum(grad_feed.astype(F32), axis=0, keepdims=True)

    feed = jnp.zeros((rows, width), F32)
    grad_normed = jnp.zeros((rows, width), F32)
    for low in range(0, hidden_width, chunk):
        high = low + chunk
        hidden = dot_nt(normed, up_weight_ref[low:high, :]) + up_bias_ref[:, low:high]
        square = hidden * hidden
        bent = jnp.tanh(hidden * (GELU_C + (GELU_C * 0.044715) * square))
        half = 0.5 + 0.5 * bent
        active = (hidden * half).astype(BF16)
        slope = half + hidden * (0.5 - 0.5 * (bent * bent)) * (
            GELU_C + (3.0 * GELU_C * 0.044715) * square
        )
        feed += dot_nt(active, down_weight_ref[:, low:high])
        grad_active = dot_nn(grad_feed, down_weight_ref[:, low:high])
        grad_hidden = (grad_active * slope).astype(BF16)
        bias_acc[2:3, low:high] += jnp.sum(grad_hidden.astype(F32), axis=0, keepdims=True)
        grad_normed += dot_nn(grad_hidden, up_weight_ref[low:high, :])
        up_acc[:, low:high] += dot_tn(normed, grad_hidden)
        down_acc[:, low:high] += dot_tn(grad_feed, active)

    feed = deep(feed + down_bias_ref[...])
    grad_normed = deep(grad_normed)
    output_ref[...] = (middle + gate_two * feed).astype(BF16)
    grad_mod_ref[:, 3:4, :] = jnp.sum(incoming * feed, axis=1, keepdims=True)
    grad_mod_ref[:, 1:2, :] = jnp.sum(grad_normed, axis=1, keepdims=True)
    grad_mod_ref[:, 2:3, :] = jnp.sum(grad_normed * normal, axis=1, keepdims=True)
    grad_middle = incoming + normalise_back(grad_normed * scale_two, normal, inverse)
    grad_middle_ref[...] = grad_middle
    grad_branch = flat((grad_middle * gate_one).astype(BF16))
    grad_mod_ref[:, 0:1, :] = jnp.sum(grad_middle * branch, axis=1, keepdims=True)
    bias_acc[1:2, :width] += jnp.sum(grad_branch.astype(F32), axis=0, keepdims=True)
    grad_attended_ref[...] = deep(dot_nn(grad_branch, out_weight_ref[...]).astype(BF16))
    out_acc[...] += dot_tn(grad_branch, attended)

    @pl.when(step == pl.num_programs(0) - 1)
    def _():
        out_grad_ref[...] = out_acc[...].astype(BF16)
        up_grad_ref[...] = up_acc[...].T.astype(BF16)
        down_grad_ref[...] = down_acc[...].astype(BF16)
        bias_grad_ref[...] = bias_acc[...]


def attention_backward_kernel(
    qkv_ref,
    lse_ref,
    grad_attended_ref,
    normed_ref,
    grad_qkv_ref,
    weight_grad_ref,
    bias_grad_ref,
    acc,
    bias_acc,
):
    step = pl.program_id(0)
    latents, length, width = grad_attended_ref.shape
    pairs = width // (2 * HEAD_DIM)
    mask = lane_low((length, 2 * HEAD_DIM))

    @pl.when(step == 0)
    def _():
        acc[...] = jnp.zeros_like(acc)
        bias_acc[...] = jnp.zeros_like(bias_acc)

    for latent in range(latents):
        for pair in range(pairs):
            low = pair * 2 * HEAD_DIM
            high = low + 2 * HEAD_DIM
            queries = qkv_ref[latent, :, low:high]
            keys_in = qkv_ref[latent, :, width + low : width + high]
            values_in = qkv_ref[latent, :, 2 * width + low : 2 * width + high]
            grad_out = grad_attended_ref[latent, :, low:high]
            sides_q = []
            sides_k = []
            sides_v = []
            for side in range(2):
                keep = mask if side == 0 else jnp.logical_not(mask)
                keys_side = jnp.where(keep, keys_in, jnp.zeros_like(keys_in))
                values_side = jnp.where(keep, values_in, jnp.zeros_like(values_in))
                scores = dot_nt(keys_side, queries) * HEAD_DIM ** (-0.5)
                head = 2 * pair + side
                probs = jnp.exp(scores - lse_ref[latent, head : head + 1, :])
                grad_probs = dot_nt(values_side, grad_out)
                row_terms = jnp.sum(probs * grad_probs, axis=0, keepdims=True)
                grad_scores = (probs * (grad_probs - row_terms)).astype(BF16)
                sides_v.append(dot_nn(probs.astype(BF16), grad_out))
                sides_k.append(dot_nn(grad_scores, queries))
                sides_q.append(dot_tn(grad_scores, keys_in))
            grad_qkv_ref[latent, :, low:high] = (
                jnp.where(mask, sides_q[0], sides_q[1]) * HEAD_DIM ** (-0.5)
            ).astype(BF16)
            grad_qkv_ref[latent, :, width + low : width + high] = (
                jnp.where(mask, sides_k[0], sides_k[1]) * HEAD_DIM ** (-0.5)
            ).astype(BF16)
            grad_qkv_ref[latent, :, 2 * width + low : 2 * width + high] = jnp.where(
                mask, sides_v[0], sides_v[1]
            ).astype(BF16)
    grad_qkv = grad_qkv_ref[...].reshape(latents * length, 3 * width)
    bias_acc[0:1, :] += jnp.sum(grad_qkv.astype(F32), axis=0, keepdims=True)
    acc[...] += dot_tn(normed_ref[...].reshape(latents * length, width), grad_qkv)

    @pl.when(step == pl.num_programs(0) - 1)
    def _():
        weight_grad_ref[...] = acc[...].T.astype(BF16)
        bias_grad_ref[...] = bias_acc[...]


def first_norm_kernel(
    grad_qkv_ref, tokens_ref, grad_middle_ref, mod_ref, weight_ref, tokens_grad_ref, grad_mod_ref
):
    latents, length, width = tokens_ref.shape
    grad_qkv = grad_qkv_ref[...].reshape(latents * length, 3 * width)
    grad_normed_all = dot_nn(grad_qkv, weight_ref[...])
    for latent in range(latents):
        normal, inverse = normalise(tokens_ref[latent].astype(F32))
        grad_normed = grad_normed_all[latent * length : (latent + 1) * length]
        grad_mod_ref[latent, 0:1, :] = jnp.sum(grad_normed, axis=0, keepdims=True)
        grad_mod_ref[latent, 1:2, :] = jnp.sum(grad_normed * normal, axis=0, keepdims=True)
        upstream = grad_normed * (1.0 + mod_ref[latent, 1:2, :])
        tokens_grad_ref[latent] = (
            grad_middle_ref[latent] + normalise_back(upstream, normal, inverse)
        ).astype(BF16)


def each(shape, count):
    zeros = (0,) * (len(shape) - 1)
    return pl.BlockSpec((count,) + tuple(shape[1:]), lambda step: (step,) + zeros)


def whole(shape):
    zeros = (0,) * len(shape)
    return pl.BlockSpec(tuple(shape), lambda step: zeros)


def run_kernel(kernel, count, streamed_out, fixed_out, scratch, streamed, fixed, cost):
    return pl.pallas_call(
        kernel,
        grid=(streamed[0].shape[0] // count,),
        in_specs=[each(item.shape, count) for item in streamed]
        + [whole(item.shape) for item in fixed],
        out_specs=[each(item.shape, count) for item in streamed_out]
        + [whole(item.shape) for item in fixed_out],
        out_shape=list(streamed_out) + list(fixed_out),
        scratch_shapes=scratch,
        compiler_params=pltpu.CompilerParams(
            dimension_semantics=("arbitrary",), vmem_limit_bytes=VMEM_LIMIT
        ),
        cost_estimate=cost,
    )(*streamed, *fixed)


def shape_of(dims, kind):
    return jax.ShapeDtypeStruct(tuple(dims), kind)


AXES = ("dp", "rep")


class Hops:
    def __init__(self, n_dp, n_rep):
        self.sizes = {"dp": n_dp, "rep": n_rep}
        self.place = {name: lax.axis_index(name) for name in AXES}

    def bits(self, name):
        return [1 << shift for shift in range(self.sizes[name].bit_length() - 1)]

    def mine(self, name, bit):
        return (self.place[name] // bit) % 2

    def swap(self, value, name, bit):
        n_dp, n_rep = self.sizes["dp"], self.sizes["rep"]
        flip_dp, flip_rep = (bit, 0) if name == "dp" else (0, bit)
        pairs = [
            (d * n_rep + r, (d ^ flip_dp) * n_rep + (r ^ flip_rep))
            for d in range(n_dp)
            for r in range(n_rep)
        ]
        return lax.ppermute(value, AXES, pairs)

    def both(self, kept, came, name, bit, axis):
        upper = self.mine(name, bit) == 1
        return jnp.stack(
            [jnp.where(upper, came, kept), jnp.where(upper, kept, came)], axis=axis
        )

    def cut(self, value, name, bit, axis):
        here = self.mine(name, bit)
        return (
            lax.dynamic_index_in_dim(value, here, axis, keepdims=False),
            lax.dynamic_index_in_dim(value, 1 - here, axis, keepdims=False),
        )


def pad_rows(values, count):
    return jnp.pad(values, ((0, 0),) * (values.ndim - 2) + ((0, count - values.shape[-2]), (0, 0)))


def up_to(count, multiple):
    return -(-count // multiple) * multiple


def body(
    n_dp,
    n_rep,
    tokens,
    conditioning,
    ada_weight,
    ada_bias,
    qkv_weight,
    qv_bias,
    out_weight,
    out_bias,
    up_weight,
    up_bias,
    down_weight,
    down_bias,
    cotangent,
):
    latents, length, width = tokens.shape
    hidden_width = up_weight.shape[1] * n_dp
    heads = width // HEAD_DIM
    rows = latents * length
    hops = Hops(n_dp, n_rep)
    dp_bits = hops.bits("dp")
    folds = hidden_width // width

    up_rows, out_rows = up_weight.shape[1], out_weight.shape[1]
    down_shard = down_weight.T.reshape(out_rows, folds, width).transpose(1, 0, 2)
    late_shard = jnp.concatenate(
        [up_weight.T, down_shard.reshape(folds * out_rows, width), out_weight.T]
    )
    late = lax.all_gather(late_shard, "dp", axis=0)
    up_all = late[:, :up_rows].reshape(hidden_width, width)
    down_all = late[:, up_rows : up_rows + folds * out_rows]
    down_all = down_all.reshape(n_dp, folds, out_rows, width).transpose(0, 2, 1, 3)
    down_all = down_all.reshape(width, hidden_width)
    out_all = late[:, up_rows + folds * out_rows :].reshape(width, width)
    silu_low = jax.nn.silu(conditioning).astype(BF16)
    ada_shard, silu_shard, _ = lax.optimization_barrier((ada_weight.T, silu_low, late))
    ada_all = lax.all_gather(ada_shard, "dp", axis=0, tiled=True)
    silu_all = lax.all_gather(silu_shard, AXES, axis=0, tiled=True)

    qkv_rows = qkv_weight.shape[1]
    half_rows = qkv_rows // 2
    core = hops.mine("rep", 1)
    bias_shard = jnp.concatenate([qv_bias, out_bias, up_bias, down_bias])
    bias_rows = up_to(bias_shard.shape[0], width) // width
    bias_block = jnp.pad(bias_shard, (0, bias_rows * width - bias_shard.shape[0]))
    front = jnp.concatenate(
        [
            lax.dynamic_slice_in_dim(qkv_weight.T, core * half_rows, half_rows, axis=0),
            silu_low,
            bias_block.reshape(bias_rows, width),
        ]
    )
    front = pad_rows(front, up_to(front.shape[0], 8))
    for done, bit in enumerate(dp_bits[::-1]):
        front = hops.both(front, hops.swap(front, "dp", bit), "dp", bit, done)
    front = front.reshape(n_dp, -1, width)
    halves = front[:, :half_rows]
    halves = hops.both(halves, hops.swap(halves, "rep", 1), "rep", 1, 1)
    qkv_full = halves.reshape(3 * width, width)
    silu_group = front[:, half_rows : half_rows + latents].reshape(n_dp * latents, width)

    bias_all = front[:, half_rows + latents : half_rows + latents + bias_rows]
    bias_all = bias_all.reshape(n_dp, -1).astype(F32)
    cuts = [0]
    for part in (qv_bias, out_bias, up_bias, down_bias):
        cuts.append(cuts[-1] + part.shape[0])
    qv_full, out_full, up_full, down_full = (
        bias_all[:, low:high].reshape(1, -1) for low, high in zip(cuts[:-1], cuts[1:])
    )
    qkv_bias = jnp.concatenate(
        [qv_full[:, :width], jnp.zeros((1, width), F32), qv_full[:, width:]], axis=1
    )

    mod = jnp.dot(silu_group, ada_weight, preferred_element_type=F32) + ada_bias.astype(F32)
    mod = mod.reshape((2,) * len(dp_bits) + (latents, -1))
    for done, bit in enumerate(dp_bits[::-1]):
        kept, sent = hops.cut(mod, "dp", bit, done)
        mod = hops.both(kept, hops.swap(sent, "dp", bit), "dp", bit, done)
    modulation = mod.reshape(n_dp, latents, -1).transpose(1, 0, 2).reshape(latents, 6, width)

    normed, qkv, lse, attended = run_kernel(
        attention_forward_kernel,
        2,
        [
            shape_of((latents, length, width), BF16),
            shape_of((latents, length, 3 * width), BF16),
            shape_of((latents, 8 * ((heads + 7) // 8), length), F32),
            shape_of((latents, length, width), BF16),
        ],
        [],
        [],
        [tokens, modulation],
        [qkv_full, qkv_bias],
        pl.CostEstimate(
            flops=2 * rows * width * (3 * width + 2 * length),
            bytes_accessed=rows * width * 12,
            transcendentals=rows * heads * length,
        ),
    )

    (
        output,
        grad_middle,
        grad_attended,
        grad_mod_two,
        out_grad,
        up_grad,
        down_grad,
        bias_grad,
    ) = run_kernel(
        functools.partial(feed_kernel, chunk=512),
        2,
        [
            shape_of((latents, length, width), BF16),
            shape_of((latents, length, width), F32),
            shape_of((latents, length, width), BF16),
            shape_of((latents, 4, width), F32),
        ],
        [
            shape_of((width, width), BF16),
            shape_of((hidden_width, width), BF16),
            shape_of((width, hidden_width), BF16),
            shape_of((8, hidden_width), F32),
        ],
        [
            pltpu.VMEM((width, width), F32),
            pltpu.VMEM((width, hidden_width), F32),
            pltpu.VMEM((width, hidden_width), F32),
            pltpu.VMEM((8, hidden_width), F32),
        ],
        [tokens, cotangent, attended, modulation],
        [out_all, out_full, up_all, up_full, down_all, down_full],
        pl.CostEstimate(
            flops=6 * rows * width * (width + 2 * hidden_width),
            bytes_accessed=rows * width * 14,
            transcendentals=rows * hidden_width,
        ),
    )

    late_grad = jnp.concatenate(
        [
            up_grad.reshape(n_dp, up_rows, width),
            down_grad.reshape(n_dp, out_rows, folds, width)
            .transpose(0, 2, 1, 3)
            .reshape(n_dp, folds * out_rows, width),
            out_grad.reshape(n_dp, out_rows, width),
        ],
        axis=1,
    )
    late_sum = lax.psum_scatter(late_grad, "dp", scatter_dimension=0, tiled=True)
    late_sum = lax.psum(late_sum, "rep").astype(F32).reshape(-1, width)
    up_owned = late_sum[:up_rows]
    down_owned = late_sum[up_rows : up_rows + folds * out_rows]
    down_owned = down_owned.reshape(folds, out_rows, width).transpose(1, 0, 2)
    down_owned = down_owned.reshape(out_rows, hidden_width)
    out_owned = late_sum[up_rows + folds * out_rows :]

    grad_qkv, qkv_grad, qkv_bias_grad = run_kernel(
        attention_backward_kernel,
        2,
        [shape_of((latents, length, 3 * width), BF16)],
        [shape_of((3 * width, width), BF16), shape_of((8, 3 * width), F32)],
        [pltpu.VMEM((width, 3 * width), F32), pltpu.VMEM((8, 3 * width), F32)],
        [qkv, lse, grad_attended, normed],
        [],
        pl.CostEstimate(
            flops=2 * rows * width * (3 * width + 5 * length),
            bytes_accessed=rows * width * 16,
            transcendentals=rows * heads * length,
        ),
    )

    qkv_columns = qkv_bias_grad[0]
    bias_blocks = jnp.concatenate(
        [
            jnp.concatenate([qkv_columns[:width], qkv_columns[2 * width :]]).reshape(n_dp, -1),
            bias_grad[1, :width].reshape(n_dp, -1),
            bias_grad[2].reshape(n_dp, -1),
            bias_grad[0, :width].reshape(n_dp, -1),
        ],
        axis=1,
    ).astype(BF16)
    bias_part = up_to(cuts[-1], n_rep) // n_rep
    bias_blocks = jnp.pad(bias_blocks, ((0, 0), (0, bias_part * n_rep - cuts[-1])))
    bias_blocks = bias_blocks.reshape(n_dp, n_rep, 1, bias_part)
    bias_blocks = jnp.pad(bias_blocks, ((0, 0), (0, 0), (0, 0), (0, width - bias_part)))
    quarter = up_to(qkv_rows, n_rep) // n_rep
    tail_rows = up_to(quarter + 1, 8)
    blocks = pad_rows(qkv_grad.reshape(n_dp, qkv_rows, width), quarter * n_rep)
    blocks = jnp.concatenate([blocks.reshape(n_dp, n_rep, quarter, width), bias_blocks], axis=2)
    blocks = pad_rows(blocks, tail_rows)
    rep_bits = hops.bits("rep")
    total = blocks.reshape((n_dp,) + (2,) * len(rep_bits) + (tail_rows, width))
    for bit in rep_bits:
        kept, sent = hops.cut(total, "rep", bit, total.ndim - 3)
        total = kept.astype(F32) + hops.swap(sent.astype(BF16), "rep", bit).astype(F32)

    tokens_grad, grad_mod_one = run_kernel(
        first_norm_kernel,
        2,
        [shape_of((latents, length, width), BF16), shape_of((latents, 2, width), F32)],
        [],
        [],
        [grad_qkv, tokens, grad_middle, modulation],
        [qkv_full],
        pl.CostEstimate(
            flops=6 * rows * width * width, bytes_accessed=rows * width * 14, transcendentals=0
        ),
    )
    grad_modulation = jnp.concatenate([grad_mod_one, grad_mod_two], axis=1).reshape(
        latents, 6 * width
    )

    own = 6 * width // n_dp
    columns = grad_modulation.reshape(latents, n_dp, own).transpose(1, 0, 2).astype(BF16)
    columns = columns.reshape((2,) * len(dp_bits) + (latents * own,))
    total = total.reshape((2,) * len(dp_bits) + (tail_rows * width,))
    axis = len(dp_bits) - 1
    for bit in dp_bits:
        kept, sent = hops.cut(total, "dp", bit, axis)
        column_kept, column_sent = hops.cut(columns, "dp", bit, axis)
        lead = sent.shape[:axis]
        column_flat = column_sent.reshape(lead + (-1,))
        came = hops.swap(
            jnp.concatenate([sent.astype(BF16), column_flat], axis=-1), "dp", bit
        )
        total = kept.astype(F32) + came[..., : tail_rows * width].astype(F32)
        column_came = came[..., tail_rows * width :].reshape(column_kept.shape)
        columns = hops.both(column_kept, column_came, "dp", bit, axis)
        columns = jnp.moveaxis(columns, axis, columns.ndim - 2)
        axis -= 1
    order = tuple(range(len(dp_bits)))[::-1]
    columns = columns.transpose(order + (len(dp_bits),)).reshape(-1)
    final = jnp.concatenate([total.astype(BF16), columns])
    for done, bit in enumerate(rep_bits):
        final = hops.both(final, hops.swap(final, "rep", bit), "rep", bit, 0)
    final = final.reshape(n_rep, -1)
    summed = final[:, : tail_rows * width].reshape(n_rep, tail_rows, width).astype(F32)
    qkv_owned = summed[:, :quarter].reshape(-1, width)[:qkv_rows]
    bias_owned = summed[:, quarter, :bias_part].reshape(-1)
    columns = final[:, tail_rows * width :].reshape(n_rep, n_dp, latents, own)
    columns = columns.transpose(1, 0, 2, 3).reshape(n_dp * n_rep * latents, own)
    ada_grad = dot_tn(columns, silu_all)
    ada_bias_grad = jnp.sum(columns.astype(F32), axis=0)

    grad_silu = lax.dot_general(
        grad_modulation,
        ada_all.astype(F32),
        (((1,), (0,)), ((), ())),
        precision=lax.Precision.HIGHEST,
    )
    _, silu_pull = jax.vjp(jax.nn.silu, conditioning)
    condition_grad = silu_pull(grad_silu)[0]

    qv_sum, out_bias_sum, up_bias_sum, down_bias_sum = (
        bias_owned[low:high] for low, high in zip(cuts[:-1], cuts[1:])
    )
    return (
        output,
        tokens_grad,
        condition_grad,
        ada_grad.T,
        ada_bias_grad,
        qkv_owned.T,
        qv_sum,
        out_owned.T,
        out_bias_sum,
        up_owned.T,
        up_bias_sum,
        down_owned.T,
        down_bias_sum,
    )


def solution(mesh):
    return jax.shard_map(
        functools.partial(body, mesh.shape["dp"], mesh.shape["rep"]),
        mesh=mesh,
        in_specs=(
            P(("dp", "rep"), None, None),
            P(("dp", "rep"), None),
            P(None, "dp"),
            P("dp"),
            P(None, "dp"),
            P("dp"),
            P(None, "dp"),
            P("dp"),
            P(None, "dp"),
            P("dp"),
            P(None, "dp"),
            P("dp"),
            P(("dp", "rep"), None, None),
        ),
        out_specs=(
            P(("dp", "rep"), None, None),
            P(("dp", "rep"), None, None),
            P(("dp", "rep"), None),
            P(None, "dp"),
            P("dp"),
            P(None, "dp"),
            P("dp"),
            P(None, "dp"),
            P("dp"),
            P(None, "dp"),
            P("dp"),
            P(None, "dp"),
            P("dp"),
        ),
        check_vma=False,
    )
```

time: 507 us -> 406 us (0.80)
  starting transfers between devices: 170 us -> 15.6 us
  blocking collectives: 0 us -> 39.6 us
  waiting for transfers between devices: 125 us -> 146 us
  Pallas kernels: 161 us -> 143 us
  between operations: 2.01 us -> 14.7 us
    ppermute x119 -> x14, starting transfers between devices: 170 us -> 15.5 us  [swap(): return lax.ppermute(value, AXES, pairs)]
    ppermute x119 -> x14, waiting for transfers between devices: 125 us -> 48.1 us  [swap(): return lax.ppermute(value, AXES, pairs)]
    all_gather x0 -> x2, waiting for transfers between devices: none -> 47.4 us  [the longest x1 47.4 us: body(): ada_all = lax.all_gather(ada_shard, 'dp', axis=0, tiled=True)]
    all_gather x0 -> x1, blocking collectives: none -> 39.6 us  [body(): silu_all = lax.all_gather(silu_shard, AXES, axis=0, tiled=True)]
    psum x0 -> x1, waiting for transfers between devices: none -> 30 us  [body(): late_sum = lax.psum(late_sum, 'rep').astype(F32).reshape(-1, width)]
    reduce_scatter x0 -> x1, waiting for transfers between devices: none -> 20.7 us  [body(): lax.psum_scatter(late_grad, 'dp', scatter_dimension=0, tiled=True)]
    pallas_call x4, Pallas kernels: 161 us -> 143 us  [run_kernel(): pl.pallas_call(kernel, grid=(streamed[0].shape[0] // count,), in_specs=[e...]
  transfers between devices with their start and end apart: 119 -> 18, of which waited for: 53 -> 13; matrix products, arithmetic and copies ran while one was open for 7% -> 6% of each run, Pallas kernels for 9% -> 10%
where the time goes in v2:
time: 406 us; the launch traced here: 405 us
  waiting for transfers between devices  146 us (36%)
  Pallas kernels  143 us (35%)
  blocking collectives  39.6 us (10%)
  local copies, waits for them, and re-layouts  27.3 us (7%)
  starting transfers between devices  15.6 us (4%)
  other arithmetic  14.9 us (4%)
  between operations  14.7 us (4%)
  matrix products  4.31 us (1%)
    pallas_call x4, Pallas kernels, run_kernel(): pl.pallas_call(kernel, grid=(streamed[0].shape[0] // count,), in_specs=[e...  143 us
    ppermute x14, waiting for transfers between devices, swap(): return lax.ppermute(value, AXES, pairs)  48.1 us
    all_gather x1, waiting for transfers between devices, body(): ada_all = lax.all_gather(ada_shard, 'dp', axis=0, tiled=True)  47.4 us
    all_gather x1, blocking collectives, body(): silu_all = lax.all_gather(silu_shard, AXES, axis=0, tiled=True)  39.6 us
    psum x1, waiting for transfers between devices, body(): late_sum = lax.psum(late_sum, 'rep').astype(F32).reshape(-1, width)  30 us
    reduce_scatter x1, waiting for transfers between devices, body(): lax.psum_scatter(late_grad, 'dp', scatter_dimension=0, tiled=True)  20.7 us
    ppermute x14, starting transfers between devices, swap(): return lax.ppermute(value, AXES, pairs)  15.5 us
  transfers between devices with their start and end apart: 18, of which 13 were waited for; matrix products, arithmetic and copies ran while one was open for 6% of the time, Pallas kernels for 10%

profile of v2, /device:TPU:0, one launch (start us, length us, event | category | flops | bytes accessed | tf_op | source)
XLA Modules:
  0.0 405.4 jit_solution(4403594823866432490)
XLA Ops:
  8.9 4.1 %collective-permute-start = (bf16[96,384]{1,0:T(8,128)(2,1)S(1)}, bf16[96,384]{1,0:T(8,128)(2,1)S(1)}, u32[]{:S(2)}, u32[]{:S(2)}) collective-permute-start(bf16[96,384]{1,0:T(8,128)(2,1)S(1)} %fusion.19), channel_id=1, source_target_pairs={{0,16},{1,17},{2,18},{3,19},{4,20},{5,21},{6,22},{7,23},{8,24},{9,... | collective-permute-start | bytes 221192 | tf_op jit(solution)/shard_map/ppermute | solution.py:314
  17.7 4.5 %collective-permute-done.1 = bf16[2,96,384]{2,1,0:T(8,128)(2,1)S(1)} collective-permute-done((bf16[2,96,384]{2,1,0:T(8,128)(2,1)S(1)}, bf16[2,96,384]{2,1,0:T(8,128)(2,1)S(1)}, u32[]{:S(2)}, u32[]{:S(2)}) %collective-permute-start.1) | collective-permute-done | bytes 147488 | tf_op jit(solution)/shard_map/ppermute | solution.py:314
  22.3 1.8 collective-permute-start.2
  24.1 8.4 %collective-permute-done.2 = bf16[2,2,96,384]{3,2,1,0:T(8,128)(2,1)S(1)} collective-permute-done((bf16[2,2,96,384]{3,2,1,0:T(8,128)(2,1)S(1)}, bf16[2,2,96,384]{3,2,1,0:T(8,128)(2,1)S(1)}, u32[]{:S(2)}, u32[]{:S(2)}) %collective-permute-start.2) | collective-permute-done | bytes 294944 | tf_op jit(solution)/shard_map/ppermute | solution.py:314
  33.1 4.2 %collective-permute-start.3 = (f32[2,2,16,288]{3,2,1,0:T(8,128)S(1)}, f32[2,2,16,288]{3,2,1,0:T(8,128)S(1)}, u32[]{:S(2)}, u32[]{:S(2)}) collective-permute-start(f32[2,2,16,288]{3,2,1,0:T(8,128)S(1)} %dynamic-slice_bitcast_fusion), channel_id=1, source_target_pairs={{0,16},{1,17},{2,18},{3,19},{4,20},{5,21},{6,22},{7,23},{8,24},{9,... | collective-permute-start | bytes 221192 | tf_op jit(solution)/shard_map/ppermute | solution.py:314
  37.6 7.7 %collective-permute-done.3 = f32[2,2,16,288]{3,2,1,0:T(8,128)S(1)} collective-permute-done((f32[2,2,16,288]{3,2,1,0:T(8,128)S(1)}, f32[2,2,16,288]{3,2,1,0:T(8,128)S(1)}, u32[]{:S(2)}, u32[]{:S(2)}) %collective-permute-start.3) | collective-permute-done | bytes 73760 | tf_op jit(solution)/shard_map/ppermute | solution.py:314
  45.5 4.6 %collective-permute-done.4 = f32[2,2,16,288]{3,2,1,0:T(8,128)S(1)} collective-permute-done((f32[2,2,16,288]{3,2,1,0:T(8,128)S(1)}, f32[2,2,16,288]{3,2,1,0:T(8,128)S(1)}, u32[]{:S(2)}, u32[]{:S(2)}) %collective-permute-start.4) | collective-permute-done | bytes 73760 | tf_op jit(solution)/shard_map/ppermute | solution.py:314
  53.0 4.0 collective-permute-done.5
  59.2 24.4 %shard_map.228 = (bf16[16,256,384]{2,1,0:T(8,128)(2,1)}, bf16[16,256,1152]{2,1,0:T(8,128)(2,1)}, f32[16,8,256]{2,1,0:T(8,128)}, bf16[16,256,384]{2,1,0:T(8,128)(2,1)}) custom-call(bf16[16,256,384]{2,1,0:T(8,128)(2,1)} %tokens_ref.5, f32[16,6,384]{2,1,0:T(8,128)} %reshape.191.mod_ref, bf16[1152,384]{1,0:T(8,128)(2,1)} %bitcast.189, f32[1,1152]{1,0:T(1,128)} %fusion.27.bias_ref), custom_call_target="tpu_custom_call" | custom-call | flops 5234491392 | bytes 18874368 | tf_op jit(solution)/shard_map/pallas_call | solution.py:272
  83.6 2.9 fusion.30
  89.9 62.6 %shard_map.229 = (bf16[16,256,384]{2,1,0:T(8,128)(2,1)}, f32[16,256,384]{2,1,0:T(8,128)}, bf16[16,256,384]{2,1,0:T(8,128)(2,1)}, f32[16,4,384]{2,1,0:T(4,128)}, ...) custom-call(bf16[16,256,384]{2,1,0:T(8,128)(2,1)} %tokens_ref.5, ...), custom_call_target="tpu_custom_call" | custom-call | flops 32614907904 | bytes 22020096 | tf_op jit(solution)/shard_map/pallas_call | solution.py:272
  153.3 41.3 %shard_map.230 = (bf16[16,256,1152]{2,1,0:T(8,128)(2,1)}, bf16[1152,384]{1,0:T(8,128)(2,1)}, f32[8,1152]{1,0:T(8,128)}) custom-call(bf16[16,256,1152]{2,1,0:T(8,128)(2,1)} %get-tuple-element.34.qkv_ref, f32[16,8,256]{2,1,0:T(8,128)} %get-tuple-element.35.lse_ref, bf16[16,256,384]{2,1,0:T(8,128)(2,1)} %get-tuple-element.36.grad_attended_ref, ...), custom_call_target="tpu_custom_call" | custom-call | flops 7650410496 | bytes 25165824 | tf_op jit(solution)/shard_map/pallas_call | solution.py:272
  197.8 14.5 %shard_map.231 = (bf16[16,256,384]{2,1,0:T(8,128)(2,1)}, f32[16,2,384]{2,1,0:T(2,128)}) custom-call(bf16[16,256,1152]{2,1,0:T(8,128)(2,1)} %get-tuple-element.38.grad_qkv_ref, bf16[16,256,384]{2,1,0:T(8,128)(2,1)} %tokens_ref.5, f32[16,256,384]{2,1,0:T(8,128)} %get-tuple-element.39.grad_middle_ref, f32[16,6,384]{2,1,0:T(8,128)} %reshape.191.mod_ref, ...), custom_call_target="tpu_custom_call" | custom-call | flops 3623878656 | bytes 22020096 | tf_op jit(solution)/shard_map/pallas_call | solution.py:272
  216.7 2.8 reshape.218
  219.8 3.2 collective-permute-done.8
  225.6 4.9 %collective-permute-done.9 = bf16[2,2,19968]{2,1,0:T(2,128)(2,1)S(1)} collective-permute-done((bf16[2,2,19968]{2,1,0:T(2,128)(2,1)S(1)}, bf16[2,2,19968]{2,1,0:T(2,128)(2,1)S(1)}, u32[]{:S(2)}, u32[]{:S(2)}) %collective-permute-start.9) | collective-permute-done | bytes 159776 | tf_op jit(solution)/shard_map/ppermute | solution.py:314
  231.6 4.4 %collective-permute-done.10 = bf16[2,24576]{1,0:T(2,128)(2,1)S(1)} collective-permute-done((bf16[2,24576]{1,0:T(2,128)(2,1)S(1)}, bf16[2,24576]{1,0:T(2,128)(2,1)S(1)}, u32[]{:S(2)}, u32[]{:S(2)}) %collective-permute-start.10) | collective-permute-done | bytes 98336 | tf_op jit(solution)/shard_map/ppermute | solution.py:314
  236.9 5.4 %collective-permute-done.11 = bf16[33792]{0:T(1024)(128)(2,1)S(1)} collective-permute-done((bf16[33792]{0:T(1024)(128)(2,1)S(1)}, bf16[33792]{0:T(1024)(128)(2,1)S(1)}, u32[]{:S(2)}, u32[]{:S(2)}) %collective-permute-start.11) | collective-permute-done | bytes 67616 | tf_op jit(solution)/shard_map/ppermute | solution.py:314
  245.5 1.8 collective-permute-start.13
  247.4 39.6 %all_gather.15 = bf16[512,384]{1,0:T(8,128)(2,1)S(1)} all-gather(bf16[16,384]{1,0:T(8,128)(2,1)S(1)} %copy-done.9), channel_id=1, replica_groups=mesh['dp'=8,'rep'=4] {'dp','rep'}, dimensions={0}, use_global_device_ids=true | all-gather | bytes 405504 | tf_op jit(solution)/shard_map/all_gather | solution.py:377
  293.6 20.7 %reduce-scatter.2.cloned.1.call-done = bf16[1,432,384]{2,1,0:T(8,128)(2,1)} async-done(((bf16[8,432,384]{2,1,0:T(8,128)(2,1)}), bf16[1,432,384]{2,1,0:T(8,128)(2,1)}) %reduce-scatter.2.cloned.1.call-update) | async-done | bytes 331792 | tf_op jit(solution)/shard_map/reduce_scatter | solution.py:489
  314.4 47.4 %all-gather.4.cloned.1.call-done = bf16[2304,384]{1,0:T(8,128)(2,1)} async-done(((bf16[288,384]{1,0:T(8,128)(2,1)}), bf16[2304,384]{1,0:T(8,128)(2,1)}) %all-gather.4.cloned.1.call-update) | async-done | bytes 1769488 | tf_op jit(solution)/shard_map/all_gather | solution.py:376
  361.8 2.9 fusion.26
  364.7 30.0 %all-reduce.5.cloned.1.call-done = bf16[1,432,384]{2,1,0:T(8,128)(2,1)} async-done(((bf16[1,432,384]{2,1,0:T(8,128)(2,1)}), bf16[1,432,384]{2,1,0:T(8,128)(2,1)}) %all-reduce.5.cloned.1.call-update) | async-done | bytes 331792 | tf_op jit(solution)/shard_map/psum | solution.py:490
  (188 shorter events, 42.8 us)
Async XLA Ops:
  7.2 16.8 %copy-start.12 = (bf16[288]{0:T(512)(128)(2,1)S(1)}, bf16[288]{0:T(512)(128)(2,1)}, u32[]{:S(2)}) copy-start(bf16[288]{0:T(512)(128)(2,1)} %param.16) | copy-start | bytes 1732
  7.2 76.4 %all-gather.6.cloned.1.call-start = ((), (), s32[]{:S(2)}) async-start(), calls=%async_computation.4 | async-start | bytes 2985984 | tf_op jit(solution)/shard_map/all_gather | solution.py:368
  8.9 8.0 %collective-permute-start = (bf16[96,384]{1,0:T(8,128)(2,1)S(1)}, bf16[96,384]{1,0:T(8,128)(2,1)S(1)}, u32[]{:S(2)}, u32[]{:S(2)}) collective-permute-start(bf16[96,384]{1,0:T(8,128)(2,1)S(1)} %fusion.19), channel_id=1, source_target_pairs={{0,16},{1,17},{2,18},{3,19},{4,20},{5,21},{6,22},{7,23},{8,24},{9,... | collective-permute-start | bytes 221192 | tf_op jit(solution)/shard_map/ppermute | solution.py:314
  14.0 18.8 %copy-start.3 = (bf16[384,288]{0,1:T(8,128)(2,1)S(1)}, bf16[384,288]{0,1:T(8,128)(2,1)}, u32[]{:S(2)}) copy-start(bf16[384,288]{0,1:T(8,128)(2,1)} %param.15) | copy-start | bytes 663556
  15.7 298.6 %reduce-scatter.2.cloned.1.call-start = ((), (), s32[]{:S(2)}) async-start(), calls=%async_computation.2 | async-start | bytes 2985984 | tf_op jit(solution)/shard_map/reduce_scatter | solution.py:489
  17.0 5.2 %collective-permute-start.1 = (bf16[2,96,384]{2,1,0:T(8,128)(2,1)S(1)}, bf16[2,96,384]{2,1,0:T(8,128)(2,1)S(1)}, u32[]{:S(2)}, u32[]{:S(2)}) collective-permute-start(bf16[2,96,384]{2,1,0:T(8,128)(2,1)S(1)} %pad_maximum_fusion.10), channel_id=1, source_target_pairs={{0,8},{1,9},{2,10},{3,11},{4,12},{5,13},{6,14},{7,15},{8,0},{9,1},... | collective-permute-start | bytes 442376 | tf_op jit(solution)/shard_map/ppermute | solution.py:314
  22.3 10.2 %collective-permute-start.2 = (bf16[2,2,96,384]{3,2,1,0:T(8,128)(2,1)S(1)}, bf16[2,2,96,384]{3,2,1,0:T(8,128)(2,1)S(1)}, u32[]{:S(2)}, u32[]{:S(2)}) collective-permute-start(bf16[2,2,96,384]{3,2,1,0:T(8,128)(2,1)S(1)} %pad_maximum_fusion.5), channel_id=1, source_target_pairs={{0,4},{1,5},{2,6},{3,7},{4,0},{5,1},{6,2},{7,3},{8,12},{9,13},{10,... | collective-permute-start | bytes 884744 | tf_op jit(solution)/shard_map/ppermute | solution.py:314
  33.1 12.2 %collective-permute-start.3 = (f32[2,2,16,288]{3,2,1,0:T(8,128)S(1)}, f32[2,2,16,288]{3,2,1,0:T(8,128)S(1)}, u32[]{:S(2)}, u32[]{:S(2)}) collective-permute-start(f32[2,2,16,288]{3,2,1,0:T(8,128)S(1)} %dynamic-slice_bitcast_fusion), channel_id=1, source_target_pairs={{0,16},{1,17},{2,18},{3,19},{4,20},{5,21},{6,22},{7,23},{8,24},{9,... | collective-permute-start | bytes 221192 | tf_op jit(solution)/shard_map/ppermute | solution.py:314
  37.5 20.5 %collective-permute-start.6 = (bf16[8,72,384]{2,1,0:T(8,128)(2,1)S(1)}, bf16[8,72,384]{2,1,0:T(8,128)(2,1)S(1)}, u32[]{:S(2)}, u32[]{:S(2)}) collective-permute-start(bf16[8,72,384]{2,1,0:T(8,128)(2,1)S(1)} %slice.161), channel_id=1, source_target_pairs={{0,1},{1,0},{2,3},{3,2},{4,5},{5,4},{6,7},{7,6},{8,9},{9,8},{10,11... | collective-permute-start | bytes 1327112 | tf_op jit(solution)/shard_map/ppermute | solution.py:314
  45.4 4.7 %collective-permute-start.4 = (f32[2,2,16,288]{3,2,1,0:T(8,128)S(1)}, f32[2,2,16,288]{3,2,1,0:T(8,128)S(1)}, u32[]{:S(2)}, u32[]{:S(2)}) collective-permute-start(f32[2,2,16,288]{3,2,1,0:T(8,128)S(1)} %fusion.13), channel_id=1, source_target_pairs={{0,8},{1,9},{2,10},{3,11},{4,12},{5,13},{6,14},{7,15},{8,0},{9,1},... | collective-permute-start | bytes 221192 | tf_op jit(solution)/shard_map/ppermute | solution.py:314
  50.1 6.9 %collective-permute-start.5 = (f32[2,2,16,288]{3,2,1,0:T(8,128)S(1)}, f32[2,2,16,288]{3,2,1,0:T(8,128)S(1)}, u32[]{:S(2)}, u32[]{:S(2)}) collective-permute-start(f32[2,2,16,288]{3,2,1,0:T(8,128)S(1)} %bitcast.226), channel_id=1, source_target_pairs={{0,4},{1,5},{2,6},{3,7},{4,0},{5,1},{6,2},{7,3},{8,12},{9,13},{10,... | collective-permute-start | bytes 221192 | tf_op jit(solution)/shard_map/ppermute | solution.py:314
  197.7 15.8 %collective-permute-start.7 = (bf16[8,2,40,384]{3,2,0,1:T(8,128)(2,1)S(1)}, bf16[8,2,40,384]{3,2,0,1:T(8,128)(2,1)S(1)}, u32[]{:S(2)}, u32[]{:S(2)}) collective-permute-start(bf16[8,2,40,384]{3,2,0,1:T(8,128)(2,1)S(1)} %bitcast.211), channel_id=1, source_target_pairs={{0,1},{1,0},{2,3},{3,2},{4,5},{5,4},{6,7},{7,6},{8,9},{9,8},{10,11... | collective-permute-start | bytes 1474568 | tf_op jit(solution)/shard_map/ppermute | solution.py:314
  214.4 8.6 %collective-permute-start.8 = (bf16[8,40,384]{2,1,0:T(8,128)(2,1)}, bf16[8,40,384]{2,1,0:T(8,128)(2,1)}, u32[]{:S(2)}, u32[]{:S(2)}) collective-permute-start(bf16[8,40,384]{2,1,0:T(8,128)(2,1)} %fusion.2), channel_id=1, source_target_pairs={{0,2},{1,3},{2,0},{3,1},{4,6},{5,7},{6,4},{7,5},{8,10},{9,11},{10,... | collective-permute-start | bytes 737288 | tf_op jit(solution)/shard_map/ppermute | solution.py:314
  224.8 18.1 %copy-start.2 = (bf16[1536,384]{1,0:T(8,128)(2,1)S(1)}, bf16[1536,384]{1,0:T(8,128)(2,1)}, u32[]{:S(2)}) copy-start(bf16[1536,384]{1,0:T(8,128)(2,1)} %get-tuple-element.48) | copy-start | bytes 3538948
  224.8 18.1 %copy-start.7 = (bf16[384,384]{1,0:T(8,128)(2,1)S(1)}, bf16[384,384]{1,0:T(8,128)(2,1)}, u32[]{:S(2)}) copy-start(bf16[384,384]{1,0:T(8,128)(2,1)} %get-tuple-element.50) | copy-start | bytes 884740
  224.8 5.7 %collective-permute-start.9 = (bf16[2,2,19968]{2,1,0:T(2,128)(2,1)S(1)}, bf16[2,2,19968]{2,1,0:T(2,128)(2,1)S(1)}, u32[]{:S(2)}, u32[]{:S(2)}) collective-permute-start(bf16[2,2,19968]{2,1,0:T(2,128)(2,1)S(1)} %pad_maximum_fusion.9), channel_id=1, source_target_pairs={{0,4},{1,5},{2,6},{3,7},{4,0},{5,1},{6,2},{7,3},{8,12},{9,13},{10,... | collective-permute-start | bytes 479240 | tf_op jit(solution)/shard_map/ppermute | solution.py:314
  231.3 4.7 %collective-permute-start.10 = (bf16[2,24576]{1,0:T(2,128)(2,1)S(1)}, bf16[2,24576]{1,0:T(2,128)(2,1)S(1)}, u32[]{:S(2)}, u32[]{:S(2)}) collective-permute-start(bf16[2,24576]{1,0:T(2,128)(2,1)S(1)} %pad_maximum_fusion.12), channel_id=1, source_target_pairs={{0,8},{1,9},{2,10},{3,11},{4,12},{5,13},{6,14},{7,15},{8,0},{9,1},... | collective-permute-start | bytes 294920 | tf_op jit(solution)/shard_map/ppermute | solution.py:314
  236.8 5.5 %collective-permute-start.11 = (bf16[33792]{0:T(1024)(128)(2,1)S(1)}, bf16[33792]{0:T(1024)(128)(2,1)S(1)}, u32[]{:S(2)}, u32[]{:S(2)}) collective-permute-start(bf16[33792]{0:T(1024)(128)(2,1)S(1)} %pad_maximum_fusion.13), channel_id=1, source_target_pairs={{0,16},{1,17},{2,18},{3,19},{4,20},{5,21},{6,22},{7,23},{8,24},{9,... | collective-permute-start | bytes 202760 | tf_op jit(solution)/shard_map/ppermute | solution.py:314
  242.8 1.9 collective-permute-start.12
  244.7 117.1 %all-gather.4.cloned.1.call-start = ((), (), s32[]{:S(2)}) async-start(), calls=%async_computation.1 | async-start | bytes 1990656 | tf_op jit(solution)/shard_map/all_gather | solution.py:376
  245.5 41.5 %collective-permute-start.13 = (bf16[2,52224]{1,0:T(2,128)(2,1)S(1)}, bf16[2,52224]{1,0:T(2,128)(2,1)S(1)}, u32[]{:S(2)}, u32[]{:S(2)}) collective-permute-start(bf16[2,52224]{1,0:T(2,128)(2,1)S(1)} %pad_maximum_fusion.6), channel_id=1, source_target_pairs={{0,2},{1,3},{2,0},{3,1},{4,6},{5,7},{6,4},{7,5},{8,10},{9,11},{10,... | collective-permute-start | bytes 626696 | tf_op jit(solution)/shard_map/ppermute | solution.py:314
  247.4 147.3 %all-reduce.5.cloned.1.call-start = ((), (), s32[]{:S(2)}) async-start(), calls=%async_computation.3 | async-start | bytes 663552 | tf_op jit(solution)/shard_map/psum | solution.py:490
  288.4 73.4 %copy-start.11 = (f32[16,384]{1,0:T(8,128)S(1)}, f32[16,384]{1,0:T(8,128)}, u32[]{:S(2)}) copy-start(f32[16,384]{1,0:T(8,128)} %param.14) | copy-start | bytes 73732
  361.8 37.1 %copy-start.1 = (bf16[384,144]{0,1:T(8,128)(2,1)S(1)}, bf16[384,144]{0,1:T(8,128)(2,1)}, u32[]{:S(2)}) copy-start(bf16[384,144]{0,1:T(8,128)(2,1)} %param.17) | copy-start | bytes 331780
  (7 other events, 50.0 us)
Sparse Core Ops, SparseCore 0:
  15.8 60.6 all-gather.5
  244.8 69.5 reduce-scatter.1
  316.8 44.9 all-gather.3
  364.1 30.5 all-reduce.4

commit v3 on v2

v3 whole, which is shorter than its diff:
```python
import functools

import jax
import jax.numpy as jnp
from jax import lax
from jax.experimental import pallas as pl
from jax.experimental.pallas import tpu as pltpu
from jax.sharding import PartitionSpec as P

HEAD_DIM = 64
EPS = 1e-06
GELU_C = 0.7978845608028654
VMEM_LIMIT = 56 * 1024 * 1024
F32 = jnp.float32
BF16 = jnp.bfloat16


def dot_nn(left, right):
    return lax.dot_general(left, right, (((1,), (0,)), ((), ())), preferred_element_type=F32)


def dot_nt(left, right):
    return lax.dot_general(left, right, (((1,), (1,)), ((), ())), preferred_element_type=F32)


def dot_tn(left, right):
    return lax.dot_general(left, right, (((0,), (0,)), ((), ())), preferred_element_type=F32)


def normalise(values):
    average = jnp.mean(values, axis=-1, keepdims=True)
    centred = values - average
    spread = jnp.mean(centred * centred, axis=-1, keepdims=True)
    inverse = lax.rsqrt(spread + EPS)
    return centred * inverse, inverse


def normalise_back(upstream, normal, inverse):
    first = jnp.mean(upstream, axis=-1, keepdims=True)
    second = jnp.mean(upstream * normal, axis=-1, keepdims=True)
    return inverse * (upstream - first - normal * second)


def beside(left, right):
    return jnp.concatenate([left, right], axis=1)


def attention_forward_kernel(
    tokens_ref, mod_ref, weight_ref, bias_ref, normed_ref, qkv_ref, lse_ref, attended_ref
):
    latents, length, width = tokens_ref.shape
    bias = beside(bias_ref[...], bias_ref[...])
    blank = jnp.zeros((HEAD_DIM, length), BF16)
    for latent in range(latents):
        normal, _ = normalise(tokens_ref[latent].astype(F32))
        normed = normal * (1.0 + mod_ref[latent, 1:2, :]) + mod_ref[latent, 0:1, :]
        normed = normed.astype(BF16)
        normed_ref[latent] = normed
        qkv = (dot_nt(weight_ref[...], normed) + bias).astype(BF16)
        qkv_ref[latent] = qkv
        keys_in = qkv[width : 2 * width].T
        for head in range(width // HEAD_DIM):
            low = head * HEAD_DIM
            high = low + HEAD_DIM
            pair = low - low % (2 * HEAD_DIM)
            queries = qkv[low:high]
            queries = jnp.concatenate([blank, queries] if low > pair else [queries, blank])
            scores = dot_nn(keys_in[:, pair : pair + 2 * HEAD_DIM], queries) * HEAD_DIM ** (-0.5)
            highest = jnp.max(scores, axis=0, keepdims=True)
            shifted = jnp.exp(scores - highest)
            total = jnp.sum(shifted, axis=0, keepdims=True)
            probs = (shifted * (1.0 / total)).astype(BF16)
            lse_ref[latent, head : head + 1, :] = highest + jnp.log(total)
            values_in = qkv[2 * width + low : 2 * width + high]
            attended_ref[latent, low:high, :] = dot_nn(values_in, probs).astype(BF16)


def feed_kernel(
    tokens_ref,
    cotangent_ref,
    attended_ref,
    mod_ref,
    out_weight_ref,
    out_bias_ref,
    up_weight_ref,
    up_bias_ref,
    down_weight_ref,
    down_bias_ref,
    output_ref,
    grad_middle_ref,
    grad_attended_ref,
    grad_mod_ref,
    out_grad_ref,
    up_grad_ref,
    down_grad_ref,
    out_bias_grad_ref,
    up_bias_grad_ref,
    down_bias_grad_ref,
    out_acc,
    up_acc,
    down_acc,
    bias_acc,
    out_back,
    up_back,
    down_back,
    active_all,
    grad_hidden_all,
    *,
    chunk,
):
    step = pl.program_id(0)
    latents, length, width = tokens_ref.shape
    hidden_width = up_weight_ref.shape[0]

    @pl.when(step == 0)
    def _():
        out_acc[...] = jnp.zeros_like(out_acc)
        up_acc[...] = jnp.zeros_like(up_acc)
        down_acc[...] = jnp.zeros_like(down_acc)
        bias_acc[...] = jnp.zeros_like(bias_acc)
        out_back[...] = out_weight_ref[...].T
        up_back[...] = up_weight_ref[...].T
        down_back[...] = down_weight_ref[...].T

    kept = []
    for latent in range(latents):
        gate_one = mod_ref[latent, 2:3, :]
        shift_two = mod_ref[latent, 3:4, :]
        scale_two = 1.0 + mod_ref[latent, 4:5, :]
        gate_two = mod_ref[latent, 5:6, :]
        branch = dot_nn(out_weight_ref[...], attended_ref[latent]).T + out_bias_ref[...]
        middle = tokens_ref[latent].astype(F32) + gate_one * branch
        normal, inverse = normalise(middle)
        normed = (normal * scale_two + shift_two).astype(BF16)
        incoming = cotangent_ref[latent].astype(F32)
        grad_feed = (incoming * gate_two).astype(BF16)
        bias_acc[0:1, :] += jnp.sum(grad_feed.astype(F32), axis=0, keepdims=True)
        kept.append((gate_one, scale_two, gate_two, branch, middle, normal, inverse, normed, incoming, grad_feed))

    for latent in range(latents):
        normed, grad_feed = kept[latent][7], kept[latent][9]
        here = slice(latent * length, (latent + 1) * length)
        for low in range(0, hidden_width, chunk):
            high = low + chunk
            bias = up_bias_ref[low:high, :]
            hidden = dot_nt(up_weight_ref[low:high, :], normed) + beside(bias, bias)
            grad_active = dot_nt(down_back[low:high, :], grad_feed)
            square = hidden * hidden
            bent = jnp.tanh(hidden * (GELU_C + (GELU_C * 0.044715) * square))
            half = 0.5 + 0.5 * bent
            active_all[low:high, here] = (hidden * half).astype(BF16)
            slope = half + hidden * (0.5 - 0.5 * (bent * bent)) * (
                GELU_C + (3.0 * GELU_C * 0.044715) * square
            )
            grad_hidden_all[low:high, here] = (grad_active * slope).astype(BF16)

    grad_branches = []
    for latent in range(latents):
        gate_one, scale_two, gate_two, branch, middle, normal, inverse, _, incoming, _ = kept[latent]
        here = slice(latent * length, (latent + 1) * length)
        feed = dot_nn(down_weight_ref[...], active_all[:, here]).T + down_bias_ref[...]
        grad_normed = dot_nn(up_back[...], grad_hidden_all[:, here]).T
        output_ref[latent] = (middle + gate_two * feed).astype(BF16)
        grad_mod_ref[latent, 3:4, :] = jnp.sum(incoming * feed, axis=0, keepdims=True)
        grad_mod_ref[latent, 1:2, :] = jnp.sum(grad_normed, axis=0, keepdims=True)
        grad_mod_ref[latent, 2:3, :] = jnp.sum(grad_normed * normal, axis=0, keepdims=True)
        grad_middle = incoming + normalise_back(grad_normed * scale_two, normal, inverse)
        grad_middle_ref[latent] = grad_middle
        grad_branch = (grad_middle * gate_one).astype(BF16)
        grad_branches.append(grad_branch)
        grad_mod_ref[latent, 0:1, :] = jnp.sum(grad_middle * branch, axis=0, keepdims=True)
        bias_acc[1:2, :] += jnp.sum(grad_branch.astype(F32), axis=0, keepdims=True)
        grad_attended_ref[latent] = dot_nt(out_back[...], grad_branch).astype(BF16)

    normed_all = jnp.concatenate([entry[7] for entry in kept])
    ones = jnp.ones((latents * length, 128), BF16)
    grad_feed_all = jnp.concatenate([entry[9] for entry in kept])
    attended_all = jnp.concatenate([attended_ref[latent] for latent in range(latents)], axis=1)
    up_acc[...] += dot_nn(grad_hidden_all[...], beside(normed_all, ones))
    down_acc[...] += dot_nn(active_all[...], grad_feed_all)
    out_acc[...] += dot_nn(attended_all, jnp.concatenate(grad_branches))

    @pl.when(step == pl.num_programs(0) - 1)
    def _():
        out_grad_ref[...] = out_acc[...].T.astype(BF16)
        up_grad_ref[...] = up_acc[:, :width].astype(BF16)
        down_grad_ref[...] = down_acc[...].T.astype(BF16)
        up_bias_grad_ref[...] = up_acc[:, width:]
        down_bias_grad_ref[...] = bias_acc[0:1, :]
        out_bias_grad_ref[...] = bias_acc[1:2, :]


def attention_backward_kernel(
    qkv_ref,
    lse_ref,
    grad_attended_ref,
    normed_ref,
    grad_qkv_ref,
    weight_grad_ref,
    bias_grad_ref,
    acc,
):
    step = pl.program_id(0)
    latents, length, width = normed_ref.shape
    blank = jnp.zeros((HEAD_DIM, length), BF16)

    @pl.when(step == 0)
    def _():
        acc[...] = jnp.zeros_like(acc)

    for latent in range(latents):
        keys_all = qkv_ref[latent, width : 2 * width, :].T
        values_all = qkv_ref[latent, 2 * width : 3 * width, :].T
        for head in range(width // HEAD_DIM):
            low = head * HEAD_DIM
            high = low + HEAD_DIM
            pair = low - low % (2 * HEAD_DIM)
            queries = qkv_ref[latent, low:high, :]
            keys_in = qkv_ref[latent, width + low : width + high, :]
            grad_out = grad_attended_ref[latent, low:high, :]
            first = low == pair
            queries_wide = jnp.concatenate([queries, blank] if first else [blank, queries])
            grad_out_wide = jnp.concatenate([grad_out, blank] if first else [blank, grad_out])
            scores = dot_nn(keys_all[:, pair : pair + 2 * HEAD_DIM], queries_wide)
            grad_probs = dot_nn(values_all[:, pair : pair + 2 * HEAD_DIM], grad_out_wide)
            probs = jnp.exp(scores * HEAD_DIM ** (-0.5) - lse_ref[latent, head : head + 1, :])
            row_terms = jnp.sum(probs * grad_probs, axis=0, keepdims=True)
            grad_scores = (probs * (grad_probs - row_terms)).astype(BF16)
            grad_qkv_ref[latent, low:high, :] = (
                dot_nn(keys_in, grad_scores) * HEAD_DIM ** (-0.5)
            ).astype(BF16)
            grad_qkv_ref[latent, width + low : width + high, :] = (
                dot_nt(queries, grad_scores) * HEAD_DIM ** (-0.5)
            ).astype(BF16)
            grad_qkv_ref[latent, 2 * width + low : 2 * width + high, :] = dot_nt(
                grad_out, probs.astype(BF16)
            ).astype(BF16)
    grad_qkv = jnp.concatenate([grad_qkv_ref[latent] for latent in range(latents)], axis=1)
    normed = normed_ref[...].reshape(latents * length, width)
    acc[...] += dot_nn(grad_qkv, beside(normed, jnp.ones((latents * length, 128), BF16)))

    @pl.when(step == pl.num_programs(0) - 1)
    def _():
        weight_grad_ref[...] = acc[:, :width].astype(BF16)
        bias_grad_ref[...] = acc[:, width:]


def first_norm_kernel(
    grad_qkv_ref,
    tokens_ref,
    grad_middle_ref,
    mod_ref,
    weight_ref,
    tokens_grad_ref,
    grad_mod_ref,
    weight_back,
):
    latents = tokens_ref.shape[0]

    @pl.when(pl.program_id(0) == 0)
    def _():
        weight_back[...] = weight_ref[...].T

    for latent in range(latents):
        normal, inverse = normalise(tokens_ref[latent].astype(F32))
        grad_normed = dot_nn(weight_back[...], grad_qkv_ref[latent]).T
        grad_mod_ref[latent, 0:1, :] = jnp.sum(grad_normed, axis=0, keepdims=True)
        grad_mod_ref[latent, 1:2, :] = jnp.sum(grad_normed * normal, axis=0, keepdims=True)
        upstream = grad_normed * (1.0 + mod_ref[latent, 1:2, :])
        tokens_grad_ref[latent] = (
            grad_middle_ref[latent] + normalise_back(upstream, normal, inverse)
        ).astype(BF16)


def each(shape, count):
    zeros = (0,) * (len(shape) - 1)
    return pl.BlockSpec((count,) + tuple(shape[1:]), lambda step: (step,) + zeros)


def whole(shape):
    zeros = (0,) * len(shape)
    return pl.BlockSpec(tuple(shape), lambda step: zeros)


def run_kernel(kernel, count, streamed_out, fixed_out, scratch, streamed, fixed, cost):
    return pl.pallas_call(
        kernel,
        grid=(streamed[0].shape[0] // count,),
        in_specs=[each(item.shape, count) for item in streamed]
        + [whole(item.shape) for item in fixed],
        out_specs=[each(item.shape, count) for item in streamed_out]
        + [whole(item.shape) for item in fixed_out],
        out_shape=list(streamed_out) + list(fixed_out),
        scratch_shapes=scratch,
        compiler_params=pltpu.CompilerParams(
            dimension_semantics=("arbitrary",), vmem_limit_bytes=VMEM_LIMIT
        ),
        cost_estimate=cost,
    )(*streamed, *fixed)


def shape_of(dims, kind):
    return jax.ShapeDtypeStruct(tuple(dims), kind)


AXES = ("dp", "rep")


class Hops:
    def __init__(self, n_dp, n_rep):
        self.sizes = {"dp": n_dp, "rep": n_rep}
        self.place = {name: lax.axis_index(name) for name in AXES}

    def bits(self, name):
        return [1 << shift for shift in range(self.sizes[name].bit_length() - 1)]

    def mine(self, name, bit):
        return (self.place[name] // bit) % 2

    def swap(self, value, name, bit):
        n_dp, n_rep = self.sizes["dp"], self.sizes["rep"]
        flip_dp, flip_rep = (bit, 0) if name == "dp" else (0, bit)
        pairs = [
            (d * n_rep + r, (d ^ flip_dp) * n_rep + (r ^ flip_rep))
            for d in range(n_dp)
            for r in range(n_rep)
        ]
        return lax.ppermute(value, AXES, pairs)

    def both(self, kept, came, name, bit, axis):
        upper = self.mine(name, bit) == 1
        return jnp.stack(
            [jnp.where(upper, came, kept), jnp.where(upper, kept, came)], axis=axis
        )

    def cut(self, value, name, bit, axis):
        here = self.mine(name, bit)
        return (
            lax.dynamic_index_in_dim(value, here, axis, keepdims=False),
            lax.dynamic_index_in_dim(value, 1 - here, axis, keepdims=False),
        )


def pad_rows(values, count):
    return jnp.pad(values, ((0, 0),) * (values.ndim - 2) + ((0, count - values.shape[-2]), (0, 0)))


def up_to(count, multiple):
    return -(-count // multiple) * multiple


def body(
    n_dp,
    n_rep,
    tokens,
    conditioning,
    ada_weight,
    ada_bias,
    qkv_weight,
    qv_bias,
    out_weight,
    out_bias,
    up_weight,
    up_bias,
    down_weight,
    down_bias,
    cotangent,
):
    latents, length, width = tokens.shape
    hidden_width = up_weight.shape[1] * n_dp
    heads = width // HEAD_DIM
    rows = latents * length
    hops = Hops(n_dp, n_rep)
    dp_bits = hops.bits("dp")
    folds = hidden_width // width

    up_rows, out_rows = up_weight.shape[1], out_weight.shape[1]
    down_shard = down_weight.T.reshape(out_rows, folds, width).transpose(1, 0, 2)
    late_shard = jnp.concatenate(
        [up_weight.T, down_shard.reshape(folds * out_rows, width), out_weight.T]
    )
    late = lax.all_gather(late_shard, "dp", axis=0)
    up_all = late[:, :up_rows].reshape(hidden_width, width)
    down_all = late[:, up_rows : up_rows + folds * out_rows]
    down_all = down_all.reshape(n_dp, folds, out_rows, width).transpose(0, 2, 1, 3)
    down_all = down_all.reshape(width, hidden_width)
    out_all = late[:, up_rows + folds * out_rows :].reshape(width, width)
    silu_low = jax.nn.silu(conditioning).astype(BF16)
    ada_shard, _ = lax.optimization_barrier((ada_weight.T, late))
    ada_all = lax.all_gather(ada_shard, "dp", axis=0, tiled=True)

    qkv_rows = qkv_weight.shape[1]
    half_rows = qkv_rows // 2
    core = hops.mine("rep", 1)
    bias_shard = jnp.concatenate([qv_bias, out_bias, up_bias, down_bias])
    bias_rows = up_to(bias_shard.shape[0], width) // width
    bias_block = jnp.pad(bias_shard, (0, bias_rows * width - bias_shard.shape[0]))
    front = jnp.concatenate(
        [
            lax.dynamic_slice_in_dim(qkv_weight.T, core * half_rows, half_rows, axis=0),
            silu_low,
            bias_block.reshape(bias_rows, width),
        ]
    )
    front = pad_rows(front, up_to(front.shape[0], 8))
    for done, bit in enumerate(dp_bits[::-1]):
        front = hops.both(front, hops.swap(front, "dp", bit), "dp", bit, done)
    front = front.reshape(n_dp, -1, width)
    front = front[:, : half_rows + latents + bias_rows]
    silu_group = front[:, half_rows : half_rows + latents].reshape(n_dp * latents, width)
    halves = front[:, : half_rows + latents]
    halves = hops.both(halves, hops.swap(halves, "rep", 1), "rep", 1, 0)
    qkv_full = halves[:, :, :half_rows].transpose(1, 0, 2, 3).reshape(3 * width, width)
    silu_all = halves[:, :, half_rows:]
    for bit in hops.bits("rep")[1:]:
        silu_all = hops.both(silu_all, hops.swap(silu_all, "rep", bit), "rep", bit, 0)
    silu_all = silu_all.reshape(n_rep, n_dp, latents, width).reshape(-1, width)

    bias_all = front[:, half_rows + latents : half_rows + latents + bias_rows]
    bias_all = bias_all.reshape(n_dp, -1).astype(F32)
    cuts = [0]
    for part in (qv_bias, out_bias, up_bias, down_bias):
        cuts.append(cuts[-1] + part.shape[0])
    qv_full, out_full, up_full, down_full = (
        bias_all[:, low:high].reshape(1, -1) for low, high in zip(cuts[:-1], cuts[1:])
    )
    qkv_bias = jnp.concatenate(
        [qv_full[:, :width], jnp.zeros((1, width), F32), qv_full[:, width:]], axis=1
    )
    qkv_bias = jnp.broadcast_to(qkv_bias.reshape(-1, 1), (3 * width, 128))
    up_full = jnp.broadcast_to(up_full.reshape(-1, 1), (hidden_width, 128))

    mod = jnp.dot(silu_group, ada_weight, preferred_element_type=F32) + ada_bias.astype(F32)
    mod = mod.reshape((2,) * len(dp_bits) + (latents, -1))
    for done, bit in enumerate(dp_bits[::-1]):
        kept, sent = hops.cut(mod, "dp", bit, done)
        mod = hops.both(kept, hops.swap(sent, "dp", bit), "dp", bit, done)
    modulation = mod.reshape(n_dp, latents, -1).transpose(1, 0, 2).reshape(latents, 6, width)

    normed, qkv, lse, attended = run_kernel(
        attention_forward_kernel,
        2,
        [
            shape_of((latents, length, width), BF16),
            shape_of((latents, 3 * width, length), BF16),
            shape_of((latents, 8 * ((heads + 7) // 8), length), F32),
            shape_of((latents, width, length), BF16),
        ],
        [],
        [],
        [tokens, modulation],
        [qkv_full, qkv_bias],
        pl.CostEstimate(
            flops=2 * rows * width * (3 * width + 2 * length),
            bytes_accessed=rows * width * 12,
            transcendentals=rows * heads * length,
        ),
    )

    (
        output,
        grad_middle,
        grad_attended,
        grad_mod_two,
        out_grad,
        up_grad,
        down_grad,
        out_bias_grad,
        up_bias_grad,
        down_bias_grad,
    ) = run_kernel(
        functools.partial(feed_kernel, chunk=512),
        2,
        [
            shape_of((latents, length, width), BF16),
            shape_of((latents, length, width), F32),
            shape_of((latents, width, length), BF16),
            shape_of((latents, 4, width), F32),
        ],
        [
            shape_of((width, width), BF16),
            shape_of((hidden_width, width), BF16),
            shape_of((width, hidden_width), BF16),
            shape_of((1, width), F32),
            shape_of((hidden_width, 128), F32),
            shape_of((1, width), F32),
        ],
        [
            pltpu.VMEM((width, width), F32),
            pltpu.VMEM((hidden_width, width + 128), F32),
            pltpu.VMEM((hidden_width, width), F32),
            pltpu.VMEM((8, width), F32),
            pltpu.VMEM((width, width), BF16),
            pltpu.VMEM((width, hidden_width), BF16),
            pltpu.VMEM((hidden_width, width), BF16),
            pltpu.VMEM((hidden_width, 2 * length), BF16),
            pltpu.VMEM((hidden_width, 2 * length), BF16),
        ],
        [tokens, cotangent, attended, modulation],
        [out_all, out_full, up_all, up_full, down_all, down_full],
        pl.CostEstimate(
            flops=6 * rows * width * (width + 2 * hidden_width),
            bytes_accessed=rows * width * 14,
            transcendentals=rows * hidden_width,
        ),
    )

    late_grad = jnp.concatenate(
        [
            up_grad.reshape(n_dp, up_rows, width),
            down_grad.reshape(n_dp, out_rows, folds, width)
            .transpose(0, 2, 1, 3)
            .reshape(n_dp, folds * out_rows, width),
            out_grad.reshape(n_dp, out_rows, width),
        ],
        axis=1,
    )
    late_sum = lax.psum_scatter(late_grad, "dp", scatter_dimension=0, tiled=True)
    late_sum = late_sum.reshape(-1, width)

    normed, ada_all = lax.optimization_barrier((normed, ada_all))
    grad_qkv, qkv_grad, qkv_bias_grad = run_kernel(
        attention_backward_kernel,
        2,
        [shape_of((latents, 3 * width, length), BF16)],
        [shape_of((3 * width, width), BF16), shape_of((3 * width, 128), F32)],
        [pltpu.VMEM((3 * width, width + 128), F32)],
        [qkv, lse, grad_attended, normed],
        [],
        pl.CostEstimate(flops=1, bytes_accessed=1, transcendentals=0),
    )

    qkv_columns = qkv_bias_grad[:, 0]
    bias_blocks = jnp.concatenate(
        [
            jnp.concatenate([qkv_columns[:width], qkv_columns[2 * width :]]).reshape(n_dp, -1),
            out_bias_grad.reshape(n_dp, -1),
            up_bias_grad[:, 0].reshape(n_dp, -1),
            down_bias_grad.reshape(n_dp, -1),
        ],
        axis=1,
    ).astype(BF16)
    bias_part = cuts[-1] // 2
    bias_blocks = bias_blocks.reshape(n_dp, 2, 1, bias_part)
    tail_rows = up_to(half_rows + 1, 8)
    bias_blocks = jnp.pad(
        bias_blocks,
        ((0, 0), (0, 0), (0, tail_rows - half_rows - 1), (0, width - bias_part)),
    )
    blocks = jnp.concatenate([qkv_grad.reshape(n_dp, 2, half_rows, width), bias_blocks], axis=2)
    kept, sent = hops.cut(blocks, "rep", 1, 1)
    total = kept.astype(F32) + hops.swap(sent, "rep", 1).astype(F32)

    tokens_grad, grad_mod_one = run_kernel(
        first_norm_kernel,
        2,
        [shape_of((latents, length, width), BF16), shape_of((latents, 2, width), F32)],
        [],
        [pltpu.VMEM((width, 3 * width), BF16)],
        [grad_qkv, tokens, grad_middle, modulation],
        [qkv_full],
        pl.CostEstimate(flops=1, bytes_accessed=1, transcendentals=0),
    )
    grad_modulation = jnp.concatenate([grad_mod_one, grad_mod_two], axis=1).reshape(
        latents, 6 * width
    )

    own = 6 * width // n_dp
    columns = grad_modulation.reshape(latents, n_dp, own).transpose(1, 0, 2).astype(BF16)
    columns = jnp.pad(columns, ((0, 0), (0, 0), (0, up_to(own, width) - own)))
    columns = columns.reshape((2,) * len(dp_bits) + (latents, width))
    total = total.reshape((2,) * len(dp_bits) + (tail_rows, width))
    axis = len(dp_bits) - 1
    for bit in dp_bits:
        kept, sent = hops.cut(total, "dp", bit, axis)
        column_kept, column_sent = hops.cut(columns, "dp", bit, axis)
        lead = sent.shape[:axis]
        sources = column_sent.shape[axis:-2]
        came = hops.swap(
            jnp.concatenate(
                [sent.astype(BF16), column_sent.reshape(lead + (-1, width))], axis=-2
            ),
            "dp",
            bit,
        )
        total = kept.astype(F32) + came[..., :tail_rows, :].astype(F32)
        column_came = came[..., tail_rows:, :].reshape(lead + sources + (latents, width))
        columns = hops.both(column_kept, column_came, "dp", bit, axis)
        axis -= 1
    columns = columns.reshape(n_dp * latents, width)

    qkv_total = total.astype(BF16)
    end = tail_rows + late_sum.shape[0]
    for bit in hops.bits("rep")[1:]:
        sums = jnp.concatenate([qkv_total, late_sum])
        came = hops.swap(jnp.concatenate([sums, columns]), "rep", bit)
        sums = (sums.astype(F32) + came[:end].astype(F32)).astype(BF16)
        qkv_total, late_sum = sums[:tail_rows], sums[tail_rows:]
        columns = hops.both(columns, came[end:], "rep", bit, 0).reshape(-1, width)
    came = hops.swap(jnp.concatenate([qkv_total, late_sum, columns]), "rep", 1)
    qkv_total = hops.both(qkv_total, came[:tail_rows], "rep", 1, 0).astype(F32)
    late_sum = late_sum.astype(F32) + came[tail_rows:end].astype(F32)
    columns = hops.both(columns, came[end:], "rep", 1, 0)
    columns = columns.reshape(2, n_rep // 2, n_dp * latents, width)[..., :own]
    columns = columns.transpose(1, 0, 2, 3).reshape(-1, own)
    qkv_owned = qkv_total[:, :half_rows].reshape(qkv_rows, width)
    bias_owned = qkv_total[:, half_rows, :bias_part].reshape(-1)
    up_owned = late_sum[:up_rows]
    down_owned = late_sum[up_rows : up_rows + folds * out_rows]
    down_owned = down_owned.reshape(folds, out_rows, width).transpose(1, 0, 2)
    down_owned = down_owned.reshape(out_rows, hidden_width)
    out_owned = late_sum[up_rows + folds * out_rows :]
    ada_grad = dot_tn(columns, silu_all)
    ada_bias_grad = jnp.sum(columns.astype(F32), axis=0)

    grad_silu = lax.dot_general(
        grad_modulation,
        ada_all.astype(F32),
        (((1,), (0,)), ((), ())),
        precision=lax.Precision.HIGHEST,
    )
    _, silu_pull = jax.vjp(jax.nn.silu, conditioning)
    condition_grad = silu_pull(grad_silu)[0]

    qv_sum, out_bias_sum, up_bias_sum, down_bias_sum = (
        bias_owned[low:high] for low, high in zip(cuts[:-1], cuts[1:])
    )
    return (
        output,
        tokens_grad,
        condition_grad,
        ada_grad.T,
        ada_bias_grad,
        qkv_owned.T,
        qv_sum,
        out_owned.T,
        out_bias_sum,
        up_owned.T,
        up_bias_sum,
        down_owned.T,
        down_bias_sum,
    )


def solution(mesh):
    return jax.shard_map(
        functools.partial(body, mesh.shape["dp"], mesh.shape["rep"]),
        mesh=mesh,
        in_specs=(
            P(("dp", "rep"), None, None),
            P(("dp", "rep"), None),
            P(None, "dp"),
            P("dp"),
            P(None, "dp"),
            P("dp"),
            P(None, "dp"),
            P("dp"),
            P(None, "dp"),
            P("dp"),
            P(None, "dp"),
            P("dp"),
            P(("dp", "rep"), None, None),
        ),
        out_specs=(
            P(("dp", "rep"), None, None),
            P(("dp", "rep"), None, None),
            P(("dp", "rep"), None),
            P(None, "dp"),
            P("dp"),
            P(None, "dp"),
            P("dp"),
            P(None, "dp"),
            P("dp"),
            P(None, "dp"),
            P("dp"),
            P(None, "dp"),
            P("dp"),
        ),
        check_vma=False,
    )
```

time: 406 us -> 312 us (0.77)
  waiting for transfers between devices: 146 us -> 60.4 us
  blocking collectives: 39.6 us -> 0 us
  Pallas kernels: 143 us -> 165 us
  starting transfers between devices: 15.6 us -> 30.1 us
    all_gather x1, waiting for transfers between devices: 47.4 us -> 0.01 us  [body(): ada_all = lax.all_gather(ada_shard, 'dp', axis=0, tiled=True)]
    all_gather x1 -> x0, blocking collectives: 39.6 us -> none  [body(): silu_all = lax.all_gather(silu_shard, AXES, axis=0, tiled=True)]
    psum x1 -> x0, waiting for transfers between devices: 30 us -> none  [body(): late_sum = lax.psum(late_sum, 'rep').astype(F32).reshape(-1, width)]
    pallas_call x4, Pallas kernels: 143 us -> 165 us  [run_kernel(): pl.pallas_call(kernel, grid=(streamed[0].shape[0] // count,), in_specs=[e...]
    reduce_scatter x1, waiting for transfers between devices: 20.7 us -> 0.02 us  [body(): lax.psum_scatter(late_grad, 'dp', scatter_dimension=0, tiled=True)]
    ppermute x14, starting transfers between devices: 15.5 us -> 29.8 us  [swap(): return lax.ppermute(value, AXES, pairs)]
    ppermute x14, waiting for transfers between devices: 48.1 us -> 60.3 us  [swap(): return lax.ppermute(value, AXES, pairs)]
  transfers between devices with their start and end apart: 18 -> 17, of which waited for: 13 -> 11; matrix products, arithmetic and copies ran while one was open for 6% -> 7% of each run, Pallas kernels for 10% -> 53%
where the time goes in v3:
time: 312 us; the launch traced here: 311 us
  Pallas kernels  165 us (53%)
  waiting for transfers between devices  60.4 us (19%)
  starting transfers between devices  30.1 us (10%)
  local copies, waits for them, and re-layouts  25.4 us (8%)
  between operations  14.5 us (5%)
  other arithmetic  13.1 us (4%)
    pallas_call x4, Pallas kernels, run_kernel(): pl.pallas_call(kernel, grid=(streamed[0].shape[0] // count,), in_specs=[e...  165 us
    ppermute x14, waiting for transfers between devices, swap(): return lax.ppermute(value, AXES, pairs)  60.3 us
    ppermute x14, starting transfers between devices, swap(): return lax.ppermute(value, AXES, pairs)  29.8 us
  transfers between devices with their start and end apart: 17, of which 11 were waited for; matrix products, arithmetic and copies ran while one was open for 7% of the time, Pallas kernels for 53%

profile of v3, /device:TPU:0, one launch (start us, length us, event | category | flops | bytes accessed | tf_op | source)
XLA Modules:
  0.0 311.5 jit_solution(14240913441764835378)
XLA Ops:
  11.6 4.1 %collective-permute-start = (bf16[96,384]{1,0:T(8,128)(2,1)S(1)}, bf16[96,384]{1,0:T(8,128)(2,1)S(1)}, u32[]{:S(2)}, u32[]{:S(2)}) collective-permute-start(bf16[96,384]{1,0:T(8,128)(2,1)S(1)} %fusion.23), channel_id=1, source_target_pairs={{0,16},{1,17},{2,18},{3,19},{4,20},{5,21},{6,22},{7,23},{8,24},{9,... | collective-permute-start | bytes 221192 | tf_op jit(solution)/shard_map/ppermute | solution.py:328
  15.7 3.9 %collective-permute-done = bf16[96,384]{1,0:T(8,128)(2,1)S(1)} collective-permute-done((bf16[96,384]{1,0:T(8,128)(2,1)S(1)}, bf16[96,384]{1,0:T(8,128)(2,1)S(1)}, u32[]{:S(2)}, u32[]{:S(2)}) %collective-permute-start) | collective-permute-done | bytes 73760 | tf_op jit(solution)/shard_map/ppermute | solution.py:328
  20.4 7.3 %collective-permute-done.1 = bf16[2,96,384]{2,1,0:T(8,128)(2,1)S(1)} collective-permute-done((bf16[2,96,384]{2,1,0:T(8,128)(2,1)S(1)}, bf16[2,96,384]{2,1,0:T(8,128)(2,1)S(1)}, u32[]{:S(2)}, u32[]{:S(2)}) %collective-permute-start.1) | collective-permute-done | bytes 147488 | tf_op jit(solution)/shard_map/ppermute | solution.py:328
  27.8 2.3 collective-permute-start.2
  30.1 4.7 %collective-permute-done.2 = bf16[2,2,96,384]{3,2,1,0:T(8,128)(2,1)S(1)} collective-permute-done((bf16[2,2,96,384]{3,2,1,0:T(8,128)(2,1)S(1)}, bf16[2,2,96,384]{3,2,1,0:T(8,128)(2,1)S(1)}, u32[]{:S(2)}, u32[]{:S(2)}) %collective-permute-start.2) | collective-permute-done | bytes 294944 | tf_op jit(solution)/shard_map/ppermute | solution.py:328
  35.4 4.8 %collective-permute-start.3 = (f32[2,2,16,288]{3,2,1,0:T(8,128)S(1)}, f32[2,2,16,288]{3,2,1,0:T(8,128)S(1)}, u32[]{:S(2)}, u32[]{:S(2)}) collective-permute-start(f32[2,2,16,288]{3,2,1,0:T(8,128)S(1)} %dynamic-slice_bitcast_fusion.1), channel_id=1, source_target_pairs={{0,16},{1,17},{2,18},{3,19},{4,20},{5,21},{6,22},{7,23},{8,24},{9,... | collective-permute-start | bytes 221192 | tf_op jit(solution)/shard_map/ppermute | solution.py:328
  40.2 2.6 collective-permute-done.3
  42.8 7.4 %collective-permute-start.4 = (f32[2,2,16,288]{3,2,1,0:T(8,128)S(1)}, f32[2,2,16,288]{3,2,1,0:T(8,128)S(1)}, u32[]{:S(2)}, u32[]{:S(2)}) collective-permute-start(f32[2,2,16,288]{3,2,1,0:T(8,128)S(1)} %fusion.17), channel_id=1, source_target_pairs={{0,8},{1,9},{2,10},{3,11},{4,12},{5,13},{6,14},{7,15},{8,0},{9,1},... | collective-permute-start | bytes 221192 | tf_op jit(solution)/shard_map/ppermute | solution.py:328
  50.5 7.8 %collective-permute-done.4 = f32[2,2,16,288]{3,2,1,0:T(8,128)S(1)} collective-permute-done((f32[2,2,16,288]{3,2,1,0:T(8,128)S(1)}, f32[2,2,16,288]{3,2,1,0:T(8,128)S(1)}, u32[]{:S(2)}, u32[]{:S(2)}) %collective-permute-start.4) | collective-permute-done | bytes 73760 | tf_op jit(solution)/shard_map/ppermute | solution.py:328
  66.3 45.6 %shard_map.228 = (bf16[16,256,384]{2,1,0:T(8,128)(2,1)}, bf16[16,1152,256]{2,1,0:T(8,128)(2,1)}, f32[16,8,256]{2,1,0:T(8,128)}, bf16[16,384,256]{2,1,0:T(8,128)(2,1)}) custom-call(bf16[16,256,384]{2,1,0:T(8,128)(2,1)} %tokens_ref.5, f32[16,6,384]{2,1,0:T(8,128)} %reshape.189.mod_ref, bf16[1152,384]{1,0:T(8,128)(2,1)} %bitcast.192, ...), custom_call_target="tpu_custom_call" | custom-call | flops 5234491392 | bytes 18874368 | tf_op jit(solution)/shard_map/pallas_call | solution.py:286
  113.6 3.0 fusion.35
  119.6 62.7 %shard_map.229 = (bf16[16,256,384]{2,1,0:T(8,128)(2,1)}, f32[16,256,384]{2,1,0:T(8,128)}, bf16[16,384,256]{2,1,0:T(8,128)(2,1)}, f32[16,4,384]{2,1,0:T(4,128)}, ...) custom-call(bf16[16,256,384]{2,1,0:T(8,128)(2,1)} %tokens_ref.5, ...), custom_call_target="tpu_custom_call" | custom-call | flops 32614907904 | bytes 22020096 | tf_op jit(solution)/shard_map/pallas_call | solution.py:286
  182.4 2.6 reshape.210
  186.0 1.8 pad_maximum_fusion
  189.3 42.0 %shard_map.230 = (bf16[16,1152,256]{2,1,0:T(8,128)(2,1)}, bf16[1152,384]{1,0:T(8,128)(2,1)}, f32[1152,128]{1,0:T(8,128)}) custom-call(bf16[16,1152,256]{2,1,0:T(8,128)(2,1)} %get-tuple-element.37.qkv_ref, f32[16,8,256]{2,1,0:T(8,128)} %get-tuple-element.38.lse_ref, bf16[16,384,256]{2,1,0:T(8,128)(2,1)} %get-tuple-element.39.grad_attended_ref, ...), custom_call_target="tpu_custom_call" | custom-call | flops 1 | bytes 1 | tf_op jit(solution)/shard_map/pallas_call | solution.py:286
  234.4 15.0 %shard_map.231 = (bf16[16,256,384]{2,1,0:T(8,128)(2,1)}, f32[16,2,384]{2,1,0:T(2,128)}) custom-call(bf16[16,1152,256]{2,1,0:T(8,128)(2,1)} %get-tuple-element.43.grad_qkv_ref, bf16[16,256,384]{2,1,0:T(8,128)(2,1)} %tokens_ref.5, f32[16,256,384]{2,1,0:T(8,128)} %get-tuple-element.44.grad_middle_ref, f32[16,6,384]{2,1,0:T(8,128)} %reshape.189.mod_ref, ...), custom_call_target="tpu_custom_call" | custom-call | flops 1 | bytes 1 | tf_op jit(solution)/shard_map/pallas_call | solution.py:286
  250.9 1.8 collective-permute-start.9
  252.6 7.6 %collective-permute-done.9 = bf16[2,2,96,384]{3,2,1,0:T(8,128)(2,1)S(1)} collective-permute-done((bf16[2,2,96,384]{3,2,1,0:T(8,128)(2,1)S(1)}, bf16[2,2,96,384]{3,2,1,0:T(8,128)(2,1)S(1)}, u32[]{:S(2)}, u32[]{:S(2)}) %collective-permute-start.9) | collective-permute-done | bytes 294944 | tf_op jit(solution)/shard_map/ppermute | solution.py:328
  260.6 5.9 %collective-permute-done.10 = bf16[2,112,384]{2,1,0:T(8,128)(2,1)S(1)} collective-permute-done((bf16[2,112,384]{2,1,0:T(8,128)(2,1)S(1)}, bf16[2,112,384]{2,1,0:T(8,128)(2,1)S(1)}, u32[]{:S(2)}, u32[]{:S(2)}) %collective-permute-start.10) | collective-permute-done | bytes 172064 | tf_op jit(solution)/shard_map/ppermute | solution.py:328
  266.7 4.6 %collective-permute-start.11 = (bf16[144,384]{1,0:T(8,128)(2,1)S(1)}, bf16[144,384]{1,0:T(8,128)(2,1)S(1)}, u32[]{:S(2)}, u32[]{:S(2)}) collective-permute-start(bf16[144,384]{1,0:T(8,128)(2,1)S(1)} %pad_maximum_fusion.15), channel_id=1, source_target_pairs={{0,16},{1,17},{2,18},{3,19},{4,20},{5,21},{6,22},{7,23},{8,24},{9,... | collective-permute-start | bytes 331784 | tf_op jit(solution)/shard_map/ppermute | solution.py:328
  271.3 4.9 %collective-permute-done.11 = bf16[144,384]{1,0:T(8,128)(2,1)S(1)} collective-permute-done((bf16[144,384]{1,0:T(8,128)(2,1)S(1)}, bf16[144,384]{1,0:T(8,128)(2,1)S(1)}, u32[]{:S(2)}, u32[]{:S(2)}) %collective-permute-start.11) | collective-permute-done | bytes 110624 | tf_op jit(solution)/shard_map/ppermute | solution.py:328
  279.7 12.0 %collective-permute-done.12 = bf16[640,384]{1,0:T(8,128)(2,1)S(1)} collective-permute-done((bf16[640,384]{1,0:T(8,128)(2,1)S(1)}, bf16[640,384]{1,0:T(8,128)(2,1)S(1)}, u32[]{:S(2)}, u32[]{:S(2)}) %collective-permute-start.12) | collective-permute-done | bytes 491552 | tf_op jit(solution)/shard_map/ppermute | solution.py:328
  292.1 1.9 collective-permute-done.7
  301.7 2.0 convert_reduce_fusion
  (170 shorter events, 38.6 us)
Async XLA Ops:
  7.2 4.4 %copy-start = (bf16[384,144]{0,1:T(8,128)(2,1)S(1)}, bf16[384,144]{0,1:T(8,128)(2,1)}, u32[]{:S(2)}) copy-start(bf16[384,144]{0,1:T(8,128)(2,1)} %param.17) | copy-start | bytes 331780
  7.2 22.9 %copy-start.13 = (bf16[288]{0:T(512)(128)(2,1)S(1)}, bf16[288]{0:T(512)(128)(2,1)}, u32[]{:S(2)}) copy-start(bf16[288]{0:T(512)(128)(2,1)} %param.16) | copy-start | bytes 1732
  7.2 104.7 %all-gather.6.cloned.1.call-start = ((), (), s32[]{:S(2)}) async-start(), calls=%async_computation.3 | async-start | bytes 2985984 | tf_op jit(solution)/shard_map/all_gather | solution.py:382
  10.0 179.3 %all-gather.4.cloned.1.call-start = ((), (), s32[]{:S(2)}) async-start(), calls=%async_computation.1 | async-start | bytes 1990656 | tf_op jit(solution)/shard_map/all_gather | solution.py:390
  11.6 8.0 %collective-permute-start = (bf16[96,384]{1,0:T(8,128)(2,1)S(1)}, bf16[96,384]{1,0:T(8,128)(2,1)S(1)}, u32[]{:S(2)}, u32[]{:S(2)}) collective-permute-start(bf16[96,384]{1,0:T(8,128)(2,1)S(1)} %fusion.23), channel_id=1, source_target_pairs={{0,16},{1,17},{2,18},{3,19},{4,20},{5,21},{6,22},{7,23},{8,24},{9,... | collective-permute-start | bytes 221192 | tf_op jit(solution)/shard_map/ppermute | solution.py:328
  19.7 15.3 %copy-start.5 = (bf16[384,288]{0,1:T(8,128)(2,1)S(1)}, bf16[384,288]{0,1:T(8,128)(2,1)}, u32[]{:S(2)}) copy-start(bf16[384,288]{0,1:T(8,128)(2,1)} %param.15) | copy-start | bytes 663556
  19.7 8.0 %collective-permute-start.1 = (bf16[2,96,384]{2,1,0:T(8,128)(2,1)S(1)}, bf16[2,96,384]{2,1,0:T(8,128)(2,1)S(1)}, u32[]{:S(2)}, u32[]{:S(2)}) collective-permute-start(bf16[2,96,384]{2,1,0:T(8,128)(2,1)S(1)} %pad_maximum_fusion.14), channel_id=1, source_target_pairs={{0,8},{1,9},{2,10},{3,11},{4,12},{5,13},{6,14},{7,15},{8,0},{9,1},... | collective-permute-start | bytes 442376 | tf_op jit(solution)/shard_map/ppermute | solution.py:328
  27.8 7.0 %collective-permute-start.2 = (bf16[2,2,96,384]{3,2,1,0:T(8,128)(2,1)S(1)}, bf16[2,2,96,384]{3,2,1,0:T(8,128)(2,1)S(1)}, u32[]{:S(2)}, u32[]{:S(2)}) collective-permute-start(bf16[2,2,96,384]{3,2,1,0:T(8,128)(2,1)S(1)} %pad_maximum_fusion.7), channel_id=1, source_target_pairs={{0,4},{1,5},{2,6},{3,7},{4,0},{5,1},{6,2},{7,3},{8,12},{9,13},{10,... | collective-permute-start | bytes 884744 | tf_op jit(solution)/shard_map/ppermute | solution.py:328
  35.4 7.4 %collective-permute-start.3 = (f32[2,2,16,288]{3,2,1,0:T(8,128)S(1)}, f32[2,2,16,288]{3,2,1,0:T(8,128)S(1)}, u32[]{:S(2)}, u32[]{:S(2)}) collective-permute-start(f32[2,2,16,288]{3,2,1,0:T(8,128)S(1)} %dynamic-slice_bitcast_fusion.1), channel_id=1, source_target_pairs={{0,16},{1,17},{2,18},{3,19},{4,20},{5,21},{6,22},{7,23},{8,24},{9,... | collective-permute-start | bytes 221192 | tf_op jit(solution)/shard_map/ppermute | solution.py:328
  42.8 15.4 %collective-permute-start.4 = (f32[2,2,16,288]{3,2,1,0:T(8,128)S(1)}, f32[2,2,16,288]{3,2,1,0:T(8,128)S(1)}, u32[]{:S(2)}, u32[]{:S(2)}) collective-permute-start(f32[2,2,16,288]{3,2,1,0:T(8,128)S(1)} %fusion.17), channel_id=1, source_target_pairs={{0,8},{1,9},{2,10},{3,11},{4,12},{5,13},{6,14},{7,15},{8,0},{9,1},... | collective-permute-start | bytes 221192 | tf_op jit(solution)/shard_map/ppermute | solution.py:328
  50.5 13.5 %collective-permute-start.6 = (bf16[8,88,384]{2,1,0:T(8,128)(2,1)S(1)}, bf16[8,88,384]{2,1,0:T(8,128)(2,1)S(1)}, u32[]{:S(2)}, u32[]{:S(2)}) collective-permute-start(bf16[8,88,384]{2,1,0:T(8,128)(2,1)S(1)} %slice.174), channel_id=1, source_target_pairs={{0,1},{1,0},{2,3},{3,2},{4,5},{5,4},{6,7},{7,6},{8,9},{9,8},{10,11... | collective-permute-start | bytes 1622024 | tf_op jit(solution)/shard_map/ppermute | solution.py:328
  58.3 4.7 %collective-permute-start.5 = (f32[2,2,16,288]{3,2,1,0:T(8,128)S(1)}, f32[2,2,16,288]{3,2,1,0:T(8,128)S(1)}, u32[]{:S(2)}, u32[]{:S(2)}) collective-permute-start(f32[2,2,16,288]{3,2,1,0:T(8,128)S(1)} %bitcast.231), channel_id=1, source_target_pairs={{0,4},{1,5},{2,6},{3,7},{4,0},{5,1},{6,2},{7,3},{8,12},{9,13},{10,... | collective-permute-start | bytes 221192 | tf_op jit(solution)/shard_map/ppermute | solution.py:328
  116.6 159.8 %reduce-scatter.2.cloned.1.call-start = ((), (), s32[]{:S(2)}) async-start(), calls=%async_computation.2 | async-start | bytes 2985984 | tf_op jit(solution)/shard_map/reduce_scatter | solution.py:518
  182.4 2.8 copy-start.4
  234.3 16.4 %collective-permute-start.8 = (bf16[8,80,384]{2,1,0:T(8,128)(2,1)S(1)}, bf16[8,80,384]{2,1,0:T(8,128)(2,1)S(1)}, u32[]{:S(2)}, u32[]{:S(2)}) collective-permute-start(bf16[8,80,384]{2,1,0:T(8,128)(2,1)S(1)} %dynamic-slice_bitcast_fusion), channel_id=1, source_target_pairs={{0,1},{1,0},{2,3},{3,2},{4,5},{5,4},{6,7},{7,6},{8,9},{9,8},{10,11... | collective-permute-start | bytes 1474568 | tf_op jit(solution)/shard_map/ppermute | solution.py:328
  234.4 15.0 %copy-start.6 = (f32[16,4,384]{2,1,0:T(4,128)S(1)}, f32[16,4,384]{2,1,0:T(4,128)}, u32[]{:S(2)}) copy-start(f32[16,4,384]{2,1,0:T(4,128)} %get-tuple-element.47) | copy-start | bytes 294916
  250.9 9.4 %collective-permute-start.9 = (bf16[2,2,96,384]{3,2,1,0:T(8,128)(2,1)S(1)}, bf16[2,2,96,384]{3,2,1,0:T(8,128)(2,1)S(1)}, u32[]{:S(2)}, u32[]{:S(2)}) collective-permute-start(bf16[2,2,96,384]{3,2,1,0:T(8,128)(2,1)S(1)} %pad_maximum_fusion.8), channel_id=1, source_target_pairs={{0,4},{1,5},{2,6},{3,7},{4,0},{5,1},{6,2},{7,3},{8,12},{9,13},{10,... | collective-permute-start | bytes 884744 | tf_op jit(solution)/shard_map/ppermute | solution.py:328
  260.5 6.1 %collective-permute-start.10 = (bf16[2,112,384]{2,1,0:T(8,128)(2,1)S(1)}, bf16[2,112,384]{2,1,0:T(8,128)(2,1)S(1)}, u32[]{:S(2)}, u32[]{:S(2)}) collective-permute-start(bf16[2,112,384]{2,1,0:T(8,128)(2,1)S(1)} %pad_maximum_fusion.13), channel_id=1, source_target_pairs={{0,8},{1,9},{2,10},{3,11},{4,12},{5,13},{6,14},{7,15},{8,0},{9,1},... | collective-permute-start | bytes 516104 | tf_op jit(solution)/shard_map/ppermute | solution.py:328
  266.7 9.5 %collective-permute-start.11 = (bf16[144,384]{1,0:T(8,128)(2,1)S(1)}, bf16[144,384]{1,0:T(8,128)(2,1)S(1)}, u32[]{:S(2)}, u32[]{:S(2)}) collective-permute-start(bf16[144,384]{1,0:T(8,128)(2,1)S(1)} %pad_maximum_fusion.15), channel_id=1, source_target_pairs={{0,16},{1,17},{2,18},{3,19},{4,20},{5,21},{6,22},{7,23},{8,24},{9,... | collective-permute-start | bytes 331784 | tf_op jit(solution)/shard_map/ppermute | solution.py:328
  276.4 15.3 %copy-start.3 = (bf16[1,432,384]{2,1,0:T(8,128)(2,1)S(1)}, bf16[1,432,384]{2,1,0:T(8,128)(2,1)}, u32[]{:S(2)}) copy-start(bf16[1,432,384]{2,1,0:T(8,128)(2,1)} %reduce-scatter.2.cloned.1.call-done) | copy-start | bytes 995332
  277.5 14.2 %collective-permute-start.12 = (bf16[640,384]{1,0:T(8,128)(2,1)S(1)}, bf16[640,384]{1,0:T(8,128)(2,1)S(1)}, u32[]{:S(2)}, u32[]{:S(2)}) collective-permute-start(bf16[640,384]{1,0:T(8,128)(2,1)S(1)} %pad_maximum_fusion.3), channel_id=1, source_target_pairs={{0,2},{1,3},{2,0},{3,1},{4,6},{5,7},{6,4},{7,5},{8,10},{9,11},{10,... | collective-permute-start | bytes 1474568 | tf_op jit(solution)/shard_map/ppermute | solution.py:328
  278.8 15.2 %collective-permute-start.7 = (bf16[2,8,16,384]{3,2,1,0:T(8,128)(2,1)S(1)}, bf16[2,8,16,384]{3,2,1,0:T(8,128)(2,1)S(1)}, u32[]{:S(2)}, u32[]{:S(2)}) collective-permute-start(bf16[2,8,16,384]{3,2,1,0:T(8,128)(2,1)S(1)} %pad_maximum_fusion.9), channel_id=1, source_target_pairs={{0,2},{1,3},{2,0},{3,1},{4,6},{5,7},{6,4},{7,5},{8,10},{9,11},{10,... | collective-permute-start | bytes 589832 | tf_op jit(solution)/shard_map/ppermute | solution.py:328
  292.0 3.7 %collective-permute-start.13 = (bf16[768,384]{1,0:T(8,128)(2,1)S(1)}, bf16[768,384]{1,0:T(8,128)(2,1)S(1)}, u32[]{:S(2)}, u32[]{:S(2)}) collective-permute-start(bf16[768,384]{1,0:T(8,128)(2,1)S(1)} %pad_maximum_fusion.2), channel_id=1, source_target_pairs={{0,1},{1,0},{2,3},{3,2},{4,5},{5,4},{6,7},{7,6},{8,9},{9,8},{10,11... | collective-permute-start | bytes 1769480 | tf_op jit(solution)/shard_map/ppermute | solution.py:328
  300.5 4.4 %copy-start.1 = (bf16[384,144]{0,1:T(8,128)(2,1)S(1)}, bf16[384,144]{0,1:T(8,128)(2,1)}, u32[]{:S(2)}) copy-start(bf16[384,144]{0,1:T(8,128)(2,1)} %param.17) | copy-start | bytes 331780
  (7 other events, 10.4 us)
Sparse Core Ops, SparseCore 0:
  10.8 60.5 all-gather.5
  116.7 49.0 all-gather.3
  187.9 74.1 reduce-scatter.1

commit v4 on v3

--- a/solution.py
+++ b/solution.py
@@ -41,38 +41,87 @@
     return inverse * (upstream - first - normal * second)
 
 
-def beside(left, right):
-    return jnp.concatenate([left, right], axis=1)
+STRIP = 64
+GROUP = 3
+
+
+def beside(*parts):
+    return jnp.concatenate(parts, axis=1)
+
+
+def above(*parts):
+    return jnp.concatenate(parts, axis=0)
+
+
+def strips(extent, size):
+    return [slice(low, low + size) for low in range(0, extent, size)]
+
+
+def head_slices(head):
+    low = head * HEAD_DIM
+    pair = low - low % (2 * HEAD_DIM)
+    return slice(low, low + HEAD_DIM), slice(pair, pair + 2 * HEAD_DIM), low == pair
+
+
+def in_groups(items, size):
+    return [items[low : low + size] for low in range(0, len(items), size)]
 
 
 def attention_forward_kernel(
     tokens_ref, mod_ref, weight_ref, bias_ref, normed_ref, qkv_ref, lse_ref, attended_ref
 ):
     latents, length, width = tokens_ref.shape
-    bias = beside(bias_ref[...], bias_ref[...])
     blank = jnp.zeros((HEAD_DIM, length), BF16)
     for latent in range(latents):
-        normal, _ = normalise(tokens_ref[latent].astype(F32))
-        normed = normal * (1.0 + mod_ref[latent, 1:2, :]) + mod_ref[latent, 0:1, :]
-        normed = normed.astype(BF16)
-        normed_ref[latent] = normed
-        qkv = (dot_nt(weight_ref[...], normed) + bias).astype(BF16)
-        qkv_ref[latent] = qkv
-        keys_in = qkv[width : 2 * width].T
-        for head in range(width // HEAD_DIM):
-            low = head * HEAD_DIM
-            high = low + HEAD_DIM
-            pair = low - low % (2 * HEAD_DIM)
-            queries = qkv[low:high]
-            queries = jnp.concatenate([blank, queries] if low > pair else [queries, blank])
-            scores = dot_nn(keys_in[:, pair : pair + 2 * HEAD_DIM], queries) * HEAD_DIM ** (-0.5)
-            highest = jnp.max(scores, axis=0, keepdims=True)
-            shifted = jnp.exp(scores - highest)
+        for rows in strips(length, STRIP):
+            normal, _ = normalise(tokens_ref[latent, rows, :].astype(F32))
+            normed = normal * (1.0 + mod_ref[latent, 1:2, :]) + mod_ref[latent, 0:1, :]
+            normed_ref[latent, rows, :] = normed.astype(BF16)
+    normed = normed_ref[...].reshape(latents * length, width)
+    for part in strips(3 * width, 2 * HEAD_DIM):
+        bias = bias_ref[part, :]
+        qkv = dot_nt(weight_ref[part, :], normed) + beside(*([bias] * (latents * length // 128)))
+        qkv = qkv.astype(BF16)
+        for latent in range(latents):
+            qkv_ref[latent, part, :] = qkv[:, latent * length : (latent + 1) * length]
+    keys_all = [qkv_ref[latent, width : 2 * width, :].T for latent in range(latents)]
+
+    def scores_of(latent, head):
+        own, pair, first = head_slices(head)
+        queries = qkv_ref[latent, own, :]
+        queries = above(queries, blank) if first else above(blank, queries)
+        return dot_nn(keys_all[latent][:, pair], queries)
+
+    def probs_of(latent, head, scores):
+        parts = []
+        for columns in strips(length, 128):
+            strip = scores[:, columns] * HEAD_DIM ** (-0.5)
+            highest = jnp.max(strip, axis=0, keepdims=True)
+            shifted = jnp.exp(strip - highest)
             total = jnp.sum(shifted, axis=0, keepdims=True)
-            probs = (shifted * (1.0 / total)).astype(BF16)
-            lse_ref[latent, head : head + 1, :] = highest + jnp.log(total)
-            values_in = qkv[2 * width + low : 2 * width + high]
-            attended_ref[latent, low:high, :] = dot_nn(values_in, probs).astype(BF16)
+            parts.append((shifted * (1.0 / total)).astype(BF16))
+            lse_ref[latent, head : head + 1, columns] = highest + jnp.log(total)
+        return beside(*parts)
+
+    def attend(latent, head, probs):
+        own, _, _ = head_slices(head)
+        values_in = qkv_ref[latent, 2 * width + own.start : 2 * width + own.stop, :]
+        attended_ref[latent, own, :] = dot_nn(values_in, probs).astype(BF16)
+
+    items = [(latent, head) for latent in range(latents) for head in range(width // HEAD_DIM)]
+    groups = in_groups(items, GROUP)
+    scores = [scores_of(*item) for item in groups[0]]
+    previous = []
+    for place, group in enumerate(groups):
+        later = groups[place + 1] if place + 1 < len(groups) else []
+        next_scores = [scores_of(*item) for item in later]
+        probs = [probs_of(*item, value) for item, value in zip(group, scores)]
+        for item, value in previous:
+            attend(*item, value)
+        previous = list(zip(group, probs))
+        scores = next_scores
+    for item, value in previous:
+        attend(*item, value)
 
 
 def feed_kernel(
@@ -105,12 +154,16 @@
     down_back,
     active_all,
     grad_hidden_all,
+    middle_all,
+    normal_all,
+    branch_all,
     *,
     chunk,
 ):
     step = pl.program_id(0)
     latents, length, width = tokens_ref.shape
     hidden_width = up_weight_ref.shape[0]
+    tokens_all = latents * length
 
     @pl.when(step == 0)
     def _():
@@ -122,63 +175,107 @@
         up_back[...] = up_weight_ref[...].T
         down_back[...] = down_weight_ref[...].T
 
-    kept = []
+    attended = beside(*[attended_ref[latent] for latent in range(latents)])
+    branch_wide = dot_nn(out_weight_ref[...], attended)
+    normed_parts = []
+    grad_feed_parts = []
+    inverses = []
+    down_sum = jnp.zeros((1, width), F32)
     for latent in range(latents):
         gate_one = mod_ref[latent, 2:3, :]
         shift_two = mod_ref[latent, 3:4, :]
         scale_two = 1.0 + mod_ref[latent, 4:5, :]
         gate_two = mod_ref[latent, 5:6, :]
-        branch = dot_nn(out_weight_ref[...], attended_ref[latent]).T + out_bias_ref[...]
-        middle = tokens_ref[latent].astype(F32) + gate_one * branch
-        normal, inverse = normalise(middle)
-        normed = (normal * scale_two + shift_two).astype(BF16)
-        incoming = cotangent_ref[latent].astype(F32)
-        grad_feed = (incoming * gate_two).astype(BF16)
-        bias_acc[0:1, :] += jnp.sum(grad_feed.astype(F32), axis=0, keepdims=True)
-        kept.append((gate_one, scale_two, gate_two, branch, middle, normal, inverse, normed, incoming, grad_feed))
-
-    for latent in range(latents):
-        normed, grad_feed = kept[latent][7], kept[latent][9]
-        here = slice(latent * length, (latent + 1) * length)
-        for low in range(0, hidden_width, chunk):
-            high = low + chunk
-            bias = up_bias_ref[low:high, :]
-            hidden = dot_nt(up_weight_ref[low:high, :], normed) + beside(bias, bias)
-            grad_active = dot_nt(down_back[low:high, :], grad_feed)
-            square = hidden * hidden
-            bent = jnp.tanh(hidden * (GELU_C + (GELU_C * 0.044715) * square))
-            half = 0.5 + 0.5 * bent
-            active_all[low:high, here] = (hidden * half).astype(BF16)
-            slope = half + hidden * (0.5 - 0.5 * (bent * bent)) * (
-                GELU_C + (3.0 * GELU_C * 0.044715) * square
-            )
-            grad_hidden_all[low:high, here] = (grad_active * slope).astype(BF16)
-
-    grad_branches = []
-    for latent in range(latents):
-        gate_one, scale_two, gate_two, branch, middle, normal, inverse, _, incoming, _ = kept[latent]
-        here = slice(latent * length, (latent + 1) * length)
-        feed = dot_nn(down_weight_ref[...], active_all[:, here]).T + down_bias_ref[...]
-        grad_normed = dot_nn(up_back[...], grad_hidden_all[:, here]).T
-        output_ref[latent] = (middle + gate_two * feed).astype(BF16)
-        grad_mod_ref[latent, 3:4, :] = jnp.sum(incoming * feed, axis=0, keepdims=True)
-        grad_mod_ref[latent, 1:2, :] = jnp.sum(grad_normed, axis=0, keepdims=True)
-        grad_mod_ref[latent, 2:3, :] = jnp.sum(grad_normed * normal, axis=0, keepdims=True)
-        grad_middle = incoming + normalise_back(grad_normed * scale_two, normal, inverse)
-        grad_middle_ref[latent] = grad_middle
-        grad_branch = (grad_middle * gate_one).astype(BF16)
-        grad_branches.append(grad_branch)
-        grad_mod_ref[latent, 0:1, :] = jnp.sum(grad_middle * branch, axis=0, keepdims=True)
-        bias_acc[1:2, :] += jnp.sum(grad_branch.astype(F32), axis=0, keepdims=True)
-        grad_attended_ref[latent] = dot_nt(out_back[...], grad_branch).astype(BF16)
-
-    normed_all = jnp.concatenate([entry[7] for entry in kept])
-    ones = jnp.ones((latents * length, 128), BF16)
-    grad_feed_all = jnp.concatenate([entry[9] for entry in kept])
-    attended_all = jnp.concatenate([attended_ref[latent] for latent in range(latents)], axis=1)
+        branch_tall = branch_wide[:, latent * length : (latent + 1) * length].T
+        for rows in strips(length, STRIP):
+            there = slice(latent * length + rows.start, latent * length + rows.stop)
+            branch = branch_tall[rows] + out_bias_ref[...]
+            branch_all[there, :] = branch
+            middle = tokens_ref[latent, rows, :].astype(F32) + gate_one * branch
+            middle_all[there, :] = middle
+            normal, inverse = normalise(middle)
+            normal_all[there, :] = normal
+            inverses.append(inverse)
+            normed_parts.append((normal * scale_two + shift_two).astype(BF16))
+            grad_feed = (cotangent_ref[latent, rows, :].astype(F32) * gate_two).astype(BF16)
+            grad_feed_parts.append(grad_feed)
+            down_sum += jnp.sum(grad_feed.astype(F32), axis=0, keepdims=True)
+    bias_acc[0:1, :] += down_sum
+    normed_all = above(*normed_parts)
+    grad_feed_all = above(*grad_feed_parts)
+
+    def products(rows):
+        return (
+            dot_nt(up_weight_ref[rows, :], normed_all),
+            dot_nt(down_back[rows, :], grad_feed_all),
+        )
+
+    parts = strips(hidden_width, chunk)
+    ahead = products(parts[0])
+    for place, part in enumerate(parts):
+        hidden_wide, grad_wide = ahead
+        if place + 1 < len(parts):
+            ahead = products(parts[place + 1])
+        for rows in strips(chunk, STRIP):
+            there = slice(part.start + rows.start, part.start + rows.stop)
+            bias = up_bias_ref[there, :]
+            bias = beside(bias, bias)
+            for columns in strips(tokens_all, 256):
+                hidden = hidden_wide[rows, columns] + bias
+                square = hidden * hidden
+                bent = jnp.tanh(hidden * (GELU_C + (GELU_C * 0.044715) * square))
+                half = 0.5 + 0.5 * bent
+                active_all[there, columns] = (hidden * half).astype(BF16)
+                slope = half + hidden * (0.5 - 0.5 * (bent * bent)) * (
+                    GELU_C + (3.0 * GELU_C * 0.044715) * square
+                )
+                grad_hidden_all[there, columns] = (grad_wide[rows, columns] * slope).astype(BF16)
+
+    feed_wide = dot_nn(down_weight_ref[...], active_all[...])
+    grad_normed_wide = dot_nn(up_back[...], grad_hidden_all[...])
+    ones = jnp.ones((tokens_all, 128), BF16)
     up_acc[...] += dot_nn(grad_hidden_all[...], beside(normed_all, ones))
     down_acc[...] += dot_nn(active_all[...], grad_feed_all)
-    out_acc[...] += dot_nn(attended_all, jnp.concatenate(grad_branches))
+
+    grad_branch_parts = []
+    out_sum = jnp.zeros((1, width), F32)
+    for latent in range(latents):
+        gate_one = mod_ref[latent, 2:3, :]
+        scale_two = 1.0 + mod_ref[latent, 4:5, :]
+        gate_two = mod_ref[latent, 5:6, :]
+        here = slice(latent * length, (latent + 1) * length)
+        feed_tall = feed_wide[:, here].T
+        grad_normed_tall = grad_normed_wide[:, here].T
+        sums = [jnp.zeros((1, width), F32) for _ in range(4)]
+        for rows in strips(length, STRIP):
+            there = slice(here.start + rows.start, here.start + rows.stop)
+            feed = feed_tall[rows] + down_bias_ref[...]
+            grad_normed = grad_normed_tall[rows]
+            incoming = cotangent_ref[latent, rows, :].astype(F32)
+            normal = normal_all[there, :]
+            output_ref[latent, rows, :] = (middle_all[there, :] + gate_two * feed).astype(BF16)
+            grad_middle = incoming + normalise_back(
+                grad_normed * scale_two, normal, inverses[there.start // STRIP]
+            )
+            grad_middle_ref[latent, rows, :] = grad_middle
+            grad_branch = (grad_middle * gate_one).astype(BF16)
+            grad_branch_parts.append(grad_branch)
+            terms = (
+                grad_middle * branch_all[there, :],
+                grad_normed,
+                grad_normed * normal,
+                incoming * feed,
+            )
+            for place, term in enumerate(terms):
+                sums[place] += jnp.sum(term, axis=0, keepdims=True)
+            out_sum += jnp.sum(grad_branch.astype(F32), axis=0, keepdims=True)
+        grad_mod_ref[latent] = above(*sums)
+    bias_acc[1:2, :] += out_sum
+    grad_branch_all = above(*grad_branch_parts)
+    grad_attended = dot_nt(out_back[...], grad_branch_all).astype(BF16)
+    for latent in range(latents):
+        grad_attended_ref[latent] = grad_attended[:, latent * length : (latent + 1) * length]
+    out_acc[...] += dot_nn(attended, grad_branch_all)
 
     @pl.when(step == pl.num_programs(0) - 1)
     def _():
@@ -208,34 +305,63 @@
     def _():
         acc[...] = jnp.zeros_like(acc)
 
-    for latent in range(latents):
-        keys_all = qkv_ref[latent, width : 2 * width, :].T
-        values_all = qkv_ref[latent, 2 * width : 3 * width, :].T
-        for head in range(width // HEAD_DIM):
-            low = head * HEAD_DIM
-            high = low + HEAD_DIM
-            pair = low - low % (2 * HEAD_DIM)
-            queries = qkv_ref[latent, low:high, :]
-            keys_in = qkv_ref[latent, width + low : width + high, :]
-            grad_out = grad_attended_ref[latent, low:high, :]
-            first = low == pair
-            queries_wide = jnp.concatenate([queries, blank] if first else [blank, queries])
-            grad_out_wide = jnp.concatenate([grad_out, blank] if first else [blank, grad_out])
-            scores = dot_nn(keys_all[:, pair : pair + 2 * HEAD_DIM], queries_wide)
-            grad_probs = dot_nn(values_all[:, pair : pair + 2 * HEAD_DIM], grad_out_wide)
-            probs = jnp.exp(scores * HEAD_DIM ** (-0.5) - lse_ref[latent, head : head + 1, :])
-            row_terms = jnp.sum(probs * grad_probs, axis=0, keepdims=True)
-            grad_scores = (probs * (grad_probs - row_terms)).astype(BF16)
-            grad_qkv_ref[latent, low:high, :] = (
-                dot_nn(keys_in, grad_scores) * HEAD_DIM ** (-0.5)
-            ).astype(BF16)
-            grad_qkv_ref[latent, width + low : width + high, :] = (
-                dot_nt(queries, grad_scores) * HEAD_DIM ** (-0.5)
-            ).astype(BF16)
-            grad_qkv_ref[latent, 2 * width + low : 2 * width + high, :] = dot_nt(
-                grad_out, probs.astype(BF16)
-            ).astype(BF16)
-    grad_qkv = jnp.concatenate([grad_qkv_ref[latent] for latent in range(latents)], axis=1)
+    keys_all = [qkv_ref[latent, width : 2 * width, :].T for latent in range(latents)]
+    values_all = [qkv_ref[latent, 2 * width : 3 * width, :].T for latent in range(latents)]
+
+    def products(latent, head):
+        own, pair, first = head_slices(head)
+        queries = qkv_ref[latent, own, :]
+        grad_out = grad_attended_ref[latent, own, :]
+        queries = above(queries, blank) if first else above(blank, queries)
+        grad_out = above(grad_out, blank) if first else above(blank, grad_out)
+        return (
+            dot_nn(keys_all[latent][:, pair], queries),
+            dot_nn(values_all[latent][:, pair], grad_out),
+        )
+
+    def middle_of(latent, head, scores, grad_probs):
+        low_parts = []
+        grad_parts = []
+        for columns in strips(length, 128):
+            total = lse_ref[latent, head : head + 1, columns]
+            probs = jnp.exp(scores[:, columns] * HEAD_DIM ** (-0.5) - total)
+            terms = probs * grad_probs[:, columns]
+            row_terms = jnp.sum(terms, axis=0, keepdims=True)
+            grad_parts.append((probs * (grad_probs[:, columns] - row_terms)).astype(BF16))
+            low_parts.append(probs.astype(BF16))
+        return beside(*low_parts), beside(*grad_parts)
+
+    def finish(latent, head, probs, grad_scores):
+        own, _, _ = head_slices(head)
+        low, high = own.start, own.stop
+        queries = qkv_ref[latent, own, :]
+        keys_in = qkv_ref[latent, width + low : width + high, :]
+        grad_out = grad_attended_ref[latent, own, :]
+        scale = HEAD_DIM ** (-0.5)
+        grad_qkv_ref[latent, own, :] = (dot_nn(keys_in, grad_scores) * scale).astype(BF16)
+        grad_qkv_ref[latent, width + low : width + high, :] = (
+            dot_nt(queries, grad_scores) * scale
+        ).astype(BF16)
+        grad_qkv_ref[latent, 2 * width + low : 2 * width + high, :] = dot_nt(
+            grad_out, probs
+        ).astype(BF16)
+
+    items = [(latent, head) for latent in range(latents) for head in range(width // HEAD_DIM)]
+    groups = in_groups(items, GROUP)
+    values = [products(*item) for item in groups[0]]
+    previous = []
+    for place, group in enumerate(groups):
+        later = groups[place + 1] if place + 1 < len(groups) else []
+        next_values = [products(*item) for item in later]
+        middles = [middle_of(*item, *value) for item, value in zip(group, values)]
+        for item, value in previous:
+            finish(*item, *value)
+        previous = list(zip(group, middles))
+        values = next_values
+    for item, value in previous:
+        finish(*item, *value)
+
+    grad_qkv = beside(*[grad_qkv_ref[latent] for latent in range(latents)])
     normed = normed_ref[...].reshape(latents * length, width)
     acc[...] += dot_nn(grad_qkv, beside(normed, jnp.ones((latents * length, 128), BF16)))
 
@@ -255,21 +381,29 @@
     grad_mod_ref,
     weight_back,
 ):
-    latents = tokens_ref.shape[0]
+    latents, length, width = tokens_ref.shape
 
     @pl.when(pl.program_id(0) == 0)
     def _():
         weight_back[...] = weight_ref[...].T
 
+    grad_qkv = beside(*[grad_qkv_ref[latent] for latent in range(latents)])
+    grad_normed_wide = dot_nn(weight_back[...], grad_qkv)
     for latent in range(latents):
-        normal, inverse = normalise(tokens_ref[latent].astype(F32))
-        grad_normed = dot_nn(weight_back[...], grad_qkv_ref[latent]).T
-        grad_mod_ref[latent, 0:1, :] = jnp.sum(grad_normed, axis=0, keepdims=True)
-        grad_mod_ref[latent, 1:2, :] = jnp.sum(grad_normed * normal, axis=0, keepdims=True)
-        upstream = grad_normed * (1.0 + mod_ref[latent, 1:2, :])
-        tokens_grad_ref[latent] = (
-            grad_middle_ref[latent] + normalise_back(upstream, normal, inverse)
-        ).astype(BF16)
+        grad_normed_tall = grad_normed_wide[:, latent * length : (latent + 1) * length].T
+        scale_one = 1.0 + mod_ref[latent, 1:2, :]
+        first = jnp.zeros((1, width), F32)
+        second = jnp.zeros((1, width), F32)
+        for rows in strips(length, STRIP):
+            normal, inverse = normalise(tokens_ref[latent, rows, :].astype(F32))
+            grad_normed = grad_normed_tall[rows]
+            first += jnp.sum(grad_normed, axis=0, keepdims=True)
+            second += jnp.sum(grad_normed * normal, axis=0, keepdims=True)
+            back = normalise_back(grad_normed * scale_one, normal, inverse)
+            tokens_grad_ref[latent, rows, :] = (grad_middle_ref[latent, rows, :] + back).astype(
+                BF16
+            )
+        grad_mod_ref[latent] = above(first, second)
 
 
 def each(shape, count):
@@ -439,7 +573,7 @@
 
     normed, qkv, lse, attended = run_kernel(
         attention_forward_kernel,
-        2,
+        4,
         [
             shape_of((latents, length, width), BF16),
             shape_of((latents, 3 * width, length), BF16),
@@ -457,6 +591,7 @@
         ),
     )
 
+    attended, silu_all = lax.optimization_barrier((attended, silu_all))
     (
         output,
         grad_middle,
@@ -469,8 +604,8 @@
         up_bias_grad,
         down_bias_grad,
     ) = run_kernel(
-        functools.partial(feed_kernel, chunk=512),
-        2,
+        functools.partial(feed_kernel, chunk=256),
+        4,
         [
             shape_of((latents, length, width), BF16),
             shape_of((latents, length, width), F32),
@@ -493,8 +628,11 @@
             pltpu.VMEM((width, width), BF16),
             pltpu.VMEM((width, hidden_width), BF16),
             pltpu.VMEM((hidden_width, width), BF16),
-            pltpu.VMEM((hidden_width, 2 * length), BF16),
-            pltpu.VMEM((hidden_width, 2 * length), BF16),
+            pltpu.VMEM((hidden_width, 4 * length), BF16),
+            pltpu.VMEM((hidden_width, 4 * length), BF16),
+            pltpu.VMEM((4 * length, width), F32),
+            pltpu.VMEM((4 * length, width), F32),
+            pltpu.VMEM((4 * length, width), F32),
         ],
         [tokens, cotangent, attended, modulation],
         [out_all, out_full, up_all, up_full, down_all, down_full],
@@ -553,7 +691,7 @@
 
     tokens_grad, grad_mod_one = run_kernel(
         first_norm_kernel,
-        2,
+        4,
         [shape_of((latents, length, width), BF16), shape_of((latents, 2, width), F32)],
         [],
         [pltpu.VMEM((width, 3 * width), BF16)],

time: 312 us -> 263 us (0.84)
  Pallas kernels: 165 us -> 123 us
  starting transfers between devices: 30.1 us -> 13.5 us
  waiting for transfers between devices: 60.4 us -> 71.2 us
    pallas_call x4, Pallas kernels: 165 us -> 123 us  [run_kernel(): pl.pallas_call(kernel, grid=(streamed[0].shape[0] // count,), in_specs=[e...]
    ppermute x14, starting transfers between devices: 29.8 us -> 13.4 us  [swap(): return lax.ppermute(value, AXES, pairs)]
    ppermute x14, waiting for transfers between devices: 60.3 us -> 71.2 us  [swap(): return lax.ppermute(value, AXES, pairs)]
  transfers between devices with their start and end apart: 17 -> 17, of which waited for: 11 -> 11; matrix products, arithmetic and copies ran while one was open for 7% -> 8% of each run, Pallas kernels for 53% -> 47%
where the time goes in v4:
time: 263 us
  Pallas kernels  123 us (47%)
  waiting for transfers between devices  71.2 us (27%)
  local copies, waits for them, and re-layouts  24.7 us (9%)
  between operations  14.6 us (6%)
  starting transfers between devices  13.5 us (5%)
  other arithmetic  13.1 us (5%)
  matrix products  2.75 us (1%)
    pallas_call x4, Pallas kernels, run_kernel(): pl.pallas_call(kernel, grid=(streamed[0].shape[0] // count,), in_specs=[e...  123 us
    ppermute x14, waiting for transfers between devices, swap(): return lax.ppermute(value, AXES, pairs)  71.2 us
    ppermute x14, starting transfers between devices, swap(): return lax.ppermute(value, AXES, pairs)  13.4 us
  transfers between devices with their start and end apart: 17, of which 11 were waited for; matrix products, arithmetic and copies ran while one was open for 8% of the time, Pallas kernels for 47%

profile of v4, /device:TPU:0, one launch (start us, length us, event | category | flops | bytes accessed | tf_op | source)
XLA Modules:
  0.0 262.6 jit_solution(4983883048391084422)
XLA Ops:
  8.9 4.1 %collective-permute-start = (bf16[96,384]{1,0:T(8,128)(2,1)S(1)}, bf16[96,384]{1,0:T(8,128)(2,1)S(1)}, u32[]{:S(2)}, u32[]{:S(2)}) collective-permute-start(bf16[96,384]{1,0:T(8,128)(2,1)S(1)} %fusion.23), channel_id=1, source_target_pairs={{0,16},{1,17},{2,18},{3,19},{4,20},{5,21},{6,22},{7,23},{8,24},{9,... | collective-permute-start | bytes 221192 | tf_op jit(solution)/shard_map/ppermute | solution.py:462
  14.0 1.7 pad_maximum_fusion.5
  17.7 4.5 %collective-permute-done.1 = bf16[2,96,384]{2,1,0:T(8,128)(2,1)S(1)} collective-permute-done((bf16[2,96,384]{2,1,0:T(8,128)(2,1)S(1)}, bf16[2,96,384]{2,1,0:T(8,128)(2,1)S(1)}, u32[]{:S(2)}, u32[]{:S(2)}) %collective-permute-start.1) | collective-permute-done | bytes 147488 | tf_op jit(solution)/shard_map/ppermute | solution.py:462
  22.3 1.8 collective-permute-start.2
  24.1 8.4 %collective-permute-done.2 = bf16[2,2,96,384]{3,2,1,0:T(8,128)(2,1)S(1)} collective-permute-done((bf16[2,2,96,384]{3,2,1,0:T(8,128)(2,1)S(1)}, bf16[2,2,96,384]{3,2,1,0:T(8,128)(2,1)S(1)}, u32[]{:S(2)}, u32[]{:S(2)}) %collective-permute-start.2) | collective-permute-done | bytes 294944 | tf_op jit(solution)/shard_map/ppermute | solution.py:462
  33.0 4.3 %collective-permute-start.3 = (f32[2,2,16,288]{3,2,1,0:T(8,128)S(1)}, f32[2,2,16,288]{3,2,1,0:T(8,128)S(1)}, u32[]{:S(2)}, u32[]{:S(2)}) collective-permute-start(f32[2,2,16,288]{3,2,1,0:T(8,128)S(1)} %dynamic-slice_bitcast_fusion.1), channel_id=1, source_target_pairs={{0,16},{1,17},{2,18},{3,19},{4,20},{5,21},{6,22},{7,23},{8,24},{9,... | collective-permute-start | bytes 221192 | tf_op jit(solution)/shard_map/ppermute | solution.py:462
  37.3 8.0 %collective-permute-done.3 = f32[2,2,16,288]{3,2,1,0:T(8,128)S(1)} collective-permute-done((f32[2,2,16,288]{3,2,1,0:T(8,128)S(1)}, f32[2,2,16,288]{3,2,1,0:T(8,128)S(1)}, u32[]{:S(2)}, u32[]{:S(2)}) %collective-permute-start.3) | collective-permute-done | bytes 73760 | tf_op jit(solution)/shard_map/ppermute | solution.py:462
  45.8 4.3 %collective-permute-done.4 = f32[2,2,16,288]{3,2,1,0:T(8,128)S(1)} collective-permute-done((f32[2,2,16,288]{3,2,1,0:T(8,128)S(1)}, f32[2,2,16,288]{3,2,1,0:T(8,128)S(1)}, u32[]{:S(2)}, u32[]{:S(2)}) %collective-permute-start.4) | collective-permute-done | bytes 73760 | tf_op jit(solution)/shard_map/ppermute | solution.py:462
  51.8 5.3 %collective-permute-done.5 = f32[2,2,16,288]{3,2,1,0:T(8,128)S(1)} collective-permute-done((f32[2,2,16,288]{3,2,1,0:T(8,128)S(1)}, f32[2,2,16,288]{3,2,1,0:T(8,128)S(1)}, u32[]{:S(2)}, u32[]{:S(2)}) %collective-permute-start.5) | collective-permute-done | bytes 73760 | tf_op jit(solution)/shard_map/ppermute | solution.py:462
  59.3 1.6 collective-permute-start.7
  61.9 23.1 %shard_map.228 = (bf16[16,256,384]{2,1,0:T(8,128)(2,1)}, bf16[16,1152,256]{2,1,0:T(8,128)(2,1)}, f32[16,8,256]{2,1,0:T(8,128)}, bf16[16,384,256]{2,1,0:T(8,128)(2,1)}) custom-call(bf16[16,256,384]{2,1,0:T(8,128)(2,1)} %tokens_ref.5, f32[16,6,384]{2,1,0:T(8,128)} %reshape.189.mod_ref, bf16[1152,384]{1,0:T(8,128)(2,1)} %bitcast.192, ...), custom_call_target="tpu_custom_call" | custom-call | flops 5234491392 | bytes 18874368 | tf_op jit(solution)/shard_map/pallas_call | solution.py:420
  85.3 1.7 slice.181
  87.0 2.9 %fusion.35 = (bf16[8,192,384]{2,1,0:T(8,128)(2,1)S(1)}, bf16[8,192,384]{2,1,0:T(8,128)(2,1)}) fusion(bf16[8,432,384]{2,1,0:T(8,128)(2,1)} %bitcast.197), kind=kLoop, calls=%fused_computation.135 | loop fusion | bytes 4718592 | tf_op jit(solution)/shard_map/slice | solution.py:518
  92.8 59.3 %shard_map.229 = (bf16[16,256,384]{2,1,0:T(8,128)(2,1)}, f32[16,256,384]{2,1,0:T(8,128)}, bf16[16,384,256]{2,1,0:T(8,128)(2,1)}, f32[16,4,384]{2,1,0:T(4,128)}, ...) custom-call(bf16[16,256,384]{2,1,0:T(8,128)(2,1)} %tokens_ref.5, ...), custom_call_target="tpu_custom_call" | custom-call | flops 32614907904 | bytes 22020096 | tf_op jit(solution)/shard_map/pallas_call | solution.py:420
  152.1 2.6 reshape.210
  154.9 1.8 pad_maximum_fusion
  158.3 26.4 %shard_map.230 = (bf16[16,1152,256]{2,1,0:T(8,128)(2,1)}, bf16[1152,384]{1,0:T(8,128)(2,1)}, f32[1152,128]{1,0:T(8,128)}) custom-call(bf16[16,1152,256]{2,1,0:T(8,128)(2,1)} %get-tuple-element.40.qkv_ref, f32[16,8,256]{2,1,0:T(8,128)} %get-tuple-element.41.lse_ref, bf16[16,384,256]{2,1,0:T(8,128)(2,1)} %get-tuple-element.42.grad_attended_ref, ...), custom_call_target="tpu_custom_call" | custom-call | flops 1 | bytes 1 | tf_op jit(solution)/shard_map/pallas_call | solution.py:420
  187.9 13.9 %shard_map.231 = (bf16[16,256,384]{2,1,0:T(8,128)(2,1)}, f32[16,2,384]{2,1,0:T(2,128)}) custom-call(bf16[16,1152,256]{2,1,0:T(8,128)(2,1)} %get-tuple-element.46.grad_qkv_ref, bf16[16,256,384]{2,1,0:T(8,128)(2,1)} %tokens_ref.5, f32[16,256,384]{2,1,0:T(8,128)} %get-tuple-element.47.grad_middle_ref, f32[16,6,384]{2,1,0:T(8,128)} %reshape.189.mod_ref, ...), custom_call_target="tpu_custom_call" | custom-call | flops 1 | bytes 1 | tf_op jit(solution)/shard_map/pallas_call | solution.py:420
  203.5 12.1 %collective-permute-done.9 = bf16[2,2,96,384]{3,2,1,0:T(8,128)(2,1)S(1)} collective-permute-done((bf16[2,2,96,384]{3,2,1,0:T(8,128)(2,1)S(1)}, bf16[2,2,96,384]{3,2,1,0:T(8,128)(2,1)S(1)}, u32[]{:S(2)}, u32[]{:S(2)}) %collective-permute-start.9) | collective-permute-done | bytes 294944 | tf_op jit(solution)/shard_map/ppermute | solution.py:462
  215.9 10.3 %collective-permute-done.10 = bf16[2,112,384]{2,1,0:T(8,128)(2,1)S(1)} collective-permute-done((bf16[2,112,384]{2,1,0:T(8,128)(2,1)S(1)}, bf16[2,112,384]{2,1,0:T(8,128)(2,1)S(1)}, u32[]{:S(2)}, u32[]{:S(2)}) %collective-permute-start.10) | collective-permute-done | bytes 172064 | tf_op jit(solution)/shard_map/ppermute | solution.py:462
  226.4 5.8 %collective-permute-done.11 = bf16[144,384]{1,0:T(8,128)(2,1)S(1)} collective-permute-done((bf16[144,384]{1,0:T(8,128)(2,1)S(1)}, bf16[144,384]{1,0:T(8,128)(2,1)S(1)}, u32[]{:S(2)}, u32[]{:S(2)}) %collective-permute-start.11) | collective-permute-done | bytes 110624 | tf_op jit(solution)/shard_map/ppermute | solution.py:462
  233.5 11.0 %collective-permute-done.12 = bf16[640,384]{1,0:T(8,128)(2,1)S(1)} collective-permute-done((bf16[640,384]{1,0:T(8,128)(2,1)S(1)}, bf16[640,384]{1,0:T(8,128)(2,1)S(1)}, u32[]{:S(2)}, u32[]{:S(2)}) %collective-permute-start.12) | collective-permute-done | bytes 491552 | tf_op jit(solution)/shard_map/ppermute | solution.py:462
  244.9 1.4 fusion.30
  251.4 2.0 convert_reduce_fusion
  (170 shorter events, 29.7 us)
Async XLA Ops:
  7.2 16.8 %copy-start.13 = (bf16[288]{0:T(512)(128)(2,1)S(1)}, bf16[288]{0:T(512)(128)(2,1)}, u32[]{:S(2)}) copy-start(bf16[288]{0:T(512)(128)(2,1)} %param.16) | copy-start | bytes 1732
  7.2 78.0 %all-gather.6.cloned.1.call-start = ((), (), s32[]{:S(2)}) async-start(), calls=%async_computation.3 | async-start | bytes 2985984 | tf_op jit(solution)/shard_map/all_gather | solution.py:516
  8.9 8.0 %collective-permute-start = (bf16[96,384]{1,0:T(8,128)(2,1)S(1)}, bf16[96,384]{1,0:T(8,128)(2,1)S(1)}, u32[]{:S(2)}, u32[]{:S(2)}) collective-permute-start(bf16[96,384]{1,0:T(8,128)(2,1)S(1)} %fusion.23), channel_id=1, source_target_pairs={{0,16},{1,17},{2,18},{3,19},{4,20},{5,21},{6,22},{7,23},{8,24},{9,... | collective-permute-start | bytes 221192 | tf_op jit(solution)/shard_map/ppermute | solution.py:462
  15.7 142.7 %all-gather.4.cloned.1.call-start = ((), (), s32[]{:S(2)}) async-start(), calls=%async_computation.1 | async-start | bytes 1990656 | tf_op jit(solution)/shard_map/all_gather | solution.py:524
  17.0 15.7 %copy-start.5 = (bf16[384,288]{0,1:T(8,128)(2,1)S(1)}, bf16[384,288]{0,1:T(8,128)(2,1)}, u32[]{:S(2)}) copy-start(bf16[384,288]{0,1:T(8,128)(2,1)} %param.15) | copy-start | bytes 663556
  17.0 5.2 %collective-permute-start.1 = (bf16[2,96,384]{2,1,0:T(8,128)(2,1)S(1)}, bf16[2,96,384]{2,1,0:T(8,128)(2,1)S(1)}, u32[]{:S(2)}, u32[]{:S(2)}) collective-permute-start(bf16[2,96,384]{2,1,0:T(8,128)(2,1)S(1)} %pad_maximum_fusion.14), channel_id=1, source_target_pairs={{0,8},{1,9},{2,10},{3,11},{4,12},{5,13},{6,14},{7,15},{8,0},{9,1},... | collective-permute-start | bytes 442376 | tf_op jit(solution)/shard_map/ppermute | solution.py:462
  22.3 10.2 %collective-permute-start.2 = (bf16[2,2,96,384]{3,2,1,0:T(8,128)(2,1)S(1)}, bf16[2,2,96,384]{3,2,1,0:T(8,128)(2,1)S(1)}, u32[]{:S(2)}, u32[]{:S(2)}) collective-permute-start(bf16[2,2,96,384]{3,2,1,0:T(8,128)(2,1)S(1)} %pad_maximum_fusion.7), channel_id=1, source_target_pairs={{0,4},{1,5},{2,6},{3,7},{4,0},{5,1},{6,2},{7,3},{8,12},{9,13},{10,... | collective-permute-start | bytes 884744 | tf_op jit(solution)/shard_map/ppermute | solution.py:462
  33.0 12.3 %collective-permute-start.3 = (f32[2,2,16,288]{3,2,1,0:T(8,128)S(1)}, f32[2,2,16,288]{3,2,1,0:T(8,128)S(1)}, u32[]{:S(2)}, u32[]{:S(2)}) collective-permute-start(f32[2,2,16,288]{3,2,1,0:T(8,128)S(1)} %dynamic-slice_bitcast_fusion.1), channel_id=1, source_target_pairs={{0,16},{1,17},{2,18},{3,19},{4,20},{5,21},{6,22},{7,23},{8,24},{9,... | collective-permute-start | bytes 221192 | tf_op jit(solution)/shard_map/ppermute | solution.py:462
  45.4 4.7 %collective-permute-start.4 = (f32[2,2,16,288]{3,2,1,0:T(8,128)S(1)}, f32[2,2,16,288]{3,2,1,0:T(8,128)S(1)}, u32[]{:S(2)}, u32[]{:S(2)}) collective-permute-start(f32[2,2,16,288]{3,2,1,0:T(8,128)S(1)} %fusion.17), channel_id=1, source_target_pairs={{0,8},{1,9},{2,10},{3,11},{4,12},{5,13},{6,14},{7,15},{8,0},{9,1},... | collective-permute-start | bytes 221192 | tf_op jit(solution)/shard_map/ppermute | solution.py:462
  45.6 12.4 %collective-permute-start.6 = (bf16[8,88,384]{2,1,0:T(8,128)(2,1)S(1)}, bf16[8,88,384]{2,1,0:T(8,128)(2,1)S(1)}, u32[]{:S(2)}, u32[]{:S(2)}) collective-permute-start(bf16[8,88,384]{2,1,0:T(8,128)(2,1)S(1)} %slice.174), channel_id=1, source_target_pairs={{0,1},{1,0},{2,3},{3,2},{4,5},{5,4},{6,7},{7,6},{8,9},{9,8},{10,11... | collective-permute-start | bytes 1622024 | tf_op jit(solution)/shard_map/ppermute | solution.py:462
  50.1 6.9 %collective-permute-start.5 = (f32[2,2,16,288]{3,2,1,0:T(8,128)S(1)}, f32[2,2,16,288]{3,2,1,0:T(8,128)S(1)}, u32[]{:S(2)}, u32[]{:S(2)}) collective-permute-start(f32[2,2,16,288]{3,2,1,0:T(8,128)S(1)} %bitcast.231), channel_id=1, source_target_pairs={{0,4},{1,5},{2,6},{3,7},{4,0},{5,1},{6,2},{7,3},{8,12},{9,13},{10,... | collective-permute-start | bytes 221192 | tf_op jit(solution)/shard_map/ppermute | solution.py:462
  59.3 25.8 %collective-permute-start.7 = (bf16[2,8,16,384]{3,2,1,0:T(8,128)(2,1)S(1)}, bf16[2,8,16,384]{3,2,1,0:T(8,128)(2,1)S(1)}, u32[]{:S(2)}, u32[]{:S(2)}) collective-permute-start(bf16[2,8,16,384]{3,2,1,0:T(8,128)(2,1)S(1)} %pad_maximum_fusion.9), channel_id=1, source_target_pairs={{0,2},{1,3},{2,0},{3,1},{4,6},{5,7},{6,4},{7,5},{8,10},{9,11},{10,... | collective-permute-start | bytes 589832 | tf_op jit(solution)/shard_map/ppermute | solution.py:462
  91.6 140.7 %reduce-scatter.2.cloned.1.call-start = ((), (), s32[]{:S(2)}) async-start(), calls=%async_computation.2 | async-start | bytes 2985984 | tf_op jit(solution)/shard_map/reduce_scatter | solution.py:656
  187.8 15.3 %collective-permute-start.8 = (bf16[8,80,384]{2,1,0:T(8,128)(2,1)S(1)}, bf16[8,80,384]{2,1,0:T(8,128)(2,1)S(1)}, u32[]{:S(2)}, u32[]{:S(2)}) collective-permute-start(bf16[8,80,384]{2,1,0:T(8,128)(2,1)S(1)} %dynamic-slice_bitcast_fusion), channel_id=1, source_target_pairs={{0,1},{1,0},{2,3},{3,2},{4,5},{5,4},{6,7},{7,6},{8,9},{9,8},{10,11... | collective-permute-start | bytes 1474568 | tf_op jit(solution)/shard_map/ppermute | solution.py:462
  187.8 13.9 %copy-start.6 = (f32[16,4,384]{2,1,0:T(4,128)S(1)}, f32[16,4,384]{2,1,0:T(4,128)}, u32[]{:S(2)}) copy-start(f32[16,4,384]{2,1,0:T(4,128)} %get-tuple-element.50) | copy-start | bytes 294916
  203.3 12.3 %collective-permute-start.9 = (bf16[2,2,96,384]{3,2,1,0:T(8,128)(2,1)S(1)}, bf16[2,2,96,384]{3,2,1,0:T(8,128)(2,1)S(1)}, u32[]{:S(2)}, u32[]{:S(2)}) collective-permute-start(bf16[2,2,96,384]{3,2,1,0:T(8,128)(2,1)S(1)} %pad_maximum_fusion.8), channel_id=1, source_target_pairs={{0,4},{1,5},{2,6},{3,7},{4,0},{5,1},{6,2},{7,3},{8,12},{9,13},{10,... | collective-permute-start | bytes 884744 | tf_op jit(solution)/shard_map/ppermute | solution.py:462
  215.8 10.4 %collective-permute-start.10 = (bf16[2,112,384]{2,1,0:T(8,128)(2,1)S(1)}, bf16[2,112,384]{2,1,0:T(8,128)(2,1)S(1)}, u32[]{:S(2)}, u32[]{:S(2)}) collective-permute-start(bf16[2,112,384]{2,1,0:T(8,128)(2,1)S(1)} %pad_maximum_fusion.13), channel_id=1, source_target_pairs={{0,8},{1,9},{2,10},{3,11},{4,12},{5,13},{6,14},{7,15},{8,0},{9,1},... | collective-permute-start | bytes 516104 | tf_op jit(solution)/shard_map/ppermute | solution.py:462
  226.3 5.9 %collective-permute-start.11 = (bf16[144,384]{1,0:T(8,128)(2,1)S(1)}, bf16[144,384]{1,0:T(8,128)(2,1)S(1)}, u32[]{:S(2)}, u32[]{:S(2)}) collective-permute-start(bf16[144,384]{1,0:T(8,128)(2,1)S(1)} %pad_maximum_fusion.15), channel_id=1, source_target_pairs={{0,16},{1,17},{2,18},{3,19},{4,20},{5,21},{6,22},{7,23},{8,24},{9,... | collective-permute-start | bytes 331784 | tf_op jit(solution)/shard_map/ppermute | solution.py:462
  232.3 12.2 %copy-start.3 = (bf16[1,432,384]{2,1,0:T(8,128)(2,1)S(1)}, bf16[1,432,384]{2,1,0:T(8,128)(2,1)}, u32[]{:S(2)}) copy-start(bf16[1,432,384]{2,1,0:T(8,128)(2,1)} %reduce-scatter.2.cloned.1.call-done) | copy-start | bytes 995332
  232.3 12.5 %copy-start.9 = (f32[16,2,384]{2,1,0:T(2,128)S(1)}, f32[16,2,384]{2,1,0:T(2,128)}, u32[]{:S(2)}) copy-start(f32[16,2,384]{2,1,0:T(2,128)} %get-tuple-element.49) | copy-start | bytes 147460
  233.4 11.5 %copy-start.2 = (bf16[2304,384]{1,0:T(8,128)(2,1)S(1)}, bf16[2304,384]{1,0:T(8,128)(2,1)}, u32[]{:S(2)}) copy-start(bf16[2304,384]{1,0:T(8,128)(2,1)} %all-gather.4.cloned.1.call-done) | copy-start | bytes 5308420
  233.4 11.5 %copy-start.10 = (f32[16,384]{1,0:T(8,128)S(1)}, f32[16,384]{1,0:T(8,128)}, u32[]{:S(2)}) copy-start(f32[16,384]{1,0:T(8,128)} %param.14) | copy-start | bytes 73732
  233.4 11.0 %collective-permute-start.12 = (bf16[640,384]{1,0:T(8,128)(2,1)S(1)}, bf16[640,384]{1,0:T(8,128)(2,1)S(1)}, u32[]{:S(2)}, u32[]{:S(2)}) collective-permute-start(bf16[640,384]{1,0:T(8,128)(2,1)S(1)} %pad_maximum_fusion.3), channel_id=1, source_target_pairs={{0,2},{1,3},{2,0},{3,1},{4,6},{5,7},{6,4},{7,5},{8,10},{9,11},{10,... | collective-permute-start | bytes 1474568 | tf_op jit(solution)/shard_map/ppermute | solution.py:462
  244.7 2.1 collective-permute-start.13
  (7 other events, 15.1 us)
Sparse Core Ops, SparseCore 0:
  15.8 60.7 all-gather.5
  91.7 42.5 all-gather.3
  156.9 70.2 reduce-scatter.1

commit v5 on v4

--- a/solution.py
+++ b/solution.py
@@ -129,19 +129,15 @@
     cotangent_ref,
     attended_ref,
     mod_ref,
-    out_weight_ref,
+    late_ref,
     out_bias_ref,
-    up_weight_ref,
-    up_bias_ref,
-    down_weight_ref,
+    up_bias_row_ref,
     down_bias_ref,
     output_ref,
     grad_middle_ref,
     grad_attended_ref,
     grad_mod_ref,
-    out_grad_ref,
-    up_grad_ref,
-    down_grad_ref,
+    late_grad_ref,
     out_bias_grad_ref,
     up_bias_grad_ref,
     down_bias_grad_ref,
@@ -149,6 +145,10 @@
     up_acc,
     down_acc,
     bias_acc,
+    out_weight_ref,
+    up_weight_ref,
+    down_weight_ref,
+    up_bias_ref,
     out_back,
     up_back,
     down_back,
@@ -161,9 +161,12 @@
     chunk,
 ):
     step = pl.program_id(0)
+    n_dp = late_ref.shape[0]
     latents, length, width = tokens_ref.shape
     hidden_width = up_weight_ref.shape[0]
     tokens_all = latents * length
+    up_rows, out_rows = hidden_width // n_dp, width // n_dp
+    out_low = up_rows + out_rows * (hidden_width // width)
 
     @pl.when(step == 0)
     def _():
@@ -171,9 +174,19 @@
         up_acc[...] = jnp.zeros_like(up_acc)
         down_acc[...] = jnp.zeros_like(down_acc)
         bias_acc[...] = jnp.zeros_like(bias_acc)
+        for owner in range(n_dp):
+            up_weight_ref[owner * up_rows : (owner + 1) * up_rows, :] = late_ref[owner, :up_rows, :]
+            outs = slice(owner * out_rows, (owner + 1) * out_rows)
+            for fold in range(hidden_width // width):
+                low = up_rows + fold * out_rows
+                down_weight_ref[outs, fold * width : (fold + 1) * width] = late_ref[
+                    owner, low : low + out_rows, :
+                ]
+            out_weight_ref[outs, :] = late_ref[owner, out_low:, :]
         out_back[...] = out_weight_ref[...].T
         up_back[...] = up_weight_ref[...].T
         down_back[...] = down_weight_ref[...].T
+        up_bias_ref[...] = jnp.broadcast_to(up_bias_row_ref[...], (128, hidden_width)).T
 
     attended = beside(*[attended_ref[latent] for latent in range(latents)])
     branch_wide = dot_nn(out_weight_ref[...], attended)
@@ -279,9 +292,18 @@
 
     @pl.when(step == pl.num_programs(0) - 1)
     def _():
-        out_grad_ref[...] = out_acc[...].T.astype(BF16)
-        up_grad_ref[...] = up_acc[:, :width].astype(BF16)
-        down_grad_ref[...] = down_acc[...].T.astype(BF16)
+        out_back[...] = out_acc[...].T.astype(BF16)
+        up_back[...] = down_acc[...].T.astype(BF16)
+        for owner in range(n_dp):
+            ups = slice(owner * up_rows, (owner + 1) * up_rows)
+            late_grad_ref[owner, :up_rows, :] = up_acc[ups, :width].astype(BF16)
+            outs = slice(owner * out_rows, (owner + 1) * out_rows)
+            for fold in range(hidden_width // width):
+                low = up_rows + fold * out_rows
+                late_grad_ref[owner, low : low + out_rows, :] = up_back[
+                    outs, fold * width : (fold + 1) * width
+                ]
+            late_grad_ref[owner, out_low:, :] = out_back[outs, :]
         up_bias_grad_ref[...] = up_acc[:, width:]
         down_bias_grad_ref[...] = bias_acc[0:1, :]
         out_bias_grad_ref[...] = bias_acc[1:2, :]
@@ -292,10 +314,17 @@
     lse_ref,
     grad_attended_ref,
     normed_ref,
-    grad_qkv_ref,
+    tokens_ref,
+    grad_middle_ref,
+    mod_ref,
+    weight_ref,
+    tokens_grad_ref,
+    grad_mod_ref,
     weight_grad_ref,
     bias_grad_ref,
     acc,
+    weight_back,
+    grad_qkv_ref,
 ):
     step = pl.program_id(0)
     latents, length, width = normed_ref.shape
@@ -304,6 +333,7 @@
     @pl.when(step == 0)
     def _():
         acc[...] = jnp.zeros_like(acc)
+        weight_back[...] = weight_ref[...].T
 
     keys_all = [qkv_ref[latent, width : 2 * width, :].T for latent in range(latents)]
     values_all = [qkv_ref[latent, 2 * width : 3 * width, :].T for latent in range(latents)]
@@ -363,32 +393,8 @@
 
     grad_qkv = beside(*[grad_qkv_ref[latent] for latent in range(latents)])
     normed = normed_ref[...].reshape(latents * length, width)
+    grad_normed_wide = dot_nn(weight_back[...], grad_qkv)
     acc[...] += dot_nn(grad_qkv, beside(normed, jnp.ones((latents * length, 128), BF16)))
-
-    @pl.when(step == pl.num_programs(0) - 1)
-    def _():
-        weight_grad_ref[...] = acc[:, :width].astype(BF16)
-        bias_grad_ref[...] = acc[:, width:]
-
-
-def first_norm_kernel(
-    grad_qkv_ref,
-    tokens_ref,
-    grad_middle_ref,
-    mod_ref,
-    weight_ref,
-    tokens_grad_ref,
-    grad_mod_ref,
-    weight_back,
-):
-    latents, length, width = tokens_ref.shape
-
-    @pl.when(pl.program_id(0) == 0)
-    def _():
-        weight_back[...] = weight_ref[...].T
-
-    grad_qkv = beside(*[grad_qkv_ref[latent] for latent in range(latents)])
-    grad_normed_wide = dot_nn(weight_back[...], grad_qkv)
     for latent in range(latents):
         grad_normed_tall = grad_normed_wide[:, latent * length : (latent + 1) * length].T
         scale_one = 1.0 + mod_ref[latent, 1:2, :]
@@ -404,6 +410,54 @@
                 BF16
             )
         grad_mod_ref[latent] = above(first, second)
+
+    @pl.when(step == pl.num_programs(0) - 1)
+    def _():
+        weight_grad_ref[...] = acc[:, :width].astype(BF16)
+        bias_grad_ref[...] = acc[:, width:]
+
+
+def finish_kernel(
+    core_ref,
+    mine_ref,
+    came_ref,
+    silu_ref,
+    ada_ref,
+    ada_bias_ref,
+    qkv_ref,
+    up_ref,
+    down_ref,
+    out_ref,
+    bias_ref,
+    *,
+    tail_rows,
+):
+    first = core_ref[0] == 0
+    own = ada_ref.shape[0]
+    half_rows = qkv_ref.shape[0] // 2
+    up_rows, out_rows = up_ref.shape[0], out_ref.shape[0]
+    width = out_ref.shape[1]
+    out_low = tail_rows + up_rows + down_ref.shape[1] // width * out_rows
+    end = out_low + out_rows
+    mine = mine_ref[:tail_rows, :].astype(F32)
+    came = came_ref[:tail_rows, :].astype(F32)
+    lower = jnp.where(first, mine, came)
+    upper = jnp.where(first, came, mine)
+    qkv_ref[:half_rows, :] = lower[:half_rows]
+    qkv_ref[half_rows:, :] = upper[:half_rows]
+    bias_ref[0:1, :] = lower[half_rows : half_rows + 1]
+    bias_ref[1:2, :] = upper[half_rows : half_rows + 1]
+    sums = mine_ref[tail_rows:end, :].astype(F32) + came_ref[tail_rows:end, :].astype(F32)
+    up_ref[...] = sums[:up_rows]
+    for fold in range(down_ref.shape[1] // width):
+        low = up_rows + fold * out_rows
+        down_ref[:, fold * width : (fold + 1) * width] = sums[low : low + out_rows]
+    out_ref[...] = sums[out_low - tail_rows :]
+    mine = mine_ref[end:, :]
+    came = came_ref[end:, :]
+    columns = above(jnp.where(first, mine, came), jnp.where(first, came, mine))
+    ada_ref[...] = dot_tn(columns, silu_ref[...])[:own]
+    ada_bias_ref[...] = jnp.sum(columns.astype(F32), axis=0, keepdims=True)
 
 
 def each(shape, count):
@@ -514,11 +568,6 @@
         [up_weight.T, down_shard.reshape(folds * out_rows, width), out_weight.T]
     )
     late = lax.all_gather(late_shard, "dp", axis=0)
-    up_all = late[:, :up_rows].reshape(hidden_width, width)
-    down_all = late[:, up_rows : up_rows + folds * out_rows]
-    down_all = down_all.reshape(n_dp, folds, out_rows, width).transpose(0, 2, 1, 3)
-    down_all = down_all.reshape(width, hidden_width)
-    out_all = late[:, up_rows + folds * out_rows :].reshape(width, width)
     silu_low = jax.nn.silu(conditioning).astype(BF16)
     ada_shard, _ = lax.optimization_barrier((ada_weight.T, late))
     ada_all = lax.all_gather(ada_shard, "dp", axis=0, tiled=True)
@@ -526,7 +575,7 @@
     qkv_rows = qkv_weight.shape[1]
     half_rows = qkv_rows // 2
     core = hops.mine("rep", 1)
-    bias_shard = jnp.concatenate([qv_bias, out_bias, up_bias, down_bias])
+    bias_shard = jnp.concatenate([qv_bias, out_bias, up_bias, down_bias, ada_bias])
     bias_rows = up_to(bias_shard.shape[0], width) // width
     bias_block = jnp.pad(bias_shard, (0, bias_rows * width - bias_shard.shape[0]))
     front = jnp.concatenate(
@@ -537,8 +586,20 @@
         ]
     )
     front = pad_rows(front, up_to(front.shape[0], 8))
-    for done, bit in enumerate(dp_bits[::-1]):
+    ada_pair = hops.both(ada_weight.T, hops.swap(ada_weight.T, "dp", 1), "dp", 1, 0)
+    high_bits = dp_bits[:0:-1]
+    for done, bit in enumerate(high_bits):
         front = hops.both(front, hops.swap(front, "dp", bit), "dp", bit, done)
+
+    silu_part = front[..., half_rows : half_rows + latents, :].reshape(-1, width)
+    mod = dot_nt(silu_part, ada_pair.reshape(-1, width))
+    mod = mod.reshape((2,) * len(high_bits) + (latents, -1))
+    for done, bit in enumerate(high_bits):
+        kept, sent = hops.cut(mod, "dp", bit, done)
+        mod = hops.both(kept, hops.swap(sent, "dp", bit), "dp", bit, done)
+    mod = mod.reshape(n_dp // 2, latents, -1).transpose(1, 0, 2).reshape(latents, -1)
+
+    front = hops.both(front, hops.swap(front, "dp", 1), "dp", 1, len(high_bits))
     front = front.reshape(n_dp, -1, width)
     front = front[:, : half_rows + latents + bias_rows]
     silu_group = front[:, half_rows : half_rows + latents].reshape(n_dp * latents, width)
@@ -548,28 +609,23 @@
     silu_all = halves[:, :, half_rows:]
     for bit in hops.bits("rep")[1:]:
         silu_all = hops.both(silu_all, hops.swap(silu_all, "rep", bit), "rep", bit, 0)
-    silu_all = silu_all.reshape(n_rep, n_dp, latents, width).reshape(-1, width)
+    silu_all = silu_all.reshape(n_rep // 2, 2, n_dp * latents, width).transpose(1, 0, 2, 3)
+    silu_all = silu_all.reshape(-1, width)
 
     bias_all = front[:, half_rows + latents : half_rows + latents + bias_rows]
     bias_all = bias_all.reshape(n_dp, -1).astype(F32)
     cuts = [0]
-    for part in (qv_bias, out_bias, up_bias, down_bias):
+    for part in (qv_bias, out_bias, up_bias, down_bias, ada_bias):
         cuts.append(cuts[-1] + part.shape[0])
-    qv_full, out_full, up_full, down_full = (
+    qv_full, out_full, up_full, down_full, ada_full = (
         bias_all[:, low:high].reshape(1, -1) for low, high in zip(cuts[:-1], cuts[1:])
     )
     qkv_bias = jnp.concatenate(
         [qv_full[:, :width], jnp.zeros((1, width), F32), qv_full[:, width:]], axis=1
     )
     qkv_bias = jnp.broadcast_to(qkv_bias.reshape(-1, 1), (3 * width, 128))
-    up_full = jnp.broadcast_to(up_full.reshape(-1, 1), (hidden_width, 128))
-
-    mod = jnp.dot(silu_group, ada_weight, preferred_element_type=F32) + ada_bias.astype(F32)
-    mod = mod.reshape((2,) * len(dp_bits) + (latents, -1))
-    for done, bit in enumerate(dp_bits[::-1]):
-        kept, sent = hops.cut(mod, "dp", bit, done)
-        mod = hops.both(kept, hops.swap(sent, "dp", bit), "dp", bit, done)
-    modulation = mod.reshape(n_dp, latents, -1).transpose(1, 0, 2).reshape(latents, 6, width)
+
+    modulation = (mod + ada_full).reshape(latents, 6, width)
 
     normed, qkv, lse, attended = run_kernel(
         attention_forward_kernel,
@@ -597,9 +653,7 @@
         grad_middle,
         grad_attended,
         grad_mod_two,
-        out_grad,
-        up_grad,
-        down_grad,
+        late_grad,
         out_bias_grad,
         up_bias_grad,
         down_bias_grad,
@@ -613,9 +667,7 @@
             shape_of((latents, 4, width), F32),
         ],
         [
-            shape_of((width, width), BF16),
-            shape_of((hidden_width, width), BF16),
-            shape_of((width, hidden_width), BF16),
+            shape_of(late.shape, BF16),
             shape_of((1, width), F32),
             shape_of((hidden_width, 128), F32),
             shape_of((1, width), F32),
@@ -626,6 +678,10 @@
             pltpu.VMEM((hidden_width, width), F32),
             pltpu.VMEM((8, width), F32),
             pltpu.VMEM((width, width), BF16),
+            pltpu.VMEM((hidden_width, width), BF16),
+            pltpu.VMEM((width, hidden_width), BF16),
+            pltpu.VMEM((hidden_width, 128), F32),
+            pltpu.VMEM((width, width), BF16),
             pltpu.VMEM((width, hidden_width), BF16),
             pltpu.VMEM((hidden_width, width), BF16),
             pltpu.VMEM((hidden_width, 4 * length), BF16),
@@ -635,7 +691,7 @@
             pltpu.VMEM((4 * length, width), F32),
         ],
         [tokens, cotangent, attended, modulation],
-        [out_all, out_full, up_all, up_full, down_all, down_full],
+        [late, out_full, up_full, down_full],
         pl.CostEstimate(
             flops=6 * rows * width * (width + 2 * hidden_width),
             bytes_accessed=rows * width * 14,
@@ -643,28 +699,22 @@
         ),
     )
 
-    late_grad = jnp.concatenate(
-        [
-            up_grad.reshape(n_dp, up_rows, width),
-            down_grad.reshape(n_dp, out_rows, folds, width)
-            .transpose(0, 2, 1, 3)
-            .reshape(n_dp, folds * out_rows, width),
-            out_grad.reshape(n_dp, out_rows, width),
-        ],
-        axis=1,
-    )
     late_sum = lax.psum_scatter(late_grad, "dp", scatter_dimension=0, tiled=True)
     late_sum = late_sum.reshape(-1, width)
 
     normed, ada_all = lax.optimization_barrier((normed, ada_all))
-    grad_qkv, qkv_grad, qkv_bias_grad = run_kernel(
+    tokens_grad, grad_mod_one, qkv_grad, qkv_bias_grad = run_kernel(
         attention_backward_kernel,
         2,
-        [shape_of((latents, 3 * width, length), BF16)],
+        [shape_of((latents, length, width), BF16), shape_of((latents, 2, width), F32)],
         [shape_of((3 * width, width), BF16), shape_of((3 * width, 128), F32)],
-        [pltpu.VMEM((3 * width, width + 128), F32)],
-        [qkv, lse, grad_attended, normed],
-        [],
+        [
+            pltpu.VMEM((3 * width, width + 128), F32),
+            pltpu.VMEM((width, 3 * width), BF16),
+            pltpu.VMEM((2, 3 * width, length), BF16),
+        ],
+        [qkv, lse, grad_attended, normed, tokens, grad_middle, modulation],
+        [qkv_full],
         pl.CostEstimate(flops=1, bytes_accessed=1, transcendentals=0),
     )
 
@@ -678,7 +728,7 @@
         ],
         axis=1,
     ).astype(BF16)
-    bias_part = cuts[-1] // 2
+    bias_part = cuts[-2] // 2
     bias_blocks = bias_blocks.reshape(n_dp, 2, 1, bias_part)
     tail_rows = up_to(half_rows + 1, 8)
     bias_blocks = jnp.pad(
@@ -689,16 +739,6 @@
     kept, sent = hops.cut(blocks, "rep", 1, 1)
     total = kept.astype(F32) + hops.swap(sent, "rep", 1).astype(F32)
 
-    tokens_grad, grad_mod_one = run_kernel(
-        first_norm_kernel,
-        4,
-        [shape_of((latents, length, width), BF16), shape_of((latents, 2, width), F32)],
-        [],
-        [pltpu.VMEM((width, 3 * width), BF16)],
-        [grad_qkv, tokens, grad_middle, modulation],
-        [qkv_full],
-        pl.CostEstimate(flops=1, bytes_accessed=1, transcendentals=0),
-    )
     grad_modulation = jnp.concatenate([grad_mod_one, grad_mod_two], axis=1).reshape(
         latents, 6 * width
     )
@@ -735,21 +775,27 @@
         sums = (sums.astype(F32) + came[:end].astype(F32)).astype(BF16)
         qkv_total, late_sum = sums[:tail_rows], sums[tail_rows:]
         columns = hops.both(columns, came[end:], "rep", bit, 0).reshape(-1, width)
-    came = hops.swap(jnp.concatenate([qkv_total, late_sum, columns]), "rep", 1)
-    qkv_total = hops.both(qkv_total, came[:tail_rows], "rep", 1, 0).astype(F32)
-    late_sum = late_sum.astype(F32) + came[tail_rows:end].astype(F32)
-    columns = hops.both(columns, came[end:], "rep", 1, 0)
-    columns = columns.reshape(2, n_rep // 2, n_dp * latents, width)[..., :own]
-    columns = columns.transpose(1, 0, 2, 3).reshape(-1, own)
-    qkv_owned = qkv_total[:, :half_rows].reshape(qkv_rows, width)
-    bias_owned = qkv_total[:, half_rows, :bias_part].reshape(-1)
-    up_owned = late_sum[:up_rows]
-    down_owned = late_sum[up_rows : up_rows + folds * out_rows]
-    down_owned = down_owned.reshape(folds, out_rows, width).transpose(1, 0, 2)
-    down_owned = down_owned.reshape(out_rows, hidden_width)
-    out_owned = late_sum[up_rows + folds * out_rows :]
-    ada_grad = dot_tn(columns, silu_all)
-    ada_bias_grad = jnp.sum(columns.astype(F32), axis=0)
+    mine = jnp.concatenate([qkv_total, late_sum, columns])
+    came = hops.swap(mine, "rep", 1)
+    smem = pl.BlockSpec(memory_space=pltpu.SMEM)
+    vmem = pl.BlockSpec(memory_space=pltpu.VMEM)
+    ada_grad, ada_bias_grad, qkv_owned, up_owned, down_owned, out_owned, bias_owned = pl.pallas_call(
+        functools.partial(finish_kernel, tail_rows=tail_rows),
+        in_specs=[smem, vmem, vmem, vmem],
+        out_specs=[vmem] * 7,
+        out_shape=[
+            shape_of((own, width), F32),
+            shape_of((1, width), F32),
+            shape_of((qkv_rows, width), F32),
+            shape_of((up_rows, width), F32),
+            shape_of((out_rows, hidden_width), F32),
+            shape_of((out_rows, width), F32),
+            shape_of((2, width), F32),
+        ],
+        compiler_params=pltpu.CompilerParams(vmem_limit_bytes=VMEM_LIMIT),
+    )(core.astype(jnp.int32).reshape(1), mine, came, silu_all)
+    ada_bias_grad = ada_bias_grad[0, :own]
+    bias_owned = bias_owned[:, :bias_part].reshape(-1)
 
     grad_silu = lax.dot_general(
         grad_modulation,
@@ -761,7 +807,7 @@
     condition_grad = silu_pull(grad_silu)[0]
 
     qv_sum, out_bias_sum, up_bias_sum, down_bias_sum = (
-        bias_owned[low:high] for low, high in zip(cuts[:-1], cuts[1:])
+        bias_owned[low:high] for low, high in zip(cuts[:-2], cuts[1:-1])
     )
     return (
         output,

time: 263 us -> 243 us (0.924)
  local copies, waits for them, and re-layouts: 24.7 us -> 16.2 us
  Pallas kernels: 123 us -> 118 us
  waiting for transfers between devices: 71.2 us -> 66.2 us
  other arithmetic: 13.1 us -> 9.04 us
  starting transfers between devices: 13.5 us -> 17.4 us
    ppermute x14, waiting for transfers between devices: 71.2 us -> 56.8 us  [swap(): return lax.ppermute(value, AXES, pairs)]
    reduce_scatter x1, waiting for transfers between devices: 0.02 us -> 7.83 us  [body(): lax.psum_scatter(late_grad, 'dp', scatter_dimension=0, tiled=True)]
    pallas_call x4 -> x3, Pallas kernels: 123 us -> 115 us  [run_kernel(): pl.pallas_call(kernel, grid=(streamed[0].shape[0] // count,), in_specs=[e...]
    slice x5 -> x2, local copies, waits for them, and re-layouts: 6.12 us -> 1.93 us  [the longest x1 1.26 us: body(): ada_bias_grad = ada_bias_grad[0, :own]]
    reshape x5 -> x2, local copies, waits for them, and re-layouts: 4.34 us -> 0.25 us  [the longest x1 0.16 us: body(): mod.reshape(n_dp // 2, latents, -1).transpose(1, 0, 2).reshape(latents, -1)]
    ppermute x14, starting transfers between devices: 13.4 us -> 17.3 us  [swap(): return lax.ppermute(value, AXES, pairs)]
    concatenate x0 -> x1, local copies, waits for them, and re-layouts: none -> 3.43 us  [body(): jnp.concatenate([qv_bias, out_bias, up_bias, down_bias, ada_bias])]
    pallas_call x0 -> x1, Pallas kernels: none -> 2.78 us  [body(): pl.pallas_call(functools.partial(finish_kernel, tail_rows=tail_rows), in_...]
  transfers between devices with their start and end apart: 17 -> 17, of which waited for: 11 -> 13; matrix products, arithmetic and copies ran while one was open for 8% -> 8% of each run, Pallas kernels for 47% -> 47%
where the time goes in v5:
time: 243 us
  Pallas kernels  118 us (49%)
  waiting for transfers between devices  66.2 us (27%)
  starting transfers between devices  17.4 us (7%)
  local copies, waits for them, and re-layouts  16.2 us (7%)
  between operations  14.5 us (6%)
  other arithmetic  9.04 us (4%)
    pallas_call x3, Pallas kernels, run_kernel(): pl.pallas_call(kernel, grid=(streamed[0].shape[0] // count,), in_specs=[e...  115 us
    ppermute x14, waiting for transfers between devices, swap(): return lax.ppermute(value, AXES, pairs)  56.8 us
    ppermute x14, starting transfers between devices, swap(): return lax.ppermute(value, AXES, pairs)  17.3 us
    reduce_scatter x1, waiting for transfers between devices, body(): lax.psum_scatter(late_grad, 'dp', scatter_dimension=0, tiled=True)  7.83 us
  transfers between devices with their start and end apart: 17, of which 13 were waited for; matrix products, arithmetic and copies ran while one was open for 8% of the time, Pallas kernels for 47%

profile of v5, /device:TPU:0, one launch (start us, length us, event | category | flops | bytes accessed | tf_op | source)
XLA Modules:
  0.0 243.0 jit_solution(2298988947168939340)
XLA Ops:
  7.3 3.0 %collective-permute-start.2 = (bf16[288,384]{1,0:T(8,128)(2,1)}, bf16[288,384]{1,0:T(8,128)(2,1)S(1)}, u32[]{:S(2)}, u32[]{:S(2)}) collective-permute-start(bf16[288,384]{1,0:T(8,128)(2,1)} %bitcast.157), channel_id=1, source_target_pairs={{0,4},{1,5},{2,6},{3,7},{4,0},{5,1},{6,2},{7,3},{8,12},{9,13},{10,... | collective-permute-start | bytes 663560 | tf_op jit(solution)/shard_map/ppermute | solution.py:516
  10.3 3.4 %concatenate.51 = bf16[672]{0:T(1024)(128)(2,1)S(1)} concatenate(bf16[96]{0:T(256)(128)(2,1)} %param.18, bf16[48]{0:T(256)(128)(2,1)} %param.20, bf16[192]{0:T(256)(128)(2,1)} %param.22, bf16[48]{0:T(256)(128)(2,1)} %param.24, bf16[288]{0:T(512)(128)(2,1)} %param.16), dimensions={0} | concatenate | bytes 2688 | tf_op jit(solution)/shard_map/concatenate | solution.py:578
  14.5 2.7 %collective-permute-start = (bf16[96,384]{1,0:T(8,128)(2,1)S(1)}, bf16[96,384]{1,0:T(8,128)(2,1)S(1)}, u32[]{:S(2)}, u32[]{:S(2)}) collective-permute-start(bf16[96,384]{1,0:T(8,128)(2,1)S(1)} %fusion.18), channel_id=1, source_target_pairs={{0,16},{1,17},{2,18},{3,19},{4,20},{5,21},{6,22},{7,23},{8,24},{9,... | collective-permute-start | bytes 221192 | tf_op jit(solution)/shard_map/ppermute | solution.py:516
  18.2 1.7 pad_maximum_fusion.6
  21.9 4.5 %collective-permute-done.1 = bf16[2,96,384]{2,1,0:T(8,128)(2,1)S(1)} collective-permute-done((bf16[2,96,384]{2,1,0:T(8,128)(2,1)S(1)}, bf16[2,96,384]{2,1,0:T(8,128)(2,1)S(1)}, u32[]{:S(2)}, u32[]{:S(2)}) %collective-permute-start.1) | collective-permute-done | bytes 147488 | tf_op jit(solution)/shard_map/ppermute | solution.py:516
  26.7 2.1 collective-permute-start.3
  28.8 8.3 %collective-permute-done.3 = f32[2,16,576]{2,1,0:T(8,128)S(1)} collective-permute-done((f32[2,16,576]{2,1,0:T(8,128)S(1)}, f32[2,16,576]{2,1,0:T(8,128)S(1)}, u32[]{:S(2)}, u32[]{:S(2)}) %collective-permute-start.3) | collective-permute-done | bytes 73760 | tf_op jit(solution)/shard_map/ppermute | solution.py:516
  38.1 5.5 %collective-permute-done.4 = f32[2,16,576]{2,1,0:T(8,128)S(1)} collective-permute-done((f32[2,16,576]{2,1,0:T(8,128)S(1)}, f32[2,16,576]{2,1,0:T(8,128)S(1)}, u32[]{:S(2)}, u32[]{:S(2)}) %collective-permute-start.4) | collective-permute-done | bytes 73760 | tf_op jit(solution)/shard_map/ppermute | solution.py:516
  49.6 1.5 collective-permute-start.7
  52.1 23.1 %shard_map.228 = (bf16[16,256,384]{2,1,0:T(8,128)(2,1)}, bf16[16,1152,256]{2,1,0:T(8,128)(2,1)}, f32[16,8,256]{2,1,0:T(8,128)}, bf16[16,384,256]{2,1,0:T(8,128)(2,1)}) custom-call(bf16[16,256,384]{2,1,0:T(8,128)(2,1)} %tokens_ref.5, f32[16,6,384]{2,1,0:T(8,128)} %broadcast_add_fusion.mod_ref, bf16[1152,384]{1,0:T(8,128)(2,1)} %bitcast.148, ...), custom_call_target="tpu_custom_call" | custom-call | flops 5234491392 | bytes 18874368 | tf_op jit(solution)/shard_map/pallas_call | solution.py:474
  75.3 1.5 all-gather.6.cloned.1.call-done
  77.7 59.2 %shard_map.229 = (bf16[16,256,384]{2,1,0:T(8,128)(2,1)}, f32[16,256,384]{2,1,0:T(8,128)}, bf16[16,384,256]{2,1,0:T(8,128)(2,1)}, f32[16,4,384]{2,1,0:T(4,128)}, ...) custom-call(bf16[16,256,384]{2,1,0:T(8,128)(2,1)} %tokens_ref.5, ...), custom_call_target="tpu_custom_call" | custom-call | flops 32614907904 | bytes 22020096 | tf_op jit(solution)/shard_map/pallas_call | solution.py:474
  138.6 32.8 %shard_map.230 = (bf16[16,256,384]{2,1,0:T(8,128)(2,1)}, f32[16,2,384]{2,1,0:T(2,128)}, bf16[1152,384]{1,0:T(8,128)(2,1)}, f32[1152,128]{1,0:T(8,128)}) custom-call(bf16[16,1152,256]{2,1,0:T(8,128)(2,1)} %get-tuple-element.44.qkv_ref, f32[16,8,256]{2,1,0:T(8,128)} %get-tuple-element.45.lse_ref, bf16[16,384,256]{2,1,0:T(8,128)(2,1)} %get-tuple-element.46.grad_attended_ref, ...), custom_call_target="tpu_custom_call" | custom-call | flops 1 | bytes 1 | tf_op jit(solution)/shard_map/pallas_call | solution.py:474
  174.9 1.5 collective-permute-done.8
  177.2 10.3 %collective-permute-done.9 = bf16[2,2,96,384]{3,2,0,1:T(8,128)(2,1)S(1)} collective-permute-done((bf16[2,2,96,384]{3,2,0,1:T(8,128)(2,1)S(1)}, bf16[2,2,96,384]{3,2,0,1:T(8,128)(2,1)S(1)}, u32[]{:S(2)}, u32[]{:S(2)}) %collective-permute-start.9) | collective-permute-done | bytes 294944 | tf_op jit(solution)/shard_map/ppermute | solution.py:516
  187.6 1.6 collective-permute-start.10
  189.2 4.5 %collective-permute-done.10 = bf16[2,112,384]{2,1,0:T(8,128)(2,1)S(1)} collective-permute-done((bf16[2,112,384]{2,1,0:T(8,128)(2,1)S(1)}, bf16[2,112,384]{2,1,0:T(8,128)(2,1)S(1)}, u32[]{:S(2)}, u32[]{:S(2)}) %collective-permute-start.10) | collective-permute-done | bytes 172064 | tf_op jit(solution)/shard_map/ppermute | solution.py:516
  193.9 2.6 %collective-permute-start.11 = (bf16[144,384]{1,0:T(8,128)(2,1)S(1)}, bf16[144,384]{1,0:T(8,128)(2,1)S(1)}, u32[]{:S(2)}, u32[]{:S(2)}) collective-permute-start(bf16[144,384]{1,0:T(8,128)(2,1)S(1)} %pad_maximum_fusion.14), channel_id=1, source_target_pairs={{0,16},{1,17},{2,18},{3,19},{4,20},{5,21},{6,22},{7,23},{8,24},{9,... | collective-permute-start | bytes 331784 | tf_op jit(solution)/shard_map/ppermute | solution.py:516
  196.5 9.3 %collective-permute-done.11 = bf16[144,384]{1,0:T(8,128)(2,1)S(1)} collective-permute-done((bf16[144,384]{1,0:T(8,128)(2,1)S(1)}, bf16[144,384]{1,0:T(8,128)(2,1)S(1)}, u32[]{:S(2)}, u32[]{:S(2)}) %collective-permute-start.11) | collective-permute-done | bytes 110624 | tf_op jit(solution)/shard_map/ppermute | solution.py:516
  205.9 7.8 %reduce-scatter.2.cloned.1.call-done = bf16[1,432,384]{2,1,0:T(8,128)(2,1)} async-done(((bf16[8,432,384]{2,1,0:T(8,128)(2,1)}), bf16[1,432,384]{2,1,0:T(8,128)(2,1)}) %reduce-scatter.2.cloned.1.call-update) | async-done | bytes 331792 | tf_op jit(solution)/shard_map/reduce_scatter | solution.py:702
  214.9 1.3 collective-permute-start.12
  216.2 10.5 %collective-permute-done.12 = bf16[640,384]{1,0:T(8,128)(2,1)S(1)} collective-permute-done((bf16[640,384]{1,0:T(8,128)(2,1)S(1)}, bf16[640,384]{1,0:T(8,128)(2,1)S(1)}, u32[]{:S(2)}, u32[]{:S(2)}) %collective-permute-start.12) | collective-permute-done | bytes 491552 | tf_op jit(solution)/shard_map/ppermute | solution.py:516
  227.2 1.4 fusion.30
  229.9 2.8 %shard_map.231 = (f32[288,384]{1,0:T(8,128)}, f32[1,384]{1,0:T(1,128)}, f32[144,384]{1,0:T(8,128)}, f32[192,384]{1,0:T(8,128)}, f32[48,1536]{1,0:T(8,128)}, /*index=5*/f32[48,384]{1,0:T(8,128)}, f32[2,384]{1,0:T(2,128)}) custom-call(s32[1]{0:T(128)} %bitcast.42.core_ref, bf16[768,384]{1,0:T(8,128)(2,1)} %copy-done.2, bf16[768,384]{1,0:T(8,128)(2,1)} %copy-done.6, ...), custom_call_target="tpu_custom_call" | custom-call | tf_op jit(solution)/shard_map/pallas_call | solution.py:782
  (149 shorter events, 25.5 us)
Async XLA Ops:
  7.2 7.3 %copy-start = (bf16[384,144]{0,1:T(8,128)(2,1)S(1)}, bf16[384,144]{0,1:T(8,128)(2,1)}, u32[]{:S(2)}) copy-start(bf16[384,144]{0,1:T(8,128)(2,1)} %param.17) | copy-start | bytes 331780
  7.2 14.6 %copy-start.5 = (bf16[384,288]{0,1:T(8,128)(2,1)S(1)}, bf16[384,288]{0,1:T(8,128)(2,1)}, u32[]{:S(2)}) copy-start(bf16[384,288]{0,1:T(8,128)(2,1)} %param.15) | copy-start | bytes 663556
  7.2 69.6 %all-gather.6.cloned.1.call-start = ((), (), s32[]{:S(2)}) async-start(), calls=%async_computation.3 | async-start | bytes 2985984 | tf_op jit(solution)/shard_map/all_gather | solution.py:570
  7.3 14.5 %collective-permute-start.2 = (bf16[288,384]{1,0:T(8,128)(2,1)}, bf16[288,384]{1,0:T(8,128)(2,1)S(1)}, u32[]{:S(2)}, u32[]{:S(2)}) collective-permute-start(bf16[288,384]{1,0:T(8,128)(2,1)} %bitcast.157), channel_id=1, source_target_pairs={{0,4},{1,5},{2,6},{3,7},{4,0},{5,1},{6,2},{7,3},{8,12},{9,13},{10,... | collective-permute-start | bytes 663560 | tf_op jit(solution)/shard_map/ppermute | solution.py:516
  14.5 6.5 %collective-permute-start = (bf16[96,384]{1,0:T(8,128)(2,1)S(1)}, bf16[96,384]{1,0:T(8,128)(2,1)S(1)}, u32[]{:S(2)}, u32[]{:S(2)}) collective-permute-start(bf16[96,384]{1,0:T(8,128)(2,1)S(1)} %fusion.18), channel_id=1, source_target_pairs={{0,16},{1,17},{2,18},{3,19},{4,20},{5,21},{6,22},{7,23},{8,24},{9,... | collective-permute-start | bytes 221192 | tf_op jit(solution)/shard_map/ppermute | solution.py:516
  19.9 118.7 %all-gather.4.cloned.1.call-start = ((), (), s32[]{:S(2)}) async-start(), calls=%async_computation.1 | async-start | bytes 1990656 | tf_op jit(solution)/shard_map/all_gather | solution.py:573
  21.1 5.2 %collective-permute-start.1 = (bf16[2,96,384]{2,1,0:T(8,128)(2,1)S(1)}, bf16[2,96,384]{2,1,0:T(8,128)(2,1)S(1)}, u32[]{:S(2)}, u32[]{:S(2)}) collective-permute-start(bf16[2,96,384]{2,1,0:T(8,128)(2,1)S(1)} %pad_maximum_fusion.13), channel_id=1, source_target_pairs={{0,8},{1,9},{2,10},{3,11},{4,12},{5,13},{6,14},{7,15},{8,0},{9,1},... | collective-permute-start | bytes 442376 | tf_op jit(solution)/shard_map/ppermute | solution.py:516
  26.7 10.4 %collective-permute-start.3 = (f32[2,16,576]{2,1,0:T(8,128)S(1)}, f32[2,16,576]{2,1,0:T(8,128)S(1)}, u32[]{:S(2)}, u32[]{:S(2)}) collective-permute-start(f32[2,16,576]{2,1,0:T(8,128)S(1)} %dynamic-slice_bitcast_fusion.1), channel_id=1, source_target_pairs={{0,16},{1,17},{2,18},{3,19},{4,20},{5,21},{6,22},{7,23},{8,24},{9,... | collective-permute-start | bytes 221192 | tf_op jit(solution)/shard_map/ppermute | solution.py:516
  37.1 6.6 %collective-permute-start.4 = (f32[2,16,576]{2,1,0:T(8,128)S(1)}, f32[2,16,576]{2,1,0:T(8,128)S(1)}, u32[]{:S(2)}, u32[]{:S(2)}) collective-permute-start(f32[2,16,576]{2,1,0:T(8,128)S(1)} %fusion.14), channel_id=1, source_target_pairs={{0,8},{1,9},{2,10},{3,11},{4,12},{5,13},{6,14},{7,15},{8,0},{9,1},... | collective-permute-start | bytes 221192 | tf_op jit(solution)/shard_map/ppermute | solution.py:516
  37.5 7.4 %collective-permute-start.5 = (bf16[2,2,96,384]{3,2,1,0:T(8,128)(2,1)S(1)}, bf16[2,2,96,384]{3,2,1,0:T(8,128)(2,1)S(1)}, u32[]{:S(2)}, u32[]{:S(2)}) collective-permute-start(bf16[2,2,96,384]{3,2,1,0:T(8,128)(2,1)S(1)} %pad_maximum_fusion.5), channel_id=1, source_target_pairs={{0,4},{1,5},{2,6},{3,7},{4,0},{5,1},{6,2},{7,3},{8,12},{9,13},{10,... | collective-permute-start | bytes 884744 | tf_op jit(solution)/shard_map/ppermute | solution.py:516
  45.2 3.1 %collective-permute-start.6 = (bf16[8,88,384]{2,1,0:T(8,128)(2,1)S(1)}, bf16[8,88,384]{2,1,0:T(8,128)(2,1)S(1)}, u32[]{:S(2)}, u32[]{:S(2)}) collective-permute-start(bf16[8,88,384]{2,1,0:T(8,128)(2,1)S(1)} %slice.134), channel_id=1, source_target_pairs={{0,1},{1,0},{2,3},{3,2},{4,5},{5,4},{6,7},{7,6},{8,9},{9,8},{10,11... | collective-permute-start | bytes 1622024 | tf_op jit(solution)/shard_map/ppermute | solution.py:516
  49.6 25.6 %collective-permute-start.7 = (bf16[2,8,16,384]{3,2,1,0:T(8,128)(2,1)S(1)}, bf16[2,8,16,384]{3,2,1,0:T(8,128)(2,1)S(1)}, u32[]{:S(2)}, u32[]{:S(2)}) collective-permute-start(bf16[2,8,16,384]{3,2,1,0:T(8,128)(2,1)S(1)} %pad_maximum_fusion.8), channel_id=1, source_target_pairs={{0,2},{1,3},{2,0},{3,1},{4,6},{5,7},{6,4},{7,5},{8,10},{9,11},{10,... | collective-permute-start | bytes 589832 | tf_op jit(solution)/shard_map/ppermute | solution.py:516
  76.9 136.9 %reduce-scatter.2.cloned.1.call-start = ((), (), s32[]{:S(2)}) async-start(), calls=%async_computation.2 | async-start | bytes 2985984 | tf_op jit(solution)/shard_map/reduce_scatter | solution.py:702
  171.4 3.2 %copy-start.7 = (f32[16,4,384]{2,1,0:T(4,128)S(1)}, f32[16,4,384]{2,1,0:T(4,128)}, u32[]{:S(2)}) copy-start(f32[16,4,384]{2,1,0:T(4,128)} %get-tuple-element.53) | copy-start | bytes 294916
  174.4 1.9 collective-permute-start.8
  176.6 10.9 %collective-permute-start.9 = (bf16[2,2,96,384]{3,2,0,1:T(8,128)(2,1)S(1)}, bf16[2,2,96,384]{3,2,0,1:T(8,128)(2,1)S(1)}, u32[]{:S(2)}, u32[]{:S(2)}) collective-permute-start(bf16[2,2,96,384]{3,2,0,1:T(8,128)(2,1)S(1)} %pad_maximum_fusion.7), channel_id=1, source_target_pairs={{0,4},{1,5},{2,6},{3,7},{4,0},{5,1},{6,2},{7,3},{8,12},{9,13},{10,... | collective-permute-start | bytes 884744 | tf_op jit(solution)/shard_map/ppermute | solution.py:516
  187.6 6.1 %collective-permute-start.10 = (bf16[2,112,384]{2,1,0:T(8,128)(2,1)S(1)}, bf16[2,112,384]{2,1,0:T(8,128)(2,1)S(1)}, u32[]{:S(2)}, u32[]{:S(2)}) collective-permute-start(bf16[2,112,384]{2,1,0:T(8,128)(2,1)S(1)} %pad_maximum_fusion.11), channel_id=1, source_target_pairs={{0,8},{1,9},{2,10},{3,11},{4,12},{5,13},{6,14},{7,15},{8,0},{9,1},... | collective-permute-start | bytes 516104 | tf_op jit(solution)/shard_map/ppermute | solution.py:516
  193.9 11.9 %collective-permute-start.11 = (bf16[144,384]{1,0:T(8,128)(2,1)S(1)}, bf16[144,384]{1,0:T(8,128)(2,1)S(1)}, u32[]{:S(2)}, u32[]{:S(2)}) collective-permute-start(bf16[144,384]{1,0:T(8,128)(2,1)S(1)} %pad_maximum_fusion.14), channel_id=1, source_target_pairs={{0,16},{1,17},{2,18},{3,19},{4,20},{5,21},{6,22},{7,23},{8,24},{9,... | collective-permute-start | bytes 331784 | tf_op jit(solution)/shard_map/ppermute | solution.py:516
  213.7 13.0 %copy-start.4 = (bf16[1,432,384]{2,1,0:T(8,128)(2,1)S(1)}, bf16[1,432,384]{2,1,0:T(8,128)(2,1)}, u32[]{:S(2)}) copy-start(bf16[1,432,384]{2,1,0:T(8,128)(2,1)} %reduce-scatter.2.cloned.1.call-done) | copy-start | bytes 995332
  214.8 12.3 %copy-start.3 = (bf16[2304,384]{1,0:T(8,128)(2,1)S(1)}, bf16[2304,384]{1,0:T(8,128)(2,1)}, u32[]{:S(2)}) copy-start(bf16[2304,384]{1,0:T(8,128)(2,1)} %all-gather.4.cloned.1.call-done) | copy-start | bytes 5308420
  214.8 12.3 %copy-start.10 = (f32[16,384]{1,0:T(8,128)S(1)}, f32[16,384]{1,0:T(8,128)}, u32[]{:S(2)}) copy-start(f32[16,384]{1,0:T(8,128)} %param.14) | copy-start | bytes 73732
  214.9 11.8 %collective-permute-start.12 = (bf16[640,384]{1,0:T(8,128)(2,1)S(1)}, bf16[640,384]{1,0:T(8,128)(2,1)S(1)}, u32[]{:S(2)}, u32[]{:S(2)}) collective-permute-start(bf16[640,384]{1,0:T(8,128)(2,1)S(1)} %pad_maximum_fusion.2), channel_id=1, source_target_pairs={{0,2},{1,3},{2,0},{3,1},{4,6},{5,7},{6,4},{7,5},{8,10},{9,11},{10,... | collective-permute-start | bytes 1474568 | tf_op jit(solution)/shard_map/ppermute | solution.py:516
  227.0 2.1 collective-permute-start.13
  227.1 9.3 %copy-start.1 = (bf16[384,144]{0,1:T(8,128)(2,1)S(1)}, bf16[384,144]{0,1:T(8,128)(2,1)}, u32[]{:S(2)}) copy-start(bf16[384,144]{0,1:T(8,128)(2,1)} %param.17) | copy-start | bytes 331780
  (6 other events, 8.6 us)
Sparse Core Ops, SparseCore 0:
  20.0 56.7 all-gather.5
  79.0 44.5 all-gather.3
  137.1 76.5 reduce-scatter.1

commit v6 on v5

--- a/solution.py
+++ b/solution.py
@@ -42,7 +42,7 @@
 
 
 STRIP = 64
-GROUP = 3
+GROUP = 6
 
 
 def beside(*parts):
@@ -68,10 +68,35 @@
 
 
 def attention_forward_kernel(
-    tokens_ref, mod_ref, weight_ref, bias_ref, normed_ref, qkv_ref, lse_ref, attended_ref
+    core_ref,
+    tokens_ref,
+    mod_ref,
+    mine_ref,
+    came_ref,
+    bias_row_ref,
+    normed_ref,
+    qkv_ref,
+    lse_ref,
+    attended_ref,
+    weight_ref,
+    bias_ref,
 ):
     latents, length, width = tokens_ref.shape
     blank = jnp.zeros((HEAD_DIM, length), BF16)
+
+    @pl.when(pl.program_id(0) == 0)
+    def _():
+        first = core_ref[0] == 0
+        n_dp = mine_ref.shape[0]
+        half_rows = weight_ref.shape[0] // (2 * n_dp)
+        for owner in range(n_dp):
+            mine = mine_ref[owner, :half_rows, :]
+            came = came_ref[owner, :half_rows, :]
+            low = 2 * owner * half_rows
+            weight_ref[low : low + half_rows, :] = jnp.where(first, mine, came)
+            weight_ref[low + half_rows : low + 2 * half_rows, :] = jnp.where(first, came, mine)
+        bias_ref[...] = jnp.broadcast_to(bias_row_ref[...], (128, 3 * width)).T
+
     for latent in range(latents):
         for rows in strips(length, STRIP):
             normal, _ = normalise(tokens_ref[latent, rows, :].astype(F32))
@@ -292,18 +317,26 @@
 
     @pl.when(step == pl.num_programs(0) - 1)
     def _():
-        out_back[...] = out_acc[...].T.astype(BF16)
+        out_tall = out_acc[...].T
         up_back[...] = down_acc[...].T.astype(BF16)
-        for owner in range(n_dp):
-            ups = slice(owner * up_rows, (owner + 1) * up_rows)
-            late_grad_ref[owner, :up_rows, :] = up_acc[ups, :width].astype(BF16)
-            outs = slice(owner * out_rows, (owner + 1) * out_rows)
-            for fold in range(hidden_width // width):
-                low = up_rows + fold * out_rows
-                late_grad_ref[owner, low : low + out_rows, :] = up_back[
-                    outs, fold * width : (fold + 1) * width
-                ]
-            late_grad_ref[owner, out_low:, :] = out_back[outs, :]
+        folds = hidden_width // width // 2
+        for side in range(2):
+            for owner in range(n_dp):
+                ups = owner * up_rows + side * (up_rows // 2)
+                late_grad_ref[side, owner, : up_rows // 2, :] = up_acc[
+                    ups : ups + up_rows // 2, :width
+                ].astype(BF16)
+                outs = slice(owner * out_rows, (owner + 1) * out_rows)
+                for place in range(folds):
+                    low = up_rows // 2 + place * out_rows
+                    fold = side * folds + place
+                    late_grad_ref[side, owner, low : low + out_rows, :] = up_back[
+                        outs, fold * width : (fold + 1) * width
+                    ]
+                outs = owner * out_rows + side * (out_rows // 2)
+                late_grad_ref[side, owner, out_low // 2 :, :] = out_tall[
+                    outs : outs + out_rows // 2
+                ].astype(BF16)
         up_bias_grad_ref[...] = up_acc[:, width:]
         down_bias_grad_ref[...] = bias_acc[0:1, :]
         out_bias_grad_ref[...] = bias_acc[1:2, :]
@@ -413,7 +446,14 @@
 
     @pl.when(step == pl.num_programs(0) - 1)
     def _():
-        weight_grad_ref[...] = acc[:, :width].astype(BF16)
+        n_dp, _, tail_rows, _ = weight_grad_ref.shape
+        half_rows = 3 * width // (2 * n_dp)
+        for owner in range(n_dp):
+            for side in range(2):
+                low = (2 * owner + side) * half_rows
+                rows = acc[low : low + half_rows, :width]
+                rest = jnp.zeros((tail_rows - half_rows, width), F32)
+                weight_grad_ref[owner, side] = above(rows, rest).astype(BF16)
         bias_grad_ref[...] = acc[:, width:]
 
 
@@ -428,36 +468,42 @@
     up_ref,
     down_ref,
     out_ref,
-    bias_ref,
+    qv_bias_ref,
+    out_bias_ref,
+    up_bias_ref,
+    down_bias_ref,
     *,
     tail_rows,
 ):
     first = core_ref[0] == 0
     own = ada_ref.shape[0]
     half_rows = qkv_ref.shape[0] // 2
-    up_rows, out_rows = up_ref.shape[0], out_ref.shape[0]
+    up_half, out_rows = up_ref.shape[0] // 2, out_ref.shape[0]
     width = out_ref.shape[1]
-    out_low = tail_rows + up_rows + down_ref.shape[1] // width * out_rows
-    end = out_low + out_rows
-    mine = mine_ref[:tail_rows, :].astype(F32)
-    came = came_ref[:tail_rows, :].astype(F32)
-    lower = jnp.where(first, mine, came)
-    upper = jnp.where(first, came, mine)
-    qkv_ref[:half_rows, :] = lower[:half_rows]
-    qkv_ref[half_rows:, :] = upper[:half_rows]
-    bias_ref[0:1, :] = lower[half_rows : half_rows + 1]
-    bias_ref[1:2, :] = upper[half_rows : half_rows + 1]
-    sums = mine_ref[tail_rows:end, :].astype(F32) + came_ref[tail_rows:end, :].astype(F32)
-    up_ref[...] = sums[:up_rows]
-    for fold in range(down_ref.shape[1] // width):
-        low = up_rows + fold * out_rows
-        down_ref[:, fold * width : (fold + 1) * width] = sums[low : low + out_rows]
-    out_ref[...] = sums[out_low - tail_rows :]
+    folds = down_ref.shape[1] // width // 2
+    out_low = tail_rows + up_half + folds * out_rows
+    end = out_low + out_rows // 2
+    mine = mine_ref[:end, :].astype(F32)
+    came = came_ref[:end, :].astype(F32)
+    for side in range(2):
+        part = jnp.where(first, mine, came) if side == 0 else jnp.where(first, came, mine)
+        qkv_ref[side * half_rows : (side + 1) * half_rows, :] = part[:half_rows]
+        up_ref[side * up_half : (side + 1) * up_half, :] = part[tail_rows : tail_rows + up_half]
+        for place in range(folds):
+            low = tail_rows + up_half + place * out_rows
+            columns = (side * folds + place) * width
+            down_ref[:, columns : columns + width] = part[low : low + out_rows]
+        out_ref[side * (out_rows // 2) : (side + 1) * (out_rows // 2), :] = part[out_low:]
+    biases = mine[half_rows : half_rows + 1] + came[half_rows : half_rows + 1]
+    low = 0
+    for ref in (qv_bias_ref, out_bias_ref, up_bias_ref, down_bias_ref):
+        ref[...] = biases[:, low : low + ref.shape[1]]
+        low += ref.shape[1]
     mine = mine_ref[end:, :]
     came = came_ref[end:, :]
     columns = above(jnp.where(first, mine, came), jnp.where(first, came, mine))
     ada_ref[...] = dot_tn(columns, silu_ref[...])[:own]
-    ada_bias_ref[...] = jnp.sum(columns.astype(F32), axis=0, keepdims=True)
+    ada_bias_ref[...] = jnp.sum(columns.astype(F32), axis=0, keepdims=True)[:, :own]
 
 
 def each(shape, count):
@@ -470,11 +516,12 @@
     return pl.BlockSpec(tuple(shape), lambda step: zeros)
 
 
-def run_kernel(kernel, count, streamed_out, fixed_out, scratch, streamed, fixed, cost):
+def run_kernel(kernel, count, streamed_out, fixed_out, scratch, streamed, fixed, cost, scalars=()):
     return pl.pallas_call(
         kernel,
         grid=(streamed[0].shape[0] // count,),
-        in_specs=[each(item.shape, count) for item in streamed]
+        in_specs=[pl.BlockSpec(memory_space=pltpu.SMEM)] * len(scalars)
+        + [each(item.shape, count) for item in streamed]
         + [whole(item.shape) for item in fixed],
         out_specs=[each(item.shape, count) for item in streamed_out]
         + [whole(item.shape) for item in fixed_out],
@@ -484,7 +531,7 @@
             dimension_semantics=("arbitrary",), vmem_limit_bytes=VMEM_LIMIT
         ),
         cost_estimate=cost,
-    )(*streamed, *fixed)
+    )(*scalars, *streamed, *fixed)
 
 
 def shape_of(dims, kind):
@@ -567,25 +614,25 @@
     late_shard = jnp.concatenate(
         [up_weight.T, down_shard.reshape(folds * out_rows, width), out_weight.T]
     )
-    late = lax.all_gather(late_shard, "dp", axis=0)
     silu_low = jax.nn.silu(conditioning).astype(BF16)
-    ada_shard, _ = lax.optimization_barrier((ada_weight.T, late))
-    ada_all = lax.all_gather(ada_shard, "dp", axis=0, tiled=True)
-
     qkv_rows = qkv_weight.shape[1]
     half_rows = qkv_rows // 2
     core = hops.mine("rep", 1)
-    bias_shard = jnp.concatenate([qv_bias, out_bias, up_bias, down_bias, ada_bias])
-    bias_rows = up_to(bias_shard.shape[0], width) // width
-    bias_block = jnp.pad(bias_shard, (0, bias_rows * width - bias_shard.shape[0]))
+    bias_shard = jnp.concatenate([qv_bias, out_bias, up_bias, down_bias])
+    bias_rows = 2
     front = jnp.concatenate(
         [
             lax.dynamic_slice_in_dim(qkv_weight.T, core * half_rows, half_rows, axis=0),
             silu_low,
-            bias_block.reshape(bias_rows, width),
+            jnp.pad(bias_shard, (0, width - bias_shard.shape[0]))[None],
+            jnp.pad(ada_bias, (0, width - ada_bias.shape[0]))[None],
         ]
     )
     front = pad_rows(front, up_to(front.shape[0], 8))
+    front, late_shard = lax.optimization_barrier((front, late_shard))
+    late = lax.all_gather(late_shard, "dp", axis=0)
+    ada_shard, _ = lax.optimization_barrier((ada_weight.T, late))
+    ada_all = lax.all_gather(ada_shard, "dp", axis=0, tiled=True)
     ada_pair = hops.both(ada_weight.T, hops.swap(ada_weight.T, "dp", 1), "dp", 1, 0)
     high_bits = dp_bits[:0:-1]
     for done, bit in enumerate(high_bits):
@@ -601,33 +648,30 @@
 
     front = hops.both(front, hops.swap(front, "dp", 1), "dp", 1, len(high_bits))
     front = front.reshape(n_dp, -1, width)
-    front = front[:, : half_rows + latents + bias_rows]
-    silu_group = front[:, half_rows : half_rows + latents].reshape(n_dp * latents, width)
-    halves = front[:, : half_rows + latents]
-    halves = hops.both(halves, hops.swap(halves, "rep", 1), "rep", 1, 0)
-    qkv_full = halves[:, :, :half_rows].transpose(1, 0, 2, 3).reshape(3 * width, width)
-    silu_all = halves[:, :, half_rows:]
+    mine = front[:, : half_rows + latents]
+    came = hops.swap(mine, "rep", 1)
+    silu_all = hops.both(mine[:, half_rows:], came[:, half_rows:], "rep", 1, 0)
     for bit in hops.bits("rep")[1:]:
         silu_all = hops.both(silu_all, hops.swap(silu_all, "rep", bit), "rep", bit, 0)
     silu_all = silu_all.reshape(n_rep // 2, 2, n_dp * latents, width).transpose(1, 0, 2, 3)
     silu_all = silu_all.reshape(-1, width)
 
-    bias_all = front[:, half_rows + latents : half_rows + latents + bias_rows]
-    bias_all = bias_all.reshape(n_dp, -1).astype(F32)
+    bias_all = front[:, half_rows + latents].astype(F32)
     cuts = [0]
-    for part in (qv_bias, out_bias, up_bias, down_bias, ada_bias):
+    for part in (qv_bias, out_bias, up_bias, down_bias):
         cuts.append(cuts[-1] + part.shape[0])
-    qv_full, out_full, up_full, down_full, ada_full = (
+    qv_full, out_full, up_full, down_full = (
         bias_all[:, low:high].reshape(1, -1) for low, high in zip(cuts[:-1], cuts[1:])
     )
+    ada_full = front[:, half_rows + latents + 1, : ada_bias.shape[0]].astype(F32).reshape(1, -1)
     qkv_bias = jnp.concatenate(
         [qv_full[:, :width], jnp.zeros((1, width), F32), qv_full[:, width:]], axis=1
     )
-    qkv_bias = jnp.broadcast_to(qkv_bias.reshape(-1, 1), (3 * width, 128))
 
     modulation = (mod + ada_full).reshape(latents, 6, width)
 
-    normed, qkv, lse, attended = run_kernel(
+    core_scalar = core.astype(jnp.int32).reshape(1)
+    normed, qkv, lse, attended, qkv_full = run_kernel(
         attention_forward_kernel,
         4,
         [
@@ -636,15 +680,16 @@
             shape_of((latents, 8 * ((heads + 7) // 8), length), F32),
             shape_of((latents, width, length), BF16),
         ],
-        [],
-        [],
+        [shape_of((3 * width, width), BF16)],
+        [pltpu.VMEM((3 * width, 128), F32)],
         [tokens, modulation],
-        [qkv_full, qkv_bias],
+        [mine, came, qkv_bias],
         pl.CostEstimate(
             flops=2 * rows * width * (3 * width + 2 * length),
             bytes_accessed=rows * width * 12,
             transcendentals=rows * heads * length,
         ),
+        [core_scalar],
     )
 
     attended, silu_all = lax.optimization_barrier((attended, silu_all))
@@ -667,7 +712,7 @@
             shape_of((latents, 4, width), F32),
         ],
         [
-            shape_of(late.shape, BF16),
+            shape_of((2, n_dp, late.shape[1] // 2, width), BF16),
             shape_of((1, width), F32),
             shape_of((hidden_width, 128), F32),
             shape_of((1, width), F32),
@@ -699,15 +744,18 @@
         ),
     )
 
-    late_sum = lax.psum_scatter(late_grad, "dp", scatter_dimension=0, tiled=True)
+    kept, sent = hops.cut(late_grad, "rep", 1, 0)
+    late_half = (kept.astype(F32) + hops.swap(sent, "rep", 1).astype(F32)).astype(BF16)
+    late_sum = lax.psum_scatter(late_half, "dp", scatter_dimension=0, tiled=True)
     late_sum = late_sum.reshape(-1, width)
 
-    normed, ada_all = lax.optimization_barrier((normed, ada_all))
+    normed, ada_all, _ = lax.optimization_barrier((normed, ada_all, late_half))
+    tail_rows = up_to(half_rows + 1, 8)
     tokens_grad, grad_mod_one, qkv_grad, qkv_bias_grad = run_kernel(
         attention_backward_kernel,
         2,
         [shape_of((latents, length, width), BF16), shape_of((latents, 2, width), F32)],
-        [shape_of((3 * width, width), BF16), shape_of((3 * width, 128), F32)],
+        [shape_of((n_dp, 2, tail_rows, width), BF16), shape_of((3 * width, 128), F32)],
         [
             pltpu.VMEM((3 * width, width + 128), F32),
             pltpu.VMEM((width, 3 * width), BF16),
@@ -727,17 +775,13 @@
             down_bias_grad.reshape(n_dp, -1),
         ],
         axis=1,
-    ).astype(BF16)
-    bias_part = cuts[-2] // 2
-    bias_blocks = bias_blocks.reshape(n_dp, 2, 1, bias_part)
-    tail_rows = up_to(half_rows + 1, 8)
+    )
     bias_blocks = jnp.pad(
-        bias_blocks,
-        ((0, 0), (0, 0), (0, tail_rows - half_rows - 1), (0, width - bias_part)),
-    )
-    blocks = jnp.concatenate([qkv_grad.reshape(n_dp, 2, half_rows, width), bias_blocks], axis=2)
-    kept, sent = hops.cut(blocks, "rep", 1, 1)
-    total = kept.astype(F32) + hops.swap(sent, "rep", 1).astype(F32)
+        bias_blocks[:, None],
+        ((0, 0), (half_rows, tail_rows - half_rows - 1), (0, width - cuts[-1])),
+    )
+    kept, sent = hops.cut(qkv_grad, "rep", 1, 1)
+    total = kept.astype(F32) + hops.swap(sent, "rep", 1).astype(F32) + bias_blocks
 
     grad_modulation = jnp.concatenate([grad_mod_one, grad_mod_two], axis=1).reshape(
         latents, 6 * width
@@ -779,23 +823,22 @@
     came = hops.swap(mine, "rep", 1)
     smem = pl.BlockSpec(memory_space=pltpu.SMEM)
     vmem = pl.BlockSpec(memory_space=pltpu.VMEM)
-    ada_grad, ada_bias_grad, qkv_owned, up_owned, down_owned, out_owned, bias_owned = pl.pallas_call(
+    ada_grad, ada_bias_grad, qkv_owned, up_owned, down_owned, out_owned, *bias_sums = pl.pallas_call(
         functools.partial(finish_kernel, tail_rows=tail_rows),
         in_specs=[smem, vmem, vmem, vmem],
-        out_specs=[vmem] * 7,
+        out_specs=[vmem] * 10,
         out_shape=[
             shape_of((own, width), F32),
-            shape_of((1, width), F32),
+            shape_of((1, own), F32),
             shape_of((qkv_rows, width), F32),
             shape_of((up_rows, width), F32),
             shape_of((out_rows, hidden_width), F32),
             shape_of((out_rows, width), F32),
-            shape_of((2, width), F32),
-        ],
+        ]
+        + [shape_of((1, part.shape[0]), F32) for part in (qv_bias, out_bias, up_bias, down_bias)],
         compiler_params=pltpu.CompilerParams(vmem_limit_bytes=VMEM_LIMIT),
-    )(core.astype(jnp.int32).reshape(1), mine, came, silu_all)
-    ada_bias_grad = ada_bias_grad[0, :own]
-    bias_owned = bias_owned[:, :bias_part].reshape(-1)
+    )(core_scalar, mine, came, silu_all)
+    ada_bias_grad = ada_bias_grad.reshape(-1)
 
     grad_silu = lax.dot_general(
         grad_modulation,
@@ -806,9 +849,7 @@
     _, silu_pull = jax.vjp(jax.nn.silu, conditioning)
     condition_grad = silu_pull(grad_silu)[0]
 
-    qv_sum, out_bias_sum, up_bias_sum, down_bias_sum = (
-        bias_owned[low:high] for low, high in zip(cuts[:-2], cuts[1:-1])
-    )
+    qv_sum, out_bias_sum, up_bias_sum, down_bias_sum = (part.reshape(-1) for part in bias_sums)
     return (
         output,
         tokens_grad,

time: 243 us -> 273 us (1.12)
  waiting for transfers between devices: 66.2 us -> 88.5 us
  starting transfers between devices: 17.4 us -> 23 us
  local copies, waits for them, and re-layouts: 16.2 us -> 11.3 us
  other arithmetic: 9.04 us -> 13.5 us
    unnamed x3 -> x4, waiting for transfers between devices: 0.05 us -> 36.8 us
    reduce_scatter x1 -> x0, waiting for transfers between devices: 7.83 us -> none  [body(): lax.psum_scatter(late_grad, 'dp', scatter_dimension=0, tiled=True)]
    ppermute x14 -> x15, starting transfers between devices: 17.3 us -> 22.9 us  [swap(): return lax.ppermute(value, AXES, pairs)]
    ppermute x14 -> x15, waiting for transfers between devices: 56.8 us -> 51.8 us  [swap(): return lax.ppermute(value, AXES, pairs)]
    squeeze x2 -> x3, local copies, waits for them, and re-layouts: 0.07 us -> 3.86 us  [cut(): lax.dynamic_index_in_dim(value, 1 - here, axis, keepdims=False)]
    slice x6 -> x1, local copies, waits for them, and re-layouts: 3.72 us -> 0.06 us  [body(): mine = front[:, :half_rows + latents]]
    concatenate x1 -> x0, local copies, waits for them, and re-layouts: 3.43 us -> none  [body(): jnp.concatenate([qv_bias, out_bias, up_bias, down_bias, ada_bias])]
    convert_element_type x0 -> x3, other arithmetic: none -> 2.78 us  [the longest x1 2.73 us: body(): (kept.astype(F32) + hops.swap(sent, 'rep', 1).astype(F32)).astype(BF16)]
  transfers between devices with their start and end apart: 17 -> 18, of which waited for: 13 -> 13; matrix products, arithmetic and copies ran while one was open for 8% -> 6% of each run, Pallas kernels for 47% -> 31%
where the time goes in v6:
time: 273 us; the launch traced here: 272 us
  Pallas kernels  120 us (44%)
  waiting for transfers between devices  88.5 us (32%)
  starting transfers between devices  23 us (8%)
  between operations  14.5 us (5%)
  other arithmetic  13.5 us (5%)
  local copies, waits for them, and re-layouts  11.3 us (4%)
    pallas_call x3, Pallas kernels, run_kernel(): pl.pallas_call(kernel, grid=(streamed[0].shape[0] // count,), in_specs=[p...  117 us
    ppermute x15, waiting for transfers between devices, swap(): return lax.ppermute(value, AXES, pairs)  51.8 us
    unnamed x4, waiting for transfers between devices  36.8 us
    ppermute x15, starting transfers between devices, swap(): return lax.ppermute(value, AXES, pairs)  22.9 us
  transfers between devices with their start and end apart: 18, of which 13 were waited for; matrix products, arithmetic and copies ran while one was open for 6% of the time, Pallas kernels for 31%

profile of v6, /device:TPU:0, one launch (start us, length us, event | category | flops | bytes accessed | tf_op | source)
XLA Modules:
  0.0 272.1 jit_solution(16306009668457486192)
XLA Ops:
  10.6 1.7 pad_maximum_fusion.5
  12.3 4.1 %collective-permute-start = (bf16[96,384]{1,0:T(8,128)(2,1)S(1)}, bf16[96,384]{1,0:T(8,128)(2,1)S(1)}, u32[]{:S(2)}, u32[]{:S(2)}) collective-permute-start(bf16[96,384]{1,0:T(8,128)(2,1)S(1)} %fusion.17), channel_id=1, source_target_pairs={{0,16},{1,17},{2,18},{3,19},{4,20},{5,21},{6,22},{7,23},{8,24},{9,... | collective-permute-start | bytes 221192 | tf_op jit(solution)/shard_map/ppermute | solution.py:563
  18.1 2.3 collective-permute-done
  21.1 2.4 collective-permute-done.2
  23.6 2.0 collective-permute-done.1
  25.9 2.7 %collective-permute-start.3 = (f32[2,16,576]{2,1,0:T(8,128)S(1)}, f32[2,16,576]{2,1,0:T(8,128)S(1)}, u32[]{:S(2)}, u32[]{:S(2)}) collective-permute-start(f32[2,16,576]{2,1,0:T(8,128)S(1)} %dynamic-slice_bitcast_fusion.2), channel_id=1, source_target_pairs={{0,16},{1,17},{2,18},{3,19},{4,20},{5,21},{6,22},{7,23},{8,24},{9,... | collective-permute-start | bytes 221192 | tf_op jit(solution)/shard_map/ppermute | solution.py:563
  28.7 9.5 %collective-permute-done.3 = f32[2,16,576]{2,1,0:T(8,128)S(1)} collective-permute-done((f32[2,16,576]{2,1,0:T(8,128)S(1)}, f32[2,16,576]{2,1,0:T(8,128)S(1)}, u32[]{:S(2)}, u32[]{:S(2)}) %collective-permute-start.3) | collective-permute-done | bytes 73760 | tf_op jit(solution)/shard_map/ppermute | solution.py:563
  38.3 1.8 collective-permute-start.5
  40.2 3.6 %collective-permute-done.4 = f32[2,16,576]{2,1,0:T(8,128)S(1)} collective-permute-done((f32[2,16,576]{2,1,0:T(8,128)S(1)}, f32[2,16,576]{2,1,0:T(8,128)S(1)}, u32[]{:S(2)}, u32[]{:S(2)}) %collective-permute-start.4) | collective-permute-done | bytes 73760 | tf_op jit(solution)/shard_map/ppermute | solution.py:563
  44.1 1.5 collective-permute-done.5
  51.2 24.4 %shard_map.228 = (bf16[16,256,384]{2,1,0:T(8,128)(2,1)}, bf16[16,1152,256]{2,1,0:T(8,128)(2,1)}, f32[16,8,256]{2,1,0:T(8,128)}, bf16[16,384,256]{2,1,0:T(8,128)(2,1)}, bf16[1152,384]{1,0:T(8,128)(2,1)}) custom-call(s32[1]{0:T(128)} %bitcast.core_ref, bf16[16,256,384]{2,1,0:T(8,128)(2,1)} %tokens_ref.5, f32[16,6,384]{2,1,0:T(8,128)} %broadcast_add_fusion.mod_ref, ...), custom_call_target="tpu_custom_call" | custom-call | flops 5234491392 | bytes 18874368 | tf_op jit(solution)/shard_map/pallas_call | solution.py:520
  76.5 59.2 %shard_map.229 = (bf16[16,256,384]{2,1,0:T(8,128)(2,1)}, f32[16,256,384]{2,1,0:T(8,128)}, bf16[16,384,256]{2,1,0:T(8,128)(2,1)}, f32[16,4,384]{2,1,0:T(4,128)}, ...) custom-call(bf16[16,256,384]{2,1,0:T(8,128)(2,1)} %tokens_ref.5, ...), custom_call_target="tpu_custom_call" | custom-call | flops 32614907904 | bytes 22020096 | tf_op jit(solution)/shard_map/pallas_call | solution.py:520
  135.8 2.7 dynamic-slice_bitcast_fusion
  138.7 3.2 %collective-permute-done.8 = bf16[8,216,384]{2,1,0:T(8,128)(2,1)} collective-permute-done((bf16[8,216,384]{2,1,0:T(8,128)(2,1)}, bf16[8,216,384]{2,1,0:T(8,128)(2,1)}, u32[]{:S(2)}, u32[]{:S(2)}) %collective-permute-start.8) | collective-permute-done | bytes 1327136 | tf_op jit(solution)/shard_map/ppermute | solution.py:563
  141.8 2.7 %fusion = bf16[8,216,384]{2,1,0:T(8,128)(2,1)} fusion(bf16[8,216,384]{2,1,0:T(8,128)(2,1)} %collective-permute-done.8, bf16[2,8,216,384]{3,2,1,0:T(8,128)(2,1)S(1)} %copy-done.2, s32[]{:T(128)S(6)} %select_n.317), kind=kLoop, calls=%fused_computation.1 | loop fusion | flops 2654208 | bytes 3981316 | tf_op jit(solution)/shard_map/convert_element_type | solution.py:748
  144.6 33.2 %shard_map.230 = (bf16[16,256,384]{2,1,0:T(8,128)(2,1)}, f32[16,2,384]{2,1,0:T(2,128)}, bf16[8,2,80,384]{3,2,1,0:T(8,128)(2,1)}, f32[1152,128]{1,0:T(8,128)}) custom-call(bf16[16,1152,256]{2,1,0:T(8,128)(2,1)} %get-tuple-element.52.qkv_ref, f32[16,8,256]{2,1,0:T(8,128)} %get-tuple-element.53.lse_ref, ...), custom_call_target="tpu_custom_call" | custom-call | flops 1 | bytes 1 | tf_op jit(solution)/shard_map/pallas_call | solution.py:520
  184.2 7.7 %collective-permute-done.10 = bf16[2,2,96,384]{3,2,0,1:T(8,128)(2,1)S(1)} collective-permute-done((bf16[2,2,96,384]{3,2,0,1:T(8,128)(2,1)S(1)}, bf16[2,2,96,384]{3,2,0,1:T(8,128)(2,1)S(1)}, u32[]{:S(2)}, u32[]{:S(2)}) %collective-permute-start.10) | collective-permute-done | bytes 294944 | tf_op jit(solution)/shard_map/ppermute | solution.py:563
  192.1 1.9 collective-permute-start.11
  194.0 6.5 %collective-permute-done.11 = bf16[2,112,384]{2,1,0:T(8,128)(2,1)S(1)} collective-permute-done((bf16[2,112,384]{2,1,0:T(8,128)(2,1)S(1)}, bf16[2,112,384]{2,1,0:T(8,128)(2,1)S(1)}, u32[]{:S(2)}, u32[]{:S(2)}) %collective-permute-start.11) | collective-permute-done | bytes 172064 | tf_op jit(solution)/shard_map/ppermute | solution.py:563
  200.8 4.9 %collective-permute-start.12 = (bf16[144,384]{1,0:T(8,128)(2,1)S(1)}, bf16[144,384]{1,0:T(8,128)(2,1)S(1)}, u32[]{:S(2)}, u32[]{:S(2)}) collective-permute-start(bf16[144,384]{1,0:T(8,128)(2,1)S(1)} %pad_maximum_fusion.14), channel_id=1, source_target_pairs={{0,16},{1,17},{2,18},{3,19},{4,20},{5,21},{6,22},{7,23},{8,24},{9,... | collective-permute-start | bytes 331784 | tf_op jit(solution)/shard_map/ppermute | solution.py:563
  205.6 6.6 %collective-permute-done.12 = bf16[144,384]{1,0:T(8,128)(2,1)S(1)} collective-permute-done((bf16[144,384]{1,0:T(8,128)(2,1)S(1)}, bf16[144,384]{1,0:T(8,128)(2,1)S(1)}, u32[]{:S(2)}, u32[]{:S(2)}) %collective-permute-start.12) | collective-permute-done | bytes 110624 | tf_op jit(solution)/shard_map/ppermute | solution.py:563
  212.3 36.7 %reduce-scatter.4.cloned.1.call-done = bf16[1,216,384]{2,1,0:T(8,128)(2,1)} async-done(((bf16[8,216,384]{2,1,0:T(8,128)(2,1)}), bf16[1,216,384]{2,1,0:T(8,128)(2,1)}) %reduce-scatter.4.cloned.1.call-update) | async-done | bytes 165904
  251.5 6.3 %collective-permute-done.13 = bf16[424,384]{1,0:T(8,128)(2,1)S(1)} collective-permute-done((bf16[424,384]{1,0:T(8,128)(2,1)S(1)}, bf16[424,384]{1,0:T(8,128)(2,1)S(1)}, u32[]{:S(2)}, u32[]{:S(2)}) %collective-permute-start.13) | collective-permute-done | bytes 325664 | tf_op jit(solution)/shard_map/ppermute | solution.py:563
  261.6 2.7 shard_map.231
  (150 shorter events, 27.1 us)
Async XLA Ops:
  7.2 69.2 %all-gather.6.cloned.1.call-start = ((), (), s32[]{:S(2)}) async-start(), calls=%async_computation.2 | async-start | bytes 2985984 | tf_op jit(solution)/shard_map/all_gather | solution.py:633
  12.3 8.0 %collective-permute-start = (bf16[96,384]{1,0:T(8,128)(2,1)S(1)}, bf16[96,384]{1,0:T(8,128)(2,1)S(1)}, u32[]{:S(2)}, u32[]{:S(2)}) collective-permute-start(bf16[96,384]{1,0:T(8,128)(2,1)S(1)} %fusion.17), channel_id=1, source_target_pairs={{0,16},{1,17},{2,18},{3,19},{4,20},{5,21},{6,22},{7,23},{8,24},{9,... | collective-permute-start | bytes 221192 | tf_op jit(solution)/shard_map/ppermute | solution.py:563
  16.4 7.1 %collective-permute-start.2 = (bf16[288,384]{1,0:T(8,128)(2,1)}, bf16[288,384]{1,0:T(8,128)(2,1)S(1)}, u32[]{:S(2)}, u32[]{:S(2)}) collective-permute-start(bf16[288,384]{1,0:T(8,128)(2,1)} %bitcast.159), channel_id=1, source_target_pairs={{0,4},{1,5},{2,6},{3,7},{4,0},{5,1},{6,2},{7,3},{8,12},{9,13},{10,... | collective-permute-start | bytes 663560 | tf_op jit(solution)/shard_map/ppermute | solution.py:563
  17.9 126.6 %all-gather.4.cloned.1.call-start = ((), (), s32[]{:S(2)}) async-start(), calls=%async_computation.1 | async-start | bytes 1990656 | tf_op jit(solution)/shard_map/all_gather | solution.py:635
  20.4 5.2 %collective-permute-start.1 = (bf16[2,96,384]{2,1,0:T(8,128)(2,1)S(1)}, bf16[2,96,384]{2,1,0:T(8,128)(2,1)S(1)}, u32[]{:S(2)}, u32[]{:S(2)}) collective-permute-start(bf16[2,96,384]{2,1,0:T(8,128)(2,1)S(1)} %pad_maximum_fusion.13), channel_id=1, source_target_pairs={{0,8},{1,9},{2,10},{3,11},{4,12},{5,13},{6,14},{7,15},{8,0},{9,1},... | collective-permute-start | bytes 442376 | tf_op jit(solution)/shard_map/ppermute | solution.py:563
  25.9 12.2 %collective-permute-start.3 = (f32[2,16,576]{2,1,0:T(8,128)S(1)}, f32[2,16,576]{2,1,0:T(8,128)S(1)}, u32[]{:S(2)}, u32[]{:S(2)}) collective-permute-start(f32[2,16,576]{2,1,0:T(8,128)S(1)} %dynamic-slice_bitcast_fusion.2), channel_id=1, source_target_pairs={{0,16},{1,17},{2,18},{3,19},{4,20},{5,21},{6,22},{7,23},{8,24},{9,... | collective-permute-start | bytes 221192 | tf_op jit(solution)/shard_map/ppermute | solution.py:563
  38.2 5.6 %collective-permute-start.4 = (f32[2,16,576]{2,1,0:T(8,128)S(1)}, f32[2,16,576]{2,1,0:T(8,128)S(1)}, u32[]{:S(2)}, u32[]{:S(2)}) collective-permute-start(f32[2,16,576]{2,1,0:T(8,128)S(1)} %fusion.12), channel_id=1, source_target_pairs={{0,8},{1,9},{2,10},{3,11},{4,12},{5,13},{6,14},{7,15},{8,0},{9,1},... | collective-permute-start | bytes 221192 | tf_op jit(solution)/shard_map/ppermute | solution.py:563
  38.3 7.3 %collective-permute-start.5 = (bf16[2,2,96,384]{3,2,1,0:T(8,128)(2,1)S(1)}, bf16[2,2,96,384]{3,2,1,0:T(8,128)(2,1)S(1)}, u32[]{:S(2)}, u32[]{:S(2)}) collective-permute-start(bf16[2,2,96,384]{3,2,1,0:T(8,128)(2,1)S(1)} %pad_maximum_fusion.4), channel_id=1, source_target_pairs={{0,4},{1,5},{2,6},{3,7},{4,0},{5,1},{6,2},{7,3},{8,12},{9,13},{10,... | collective-permute-start | bytes 884744 | tf_op jit(solution)/shard_map/ppermute | solution.py:563
  46.0 3.6 %collective-permute-start.6 = (bf16[8,88,384]{2,1,0:T(8,128)(2,1)S(1)}, bf16[8,88,384]{2,1,0:T(8,128)(2,1)S(1)}, u32[]{:S(2)}, u32[]{:S(2)}) collective-permute-start(bf16[8,88,384]{2,1,0:T(8,128)(2,1)S(1)} %slice.104.mine_ref), channel_id=1, source_target_pairs={{0,1},{1,0},{2,3},{3,2},{4,5},{5,4},{6,7},{7,6},{8,9},{9,8},{10,11... | collective-permute-start | bytes 1622024 | tf_op jit(solution)/shard_map/ppermute | solution.py:563
  49.7 25.9 %collective-permute-start.7 = (bf16[2,8,16,384]{3,2,1,0:T(8,128)(2,1)S(1)}, bf16[2,8,16,384]{3,2,1,0:T(8,128)(2,1)S(1)}, u32[]{:S(2)}, u32[]{:S(2)}) collective-permute-start(bf16[2,8,16,384]{3,2,1,0:T(8,128)(2,1)S(1)} %pad_maximum_fusion.8), channel_id=1, source_target_pairs={{0,2},{1,3},{2,0},{3,1},{4,6},{5,7},{6,4},{7,5},{8,10},{9,11},{10,... | collective-permute-start | bytes 589832 | tf_op jit(solution)/shard_map/ppermute | solution.py:563
  76.5 172.6 %reduce-scatter.4.cloned.1.call-start = ((), (), s32[]{:S(2)}) async-start(), calls=%async_computation.3 | async-start | bytes 1492992
  138.4 3.4 %collective-permute-start.8 = (bf16[8,216,384]{2,1,0:T(8,128)(2,1)}, bf16[8,216,384]{2,1,0:T(8,128)(2,1)}, u32[]{:S(2)}, u32[]{:S(2)}) collective-permute-start(bf16[8,216,384]{2,1,0:T(8,128)(2,1)} %dynamic-slice_bitcast_fusion), channel_id=1, source_target_pairs={{0,1},{1,0},{2,3},{3,2},{4,5},{5,4},{6,7},{7,6},{8,9},{9,8},{10,11... | collective-permute-start | bytes 3981320 | tf_op jit(solution)/shard_map/ppermute | solution.py:563
  144.6 35.0 %copy-start.15 = (f32[1,384]{1,0:T(1,128)S(1)}, f32[1,384]{1,0:T(1,128)}, u32[]{:S(2)}) copy-start(f32[1,384]{1,0:T(1,128)} %get-tuple-element.67) | copy-start | bytes 4612
  144.6 35.1 %copy-start.14 = (f32[1,384]{1,0:T(1,128)S(1)}, f32[1,384]{1,0:T(1,128)}, u32[]{:S(2)}) copy-start(f32[1,384]{1,0:T(1,128)} %get-tuple-element.69) | copy-start | bytes 4612
  144.6 36.7 %copy-start.10 = (f32[16,4,384]{2,1,0:T(4,128)S(1)}, f32[16,4,384]{2,1,0:T(4,128)}, u32[]{:S(2)}) copy-start(f32[16,4,384]{2,1,0:T(4,128)} %get-tuple-element.63) | copy-start | bytes 294916
  179.0 3.4 %collective-permute-start.9 = (bf16[8,80,384]{2,1,0:T(8,128)(2,1)S(1)}, bf16[8,80,384]{2,1,0:T(8,128)(2,1)S(1)}, u32[]{:S(2)}, u32[]{:S(2)}) collective-permute-start(bf16[8,80,384]{2,1,0:T(8,128)(2,1)S(1)} %dynamic-slice_bitcast_fusion.1), channel_id=1, source_target_pairs={{0,1},{1,0},{2,3},{3,2},{4,5},{5,4},{6,7},{7,6},{8,9},{9,8},{10,11... | collective-permute-start | bytes 1474568 | tf_op jit(solution)/shard_map/ppermute | solution.py:563
  182.6 9.3 %collective-permute-start.10 = (bf16[2,2,96,384]{3,2,0,1:T(8,128)(2,1)S(1)}, bf16[2,2,96,384]{3,2,0,1:T(8,128)(2,1)S(1)}, u32[]{:S(2)}, u32[]{:S(2)}) collective-permute-start(bf16[2,2,96,384]{3,2,0,1:T(8,128)(2,1)S(1)} %pad_maximum_fusion.7), channel_id=1, source_target_pairs={{0,4},{1,5},{2,6},{3,7},{4,0},{5,1},{6,2},{7,3},{8,12},{9,13},{10,... | collective-permute-start | bytes 884744 | tf_op jit(solution)/shard_map/ppermute | solution.py:563
  192.1 8.5 %collective-permute-start.11 = (bf16[2,112,384]{2,1,0:T(8,128)(2,1)S(1)}, bf16[2,112,384]{2,1,0:T(8,128)(2,1)S(1)}, u32[]{:S(2)}, u32[]{:S(2)}) collective-permute-start(bf16[2,112,384]{2,1,0:T(8,128)(2,1)S(1)} %pad_maximum_fusion.11), channel_id=1, source_target_pairs={{0,8},{1,9},{2,10},{3,11},{4,12},{5,13},{6,14},{7,15},{8,0},{9,1},... | collective-permute-start | bytes 516104 | tf_op jit(solution)/shard_map/ppermute | solution.py:563
  200.6 58.5 %copy-start.11 = (f32[16,2,384]{2,1,0:T(2,128)S(1)}, f32[16,2,384]{2,1,0:T(2,128)}, u32[]{:S(2)}) copy-start(f32[16,2,384]{2,1,0:T(2,128)} %get-tuple-element.62) | copy-start | bytes 147460
  200.7 58.5 %copy-start.3 = (bf16[2304,384]{1,0:T(8,128)(2,1)S(1)}, bf16[2304,384]{1,0:T(8,128)(2,1)}, u32[]{:S(2)}) copy-start(bf16[2304,384]{1,0:T(8,128)(2,1)} %all-gather.4.cloned.1.call-done) | copy-start | bytes 5308420
  200.7 58.5 %copy-start.12 = (f32[16,384]{1,0:T(8,128)S(1)}, f32[16,384]{1,0:T(8,128)}, u32[]{:S(2)}) copy-start(f32[16,384]{1,0:T(8,128)} %param.14) | copy-start | bytes 73732
  200.8 11.5 %collective-permute-start.12 = (bf16[144,384]{1,0:T(8,128)(2,1)S(1)}, bf16[144,384]{1,0:T(8,128)(2,1)S(1)}, u32[]{:S(2)}, u32[]{:S(2)}) collective-permute-start(bf16[144,384]{1,0:T(8,128)(2,1)S(1)} %pad_maximum_fusion.14), channel_id=1, source_target_pairs={{0,16},{1,17},{2,18},{3,19},{4,20},{5,21},{6,22},{7,23},{8,24},{9,... | collective-permute-start | bytes 331784 | tf_op jit(solution)/shard_map/ppermute | solution.py:563
  250.0 7.8 %collective-permute-start.13 = (bf16[424,384]{1,0:T(8,128)(2,1)S(1)}, bf16[424,384]{1,0:T(8,128)(2,1)S(1)}, u32[]{:S(2)}, u32[]{:S(2)}) collective-permute-start(bf16[424,384]{1,0:T(8,128)(2,1)S(1)} %pad_maximum_fusion.6), channel_id=1, source_target_pairs={{0,2},{1,3},{2,0},{3,1},{4,6},{5,7},{6,4},{7,5},{8,10},{9,11},{10,... | collective-permute-start | bytes 976904 | tf_op jit(solution)/shard_map/ppermute | solution.py:563
  259.0 1.8 collective-permute-start.14
  (10 other events, 82.2 us)
Sparse Core Ops, SparseCore 0:
  18.1 57.6 all-gather.5
  77.9 44.7 all-gather.3
  184.3 64.6 reduce-scatter.3

commit v7 on v6

--- a/solution.py
+++ b/solution.py
@@ -42,7 +42,7 @@
 
 
 STRIP = 64
-GROUP = 6
+GROUP = 3
 
 
 def beside(*parts):
@@ -149,7 +149,18 @@
         attend(*item, value)
 
 
+def by_side(core_ref, side, kept_ref, sent_ref, write):
+    @pl.when(core_ref[0] == side)
+    def _():
+        write(kept_ref)
+
+    @pl.when(core_ref[0] != side)
+    def _():
+        write(sent_ref)
+
+
 def feed_kernel(
+    core_ref,
     tokens_ref,
     cotangent_ref,
     attended_ref,
@@ -162,7 +173,8 @@
     grad_middle_ref,
     grad_attended_ref,
     grad_mod_ref,
-    late_grad_ref,
+    late_kept_ref,
+    late_sent_ref,
     out_bias_grad_ref,
     up_bias_grad_ref,
     down_bias_grad_ref,
@@ -317,32 +329,38 @@
 
     @pl.when(step == pl.num_programs(0) - 1)
     def _():
-        out_tall = out_acc[...].T
+        out_acc[...] = out_acc[...].T
         up_back[...] = down_acc[...].T.astype(BF16)
         folds = hidden_width // width // 2
+        out_back_rows = out_rows // 2
         for side in range(2):
-            for owner in range(n_dp):
-                ups = owner * up_rows + side * (up_rows // 2)
-                late_grad_ref[side, owner, : up_rows // 2, :] = up_acc[
-                    ups : ups + up_rows // 2, :width
-                ].astype(BF16)
-                outs = slice(owner * out_rows, (owner + 1) * out_rows)
-                for place in range(folds):
-                    low = up_rows // 2 + place * out_rows
-                    fold = side * folds + place
-                    late_grad_ref[side, owner, low : low + out_rows, :] = up_back[
-                        outs, fold * width : (fold + 1) * width
-                    ]
-                outs = owner * out_rows + side * (out_rows // 2)
-                late_grad_ref[side, owner, out_low // 2 :, :] = out_tall[
-                    outs : outs + out_rows // 2
-                ].astype(BF16)
+
+            def write(ref, side=side):
+                for owner in range(n_dp):
+                    ups = owner * up_rows + side * (up_rows // 2)
+                    ref[owner, : up_rows // 2, :] = up_acc[
+                        ups : ups + up_rows // 2, :width
+                    ].astype(BF16)
+                    outs = slice(owner * out_rows, (owner + 1) * out_rows)
+                    for place in range(folds):
+                        low = up_rows // 2 + place * out_rows
+                        fold = side * folds + place
+                        ref[owner, low : low + out_rows, :] = up_back[
+                            outs, fold * width : (fold + 1) * width
+                        ]
+                    outs = owner * out_rows + side * out_back_rows
+                    ref[owner, out_low // 2 :, :] = out_acc[
+                        outs : outs + out_back_rows
+                    ].astype(BF16)
+
+            by_side(core_ref, side, late_kept_ref, late_sent_ref, write)
         up_bias_grad_ref[...] = up_acc[:, width:]
         down_bias_grad_ref[...] = bias_acc[0:1, :]
         out_bias_grad_ref[...] = bias_acc[1:2, :]
 
 
 def attention_backward_kernel(
+    core_ref,
     qkv_ref,
     lse_ref,
     grad_attended_ref,
@@ -353,7 +371,8 @@
     weight_ref,
     tokens_grad_ref,
     grad_mod_ref,
-    weight_grad_ref,
+    kept_ref,
+    sent_ref,
     bias_grad_ref,
     acc,
     weight_back,
@@ -446,14 +465,18 @@
 
     @pl.when(step == pl.num_programs(0) - 1)
     def _():
-        n_dp, _, tail_rows, _ = weight_grad_ref.shape
+        n_dp, tail_rows, _ = kept_ref.shape
         half_rows = 3 * width // (2 * n_dp)
-        for owner in range(n_dp):
-            for side in range(2):
-                low = (2 * owner + side) * half_rows
-                rows = acc[low : low + half_rows, :width]
-                rest = jnp.zeros((tail_rows - half_rows, width), F32)
-                weight_grad_ref[owner, side] = above(rows, rest).astype(BF16)
+        for side in range(2):
+
+            def write(ref, side=side):
+                for owner in range(n_dp):
+                    low = (2 * owner + side) * half_rows
+                    rows = acc[low : low + half_rows, :width]
+                    rest = jnp.zeros((tail_rows - half_rows, width), F32)
+                    ref[owner] = above(rows, rest).astype(BF16)
+
+            by_side(core_ref, side, kept_ref, sent_ref, write)
         bias_grad_ref[...] = acc[:, width:]
 
 
@@ -698,7 +721,8 @@
         grad_middle,
         grad_attended,
         grad_mod_two,
-        late_grad,
+        late_kept,
+        late_sent,
         out_bias_grad,
         up_bias_grad,
         down_bias_grad,
@@ -712,7 +736,8 @@
             shape_of((latents, 4, width), F32),
         ],
         [
-            shape_of((2, n_dp, late.shape[1] // 2, width), BF16),
+            shape_of((n_dp, late.shape[1] // 2, width), BF16),
+            shape_of((n_dp, late.shape[1] // 2, width), BF16),
             shape_of((1, width), F32),
             shape_of((hidden_width, 128), F32),
             shape_of((1, width), F32),
@@ -742,20 +767,24 @@
             bytes_accessed=rows * width * 14,
             transcendentals=rows * hidden_width,
         ),
-    )
-
-    kept, sent = hops.cut(late_grad, "rep", 1, 0)
-    late_half = (kept.astype(F32) + hops.swap(sent, "rep", 1).astype(F32)).astype(BF16)
-    late_sum = lax.psum_scatter(late_half, "dp", scatter_dimension=0, tiled=True)
-    late_sum = late_sum.reshape(-1, width)
+        [core_scalar],
+    )
+
+    late_half = late_kept.astype(F32) + hops.swap(late_sent, "rep", 1).astype(F32)
+    late_half = late_half.astype(BF16)
+    late_parts = lax.all_to_all(late_half, "dp", 0, 0, tiled=True)
 
     normed, ada_all, _ = lax.optimization_barrier((normed, ada_all, late_half))
     tail_rows = up_to(half_rows + 1, 8)
-    tokens_grad, grad_mod_one, qkv_grad, qkv_bias_grad = run_kernel(
+    tokens_grad, grad_mod_one, qkv_kept, qkv_sent, qkv_bias_grad = run_kernel(
         attention_backward_kernel,
         2,
         [shape_of((latents, length, width), BF16), shape_of((latents, 2, width), F32)],
-        [shape_of((n_dp, 2, tail_rows, width), BF16), shape_of((3 * width, 128), F32)],
+        [
+            shape_of((n_dp, tail_rows, width), BF16),
+            shape_of((n_dp, tail_rows, width), BF16),
+            shape_of((3 * width, 128), F32),
+        ],
         [
             pltpu.VMEM((3 * width, width + 128), F32),
             pltpu.VMEM((width, 3 * width), BF16),
@@ -764,7 +793,10 @@
         [qkv, lse, grad_attended, normed, tokens, grad_middle, modulation],
         [qkv_full],
         pl.CostEstimate(flops=1, bytes_accessed=1, transcendentals=0),
-    )
+        [core_scalar],
+    )
+    qkv_sent, late_parts = lax.optimization_barrier((qkv_sent, late_parts))
+    late_sum = jnp.sum(late_parts.astype(F32), axis=0).astype(BF16)
 
     qkv_columns = qkv_bias_grad[:, 0]
     bias_blocks = jnp.concatenate(
@@ -780,8 +812,7 @@
         bias_blocks[:, None],
         ((0, 0), (half_rows, tail_rows - half_rows - 1), (0, width - cuts[-1])),
     )
-    kept, sent = hops.cut(qkv_grad, "rep", 1, 1)
-    total = kept.astype(F32) + hops.swap(sent, "rep", 1).astype(F32) + bias_blocks
+    total = qkv_kept.astype(F32) + hops.swap(qkv_sent, "rep", 1).astype(F32) + bias_blocks
 
     grad_modulation = jnp.concatenate([grad_mod_one, grad_mod_two], axis=1).reshape(
         latents, 6 * width

time: 273 us -> 282 us (1.033)
  waiting for transfers between devices: 88.5 us -> 106 us
  local copies, waits for them, and re-layouts: 11.3 us -> 7.43 us
    all_gather x1, waiting for transfers between devices: 0.01 us -> 52.5 us  [body(): ada_all = lax.all_gather(ada_shard, 'dp', axis=0, tiled=True)]
    unnamed x4 -> x2, waiting for transfers between devices: 36.8 us -> 0.03 us
    ppermute x15, starting transfers between devices: 22.9 us -> 14.9 us  [swap(): return lax.ppermute(value, AXES, pairs)]
    all_to_all x0 -> x1, starting transfers between devices: none -> 5.43 us  [body(): late_parts = lax.all_to_all(late_half, 'dp', 0, 0, tiled=True)]
    squeeze x3 -> x1, local copies, waits for them, and re-layouts: 3.86 us -> 0.02 us  [cut(): lax.dynamic_index_in_dim(value, 1 - here, axis, keepdims=False)]
  transfers between devices with their start and end apart: 18 -> 18, of which waited for: 13 -> 13; matrix products, arithmetic and copies ran while one was open for 6% -> 5% of each run, Pallas kernels for 31% -> 20%
where the time goes in v7:
time: 282 us
  Pallas kernels  119 us (42%)
  waiting for transfers between devices  106 us (38%)
  starting transfers between devices  20.4 us (7%)
  between operations  14.8 us (5%)
  other arithmetic  11.8 us (4%)
  local copies, waits for them, and re-layouts  7.43 us (3%)
    pallas_call x3, Pallas kernels, run_kernel(): pl.pallas_call(kernel, grid=(streamed[0].shape[0] // count,), in_specs=[p...  116 us
    ppermute x15, waiting for transfers between devices, swap(): return lax.ppermute(value, AXES, pairs)  53.8 us
    all_gather x1, waiting for transfers between devices, body(): ada_all = lax.all_gather(ada_shard, 'dp', axis=0, tiled=True)  52.5 us
    ppermute x15, starting transfers between devices, swap(): return lax.ppermute(value, AXES, pairs)  14.9 us
  transfers between devices with their start and end apart: 18, of which 13 were waited for; matrix products, arithmetic and copies ran while one was open for 5% of the time, Pallas kernels for 20%

profile of v7, /device:TPU:0, one launch (start us, length us, event | category | flops | bytes accessed | tf_op | source)
XLA Modules:
  0.0 281.5 jit_solution(15188821004101670671)
XLA Ops:
  10.6 1.7 pad_maximum_fusion.5
  12.3 4.1 %collective-permute-start = (bf16[96,384]{1,0:T(8,128)(2,1)S(1)}, bf16[96,384]{1,0:T(8,128)(2,1)S(1)}, u32[]{:S(2)}, u32[]{:S(2)}) collective-permute-start(bf16[96,384]{1,0:T(8,128)(2,1)S(1)} %fusion.15), channel_id=1, source_target_pairs={{0,16},{1,17},{2,18},{3,19},{4,20},{5,21},{6,22},{7,23},{8,24},{9,... | collective-permute-start | bytes 221192 | tf_op jit(solution)/shard_map/ppermute | solution.py:586
  16.4 1.5 collective-permute-start.2
  18.0 2.3 collective-permute-done
  21.1 2.4 collective-permute-done.2
  23.6 2.0 collective-permute-done.1
  25.9 2.7 collective-permute-start.3
  28.7 9.5 %collective-permute-done.3 = f32[2,16,576]{2,1,0:T(8,128)S(1)} collective-permute-done((f32[2,16,576]{2,1,0:T(8,128)S(1)}, f32[2,16,576]{2,1,0:T(8,128)S(1)}, u32[]{:S(2)}, u32[]{:S(2)}) %collective-permute-start.3) | collective-permute-done | bytes 73760 | tf_op jit(solution)/shard_map/ppermute | solution.py:586
  38.3 1.8 collective-permute-start.5
  40.2 3.6 %collective-permute-done.4 = f32[2,16,576]{2,1,0:T(8,128)S(1)} collective-permute-done((f32[2,16,576]{2,1,0:T(8,128)S(1)}, f32[2,16,576]{2,1,0:T(8,128)S(1)}, u32[]{:S(2)}, u32[]{:S(2)}) %collective-permute-start.4) | collective-permute-done | bytes 73760 | tf_op jit(solution)/shard_map/ppermute | solution.py:586
  44.1 1.5 collective-permute-done.5
  49.7 1.5 collective-permute-start.7
  51.2 23.8 %shard_map.228 = (bf16[16,256,384]{2,1,0:T(8,128)(2,1)}, bf16[16,1152,256]{2,1,0:T(8,128)(2,1)}, f32[16,8,256]{2,1,0:T(8,128)}, bf16[16,384,256]{2,1,0:T(8,128)(2,1)}, bf16[1152,384]{1,0:T(8,128)(2,1)}) custom-call(s32[1]{0:T(128)} %bitcast.core_ref, bf16[16,256,384]{2,1,0:T(8,128)(2,1)} %tokens_ref.5, f32[16,6,384]{2,1,0:T(8,128)} %broadcast_add_fusion.mod_ref, ...), custom_call_target="tpu_custom_call" | custom-call | flops 5234491392 | bytes 18874368 | tf_op jit(solution)/shard_map/pallas_call | solution.py:543
  75.8 59.4 %shard_map.229 = (bf16[16,256,384]{2,1,0:T(8,128)(2,1)}, f32[16,256,384]{2,1,0:T(8,128)}, bf16[16,384,256]{2,1,0:T(8,128)(2,1)}, f32[16,4,384]{2,1,0:T(4,128)}, ...) custom-call(s32[1]{0:T(128)} %bitcast.core_ref, ...), custom_call_target="tpu_custom_call" | custom-call | flops 32614907904 | bytes 22020096 | tf_op jit(solution)/shard_map/pallas_call | solution.py:543
  135.6 3.0 %collective-permute-done.8 = bf16[8,216,384]{2,1,0:T(8,128)(2,1)S(1)} collective-permute-done((bf16[8,216,384]{2,1,0:T(8,128)(2,1)}, bf16[8,216,384]{2,1,0:T(8,128)(2,1)S(1)}, u32[]{:S(2)}, u32[]{:S(2)}) %collective-permute-start.8) | collective-permute-done | bytes 1327136 | tf_op jit(solution)/shard_map/ppermute | solution.py:586
  138.6 2.8 add_convert_fusion
  141.4 5.4 %all-to-all-start = ((bf16[8,216,384]{2,1,0:T(8,128)(2,1)}), bf16[8,216,384]{2,1,0:T(8,128)(2,1)S(1)}, u32[]{:S(2)}, u32[]{:S(2)}) async-start(bf16[8,216,384]{2,1,0:T(8,128)(2,1)} %add_convert_fusion), calls=%async_computation | async-start | bytes 2654208 | tf_op jit(solution)/shard_map/all_to_all | solution.py:775
  146.8 52.5 %all-gather.4.cloned.1.call-done = bf16[2304,384]{1,0:T(8,128)(2,1)} async-done(((bf16[288,384]{1,0:T(8,128)(2,1)}), bf16[2304,384]{1,0:T(8,128)(2,1)}) %all-gather.4.cloned.1.call-update) | async-done | bytes 1769488 | tf_op jit(solution)/shard_map/all_gather | solution.py:658
  199.4 33.1 %shard_map.230 = (bf16[16,256,384]{2,1,0:T(8,128)(2,1)}, f32[16,2,384]{2,1,0:T(2,128)}, bf16[8,80,384]{2,1,0:T(8,128)(2,1)}, bf16[8,80,384]{2,1,0:T(8,128)(2,1)}, f32[1152,128]{1,0:T(8,128)}) custom-call(s32[1]{0:T(128)} %bitcast.core_ref, bf16[16,1152,256]{2,1,0:T(8,128)(2,1)} %get-tuple-element.56.qkv_ref, f32[16,8,256]{2,1,0:T(8,128)} %get-tuple-element.57.lse_ref, ...), custom_call_target="tpu_custom_call" | custom-call | flops 1 | bytes 1 | tf_op jit(solution)/shard_map/pallas_call | solution.py:543
  236.7 8.7 %collective-permute-done.10 = bf16[2,2,96,384]{3,2,0,1:T(8,128)(2,1)S(1)} collective-permute-done((bf16[2,2,96,384]{3,2,0,1:T(8,128)(2,1)S(1)}, bf16[2,2,96,384]{3,2,0,1:T(8,128)(2,1)S(1)}, u32[]{:S(2)}, u32[]{:S(2)}) %collective-permute-start.10) | collective-permute-done | bytes 294944 | tf_op jit(solution)/shard_map/ppermute | solution.py:586
  245.6 6.0 %collective-permute-done.11 = bf16[2,112,384]{2,1,0:T(8,128)(2,1)S(1)} collective-permute-done((bf16[2,112,384]{2,1,0:T(8,128)(2,1)S(1)}, bf16[2,112,384]{2,1,0:T(8,128)(2,1)S(1)}, u32[]{:S(2)}, u32[]{:S(2)}) %collective-permute-start.11) | collective-permute-done | bytes 172064 | tf_op jit(solution)/shard_map/ppermute | solution.py:586
  252.1 6.8 %collective-permute-done.12 = bf16[144,384]{1,0:T(8,128)(2,1)S(1)} collective-permute-done((bf16[144,384]{1,0:T(8,128)(2,1)S(1)}, bf16[144,384]{1,0:T(8,128)(2,1)S(1)}, u32[]{:S(2)}, u32[]{:S(2)}) %collective-permute-start.12) | collective-permute-done | bytes 110624 | tf_op jit(solution)/shard_map/ppermute | solution.py:586
  260.1 7.8 %collective-permute-done.13 = bf16[424,384]{1,0:T(8,128)(2,1)S(1)} collective-permute-done((bf16[424,384]{1,0:T(8,128)(2,1)S(1)}, bf16[424,384]{1,0:T(8,128)(2,1)S(1)}, u32[]{:S(2)}, u32[]{:S(2)}) %collective-permute-start.13) | collective-permute-done | bytes 325664 | tf_op jit(solution)/shard_map/ppermute | solution.py:586
  270.8 2.7 shard_map.231
  (146 shorter events, 20.1 us)
Async XLA Ops:
  7.2 16.3 %copy-start.4 = (bf16[384,288]{0,1:T(8,128)(2,1)S(1)}, bf16[384,288]{0,1:T(8,128)(2,1)}, u32[]{:S(2)}) copy-start(bf16[384,288]{0,1:T(8,128)(2,1)} %param.15) | copy-start | bytes 663556
  7.2 68.6 %all-gather.6.cloned.1.call-start = ((), (), s32[]{:S(2)}) async-start(), calls=%async_computation.2 | async-start | bytes 2985984 | tf_op jit(solution)/shard_map/all_gather | solution.py:656
  12.3 8.0 %collective-permute-start = (bf16[96,384]{1,0:T(8,128)(2,1)S(1)}, bf16[96,384]{1,0:T(8,128)(2,1)S(1)}, u32[]{:S(2)}, u32[]{:S(2)}) collective-permute-start(bf16[96,384]{1,0:T(8,128)(2,1)S(1)} %fusion.15), channel_id=1, source_target_pairs={{0,16},{1,17},{2,18},{3,19},{4,20},{5,21},{6,22},{7,23},{8,24},{9,... | collective-permute-start | bytes 221192 | tf_op jit(solution)/shard_map/ppermute | solution.py:586
  16.4 7.1 %collective-permute-start.2 = (bf16[288,384]{1,0:T(8,128)(2,1)}, bf16[288,384]{1,0:T(8,128)(2,1)S(1)}, u32[]{:S(2)}, u32[]{:S(2)}) collective-permute-start(bf16[288,384]{1,0:T(8,128)(2,1)} %bitcast.147), channel_id=1, source_target_pairs={{0,4},{1,5},{2,6},{3,7},{4,0},{5,1},{6,2},{7,3},{8,12},{9,13},{10,... | collective-permute-start | bytes 663560 | tf_op jit(solution)/shard_map/ppermute | solution.py:586
  17.9 181.4 %all-gather.4.cloned.1.call-start = ((), (), s32[]{:S(2)}) async-start(), calls=%async_computation.1 | async-start | bytes 1990656 | tf_op jit(solution)/shard_map/all_gather | solution.py:658
  20.4 5.2 %collective-permute-start.1 = (bf16[2,96,384]{2,1,0:T(8,128)(2,1)S(1)}, bf16[2,96,384]{2,1,0:T(8,128)(2,1)S(1)}, u32[]{:S(2)}, u32[]{:S(2)}) collective-permute-start(bf16[2,96,384]{2,1,0:T(8,128)(2,1)S(1)} %pad_maximum_fusion.13), channel_id=1, source_target_pairs={{0,8},{1,9},{2,10},{3,11},{4,12},{5,13},{6,14},{7,15},{8,0},{9,1},... | collective-permute-start | bytes 442376 | tf_op jit(solution)/shard_map/ppermute | solution.py:586
  25.9 12.2 %collective-permute-start.3 = (f32[2,16,576]{2,1,0:T(8,128)S(1)}, f32[2,16,576]{2,1,0:T(8,128)S(1)}, u32[]{:S(2)}, u32[]{:S(2)}) collective-permute-start(f32[2,16,576]{2,1,0:T(8,128)S(1)} %dynamic-slice_bitcast_fusion), channel_id=1, source_target_pairs={{0,16},{1,17},{2,18},{3,19},{4,20},{5,21},{6,22},{7,23},{8,24},{9,... | collective-permute-start | bytes 221192 | tf_op jit(solution)/shard_map/ppermute | solution.py:586
  38.2 5.6 %collective-permute-start.4 = (f32[2,16,576]{2,1,0:T(8,128)S(1)}, f32[2,16,576]{2,1,0:T(8,128)S(1)}, u32[]{:S(2)}, u32[]{:S(2)}) collective-permute-start(f32[2,16,576]{2,1,0:T(8,128)S(1)} %fusion.10), channel_id=1, source_target_pairs={{0,8},{1,9},{2,10},{3,11},{4,12},{5,13},{6,14},{7,15},{8,0},{9,1},... | collective-permute-start | bytes 221192 | tf_op jit(solution)/shard_map/ppermute | solution.py:586
  38.3 7.3 %collective-permute-start.5 = (bf16[2,2,96,384]{3,2,1,0:T(8,128)(2,1)S(1)}, bf16[2,2,96,384]{3,2,1,0:T(8,128)(2,1)S(1)}, u32[]{:S(2)}, u32[]{:S(2)}) collective-permute-start(bf16[2,2,96,384]{3,2,1,0:T(8,128)(2,1)S(1)} %pad_maximum_fusion.4), channel_id=1, source_target_pairs={{0,4},{1,5},{2,6},{3,7},{4,0},{5,1},{6,2},{7,3},{8,12},{9,13},{10,... | collective-permute-start | bytes 884744 | tf_op jit(solution)/shard_map/ppermute | solution.py:586
  46.0 3.6 %collective-permute-start.6 = (bf16[8,88,384]{2,1,0:T(8,128)(2,1)S(1)}, bf16[8,88,384]{2,1,0:T(8,128)(2,1)S(1)}, u32[]{:S(2)}, u32[]{:S(2)}) collective-permute-start(bf16[8,88,384]{2,1,0:T(8,128)(2,1)S(1)} %slice.104.mine_ref), channel_id=1, source_target_pairs={{0,1},{1,0},{2,3},{3,2},{4,5},{5,4},{6,7},{7,6},{8,9},{9,8},{10,11... | collective-permute-start | bytes 1622024 | tf_op jit(solution)/shard_map/ppermute | solution.py:586
  49.7 25.3 %collective-permute-start.7 = (bf16[2,8,16,384]{3,2,1,0:T(8,128)(2,1)S(1)}, bf16[2,8,16,384]{3,2,1,0:T(8,128)(2,1)S(1)}, u32[]{:S(2)}, u32[]{:S(2)}) collective-permute-start(bf16[2,8,16,384]{3,2,1,0:T(8,128)(2,1)S(1)} %pad_maximum_fusion.8), channel_id=1, source_target_pairs={{0,2},{1,3},{2,0},{3,1},{4,6},{5,7},{6,4},{7,5},{8,10},{9,11},{10,... | collective-permute-start | bytes 589832 | tf_op jit(solution)/shard_map/ppermute | solution.py:586
  135.3 3.3 %collective-permute-start.8 = (bf16[8,216,384]{2,1,0:T(8,128)(2,1)}, bf16[8,216,384]{2,1,0:T(8,128)(2,1)S(1)}, u32[]{:S(2)}, u32[]{:S(2)}) collective-permute-start(bf16[8,216,384]{2,1,0:T(8,128)(2,1)} %get-tuple-element.62), channel_id=1, source_target_pairs={{0,1},{1,0},{2,3},{3,2},{4,5},{5,4},{6,7},{7,6},{8,9},{9,8},{10,11... | collective-permute-start | bytes 3981320 | tf_op jit(solution)/shard_map/ppermute | solution.py:586
  141.4 91.0 %all-to-all-start = ((bf16[8,216,384]{2,1,0:T(8,128)(2,1)}), bf16[8,216,384]{2,1,0:T(8,128)(2,1)S(1)}, u32[]{:S(2)}, u32[]{:S(2)}) async-start(bf16[8,216,384]{2,1,0:T(8,128)(2,1)} %add_convert_fusion), calls=%async_computation | async-start | bytes 2654208 | tf_op jit(solution)/shard_map/all_to_all | solution.py:775
  199.4 33.2 %copy-start.5 = (f32[1536,128]{1,0:T(8,128)S(1)}, f32[1536,128]{1,0:T(8,128)}, u32[]{:S(2)}) copy-start(f32[1536,128]{1,0:T(8,128)} %get-tuple-element.75) | copy-start | bytes 2359300
  199.4 33.5 %copy-start.14 = (f32[1,384]{1,0:T(1,128)S(1)}, f32[1,384]{1,0:T(1,128)}, u32[]{:S(2)}) copy-start(f32[1,384]{1,0:T(1,128)} %get-tuple-element.74) | copy-start | bytes 4612
  199.4 33.6 %copy-start.13 = (f32[1,384]{1,0:T(1,128)S(1)}, f32[1,384]{1,0:T(1,128)}, u32[]{:S(2)}) copy-start(f32[1,384]{1,0:T(1,128)} %get-tuple-element.76) | copy-start | bytes 4612
  199.4 35.2 %copy-start.9 = (f32[16,4,384]{2,1,0:T(4,128)S(1)}, f32[16,4,384]{2,1,0:T(4,128)}, u32[]{:S(2)}) copy-start(f32[16,4,384]{2,1,0:T(4,128)} %get-tuple-element.68) | copy-start | bytes 294916
  232.4 3.2 %collective-permute-start.9 = (bf16[8,80,384]{2,1,0:T(8,128)(2,1)}, bf16[8,80,384]{2,1,0:T(8,128)(2,1)S(1)}, u32[]{:S(2)}, u32[]{:S(2)}) collective-permute-start(bf16[8,80,384]{2,1,0:T(8,128)(2,1)} %get-tuple-element.72), channel_id=1, source_target_pairs={{0,1},{1,0},{2,3},{3,2},{4,5},{5,4},{6,7},{7,6},{8,9},{9,8},{10,11... | collective-permute-start | bytes 1474568 | tf_op jit(solution)/shard_map/ppermute | solution.py:586
  235.9 9.5 %collective-permute-start.10 = (bf16[2,2,96,384]{3,2,0,1:T(8,128)(2,1)S(1)}, bf16[2,2,96,384]{3,2,0,1:T(8,128)(2,1)S(1)}, u32[]{:S(2)}, u32[]{:S(2)}) collective-permute-start(bf16[2,2,96,384]{3,2,0,1:T(8,128)(2,1)S(1)} %pad_maximum_fusion.7), channel_id=1, source_target_pairs={{0,4},{1,5},{2,6},{3,7},{4,0},{5,1},{6,2},{7,3},{8,12},{9,13},{10,... | collective-permute-start | bytes 884744 | tf_op jit(solution)/shard_map/ppermute | solution.py:586
  245.6 6.1 %collective-permute-start.11 = (bf16[2,112,384]{2,1,0:T(8,128)(2,1)S(1)}, bf16[2,112,384]{2,1,0:T(8,128)(2,1)S(1)}, u32[]{:S(2)}, u32[]{:S(2)}) collective-permute-start(bf16[2,112,384]{2,1,0:T(8,128)(2,1)S(1)} %pad_maximum_fusion.11), channel_id=1, source_target_pairs={{0,8},{1,9},{2,10},{3,11},{4,12},{5,13},{6,14},{7,15},{8,0},{9,1},... | collective-permute-start | bytes 516104 | tf_op jit(solution)/shard_map/ppermute | solution.py:586
  251.8 16.5 %copy-start.10 = (f32[16,2,384]{2,1,0:T(2,128)S(1)}, f32[16,2,384]{2,1,0:T(2,128)}, u32[]{:S(2)}) copy-start(f32[16,2,384]{2,1,0:T(2,128)} %get-tuple-element.67) | copy-start | bytes 147460
  251.8 7.1 %collective-permute-start.12 = (bf16[144,384]{1,0:T(8,128)(2,1)S(1)}, bf16[144,384]{1,0:T(8,128)(2,1)S(1)}, u32[]{:S(2)}, u32[]{:S(2)}) collective-permute-start(bf16[144,384]{1,0:T(8,128)(2,1)S(1)} %pad_maximum_fusion.14), channel_id=1, source_target_pairs={{0,16},{1,17},{2,18},{3,19},{4,20},{5,21},{6,22},{7,23},{8,24},{9,... | collective-permute-start | bytes 331784 | tf_op jit(solution)/shard_map/ppermute | solution.py:586
  259.0 8.9 %collective-permute-start.13 = (bf16[424,384]{1,0:T(8,128)(2,1)S(1)}, bf16[424,384]{1,0:T(8,128)(2,1)S(1)}, u32[]{:S(2)}, u32[]{:S(2)}) collective-permute-start(bf16[424,384]{1,0:T(8,128)(2,1)S(1)} %pad_maximum_fusion.6), channel_id=1, source_target_pairs={{0,2},{1,3},{2,0},{3,1},{4,6},{5,7},{6,4},{7,5},{8,10},{9,11},{10,... | collective-permute-start | bytes 976904 | tf_op jit(solution)/shard_map/ppermute | solution.py:586
  268.2 1.8 collective-permute-start.14
  (9 other events, 55.4 us)
Sparse Core Ops, SparseCore 0:
  18.0 57.6 all-gather.5
  135.7 63.6 all-gather.3

commit v8 on v7

--- a/solution.py
+++ b/solution.py
@@ -629,7 +629,6 @@
     heads = width // HEAD_DIM
     rows = latents * length
     hops = Hops(n_dp, n_rep)
-    dp_bits = hops.bits("dp")
     folds = hidden_width // width
 
     up_rows, out_rows = up_weight.shape[1], out_weight.shape[1]
@@ -642,13 +641,12 @@
     half_rows = qkv_rows // 2
     core = hops.mine("rep", 1)
     bias_shard = jnp.concatenate([qv_bias, out_bias, up_bias, down_bias])
-    bias_rows = 2
+    bias_rows = 1
     front = jnp.concatenate(
         [
             lax.dynamic_slice_in_dim(qkv_weight.T, core * half_rows, half_rows, axis=0),
             silu_low,
             jnp.pad(bias_shard, (0, width - bias_shard.shape[0]))[None],
-            jnp.pad(ada_bias, (0, width - ada_bias.shape[0]))[None],
         ]
     )
     front = pad_rows(front, up_to(front.shape[0], 8))
@@ -656,21 +654,15 @@
     late = lax.all_gather(late_shard, "dp", axis=0)
     ada_shard, _ = lax.optimization_barrier((ada_weight.T, late))
     ada_all = lax.all_gather(ada_shard, "dp", axis=0, tiled=True)
-    ada_pair = hops.both(ada_weight.T, hops.swap(ada_weight.T, "dp", 1), "dp", 1, 0)
-    high_bits = dp_bits[:0:-1]
-    for done, bit in enumerate(high_bits):
-        front = hops.both(front, hops.swap(front, "dp", bit), "dp", bit, done)
-
-    silu_part = front[..., half_rows : half_rows + latents, :].reshape(-1, width)
-    mod = dot_nt(silu_part, ada_pair.reshape(-1, width))
-    mod = mod.reshape((2,) * len(high_bits) + (latents, -1))
-    for done, bit in enumerate(high_bits):
-        kept, sent = hops.cut(mod, "dp", bit, done)
-        mod = hops.both(kept, hops.swap(sent, "dp", bit), "dp", bit, done)
-    mod = mod.reshape(n_dp // 2, latents, -1).transpose(1, 0, 2).reshape(latents, -1)
-
-    front = hops.both(front, hops.swap(front, "dp", 1), "dp", 1, len(high_bits))
-    front = front.reshape(n_dp, -1, width)
+    front = lax.all_to_all(
+        jnp.broadcast_to(front, (n_dp,) + front.shape), "dp", 0, 0, tiled=True
+    )
+
+    silu_group = front[:, half_rows : half_rows + latents].reshape(n_dp * latents, width)
+    mod = jnp.dot(silu_group, ada_weight, preferred_element_type=F32) + ada_bias.astype(F32)
+    mod = lax.all_to_all(mod.reshape(n_dp, latents, -1), "dp", 0, 0, tiled=True)
+    modulation = mod.transpose(1, 0, 2).reshape(latents, 6, width)
+
     mine = front[:, : half_rows + latents]
     came = hops.swap(mine, "rep", 1)
     silu_all = hops.both(mine[:, half_rows:], came[:, half_rows:], "rep", 1, 0)
@@ -686,12 +678,9 @@
     qv_full, out_full, up_full, down_full = (
         bias_all[:, low:high].reshape(1, -1) for low, high in zip(cuts[:-1], cuts[1:])
     )
-    ada_full = front[:, half_rows + latents + 1, : ada_bias.shape[0]].astype(F32).reshape(1, -1)
     qkv_bias = jnp.concatenate(
         [qv_full[:, :width], jnp.zeros((1, width), F32), qv_full[:, width:]], axis=1
     )
-
-    modulation = (mod + ada_full).reshape(latents, 6, width)
 
     core_scalar = core.astype(jnp.int32).reshape(1)
     normed, qkv, lse, attended, qkv_full = run_kernel(
@@ -770,11 +759,12 @@
         [core_scalar],
     )
 
+    late_sent, ada_all = lax.optimization_barrier((late_sent, ada_all))
     late_half = late_kept.astype(F32) + hops.swap(late_sent, "rep", 1).astype(F32)
     late_half = late_half.astype(BF16)
     late_parts = lax.all_to_all(late_half, "dp", 0, 0, tiled=True)
 
-    normed, ada_all, _ = lax.optimization_barrier((normed, ada_all, late_half))
+    normed, _ = lax.optimization_barrier((normed, late_half))
     tail_rows = up_to(half_rows + 1, 8)
     tokens_grad, grad_mod_one, qkv_kept, qkv_sent, qkv_bias_grad = run_kernel(
         attention_backward_kernel,
@@ -821,26 +811,11 @@
     own = 6 * width // n_dp
     columns = grad_modulation.reshape(latents, n_dp, own).transpose(1, 0, 2).astype(BF16)
     columns = jnp.pad(columns, ((0, 0), (0, 0), (0, up_to(own, width) - own)))
-    columns = columns.reshape((2,) * len(dp_bits) + (latents, width))
-    total = total.reshape((2,) * len(dp_bits) + (tail_rows, width))
-    axis = len(dp_bits) - 1
-    for bit in dp_bits:
-        kept, sent = hops.cut(total, "dp", bit, axis)
-        column_kept, column_sent = hops.cut(columns, "dp", bit, axis)
-        lead = sent.shape[:axis]
-        sources = column_sent.shape[axis:-2]
-        came = hops.swap(
-            jnp.concatenate(
-                [sent.astype(BF16), column_sent.reshape(lead + (-1, width))], axis=-2
-            ),
-            "dp",
-            bit,
-        )
-        total = kept.astype(F32) + came[..., :tail_rows, :].astype(F32)
-        column_came = came[..., tail_rows:, :].reshape(lead + sources + (latents, width))
-        columns = hops.both(column_kept, column_came, "dp", bit, axis)
-        axis -= 1
-    columns = columns.reshape(n_dp * latents, width)
+    parts = lax.all_to_all(
+        jnp.concatenate([total.astype(BF16), columns], axis=1), "dp", 0, 0, tiled=True
+    )
+    total = jnp.sum(parts[:, :tail_rows].astype(F32), axis=0)
+    columns = parts[:, tail_rows:].reshape(n_dp * latents, width)
 
     qkv_total = total.astype(BF16)
     end = tail_rows + late_sum.shape[0]

time: 282 us -> 256 us (0.908)
  waiting for transfers between devices: 106 us -> 76.3 us
  starting transfers between devices: 20.4 us -> 23.9 us
    all_to_all x0 -> x3, waiting for transfers between devices: none -> 54.6 us  [the longest x1 26.4 us: body(): lax.all_to_all(jnp.broadcast_to(front, (n_dp,) + front.shape), 'dp', 0, 0...]
    all_gather x1, waiting for transfers between devices: 52.5 us -> 0.02 us  [body(): ada_all = lax.all_gather(ada_shard, 'dp', axis=0, tiled=True)]
    ppermute x15 -> x6, waiting for transfers between devices: 53.8 us -> 12.1 us  [swap(): return lax.ppermute(value, AXES, pairs)]
    all_to_all x0 -> x3, starting transfers between devices: none -> 16.6 us  [the longest x1 7.38 us: body(): lax.all_to_all(jnp.broadcast_to(front, (n_dp,) + front.shape), 'dp', 0, 0...]
    ppermute x15 -> x6, starting transfers between devices: 14.9 us -> 3.62 us  [swap(): return lax.ppermute(value, AXES, pairs)]
    all_gather x1, waiting for transfers between devices: 0.01 us -> 9.48 us  [body(): late = lax.all_gather(late_shard, 'dp', axis=0)]
  transfers between devices with their start and end apart: 18 -> 12, of which waited for: 13 -> 8; matrix products, arithmetic and copies ran while one was open for 5% -> 4% of each run, Pallas kernels for 20% -> 46%
where the time goes in v8:
time: 256 us; the launch traced here: 255 us
  Pallas kernels  119 us (46%)
  waiting for transfers between devices  76.3 us (30%)
  starting transfers between devices  23.9 us (9%)
  between operations  14.5 us (6%)
  other arithmetic  11.3 us (4%)
  local copies, waits for them, and re-layouts  8.76 us (3%)
    pallas_call x3, Pallas kernels, run_kernel(): pl.pallas_call(kernel, grid=(streamed[0].shape[0] // count,), in_specs=[p...  116 us
    all_to_all x1, waiting for transfers between devices, body(): lax.all_to_all(jnp.broadcast_to(front, (n_dp,) + front.shape), 'dp', 0, 0...  26.4 us
    all_to_all x1, waiting for transfers between devices, body(): lax.all_to_all(jnp.concatenate([total.astype(BF16), columns], axis=1), 'd...  16.4 us
    ppermute x6, waiting for transfers between devices, swap(): return lax.ppermute(value, AXES, pairs)  12.1 us
    all_to_all x1, waiting for transfers between devices, body(): mod = lax.all_to_all(mod.reshape(n_dp, latents, -1), 'dp', 0, 0, tiled=True)  11.9 us
    all_gather x1, waiting for transfers between devices, body(): late = lax.all_gather(late_shard, 'dp', axis=0)  9.48 us
    all_to_all x1, starting transfers between devices, body(): lax.all_to_all(jnp.broadcast_to(front, (n_dp,) + front.shape), 'dp', 0, 0...  7.38 us
    all_to_all x1, starting transfers between devices, body(): lax.all_to_all(jnp.concatenate([total.astype(BF16), columns], axis=1), 'd...  5.81 us
  transfers between devices with their start and end apart: 12, of which 8 were waited for; matrix products, arithmetic and copies ran while one was open for 4% of the time, Pallas kernels for 46%

profile of v8, /device:TPU:0, one launch (start us, length us, event | category | flops | bytes accessed | tf_op | source)
XLA Modules:
  0.0 255.2 jit_solution(15304176020490795381)
XLA Ops:
  8.8 0.9 reshape.106
  9.9 1.7 pad_maximum_fusion.2
  12.4 7.4 %all-to-all-start = ((bf16[8,96,384]{2,1,0:T(8,128)(2,1)}), bf16[8,96,384]{2,1,0:T(8,128)(2,1)S(1)}, u32[]{:S(2)}, u32[]{:S(2)}) async-start(bf16[8,96,384]{2,1,0:T(8,128)(2,1)} %broadcast_in_dim.14), calls=%async_computation | async-start | bytes 1179648 | tf_op jit(solution)/shard_map/all_to_all | solution.py:657
  19.9 26.4 %all-to-all-done = bf16[8,96,384]{2,1,0:T(8,128)(2,1)S(1)} async-done(((bf16[8,96,384]{2,1,0:T(8,128)(2,1)}), bf16[8,96,384]{2,1,0:T(8,128)(2,1)S(1)}, u32[]{:S(2)}, u32[]{:S(2)}) %all-to-all-start) | async-done | bytes 589856 | tf_op jit(solution)/shard_map/all_to_all | solution.py:657
  49.3 1.6 collective-permute-start.1
  52.0 3.4 %all-to-all-start.1 = ((f32[8,16,288]{2,1,0:T(8,128)}), f32[8,16,288]{2,1,0:T(8,128)S(1)}, u32[]{:S(2)}, u32[]{:S(2)}) async-start(f32[8,16,288]{2,1,0:T(8,128)} %bitcast.8), calls=%async_computation.1 | async-start | bytes 393216 | tf_op jit(solution)/shard_map/all_to_all | solution.py:663
  55.5 1.2 collective-permute-done.1
  57.5 11.9 %all-to-all-done.1 = f32[8,16,288]{2,1,0:T(8,128)S(1)} async-done(((f32[8,16,288]{2,1,0:T(8,128)}), f32[8,16,288]{2,1,0:T(8,128)S(1)}, u32[]{:S(2)}, u32[]{:S(2)}) %all-to-all-start.1) | async-done | bytes 147488 | tf_op jit(solution)/shard_map/all_to_all | solution.py:663
  70.3 9.5 %all-gather.6.cloned.1.call-done = bf16[3456,384]{1,0:T(8,128)(2,1)} async-done(((bf16[432,384]{1,0:T(8,128)(2,1)}), bf16[3456,384]{1,0:T(8,128)(2,1)}) %all-gather.6.cloned.1.call-update) | async-done | bytes 2654224 | tf_op jit(solution)/shard_map/all_gather | solution.py:654
  79.8 23.8 %shard_map.228 = (bf16[16,256,384]{2,1,0:T(8,128)(2,1)}, bf16[16,1152,256]{2,1,0:T(8,128)(2,1)}, f32[16,8,256]{2,1,0:T(8,128)}, bf16[16,384,256]{2,1,0:T(8,128)(2,1)}, bf16[1152,384]{1,0:T(8,128)(2,1)}) custom-call(s32[1]{0:T(128)} %bitcast.core_ref, bf16[16,256,384]{2,1,0:T(8,128)(2,1)} %tokens_ref.5, f32[16,6,384]{2,1,0:T(8,128)} %reshape.110.mod_ref, ...), custom_call_target="tpu_custom_call" | custom-call | flops 5234491392 | bytes 18874368 | tf_op jit(solution)/shard_map/pallas_call | solution.py:543
  103.6 59.3 %shard_map.229 = (bf16[16,256,384]{2,1,0:T(8,128)(2,1)}, f32[16,256,384]{2,1,0:T(8,128)}, bf16[16,384,256]{2,1,0:T(8,128)(2,1)}, f32[16,4,384]{2,1,0:T(4,128)}, ...) custom-call(s32[1]{0:T(128)} %bitcast.core_ref, ...), custom_call_target="tpu_custom_call" | custom-call | flops 32614907904 | bytes 22020096 | tf_op jit(solution)/shard_map/pallas_call | solution.py:543
  163.1 3.3 %collective-permute-done.2 = bf16[8,216,384]{2,1,0:T(8,128)(2,1)S(1)} collective-permute-done((bf16[8,216,384]{2,1,0:T(8,128)(2,1)}, bf16[8,216,384]{2,1,0:T(8,128)(2,1)S(1)}, u32[]{:S(2)}, u32[]{:S(2)}) %collective-permute-start.2) | collective-permute-done | bytes 1327136 | tf_op jit(solution)/shard_map/ppermute | solution.py:586
  166.3 2.8 %add_convert_fusion = bf16[8,216,384]{2,1,0:T(8,128)(2,1)} fusion(bf16[8,216,384]{2,1,0:T(8,128)(2,1)S(1)} %collective-permute-done.2, bf16[8,216,384]{2,1,0:T(8,128)(2,1)} %get-tuple-element.61), kind=kLoop, calls=%fused_computation | loop fusion | flops 2654208 | bytes 3981312 | tf_op jit(solution)/shard_map/convert_element_type | solution.py:764
  169.1 3.6 %all-to-all-start.2 = ((bf16[8,216,384]{2,1,0:T(8,128)(2,1)}), bf16[8,216,384]{2,1,0:T(8,128)(2,1)S(1)}, u32[]{:S(2)}, u32[]{:S(2)}) async-start(bf16[8,216,384]{2,1,0:T(8,128)(2,1)} %add_convert_fusion), calls=%async_computation.2 | async-start | bytes 2654208 | tf_op jit(solution)/shard_map/all_to_all | solution.py:765
  172.7 33.1 %shard_map.230 = (bf16[16,256,384]{2,1,0:T(8,128)(2,1)}, f32[16,2,384]{2,1,0:T(2,128)}, bf16[8,80,384]{2,1,0:T(8,128)(2,1)}, bf16[8,80,384]{2,1,0:T(8,128)(2,1)}, f32[1152,128]{1,0:T(8,128)}) custom-call(s32[1]{0:T(128)} %bitcast.core_ref, bf16[16,1152,256]{2,1,0:T(8,128)(2,1)} %get-tuple-element.57.qkv_ref, f32[16,8,256]{2,1,0:T(8,128)} %get-tuple-element.58.lse_ref, ...), custom_call_target="tpu_custom_call" | custom-call | flops 1 | bytes 1 | tf_op jit(solution)/shard_map/pallas_call | solution.py:543
  206.6 1.2 slice_reduce_fusion.3
  209.3 0.9 fusion.1
  210.2 5.8 %all-to-all-start.3 = ((bf16[8,96,384]{2,1,0:T(8,128)(2,1)}), bf16[8,96,384]{2,1,0:T(8,128)(2,1)S(1)}, u32[]{:S(2)}, u32[]{:S(2)}) async-start(bf16[8,96,384]{2,1,0:T(8,128)(2,1)} %fusion.1), calls=%async_computation.3 | async-start | bytes 1179648 | tf_op jit(solution)/shard_map/all_to_all | solution.py:814
  216.1 16.4 %all-to-all-done.3 = bf16[8,96,384]{2,1,0:T(8,128)(2,1)S(1)} async-done(((bf16[8,96,384]{2,1,0:T(8,128)(2,1)}), bf16[8,96,384]{2,1,0:T(8,128)(2,1)S(1)}, u32[]{:S(2)}, u32[]{:S(2)}) %all-to-all-start.3) | async-done | bytes 589856 | tf_op jit(solution)/shard_map/all_to_all | solution.py:814
  232.7 1.6 collective-permute-start.4
  234.2 7.5 %collective-permute-done.4 = bf16[424,384]{1,0:T(8,128)(2,1)S(1)} collective-permute-done((bf16[424,384]{1,0:T(8,128)(2,1)S(1)}, bf16[424,384]{1,0:T(8,128)(2,1)S(1)}, u32[]{:S(2)}, u32[]{:S(2)}) %collective-permute-start.4) | collective-permute-done | bytes 325664 | tf_op jit(solution)/shard_map/ppermute | solution.py:586
  242.1 1.4 fusion.8
  244.5 2.7 %shard_map.231 = (f32[288,384]{1,0:T(8,128)}, f32[1,288]{1,0:T(1,128)}, f32[144,384]{1,0:T(8,128)}, f32[192,384]{1,0:T(8,128)}, f32[48,1536]{1,0:T(8,128)}, /*in...) custom-call(s32[1]{0:T(128)} %bitcast.core_ref, ...), custom_call_target="tpu_custom_call" | custom-call | tf_op jit(solution)/shard_map/pallas_call | solution.py:832
  247.2 1.2 reduce.7
  (97 shorter events, 12.3 us)
Async XLA Ops:
  7.2 72.6 %all-gather.6.cloned.1.call-start = ((), (), s32[]{:S(2)}) async-start(), calls=%async_computation.5 | async-start | bytes 2985984 | tf_op jit(solution)/shard_map/all_gather | solution.py:654
  9.8 10.1 %copy-start.14 = (bf16[288]{0:T(512)(128)(2,1)S(1)}, bf16[288]{0:T(512)(128)(2,1)}, u32[]{:S(2)}) copy-start(bf16[288]{0:T(512)(128)(2,1)} %param.16) | copy-start | bytes 1732
  12.4 38.5 %copy-start.3 = (bf16[384,288]{0,1:T(8,128)(2,1)S(1)}, bf16[384,288]{0,1:T(8,128)(2,1)}, u32[]{:S(2)}) copy-start(bf16[384,288]{0,1:T(8,128)(2,1)} %param.15) | copy-start | bytes 663556
  12.4 33.8 %all-to-all-start = ((bf16[8,96,384]{2,1,0:T(8,128)(2,1)}), bf16[8,96,384]{2,1,0:T(8,128)(2,1)S(1)}, u32[]{:S(2)}, u32[]{:S(2)}) async-start(bf16[8,96,384]{2,1,0:T(8,128)(2,1)} %broadcast_in_dim.14), calls=%async_computation | async-start | bytes 1179648 | tf_op jit(solution)/shard_map/all_to_all | solution.py:657
  46.3 11.2 %copy-start.5 = (bf16[8,88,384]{2,1,0:T(8,128)(2,1)}, bf16[8,88,384]{2,1,0:T(8,128)(2,1)S(1)}, u32[]{:S(2)}) copy-start(bf16[8,88,384]{2,1,0:T(8,128)(2,1)S(1)} %slice.79.mine_ref) | copy-start | bytes 1622020
  46.3 2.9 %collective-permute-start = (bf16[8,88,384]{2,1,0:T(8,128)(2,1)S(1)}, bf16[8,88,384]{2,1,0:T(8,128)(2,1)S(1)}, u32[]{:S(2)}, u32[]{:S(2)}) collective-permute-start(bf16[8,88,384]{2,1,0:T(8,128)(2,1)S(1)} %slice.79.mine_ref), channel_id=1, source_target_pairs={{0,1},{1,0},{2,3},{3,2},{4,5},{5,4},{6,7},{7,6},{8,9},{9,8},{10,11... | collective-permute-start | bytes 1622024 | tf_op jit(solution)/shard_map/ppermute | solution.py:586
  49.3 8.3 %copy-start.11 = (bf16[8,88,384]{2,1,0:T(8,128)(2,1)}, bf16[8,88,384]{2,1,0:T(8,128)(2,1)S(1)}, u32[]{:S(2)}) copy-start(bf16[8,88,384]{2,1,0:T(8,128)(2,1)S(1)} %collective-permute-done.came_ref) | copy-start | bytes 1622020
  49.3 7.4 %collective-permute-start.1 = (bf16[2,8,16,384]{3,2,1,0:T(8,128)(2,1)S(1)}, bf16[2,8,16,384]{3,2,1,0:T(8,128)(2,1)S(1)}, u32[]{:S(2)}, u32[]{:S(2)}) collective-permute-start(bf16[2,8,16,384]{3,2,1,0:T(8,128)(2,1)S(1)} %pad_maximum_fusion.4), channel_id=1, source_target_pairs={{0,2},{1,3},{2,0},{3,1},{4,6},{5,7},{6,4},{7,5},{8,10},{9,11},{10,... | collective-permute-start | bytes 589832 | tf_op jit(solution)/shard_map/ppermute | solution.py:586
  52.0 17.4 %all-to-all-start.1 = ((f32[8,16,288]{2,1,0:T(8,128)}), f32[8,16,288]{2,1,0:T(8,128)S(1)}, u32[]{:S(2)}, u32[]{:S(2)}) async-start(f32[8,16,288]{2,1,0:T(8,128)} %bitcast.8), calls=%async_computation.1 | async-start | bytes 393216 | tf_op jit(solution)/shard_map/all_to_all | solution.py:663
  55.4 107.6 %all-gather.4.cloned.1.call-start = ((), (), s32[]{:S(2)}) async-start(), calls=%async_computation.4 | async-start | bytes 1990656 | tf_op jit(solution)/shard_map/all_gather | solution.py:656
  163.0 3.3 %collective-permute-start.2 = (bf16[8,216,384]{2,1,0:T(8,128)(2,1)}, bf16[8,216,384]{2,1,0:T(8,128)(2,1)S(1)}, u32[]{:S(2)}, u32[]{:S(2)}) collective-permute-start(bf16[8,216,384]{2,1,0:T(8,128)(2,1)} %get-tuple-element.64), channel_id=1, source_target_pairs={{0,1},{1,0},{2,3},{3,2},{4,5},{5,4},{6,7},{7,6},{8,9},{9,8},{10,11... | collective-permute-start | bytes 3981320 | tf_op jit(solution)/shard_map/ppermute | solution.py:586
  169.1 36.7 %all-to-all-start.2 = ((bf16[8,216,384]{2,1,0:T(8,128)(2,1)}), bf16[8,216,384]{2,1,0:T(8,128)(2,1)S(1)}, u32[]{:S(2)}, u32[]{:S(2)}) async-start(bf16[8,216,384]{2,1,0:T(8,128)(2,1)} %add_convert_fusion), calls=%async_computation.2 | async-start | bytes 2654208 | tf_op jit(solution)/shard_map/all_to_all | solution.py:765
  172.7 33.3 %copy-start.4 = (f32[1536,128]{1,0:T(8,128)S(1)}, f32[1536,128]{1,0:T(8,128)}, u32[]{:S(2)}) copy-start(f32[1536,128]{1,0:T(8,128)} %get-tuple-element.77) | copy-start | bytes 2359300
  172.7 33.7 %copy-start.13 = (f32[1,384]{1,0:T(1,128)S(1)}, f32[1,384]{1,0:T(1,128)}, u32[]{:S(2)}) copy-start(f32[1,384]{1,0:T(1,128)} %get-tuple-element.76) | copy-start | bytes 4612
  172.7 33.8 %copy-start.12 = (f32[1,384]{1,0:T(1,128)S(1)}, f32[1,384]{1,0:T(1,128)}, u32[]{:S(2)}) copy-start(f32[1,384]{1,0:T(1,128)} %get-tuple-element.78) | copy-start | bytes 4612
  172.7 35.3 %copy-start.8 = (f32[16,4,384]{2,1,0:T(4,128)S(1)}, f32[16,4,384]{2,1,0:T(4,128)}, u32[]{:S(2)}) copy-start(f32[16,4,384]{2,1,0:T(4,128)} %get-tuple-element.70) | copy-start | bytes 294916
  205.8 3.3 %copy-start.6 = (bf16[8,80,384]{2,1,0:T(8,128)(2,1)S(1)}, bf16[8,80,384]{2,1,0:T(8,128)(2,1)}, u32[]{:S(2)}) copy-start(bf16[8,80,384]{2,1,0:T(8,128)(2,1)} %get-tuple-element.72) | copy-start | bytes 1474564
  205.8 3.3 %collective-permute-start.3 = (bf16[8,80,384]{2,1,0:T(8,128)(2,1)}, bf16[8,80,384]{2,1,0:T(8,128)(2,1)S(1)}, u32[]{:S(2)}, u32[]{:S(2)}) collective-permute-start(bf16[8,80,384]{2,1,0:T(8,128)(2,1)} %get-tuple-element.74), channel_id=1, source_target_pairs={{0,1},{1,0},{2,3},{3,2},{4,5},{5,4},{6,7},{7,6},{8,9},{9,8},{10,11... | collective-permute-start | bytes 1474568 | tf_op jit(solution)/shard_map/ppermute | solution.py:586
  210.2 22.4 %all-to-all-start.3 = ((bf16[8,96,384]{2,1,0:T(8,128)(2,1)}), bf16[8,96,384]{2,1,0:T(8,128)(2,1)S(1)}, u32[]{:S(2)}, u32[]{:S(2)}) async-start(bf16[8,96,384]{2,1,0:T(8,128)(2,1)} %fusion.1), calls=%async_computation.3 | async-start | bytes 1179648 | tf_op jit(solution)/shard_map/all_to_all | solution.py:814
  232.5 9.5 %copy-start.9 = (f32[16,2,384]{2,1,0:T(2,128)S(1)}, f32[16,2,384]{2,1,0:T(2,128)}, u32[]{:S(2)}) copy-start(f32[16,2,384]{2,1,0:T(2,128)} %get-tuple-element.69) | copy-start | bytes 147460
  232.6 9.5 %copy-start.1 = (bf16[2304,384]{1,0:T(8,128)(2,1)S(1)}, bf16[2304,384]{1,0:T(8,128)(2,1)}, u32[]{:S(2)}) copy-start(bf16[2304,384]{1,0:T(8,128)(2,1)} %all-gather.4.cloned.1.call-done) | copy-start | bytes 5308420
  232.6 9.5 %copy-start.10 = (f32[16,384]{1,0:T(8,128)S(1)}, f32[16,384]{1,0:T(8,128)}, u32[]{:S(2)}) copy-start(f32[16,384]{1,0:T(8,128)} %param.14) | copy-start | bytes 73732
  232.7 9.0 %collective-permute-start.4 = (bf16[424,384]{1,0:T(8,128)(2,1)S(1)}, bf16[424,384]{1,0:T(8,128)(2,1)S(1)}, u32[]{:S(2)}, u32[]{:S(2)}) collective-permute-start(bf16[424,384]{1,0:T(8,128)(2,1)S(1)} %pad_maximum_fusion.3), channel_id=1, source_target_pairs={{0,2},{1,3},{2,0},{3,1},{4,6},{5,7},{6,4},{7,5},{8,10},{9,11},{10,... | collective-permute-start | bytes 976904 | tf_op jit(solution)/shard_map/ppermute | solution.py:586
  241.9 1.8 collective-permute-start.5
  (3 other events, 5.2 us)
Sparse Core Ops, SparseCore 0:
  11.7 68.0 all-gather.5
  82.0 44.8 all-gather.3

commit v9 on v7

--- a/solution.py
+++ b/solution.py
@@ -41,7 +41,7 @@
     return inverse * (upstream - first - normal * second)
 
 
-STRIP = 64
+STRIP = 32
 GROUP = 3
 
 
@@ -166,9 +166,7 @@
     attended_ref,
     mod_ref,
     late_ref,
-    out_bias_ref,
-    up_bias_row_ref,
-    down_bias_ref,
+    biases_ref,
     output_ref,
     grad_middle_ref,
     grad_attended_ref,
@@ -186,6 +184,9 @@
     up_weight_ref,
     down_weight_ref,
     up_bias_ref,
+    out_bias_ref,
+    down_bias_ref,
+    up_bias_row_ref,
     out_back,
     up_back,
     down_back,
@@ -223,6 +224,13 @@
         out_back[...] = out_weight_ref[...].T
         up_back[...] = up_weight_ref[...].T
         down_back[...] = down_weight_ref[...].T
+        low = biases_ref.shape[1] - 2 * out_rows - up_rows
+        for ref, size in ((out_bias_ref, out_rows), (up_bias_row_ref, up_rows), (down_bias_ref, out_rows)):
+            for owner in range(n_dp):
+                ref[0:1, owner * size : (owner + 1) * size] = biases_ref[
+                    owner : owner + 1, low : low + size
+                ]
+            low += size
         up_bias_ref[...] = jnp.broadcast_to(up_bias_row_ref[...], (128, hidden_width)).T
 
     attended = beside(*[attended_ref[latent] for latent in range(latents)])
@@ -683,9 +691,8 @@
     cuts = [0]
     for part in (qv_bias, out_bias, up_bias, down_bias):
         cuts.append(cuts[-1] + part.shape[0])
-    qv_full, out_full, up_full, down_full = (
-        bias_all[:, low:high].reshape(1, -1) for low, high in zip(cuts[:-1], cuts[1:])
-    )
+    bias_all = bias_all[:, : cuts[-1]]
+    qv_full = bias_all[:, : cuts[1]].reshape(1, -1)
     ada_full = front[:, half_rows + latents + 1, : ada_bias.shape[0]].astype(F32).reshape(1, -1)
     qkv_bias = jnp.concatenate(
         [qv_full[:, :width], jnp.zeros((1, width), F32), qv_full[:, width:]], axis=1
@@ -751,6 +758,9 @@
             pltpu.VMEM((hidden_width, width), BF16),
             pltpu.VMEM((width, hidden_width), BF16),
             pltpu.VMEM((hidden_width, 128), F32),
+            pltpu.VMEM((1, width), F32),
+            pltpu.VMEM((1, width), F32),
+            pltpu.VMEM((1, hidden_width), F32),
             pltpu.VMEM((width, width), BF16),
             pltpu.VMEM((width, hidden_width), BF16),
             pltpu.VMEM((hidden_width, width), BF16),
@@ -761,7 +771,7 @@
             pltpu.VMEM((4 * length, width), F32),
         ],
         [tokens, cotangent, attended, modulation],
-        [late, out_full, up_full, down_full],
+        [late, bias_all],
         pl.CostEstimate(
             flops=6 * rows * width * (width + 2 * hidden_width),
             bytes_accessed=rows * width * 14,
@@ -770,11 +780,12 @@
         [core_scalar],
     )
 
+    late_sent, ada_all = lax.optimization_barrier((late_sent, ada_all))
     late_half = late_kept.astype(F32) + hops.swap(late_sent, "rep", 1).astype(F32)
     late_half = late_half.astype(BF16)
     late_parts = lax.all_to_all(late_half, "dp", 0, 0, tiled=True)
 
-    normed, ada_all, _ = lax.optimization_barrier((normed, ada_all, late_half))
+    normed, _ = lax.optimization_barrier((normed, late_half))
     tail_rows = up_to(half_rows + 1, 8)
     tokens_grad, grad_mod_one, qkv_kept, qkv_sent, qkv_bias_grad = run_kernel(
         attention_backward_kernel,
@@ -797,6 +808,9 @@
     )
     qkv_sent, late_parts = lax.optimization_barrier((qkv_sent, late_parts))
     late_sum = jnp.sum(late_parts.astype(F32), axis=0).astype(BF16)
+    for bit in hops.bits("rep")[1:]:
+        late_sum = late_sum.astype(F32) + hops.swap(late_sum, "rep", bit).astype(F32)
+        late_sum = late_sum.astype(BF16)
 
     qkv_columns = qkv_bias_grad[:, 0]
     bias_blocks = jnp.concatenate(
@@ -843,13 +857,10 @@
     columns = columns.reshape(n_dp * latents, width)
 
     qkv_total = total.astype(BF16)
-    end = tail_rows + late_sum.shape[0]
     for bit in hops.bits("rep")[1:]:
-        sums = jnp.concatenate([qkv_total, late_sum])
-        came = hops.swap(jnp.concatenate([sums, columns]), "rep", bit)
-        sums = (sums.astype(F32) + came[:end].astype(F32)).astype(BF16)
-        qkv_total, late_sum = sums[:tail_rows], sums[tail_rows:]
-        columns = hops.both(columns, came[end:], "rep", bit, 0).reshape(-1, width)
+        came = hops.swap(jnp.concatenate([qkv_total, columns]), "rep", bit)
+        qkv_total = (qkv_total.astype(F32) + came[:tail_rows].astype(F32)).astype(BF16)
+        columns = hops.both(columns, came[tail_rows:], "rep", bit, 0).reshape(-1, width)
     mine = jnp.concatenate([qkv_total, late_sum, columns])
     came = hops.swap(mine, "rep", 1)
     smem = pl.BlockSpec(memory_space=pltpu.SMEM)

time: 282 us -> 231 us (0.82)
  waiting for transfers between devices: 106 us -> 47 us
  starting transfers between devices: 20.4 us -> 24.7 us
    all_gather x1, waiting for transfers between devices: 52.5 us -> 0.02 us  [body(): ada_all = lax.all_gather(ada_shard, 'dp', axis=0, tiled=True)]
    ppermute x15 -> x16, waiting for transfers between devices: 53.8 us -> 46 us  [swap(): return lax.ppermute(value, AXES, pairs)]
    ppermute x15 -> x16, starting transfers between devices: 14.9 us -> 20.2 us  [swap(): return lax.ppermute(value, AXES, pairs)]
  transfers between devices with their start and end apart: 18 -> 19, of which waited for: 13 -> 13; matrix products, arithmetic and copies ran while one was open for 5% -> 6% of each run, Pallas kernels for 20% -> 51%
where the time goes in v9:
time: 231 us
  Pallas kernels  120 us (52%)
  waiting for transfers between devices  47 us (20%)
  starting transfers between devices  24.7 us (11%)
  between operations  14.9 us (6%)
  other arithmetic  13.3 us (6%)
  local copies, waits for them, and re-layouts  9.5 us (4%)
    pallas_call x3, Pallas kernels, run_kernel(): pl.pallas_call(kernel, grid=(streamed[0].shape[0] // count,), in_specs=[p...  117 us
    ppermute x16, waiting for transfers between devices, swap(): return lax.ppermute(value, AXES, pairs)  46 us
    ppermute x16, starting transfers between devices, swap(): return lax.ppermute(value, AXES, pairs)  20.2 us
  transfers between devices with their start and end apart: 19, of which 13 were waited for; matrix products, arithmetic and copies ran while one was open for 6% of the time, Pallas kernels for 51%

profile of v9, /device:TPU:0, one launch (start us, length us, event | category | flops | bytes accessed | tf_op | source)
XLA Modules:
  0.0 230.7 jit_solution(3541834427808405816)
XLA Ops:
  10.6 1.7 pad_maximum_fusion.4
  12.3 4.1 %collective-permute-start = (bf16[96,384]{1,0:T(8,128)(2,1)S(1)}, bf16[96,384]{1,0:T(8,128)(2,1)S(1)}, u32[]{:S(2)}, u32[]{:S(2)}) collective-permute-start(bf16[96,384]{1,0:T(8,128)(2,1)S(1)} %fusion.15), channel_id=1, source_target_pairs={{0,16},{1,17},{2,18},{3,19},{4,20},{5,21},{6,22},{7,23},{8,24},{9,... | collective-permute-start | bytes 221192 | tf_op jit(solution)/shard_map/ppermute | solution.py:594
  18.1 2.3 collective-permute-done
  21.1 2.4 %collective-permute-done.2 = bf16[288,384]{1,0:T(8,128)(2,1)S(1)} collective-permute-done((bf16[288,384]{1,0:T(8,128)(2,1)}, bf16[288,384]{1,0:T(8,128)(2,1)S(1)}, u32[]{:S(2)}, u32[]{:S(2)}) %collective-permute-start.2) | collective-permute-done | bytes 221216 | tf_op jit(solution)/shard_map/ppermute | solution.py:594
  23.6 2.0 collective-permute-done.1
  25.9 2.7 %collective-permute-start.3 = (f32[2,16,576]{2,1,0:T(8,128)S(1)}, f32[2,16,576]{2,1,0:T(8,128)S(1)}, u32[]{:S(2)}, u32[]{:S(2)}) collective-permute-start(f32[2,16,576]{2,1,0:T(8,128)S(1)} %dynamic-slice_bitcast_fusion), channel_id=1, source_target_pairs={{0,16},{1,17},{2,18},{3,19},{4,20},{5,21},{6,22},{7,23},{8,24},{9,... | collective-permute-start | bytes 221192 | tf_op jit(solution)/shard_map/ppermute | solution.py:594
  28.7 9.5 %collective-permute-done.3 = f32[2,16,576]{2,1,0:T(8,128)S(1)} collective-permute-done((f32[2,16,576]{2,1,0:T(8,128)S(1)}, f32[2,16,576]{2,1,0:T(8,128)S(1)}, u32[]{:S(2)}, u32[]{:S(2)}) %collective-permute-start.3) | collective-permute-done | bytes 73760 | tf_op jit(solution)/shard_map/ppermute | solution.py:594
  38.3 1.8 collective-permute-start.5
  40.2 3.6 %collective-permute-done.4 = f32[2,16,576]{2,1,0:T(8,128)S(1)} collective-permute-done((f32[2,16,576]{2,1,0:T(8,128)S(1)}, f32[2,16,576]{2,1,0:T(8,128)S(1)}, u32[]{:S(2)}, u32[]{:S(2)}) %collective-permute-start.4) | collective-permute-done | bytes 73760 | tf_op jit(solution)/shard_map/ppermute | solution.py:594
  44.1 1.5 collective-permute-done.5
  51.5 23.1 %shard_map.228 = (bf16[16,256,384]{2,1,0:T(8,128)(2,1)}, bf16[16,1152,256]{2,1,0:T(8,128)(2,1)}, f32[16,8,256]{2,1,0:T(8,128)}, bf16[16,384,256]{2,1,0:T(8,128)(2,1)}, bf16[1152,384]{1,0:T(8,128)(2,1)}) custom-call(s32[1]{0:T(128)} %bitcast.core_ref, bf16[16,256,384]{2,1,0:T(8,128)(2,1)} %tokens_ref.5, f32[16,6,384]{2,1,0:T(8,128)} %broadcast_add_fusion.mod_ref, ...), custom_call_target="tpu_custom_call" | custom-call | flops 5234491392 | bytes 18874368 | tf_op jit(solution)/shard_map/pallas_call | solution.py:551
  76.7 60.4 %shard_map.229 = (bf16[16,256,384]{2,1,0:T(8,128)(2,1)}, f32[16,256,384]{2,1,0:T(8,128)}, bf16[16,384,256]{2,1,0:T(8,128)(2,1)}, f32[16,4,384]{2,1,0:T(4,128)}, ...) custom-call(s32[1]{0:T(128)} %bitcast.core_ref, ...), custom_call_target="tpu_custom_call" | custom-call | flops 32614907904 | bytes 22020096 | tf_op jit(solution)/shard_map/pallas_call | solution.py:551
  137.2 3.3 %collective-permute-done.8 = bf16[8,216,384]{2,1,0:T(8,128)(2,1)S(1)} collective-permute-done((bf16[8,216,384]{2,1,0:T(8,128)(2,1)}, bf16[8,216,384]{2,1,0:T(8,128)(2,1)S(1)}, u32[]{:S(2)}, u32[]{:S(2)}) %collective-permute-start.8) | collective-permute-done | bytes 1327136 | tf_op jit(solution)/shard_map/ppermute | solution.py:594
  140.4 2.8 %add_convert_fusion = bf16[8,216,384]{2,1,0:T(8,128)(2,1)} fusion(bf16[8,216,384]{2,1,0:T(8,128)(2,1)S(1)} %collective-permute-done.8, bf16[8,216,384]{2,1,0:T(8,128)(2,1)} %get-tuple-element.61), kind=kLoop, calls=%fused_computation | loop fusion | flops 2654208 | bytes 3981312 | tf_op jit(solution)/shard_map/convert_element_type | solution.py:785
  143.2 4.5 %all-to-all-start = ((bf16[8,216,384]{2,1,0:T(8,128)(2,1)}), bf16[8,216,384]{2,1,0:T(8,128)(2,1)S(1)}, u32[]{:S(2)}, u32[]{:S(2)}) async-start(bf16[8,216,384]{2,1,0:T(8,128)(2,1)} %add_convert_fusion), calls=%async_computation | async-start | bytes 2654208 | tf_op jit(solution)/shard_map/all_to_all | solution.py:786
  147.7 33.3 %shard_map.230 = (bf16[16,256,384]{2,1,0:T(8,128)(2,1)}, f32[16,2,384]{2,1,0:T(2,128)}, bf16[8,80,384]{2,1,0:T(8,128)(2,1)}, bf16[8,80,384]{2,1,0:T(8,128)(2,1)}, f32[1152,128]{1,0:T(8,128)}) custom-call(s32[1]{0:T(128)} %bitcast.core_ref, bf16[16,1152,256]{2,1,0:T(8,128)(2,1)} %get-tuple-element.57.qkv_ref, f32[16,8,256]{2,1,0:T(8,128)} %get-tuple-element.58.lse_ref, ...), custom_call_target="tpu_custom_call" | custom-call | flops 1 | bytes 1 | tf_op jit(solution)/shard_map/pallas_call | solution.py:551
  184.5 2.1 collective-permute-start.10
  186.6 7.7 %collective-permute-done.10 = bf16[2,2,96,384]{3,2,0,1:T(8,128)(2,1)S(1)} collective-permute-done((bf16[2,2,96,384]{3,2,0,1:T(8,128)(2,1)S(1)}, bf16[2,2,96,384]{3,2,0,1:T(8,128)(2,1)S(1)}, u32[]{:S(2)}, u32[]{:S(2)}) %collective-permute-start.10) | collective-permute-done | bytes 294944 | tf_op jit(solution)/shard_map/ppermute | solution.py:594
  194.5 1.8 collective-permute-start.11
  196.3 4.4 %collective-permute-done.11 = bf16[2,112,384]{2,1,0:T(8,128)(2,1)S(1)} collective-permute-done((bf16[2,112,384]{2,1,0:T(8,128)(2,1)S(1)}, bf16[2,112,384]{2,1,0:T(8,128)(2,1)S(1)}, u32[]{:S(2)}, u32[]{:S(2)}) %collective-permute-start.11) | collective-permute-done | bytes 172064 | tf_op jit(solution)/shard_map/ppermute | solution.py:594
  201.5 2.5 %collective-permute-start.12 = (bf16[144,384]{1,0:T(8,128)(2,1)}, bf16[144,384]{1,0:T(8,128)(2,1)}, u32[]{:S(2)}, u32[]{:S(2)}) collective-permute-start(bf16[144,384]{1,0:T(8,128)(2,1)} %pad_maximum_fusion.13), channel_id=1, source_target_pairs={{0,16},{1,17},{2,18},{3,19},{4,20},{5,21},{6,22},{7,23},{8,24},{9,... | collective-permute-start | bytes 331784 | tf_op jit(solution)/shard_map/ppermute | solution.py:594
  204.9 4.3 %collective-permute-done.12 = bf16[144,384]{1,0:T(8,128)(2,1)} collective-permute-done((bf16[144,384]{1,0:T(8,128)(2,1)}, bf16[144,384]{1,0:T(8,128)(2,1)}, u32[]{:S(2)}, u32[]{:S(2)}) %collective-permute-start.12) | collective-permute-done | bytes 110624 | tf_op jit(solution)/shard_map/ppermute | solution.py:594
  212.2 4.9 %collective-permute-done.13 = bf16[208,384]{1,0:T(8,128)(2,1)S(1)} collective-permute-done((bf16[208,384]{1,0:T(8,128)(2,1)S(1)}, bf16[208,384]{1,0:T(8,128)(2,1)S(1)}, u32[]{:S(2)}, u32[]{:S(2)}) %collective-permute-start.13) | collective-permute-done | bytes 159776 | tf_op jit(solution)/shard_map/ppermute | solution.py:594
  219.9 2.7 %shard_map.231 = (f32[288,384]{1,0:T(8,128)}, f32[1,288]{1,0:T(1,128)}, f32[144,384]{1,0:T(8,128)}, f32[192,384]{1,0:T(8,128)}, f32[48,1536]{1,0:T(8,128)}, /*in...) custom-call(s32[1]{0:T(128)} %bitcast.core_ref, ...), custom_call_target="tpu_custom_call" | custom-call | tf_op jit(solution)/shard_map/pallas_call | solution.py:868
  (153 shorter events, 26.4 us)
Async XLA Ops:
  7.2 68.6 %all-gather.6.cloned.1.call-start = ((), (), s32[]{:S(2)}) async-start(), calls=%async_computation.2 | async-start | bytes 2985984 | tf_op jit(solution)/shard_map/all_gather | solution.py:664
  12.3 8.0 %collective-permute-start = (bf16[96,384]{1,0:T(8,128)(2,1)S(1)}, bf16[96,384]{1,0:T(8,128)(2,1)S(1)}, u32[]{:S(2)}, u32[]{:S(2)}) collective-permute-start(bf16[96,384]{1,0:T(8,128)(2,1)S(1)} %fusion.15), channel_id=1, source_target_pairs={{0,16},{1,17},{2,18},{3,19},{4,20},{5,21},{6,22},{7,23},{8,24},{9,... | collective-permute-start | bytes 221192 | tf_op jit(solution)/shard_map/ppermute | solution.py:594
  16.4 7.1 %collective-permute-start.2 = (bf16[288,384]{1,0:T(8,128)(2,1)}, bf16[288,384]{1,0:T(8,128)(2,1)S(1)}, u32[]{:S(2)}, u32[]{:S(2)}) collective-permute-start(bf16[288,384]{1,0:T(8,128)(2,1)} %bitcast.144), channel_id=1, source_target_pairs={{0,4},{1,5},{2,6},{3,7},{4,0},{5,1},{6,2},{7,3},{8,12},{9,13},{10,... | collective-permute-start | bytes 663560 | tf_op jit(solution)/shard_map/ppermute | solution.py:594
  17.9 119.2 %all-gather.4.cloned.1.call-start = ((), (), s32[]{:S(2)}) async-start(), calls=%async_computation.1 | async-start | bytes 1990656 | tf_op jit(solution)/shard_map/all_gather | solution.py:666
  20.4 5.2 %collective-permute-start.1 = (bf16[2,96,384]{2,1,0:T(8,128)(2,1)S(1)}, bf16[2,96,384]{2,1,0:T(8,128)(2,1)S(1)}, u32[]{:S(2)}, u32[]{:S(2)}) collective-permute-start(bf16[2,96,384]{2,1,0:T(8,128)(2,1)S(1)} %pad_maximum_fusion.12), channel_id=1, source_target_pairs={{0,8},{1,9},{2,10},{3,11},{4,12},{5,13},{6,14},{7,15},{8,0},{9,1},... | collective-permute-start | bytes 442376 | tf_op jit(solution)/shard_map/ppermute | solution.py:594
  25.9 12.2 %collective-permute-start.3 = (f32[2,16,576]{2,1,0:T(8,128)S(1)}, f32[2,16,576]{2,1,0:T(8,128)S(1)}, u32[]{:S(2)}, u32[]{:S(2)}) collective-permute-start(f32[2,16,576]{2,1,0:T(8,128)S(1)} %dynamic-slice_bitcast_fusion), channel_id=1, source_target_pairs={{0,16},{1,17},{2,18},{3,19},{4,20},{5,21},{6,22},{7,23},{8,24},{9,... | collective-permute-start | bytes 221192 | tf_op jit(solution)/shard_map/ppermute | solution.py:594
  38.2 5.6 %collective-permute-start.4 = (f32[2,16,576]{2,1,0:T(8,128)S(1)}, f32[2,16,576]{2,1,0:T(8,128)S(1)}, u32[]{:S(2)}, u32[]{:S(2)}) collective-permute-start(f32[2,16,576]{2,1,0:T(8,128)S(1)} %fusion.10), channel_id=1, source_target_pairs={{0,8},{1,9},{2,10},{3,11},{4,12},{5,13},{6,14},{7,15},{8,0},{9,1},... | collective-permute-start | bytes 221192 | tf_op jit(solution)/shard_map/ppermute | solution.py:594
  38.3 7.3 %collective-permute-start.5 = (bf16[2,2,96,384]{3,2,1,0:T(8,128)(2,1)S(1)}, bf16[2,2,96,384]{3,2,1,0:T(8,128)(2,1)S(1)}, u32[]{:S(2)}, u32[]{:S(2)}) collective-permute-start(bf16[2,2,96,384]{3,2,1,0:T(8,128)(2,1)S(1)} %pad_maximum_fusion.3), channel_id=1, source_target_pairs={{0,4},{1,5},{2,6},{3,7},{4,0},{5,1},{6,2},{7,3},{8,12},{9,13},{10,... | collective-permute-start | bytes 884744 | tf_op jit(solution)/shard_map/ppermute | solution.py:594
  46.7 2.4 %collective-permute-start.6 = (bf16[8,88,384]{2,0,1:T(8,128)(2,1)S(1)}, bf16[8,88,384]{2,0,1:T(8,128)(2,1)S(1)}, u32[]{:S(2)}, u32[]{:S(2)}) collective-permute-start(bf16[8,88,384]{2,0,1:T(8,128)(2,1)S(1)} %slice.89), channel_id=1, source_target_pairs={{0,1},{1,0},{2,3},{3,2},{4,5},{5,4},{6,7},{7,6},{8,9},{9,8},{10,11... | collective-permute-start | bytes 1622024 | tf_op jit(solution)/shard_map/ppermute | solution.py:594
  46.8 27.9 %copy-start.14 = (f32[8,384]{1,0:T(8,128)}, f32[8,384]{1,0:T(8,128)S(1)}, u32[]{:S(2)}) copy-start(f32[8,384]{1,0:T(8,128)S(1)} %fusion.28.biases_ref) | copy-start | bytes 36868
  49.2 25.5 %collective-permute-start.7 = (bf16[2,8,16,384]{3,1,2,0:T(8,128)(2,1)S(1)}, bf16[2,8,16,384]{3,1,2,0:T(8,128)(2,1)S(1)}, u32[]{:S(2)}, u32[]{:S(2)}) collective-permute-start(bf16[2,8,16,384]{3,1,2,0:T(8,128)(2,1)S(1)} %pad_maximum_fusion.6), channel_id=1, source_target_pairs={{0,2},{1,3},{2,0},{3,1},{4,6},{5,7},{6,4},{7,5},{8,10},{9,11},{10,... | collective-permute-start | bytes 589832 | tf_op jit(solution)/shard_map/ppermute | solution.py:594
  137.1 3.3 %collective-permute-start.8 = (bf16[8,216,384]{2,1,0:T(8,128)(2,1)}, bf16[8,216,384]{2,1,0:T(8,128)(2,1)S(1)}, u32[]{:S(2)}, u32[]{:S(2)}) collective-permute-start(bf16[8,216,384]{2,1,0:T(8,128)(2,1)} %get-tuple-element.64), channel_id=1, source_target_pairs={{0,1},{1,0},{2,3},{3,2},{4,5},{5,4},{6,7},{7,6},{8,9},{9,8},{10,11... | collective-permute-start | bytes 3981320 | tf_op jit(solution)/shard_map/ppermute | solution.py:594
  143.2 37.9 %all-to-all-start = ((bf16[8,216,384]{2,1,0:T(8,128)(2,1)}), bf16[8,216,384]{2,1,0:T(8,128)(2,1)S(1)}, u32[]{:S(2)}, u32[]{:S(2)}) async-start(bf16[8,216,384]{2,1,0:T(8,128)(2,1)} %add_convert_fusion), calls=%async_computation | async-start | bytes 2654208 | tf_op jit(solution)/shard_map/all_to_all | solution.py:786
  147.7 33.5 %copy-start.5 = (f32[1536,128]{1,0:T(8,128)S(1)}, f32[1536,128]{1,0:T(8,128)}, u32[]{:S(2)}) copy-start(f32[1536,128]{1,0:T(8,128)} %get-tuple-element.77) | copy-start | bytes 2359300
  147.7 33.8 %copy-start.16 = (f32[1,384]{1,0:T(1,128)S(1)}, f32[1,384]{1,0:T(1,128)}, u32[]{:S(2)}) copy-start(f32[1,384]{1,0:T(1,128)} %get-tuple-element.76) | copy-start | bytes 4612
  147.7 33.9 %copy-start.15 = (f32[1,384]{1,0:T(1,128)S(1)}, f32[1,384]{1,0:T(1,128)}, u32[]{:S(2)}) copy-start(f32[1,384]{1,0:T(1,128)} %get-tuple-element.78) | copy-start | bytes 4612
  147.7 35.5 %copy-start.10 = (f32[16,4,384]{2,1,0:T(4,128)S(1)}, f32[16,4,384]{2,1,0:T(4,128)}, u32[]{:S(2)}) copy-start(f32[16,4,384]{2,1,0:T(4,128)} %get-tuple-element.70) | copy-start | bytes 294916
  181.1 3.2 %collective-permute-start.9 = (bf16[8,80,384]{2,1,0:T(8,128)(2,1)}, bf16[8,80,384]{2,1,0:T(8,128)(2,1)S(1)}, u32[]{:S(2)}, u32[]{:S(2)}) collective-permute-start(bf16[8,80,384]{2,1,0:T(8,128)(2,1)} %get-tuple-element.74), channel_id=1, source_target_pairs={{0,1},{1,0},{2,3},{3,2},{4,5},{5,4},{6,7},{7,6},{8,9},{9,8},{10,11... | collective-permute-start | bytes 1474568 | tf_op jit(solution)/shard_map/ppermute | solution.py:594
  184.5 9.7 %collective-permute-start.10 = (bf16[2,2,96,384]{3,2,0,1:T(8,128)(2,1)S(1)}, bf16[2,2,96,384]{3,2,0,1:T(8,128)(2,1)S(1)}, u32[]{:S(2)}, u32[]{:S(2)}) collective-permute-start(bf16[2,2,96,384]{3,2,0,1:T(8,128)(2,1)S(1)} %pad_maximum_fusion.5), channel_id=1, source_target_pairs={{0,4},{1,5},{2,6},{3,7},{4,0},{5,1},{6,2},{7,3},{8,12},{9,13},{10,... | collective-permute-start | bytes 884744 | tf_op jit(solution)/shard_map/ppermute | solution.py:594
  194.5 6.2 %collective-permute-start.11 = (bf16[2,112,384]{2,1,0:T(8,128)(2,1)S(1)}, bf16[2,112,384]{2,1,0:T(8,128)(2,1)S(1)}, u32[]{:S(2)}, u32[]{:S(2)}) collective-permute-start(bf16[2,112,384]{2,1,0:T(8,128)(2,1)S(1)} %pad_maximum_fusion.9), channel_id=1, source_target_pairs={{0,8},{1,9},{2,10},{3,11},{4,12},{5,13},{6,14},{7,15},{8,0},{9,1},... | collective-permute-start | bytes 516104 | tf_op jit(solution)/shard_map/ppermute | solution.py:594
  201.5 7.7 %collective-permute-start.12 = (bf16[144,384]{1,0:T(8,128)(2,1)}, bf16[144,384]{1,0:T(8,128)(2,1)}, u32[]{:S(2)}, u32[]{:S(2)}) collective-permute-start(bf16[144,384]{1,0:T(8,128)(2,1)} %pad_maximum_fusion.13), channel_id=1, source_target_pairs={{0,16},{1,17},{2,18},{3,19},{4,20},{5,21},{6,22},{7,23},{8,24},{9,... | collective-permute-start | bytes 331784 | tf_op jit(solution)/shard_map/ppermute | solution.py:594
  204.3 7.9 %collective-permute-start.14 = (bf16[216,384]{1,0:T(8,128)(2,1)S(1)}, bf16[216,384]{1,0:T(8,128)(2,1)S(1)}, u32[]{:S(2)}, u32[]{:S(2)}) collective-permute-start(bf16[216,384]{1,0:T(8,128)(2,1)S(1)} %reduce_sum.12), channel_id=1, source_target_pairs={{0,2},{1,3},{2,0},{3,1},{4,6},{5,7},{6,4},{7,5},{8,10},{9,11},{10,... | collective-permute-start | bytes 497672 | tf_op jit(solution)/shard_map/ppermute | solution.py:594
  211.8 5.3 %collective-permute-start.13 = (bf16[208,384]{1,0:T(8,128)(2,1)S(1)}, bf16[208,384]{1,0:T(8,128)(2,1)S(1)}, u32[]{:S(2)}, u32[]{:S(2)}) collective-permute-start(bf16[208,384]{1,0:T(8,128)(2,1)S(1)} %pad_maximum_fusion.11), channel_id=1, source_target_pairs={{0,2},{1,3},{2,0},{3,1},{4,6},{5,7},{6,4},{7,5},{8,10},{9,11},{10,... | collective-permute-start | bytes 479240 | tf_op jit(solution)/shard_map/ppermute | solution.py:594
  217.3 1.8 collective-permute-start.15
  (12 other events, 91.8 us)
Sparse Core Ops, SparseCore 0:
  18.0 57.6 all-gather.5
  77.9 44.5 all-gather.3

commit v10 on v9

--- a/solution.py
+++ b/solution.py
@@ -61,6 +61,16 @@
     low = head * HEAD_DIM
     pair = low - low % (2 * HEAD_DIM)
     return slice(low, low + HEAD_DIM), slice(pair, pair + 2 * HEAD_DIM), low == pair
+
+
+def interleave(first, second):
+    done = 0
+    for place, call in enumerate(first):
+        call()
+        until = (place + 1) * len(second) // len(first)
+        for other in second[done:until]:
+            other()
+        done = until
 
 
 def in_groups(items, size):
@@ -97,18 +107,39 @@
             weight_ref[low + half_rows : low + 2 * half_rows, :] = jnp.where(first, came, mine)
         bias_ref[...] = jnp.broadcast_to(bias_row_ref[...], (128, 3 * width)).T
 
-    for latent in range(latents):
-        for rows in strips(length, STRIP):
-            normal, _ = normalise(tokens_ref[latent, rows, :].astype(F32))
-            normed = normal * (1.0 + mod_ref[latent, 1:2, :]) + mod_ref[latent, 0:1, :]
-            normed_ref[latent, rows, :] = normed.astype(BF16)
-    normed = normed_ref[...].reshape(latents * length, width)
-    for part in strips(3 * width, 2 * HEAD_DIM):
+
+    def norm(latent, rows):
+        normal, _ = normalise(tokens_ref[latent, rows, :].astype(F32))
+        normed = normal * (1.0 + mod_ref[latent, 1:2, :]) + mod_ref[latent, 0:1, :]
+        normed_ref[latent, rows, :] = normed.astype(BF16)
+
+    def project(batch, part):
+        normed = normed_ref[batch, :, :].reshape(-1, width)
         bias = bias_ref[part, :]
-        qkv = dot_nt(weight_ref[part, :], normed) + beside(*([bias] * (latents * length // 128)))
+        qkv = dot_nt(weight_ref[part, :], normed) + beside(*([bias] * (normed.shape[0] // 128)))
         qkv = qkv.astype(BF16)
-        for latent in range(latents):
-            qkv_ref[latent, part, :] = qkv[:, latent * length : (latent + 1) * length]
+        for place, latent in enumerate(range(batch.start, batch.stop)):
+            qkv_ref[latent, part, :] = qkv[:, place * length : (place + 1) * length]
+
+    def norms(batch):
+        return [
+            functools.partial(norm, latent, rows)
+            for latent in range(batch.start, batch.stop)
+            for rows in strips(length, STRIP)
+        ]
+
+    def projections(batch):
+        return [
+            functools.partial(project, batch, part) for part in strips(3 * width, width)
+        ]
+
+    batches = strips(latents, 2)
+    for call in norms(batches[0]):
+        call()
+    for batch, later in zip(batches[:-1], batches[1:]):
+        interleave(projections(batch), norms(later))
+    for call in projections(batches[-1]):
+        call()
     keys_all = [qkv_ref[latent, width : 2 * width, :].T for latent in range(latents)]
 
     def scores_of(latent, head):
@@ -292,9 +323,17 @@
     feed_wide = dot_nn(down_weight_ref[...], active_all[...])
     grad_normed_wide = dot_nn(up_back[...], grad_hidden_all[...])
     ones = jnp.ones((tokens_all, 128), BF16)
-    up_acc[...] += dot_nn(grad_hidden_all[...], beside(normed_all, ones))
-    down_acc[...] += dot_nn(active_all[...], grad_feed_all)
-
+    normed_ones = beside(normed_all, ones)
+
+    def up_product(part):
+        up_acc[part, :] += dot_nn(grad_hidden_all[part, :], normed_ones)
+
+    def down_product(part):
+        down_acc[part, :] += dot_nn(active_all[part, :], grad_feed_all)
+
+    products_left = [functools.partial(up_product, part) for part in strips(hidden_width, chunk)]
+    products_left += [functools.partial(down_product, part) for part in strips(hidden_width, chunk)]
+    share = -(-len(products_left) // latents)
     grad_branch_parts = []
     out_sum = jnp.zeros((1, width), F32)
     for latent in range(latents):
@@ -305,7 +344,10 @@
         feed_tall = feed_wide[:, here].T
         grad_normed_tall = grad_normed_wide[:, here].T
         sums = [jnp.zeros((1, width), F32) for _ in range(4)]
-        for rows in strips(length, STRIP):
+        branch_parts = []
+        out_sums = []
+
+        def finish_rows(rows):
             there = slice(here.start + rows.start, here.start + rows.stop)
             feed = feed_tall[rows] + down_bias_ref[...]
             grad_normed = grad_normed_tall[rows]
@@ -317,7 +359,7 @@
             )
             grad_middle_ref[latent, rows, :] = grad_middle
             grad_branch = (grad_middle * gate_one).astype(BF16)
-            grad_branch_parts.append(grad_branch)
+            branch_parts.append(grad_branch)
             terms = (
                 grad_middle * branch_all[there, :],
                 grad_normed,
@@ -326,7 +368,15 @@
             )
             for place, term in enumerate(terms):
                 sums[place] += jnp.sum(term, axis=0, keepdims=True)
-            out_sum += jnp.sum(grad_branch.astype(F32), axis=0, keepdims=True)
+            out_sums.append(jnp.sum(grad_branch.astype(F32), axis=0, keepdims=True))
+
+        interleave(
+            [functools.partial(finish_rows, rows) for rows in strips(length, STRIP)],
+            products_left[latent * share : (latent + 1) * share],
+        )
+        grad_branch_parts += branch_parts
+        for value in out_sums:
+            out_sum += value
         grad_mod_ref[latent] = above(*sums)
     bias_acc[1:2, :] += out_sum
     grad_branch_all = above(*grad_branch_parts)
@@ -362,7 +412,7 @@
                     ].astype(BF16)
 
             by_side(core_ref, side, late_kept_ref, late_sent_ref, write)
-        up_bias_grad_ref[...] = up_acc[:, width:]
+        up_bias_grad_ref[...] = up_acc[:, width:].T[0:1, :]
         down_bias_grad_ref[...] = bias_acc[0:1, :]
         out_bias_grad_ref[...] = bias_acc[1:2, :]
 
@@ -454,22 +504,33 @@
     grad_qkv = beside(*[grad_qkv_ref[latent] for latent in range(latents)])
     normed = normed_ref[...].reshape(latents * length, width)
     grad_normed_wide = dot_nn(weight_back[...], grad_qkv)
-    acc[...] += dot_nn(grad_qkv, beside(normed, jnp.ones((latents * length, 128), BF16)))
+    normed_ones = beside(normed, jnp.ones((latents * length, 128), BF16))
+
+    def product(part):
+        acc[part, :] += dot_nn(grad_qkv[part, :], normed_ones)
+
+    products_left = [functools.partial(product, part) for part in strips(3 * width, 3 * width // 2)]
+    share = -(-len(products_left) // latents)
     for latent in range(latents):
         grad_normed_tall = grad_normed_wide[:, latent * length : (latent + 1) * length].T
         scale_one = 1.0 + mod_ref[latent, 1:2, :]
-        first = jnp.zeros((1, width), F32)
-        second = jnp.zeros((1, width), F32)
-        for rows in strips(length, STRIP):
+        sums = [jnp.zeros((1, width), F32) for _ in range(2)]
+
+        def finish_rows(rows):
             normal, inverse = normalise(tokens_ref[latent, rows, :].astype(F32))
             grad_normed = grad_normed_tall[rows]
-            first += jnp.sum(grad_normed, axis=0, keepdims=True)
-            second += jnp.sum(grad_normed * normal, axis=0, keepdims=True)
+            sums[0] += jnp.sum(grad_normed, axis=0, keepdims=True)
+            sums[1] += jnp.sum(grad_normed * normal, axis=0, keepdims=True)
             back = normalise_back(grad_normed * scale_one, normal, inverse)
             tokens_grad_ref[latent, rows, :] = (grad_middle_ref[latent, rows, :] + back).astype(
                 BF16
             )
-        grad_mod_ref[latent] = above(first, second)
+
+        interleave(
+            [functools.partial(finish_rows, rows) for rows in strips(length, STRIP)],
+            products_left[latent * share : (latent + 1) * share],
+        )
+        grad_mod_ref[latent] = above(*sums)
 
     @pl.when(step == pl.num_programs(0) - 1)
     def _():
@@ -485,7 +546,7 @@
                     ref[owner] = above(rows, rest).astype(BF16)
 
             by_side(core_ref, side, kept_ref, sent_ref, write)
-        bias_grad_ref[...] = acc[:, width:]
+        bias_grad_ref[...] = acc[:, width:].T[0:1, :]
 
 
 def finish_kernel(
@@ -734,7 +795,7 @@
         up_bias_grad,
         down_bias_grad,
     ) = run_kernel(
-        functools.partial(feed_kernel, chunk=256),
+        functools.partial(feed_kernel, chunk=768),
         4,
         [
             shape_of((latents, length, width), BF16),
@@ -746,7 +807,7 @@
             shape_of((n_dp, late.shape[1] // 2, width), BF16),
             shape_of((n_dp, late.shape[1] // 2, width), BF16),
             shape_of((1, width), F32),
-            shape_of((hidden_width, 128), F32),
+            shape_of((1, hidden_width), F32),
             shape_of((1, width), F32),
         ],
         [
@@ -794,7 +855,7 @@
         [
             shape_of((n_dp, tail_rows, width), BF16),
             shape_of((n_dp, tail_rows, width), BF16),
-            shape_of((3 * width, 128), F32),
+            shape_of((1, 3 * width), F32),
         ],
         [
             pltpu.VMEM((3 * width, width + 128), F32),
@@ -812,12 +873,12 @@
         late_sum = late_sum.astype(F32) + hops.swap(late_sum, "rep", bit).astype(F32)
         late_sum = late_sum.astype(BF16)
 
-    qkv_columns = qkv_bias_grad[:, 0]
+    qkv_columns = qkv_bias_grad[0]
     bias_blocks = jnp.concatenate(
         [
             jnp.concatenate([qkv_columns[:width], qkv_columns[2 * width :]]).reshape(n_dp, -1),
             out_bias_grad.reshape(n_dp, -1),
-            up_bias_grad[:, 0].reshape(n_dp, -1),
+            up_bias_grad.reshape(n_dp, -1),
             down_bias_grad.reshape(n_dp, -1),
         ],
         axis=1,

time: 231 us -> 230 us (level)
  Pallas kernels: 120 us -> 115 us
    pallas_call x3, Pallas kernels: 117 us -> 112 us  [run_kernel(): pl.pallas_call(kernel, grid=(streamed[0].shape[0] // count,), in_specs=[p...]
    all_gather x1, waiting for transfers between devices: 0.97 us -> 4.78 us  [body(): late = lax.all_gather(late_shard, 'dp', axis=0)]
    ppermute x16, waiting for transfers between devices: 46 us -> 43.3 us  [swap(): return lax.ppermute(value, AXES, pairs)]
  transfers between devices with their start and end apart: 19 -> 19, of which waited for: 13 -> 13; matrix products, arithmetic and copies ran while one was open for 6% -> 6% of each run, Pallas kernels for 51% -> 49%
where the time goes in v10:
time: 230 us; the launch traced here: 229 us
  Pallas kernels  115 us (50%)
  waiting for transfers between devices  48.2 us (21%)
  starting transfers between devices  26 us (11%)
  between operations  14.9 us (6%)
  other arithmetic  14.3 us (6%)
  local copies, waits for them, and re-layouts  8.72 us (4%)
    pallas_call x3, Pallas kernels, run_kernel(): pl.pallas_call(kernel, grid=(streamed[0].shape[0] // count,), in_specs=[p...  112 us
    ppermute x16, waiting for transfers between devices, swap(): return lax.ppermute(value, AXES, pairs)  43.3 us
    ppermute x16, starting transfers between devices, swap(): return lax.ppermute(value, AXES, pairs)  22.3 us
    all_gather x1, waiting for transfers between devices, body(): late = lax.all_gather(late_shard, 'dp', axis=0)  4.78 us
  transfers between devices with their start and end apart: 19, of which 13 were waited for; matrix products, arithmetic and copies ran while one was open for 6% of the time, Pallas kernels for 49%

profile of v10, /device:TPU:0, one launch (start us, length us, event | category | flops | bytes accessed | tf_op | source)
XLA Modules:
  0.0 228.9 jit_solution(17004331286004370429)
XLA Ops:
  10.6 1.7 pad_maximum_fusion.4
  12.3 4.1 %collective-permute-start = (bf16[96,384]{1,0:T(8,128)(2,1)S(1)}, bf16[96,384]{1,0:T(8,128)(2,1)S(1)}, u32[]{:S(2)}, u32[]{:S(2)}) collective-permute-start(bf16[96,384]{1,0:T(8,128)(2,1)S(1)} %fusion.15), channel_id=1, source_target_pairs={{0,16},{1,17},{2,18},{3,19},{4,20},{5,21},{6,22},{7,23},{8,24},{9,... | collective-permute-start | bytes 221192 | tf_op jit(solution)/shard_map/ppermute | solution.py:655
  18.1 2.3 collective-permute-done
  21.1 2.4 %collective-permute-done.2 = bf16[288,384]{1,0:T(8,128)(2,1)S(1)} collective-permute-done((bf16[288,384]{1,0:T(8,128)(2,1)}, bf16[288,384]{1,0:T(8,128)(2,1)S(1)}, u32[]{:S(2)}, u32[]{:S(2)}) %collective-permute-start.2) | collective-permute-done | bytes 221216 | tf_op jit(solution)/shard_map/ppermute | solution.py:655
  23.6 2.0 collective-permute-done.1
  25.9 2.7 %collective-permute-start.3 = (f32[2,16,576]{2,1,0:T(8,128)S(1)}, f32[2,16,576]{2,1,0:T(8,128)S(1)}, u32[]{:S(2)}, u32[]{:S(2)}) collective-permute-start(f32[2,16,576]{2,1,0:T(8,128)S(1)} %dynamic-slice_bitcast_fusion), channel_id=1, source_target_pairs={{0,16},{1,17},{2,18},{3,19},{4,20},{5,21},{6,22},{7,23},{8,24},{9,... | collective-permute-start | bytes 221192 | tf_op jit(solution)/shard_map/ppermute | solution.py:655
  28.7 9.5 %collective-permute-done.3 = f32[2,16,576]{2,1,0:T(8,128)S(1)} collective-permute-done((f32[2,16,576]{2,1,0:T(8,128)S(1)}, f32[2,16,576]{2,1,0:T(8,128)S(1)}, u32[]{:S(2)}, u32[]{:S(2)}) %collective-permute-start.3) | collective-permute-done | bytes 73760 | tf_op jit(solution)/shard_map/ppermute | solution.py:655
  38.3 1.8 collective-permute-start.5
  40.2 3.6 %collective-permute-done.4 = f32[2,16,576]{2,1,0:T(8,128)S(1)} collective-permute-done((f32[2,16,576]{2,1,0:T(8,128)S(1)}, f32[2,16,576]{2,1,0:T(8,128)S(1)}, u32[]{:S(2)}, u32[]{:S(2)}) %collective-permute-start.4) | collective-permute-done | bytes 73760 | tf_op jit(solution)/shard_map/ppermute | solution.py:655
  51.5 19.3 %shard_map.228 = (bf16[16,256,384]{2,1,0:T(8,128)(2,1)}, bf16[16,1152,256]{2,1,0:T(8,128)(2,1)}, f32[16,8,256]{2,1,0:T(8,128)}, bf16[16,384,256]{2,1,0:T(8,128)(2,1)}, bf16[1152,384]{1,0:T(8,128)(2,1)}) custom-call(s32[1]{0:T(128)} %bitcast.core_ref, bf16[16,256,384]{2,1,0:T(8,128)(2,1)} %tokens_ref.5, f32[16,6,384]{2,1,0:T(8,128)} %broadcast_add_fusion.mod_ref, ...), custom_call_target="tpu_custom_call" | custom-call | flops 5234491392 | bytes 18874368 | tf_op jit(solution)/shard_map/pallas_call | solution.py:612
  71.0 4.8 %all-gather.6.cloned.1.call-done = bf16[3456,384]{1,0:T(8,128)(2,1)} async-done(((bf16[432,384]{1,0:T(8,128)(2,1)}), bf16[3456,384]{1,0:T(8,128)(2,1)}) %all-gather.6.cloned.1.call-update) | async-done | bytes 2654224 | tf_op jit(solution)/shard_map/all_gather | solution.py:725
  76.6 60.1 %shard_map.229 = (bf16[16,256,384]{2,1,0:T(8,128)(2,1)}, f32[16,256,384]{2,1,0:T(8,128)}, bf16[16,384,256]{2,1,0:T(8,128)(2,1)}, f32[16,4,384]{2,1,0:T(4,128)}, ...) custom-call(s32[1]{0:T(128)} %bitcast.core_ref, ...), custom_call_target="tpu_custom_call" | custom-call | flops 32614907904 | bytes 22020096 | tf_op jit(solution)/shard_map/pallas_call | solution.py:612
  136.8 3.3 %collective-permute-done.8 = bf16[8,216,384]{2,1,0:T(8,128)(2,1)S(1)} collective-permute-done((bf16[8,216,384]{2,1,0:T(8,128)(2,1)}, bf16[8,216,384]{2,1,0:T(8,128)(2,1)S(1)}, u32[]{:S(2)}, u32[]{:S(2)}) %collective-permute-start.8) | collective-permute-done | bytes 1327136 | tf_op jit(solution)/shard_map/ppermute | solution.py:655
  140.1 2.8 %add_convert_fusion = bf16[8,216,384]{2,1,0:T(8,128)(2,1)} fusion(bf16[8,216,384]{2,1,0:T(8,128)(2,1)S(1)} %collective-permute-done.8, bf16[8,216,384]{2,1,0:T(8,128)(2,1)} %get-tuple-element.61), kind=kLoop, calls=%fused_computation | loop fusion | flops 2654208 | bytes 3981312 | tf_op jit(solution)/shard_map/convert_element_type | solution.py:846
  142.8 3.6 %all-to-all-start = ((bf16[8,216,384]{2,1,0:T(8,128)(2,1)}), bf16[8,216,384]{2,1,0:T(8,128)(2,1)S(1)}, u32[]{:S(2)}, u32[]{:S(2)}) async-start(bf16[8,216,384]{2,1,0:T(8,128)(2,1)} %add_convert_fusion), calls=%async_computation | async-start | bytes 2654208 | tf_op jit(solution)/shard_map/all_to_all | solution.py:847
  146.4 33.1 %shard_map.230 = (bf16[16,256,384]{2,1,0:T(8,128)(2,1)}, f32[16,2,384]{2,1,0:T(2,128)}, bf16[8,80,384]{2,1,0:T(8,128)(2,1)}, bf16[8,80,384]{2,1,0:T(8,128)(2,1)}, f32[1,1152]{1,0:T(1,128)}) custom-call(s32[1]{0:T(128)} %bitcast.core_ref, bf16[16,1152,256]{2,1,0:T(8,128)(2,1)} %get-tuple-element.57.qkv_ref, f32[16,8,256]{2,1,0:T(8,128)} %get-tuple-element.58.lse_ref, ...), custom_call_target="tpu_custom_call" | custom-call | flops 1 | bytes 1 | tf_op jit(solution)/shard_map/pallas_call | solution.py:612
  183.4 1.9 collective-permute-start.10
  185.3 7.6 %collective-permute-done.10 = bf16[2,2,96,384]{3,2,0,1:T(8,128)(2,1)S(1)} collective-permute-done((bf16[2,2,96,384]{3,2,0,1:T(8,128)(2,1)S(1)}, bf16[2,2,96,384]{3,2,0,1:T(8,128)(2,1)S(1)}, u32[]{:S(2)}, u32[]{:S(2)}) %collective-permute-start.10) | collective-permute-done | bytes 294944 | tf_op jit(solution)/shard_map/ppermute | solution.py:655
  193.1 1.8 collective-permute-start.11
  194.9 4.2 %collective-permute-done.11 = bf16[2,112,384]{2,1,0:T(8,128)(2,1)S(1)} collective-permute-done((bf16[2,112,384]{2,1,0:T(8,128)(2,1)S(1)}, bf16[2,112,384]{2,1,0:T(8,128)(2,1)S(1)}, u32[]{:S(2)}, u32[]{:S(2)}) %collective-permute-start.11) | collective-permute-done | bytes 172064 | tf_op jit(solution)/shard_map/ppermute | solution.py:655
  200.0 2.7 %collective-permute-start.12 = (bf16[144,384]{1,0:T(8,128)(2,1)}, bf16[144,384]{1,0:T(8,128)(2,1)}, u32[]{:S(2)}, u32[]{:S(2)}) collective-permute-start(bf16[144,384]{1,0:T(8,128)(2,1)} %pad_maximum_fusion.13), channel_id=1, source_target_pairs={{0,16},{1,17},{2,18},{3,19},{4,20},{5,21},{6,22},{7,23},{8,24},{9,... | collective-permute-start | bytes 331784 | tf_op jit(solution)/shard_map/ppermute | solution.py:655
  204.5 3.0 %collective-permute-done.12 = bf16[144,384]{1,0:T(8,128)(2,1)} collective-permute-done((bf16[144,384]{1,0:T(8,128)(2,1)}, bf16[144,384]{1,0:T(8,128)(2,1)}, u32[]{:S(2)}, u32[]{:S(2)}) %collective-permute-start.12) | collective-permute-done | bytes 110624 | tf_op jit(solution)/shard_map/ppermute | solution.py:655
  211.6 3.7 %collective-permute-done.13 = bf16[208,384]{1,0:T(8,128)(2,1)S(1)} collective-permute-done((bf16[208,384]{1,0:T(8,128)(2,1)S(1)}, bf16[208,384]{1,0:T(8,128)(2,1)S(1)}, u32[]{:S(2)}, u32[]{:S(2)}) %collective-permute-start.13) | collective-permute-done | bytes 159776 | tf_op jit(solution)/shard_map/ppermute | solution.py:655
  218.1 2.7 %shard_map.231 = (f32[288,384]{1,0:T(8,128)}, f32[1,288]{1,0:T(1,128)}, f32[144,384]{1,0:T(8,128)}, f32[192,384]{1,0:T(8,128)}, f32[48,1536]{1,0:T(8,128)}, /*in...) custom-call(s32[1]{0:T(128)} %bitcast.core_ref, ...), custom_call_target="tpu_custom_call" | custom-call | tf_op jit(solution)/shard_map/pallas_call | solution.py:929
  (151 shorter events, 29.4 us)
Async XLA Ops:
  7.2 68.6 %all-gather.6.cloned.1.call-start = ((), (), s32[]{:S(2)}) async-start(), calls=%async_computation.2 | async-start | bytes 2985984 | tf_op jit(solution)/shard_map/all_gather | solution.py:725
  12.3 8.0 %collective-permute-start = (bf16[96,384]{1,0:T(8,128)(2,1)S(1)}, bf16[96,384]{1,0:T(8,128)(2,1)S(1)}, u32[]{:S(2)}, u32[]{:S(2)}) collective-permute-start(bf16[96,384]{1,0:T(8,128)(2,1)S(1)} %fusion.15), channel_id=1, source_target_pairs={{0,16},{1,17},{2,18},{3,19},{4,20},{5,21},{6,22},{7,23},{8,24},{9,... | collective-permute-start | bytes 221192 | tf_op jit(solution)/shard_map/ppermute | solution.py:655
  16.4 7.1 %collective-permute-start.2 = (bf16[288,384]{1,0:T(8,128)(2,1)}, bf16[288,384]{1,0:T(8,128)(2,1)S(1)}, u32[]{:S(2)}, u32[]{:S(2)}) collective-permute-start(bf16[288,384]{1,0:T(8,128)(2,1)} %bitcast.144), channel_id=1, source_target_pairs={{0,4},{1,5},{2,6},{3,7},{4,0},{5,1},{6,2},{7,3},{8,12},{9,13},{10,... | collective-permute-start | bytes 663560 | tf_op jit(solution)/shard_map/ppermute | solution.py:655
  17.9 118.8 %all-gather.4.cloned.1.call-start = ((), (), s32[]{:S(2)}) async-start(), calls=%async_computation.1 | async-start | bytes 1990656 | tf_op jit(solution)/shard_map/all_gather | solution.py:727
  20.4 5.2 %collective-permute-start.1 = (bf16[2,96,384]{2,1,0:T(8,128)(2,1)S(1)}, bf16[2,96,384]{2,1,0:T(8,128)(2,1)S(1)}, u32[]{:S(2)}, u32[]{:S(2)}) collective-permute-start(bf16[2,96,384]{2,1,0:T(8,128)(2,1)S(1)} %pad_maximum_fusion.12), channel_id=1, source_target_pairs={{0,8},{1,9},{2,10},{3,11},{4,12},{5,13},{6,14},{7,15},{8,0},{9,1},... | collective-permute-start | bytes 442376 | tf_op jit(solution)/shard_map/ppermute | solution.py:655
  25.9 12.2 %collective-permute-start.3 = (f32[2,16,576]{2,1,0:T(8,128)S(1)}, f32[2,16,576]{2,1,0:T(8,128)S(1)}, u32[]{:S(2)}, u32[]{:S(2)}) collective-permute-start(f32[2,16,576]{2,1,0:T(8,128)S(1)} %dynamic-slice_bitcast_fusion), channel_id=1, source_target_pairs={{0,16},{1,17},{2,18},{3,19},{4,20},{5,21},{6,22},{7,23},{8,24},{9,... | collective-permute-start | bytes 221192 | tf_op jit(solution)/shard_map/ppermute | solution.py:655
  38.2 5.6 %collective-permute-start.4 = (f32[2,16,576]{2,1,0:T(8,128)S(1)}, f32[2,16,576]{2,1,0:T(8,128)S(1)}, u32[]{:S(2)}, u32[]{:S(2)}) collective-permute-start(f32[2,16,576]{2,1,0:T(8,128)S(1)} %fusion.10), channel_id=1, source_target_pairs={{0,8},{1,9},{2,10},{3,11},{4,12},{5,13},{6,14},{7,15},{8,0},{9,1},... | collective-permute-start | bytes 221192 | tf_op jit(solution)/shard_map/ppermute | solution.py:655
  38.3 7.3 %collective-permute-start.5 = (bf16[2,2,96,384]{3,2,1,0:T(8,128)(2,1)S(1)}, bf16[2,2,96,384]{3,2,1,0:T(8,128)(2,1)S(1)}, u32[]{:S(2)}, u32[]{:S(2)}) collective-permute-start(bf16[2,2,96,384]{3,2,1,0:T(8,128)(2,1)S(1)} %pad_maximum_fusion.3), channel_id=1, source_target_pairs={{0,4},{1,5},{2,6},{3,7},{4,0},{5,1},{6,2},{7,3},{8,12},{9,13},{10,... | collective-permute-start | bytes 884744 | tf_op jit(solution)/shard_map/ppermute | solution.py:655
  46.7 2.4 %collective-permute-start.6 = (bf16[8,88,384]{2,0,1:T(8,128)(2,1)S(1)}, bf16[8,88,384]{2,0,1:T(8,128)(2,1)S(1)}, u32[]{:S(2)}, u32[]{:S(2)}) collective-permute-start(bf16[8,88,384]{2,0,1:T(8,128)(2,1)S(1)} %slice.82), channel_id=1, source_target_pairs={{0,1},{1,0},{2,3},{3,2},{4,5},{5,4},{6,7},{7,6},{8,9},{9,8},{10,11... | collective-permute-start | bytes 1622024 | tf_op jit(solution)/shard_map/ppermute | solution.py:655
  46.8 24.1 %copy-start.12 = (f32[8,384]{1,0:T(8,128)}, f32[8,384]{1,0:T(8,128)S(1)}, u32[]{:S(2)}) copy-start(f32[8,384]{1,0:T(8,128)S(1)} %fusion.28.biases_ref) | copy-start | bytes 36868
  49.2 21.7 %collective-permute-start.7 = (bf16[2,8,16,384]{3,1,2,0:T(8,128)(2,1)S(1)}, bf16[2,8,16,384]{3,1,2,0:T(8,128)(2,1)S(1)}, u32[]{:S(2)}, u32[]{:S(2)}) collective-permute-start(bf16[2,8,16,384]{3,1,2,0:T(8,128)(2,1)S(1)} %pad_maximum_fusion.6), channel_id=1, source_target_pairs={{0,2},{1,3},{2,0},{3,1},{4,6},{5,7},{6,4},{7,5},{8,10},{9,11},{10,... | collective-permute-start | bytes 589832 | tf_op jit(solution)/shard_map/ppermute | solution.py:655
  136.7 3.3 %collective-permute-start.8 = (bf16[8,216,384]{2,1,0:T(8,128)(2,1)}, bf16[8,216,384]{2,1,0:T(8,128)(2,1)S(1)}, u32[]{:S(2)}, u32[]{:S(2)}) collective-permute-start(bf16[8,216,384]{2,1,0:T(8,128)(2,1)} %get-tuple-element.64), channel_id=1, source_target_pairs={{0,1},{1,0},{2,3},{3,2},{4,5},{5,4},{6,7},{7,6},{8,9},{9,8},{10,11... | collective-permute-start | bytes 3981320 | tf_op jit(solution)/shard_map/ppermute | solution.py:655
  142.8 36.8 %all-to-all-start = ((bf16[8,216,384]{2,1,0:T(8,128)(2,1)}), bf16[8,216,384]{2,1,0:T(8,128)(2,1)S(1)}, u32[]{:S(2)}, u32[]{:S(2)}) async-start(bf16[8,216,384]{2,1,0:T(8,128)(2,1)} %add_convert_fusion), calls=%async_computation | async-start | bytes 2654208 | tf_op jit(solution)/shard_map/all_to_all | solution.py:847
  146.4 33.4 %copy-start.13 = (f32[1,1536]{1,0:T(1,128)S(1)}, f32[1,1536]{1,0:T(1,128)}, u32[]{:S(2)}) copy-start(f32[1,1536]{1,0:T(1,128)} %get-tuple-element.77) | copy-start | bytes 18436
  146.4 33.5 %copy-start.15 = (f32[1,384]{1,0:T(1,128)S(1)}, f32[1,384]{1,0:T(1,128)}, u32[]{:S(2)}) copy-start(f32[1,384]{1,0:T(1,128)} %get-tuple-element.76) | copy-start | bytes 4612
  146.4 33.6 %copy-start.14 = (f32[1,384]{1,0:T(1,128)S(1)}, f32[1,384]{1,0:T(1,128)}, u32[]{:S(2)}) copy-start(f32[1,384]{1,0:T(1,128)} %get-tuple-element.78) | copy-start | bytes 4612
  146.4 34.6 %copy-start.8 = (f32[16,4,384]{2,1,0:T(4,128)S(1)}, f32[16,4,384]{2,1,0:T(4,128)}, u32[]{:S(2)}) copy-start(f32[16,4,384]{2,1,0:T(4,128)} %get-tuple-element.70) | copy-start | bytes 294916
  179.6 2.6 %collective-permute-start.9 = (bf16[8,80,384]{2,1,0:T(8,128)(2,1)}, bf16[8,80,384]{2,1,0:T(8,128)(2,1)S(1)}, u32[]{:S(2)}, u32[]{:S(2)}) collective-permute-start(bf16[8,80,384]{2,1,0:T(8,128)(2,1)} %get-tuple-element.74), channel_id=1, source_target_pairs={{0,1},{1,0},{2,3},{3,2},{4,5},{5,4},{6,7},{7,6},{8,9},{9,8},{10,11... | collective-permute-start | bytes 1474568 | tf_op jit(solution)/shard_map/ppermute | solution.py:655
  183.4 9.5 %collective-permute-start.10 = (bf16[2,2,96,384]{3,2,0,1:T(8,128)(2,1)S(1)}, bf16[2,2,96,384]{3,2,0,1:T(8,128)(2,1)S(1)}, u32[]{:S(2)}, u32[]{:S(2)}) collective-permute-start(bf16[2,2,96,384]{3,2,0,1:T(8,128)(2,1)S(1)} %pad_maximum_fusion.5), channel_id=1, source_target_pairs={{0,4},{1,5},{2,6},{3,7},{4,0},{5,1},{6,2},{7,3},{8,12},{9,13},{10,... | collective-permute-start | bytes 884744 | tf_op jit(solution)/shard_map/ppermute | solution.py:655
  193.1 6.1 %collective-permute-start.11 = (bf16[2,112,384]{2,1,0:T(8,128)(2,1)S(1)}, bf16[2,112,384]{2,1,0:T(8,128)(2,1)S(1)}, u32[]{:S(2)}, u32[]{:S(2)}) collective-permute-start(bf16[2,112,384]{2,1,0:T(8,128)(2,1)S(1)} %pad_maximum_fusion.9), channel_id=1, source_target_pairs={{0,8},{1,9},{2,10},{3,11},{4,12},{5,13},{6,14},{7,15},{8,0},{9,1},... | collective-permute-start | bytes 516104 | tf_op jit(solution)/shard_map/ppermute | solution.py:655
  200.0 7.5 %collective-permute-start.12 = (bf16[144,384]{1,0:T(8,128)(2,1)}, bf16[144,384]{1,0:T(8,128)(2,1)}, u32[]{:S(2)}, u32[]{:S(2)}) collective-permute-start(bf16[144,384]{1,0:T(8,128)(2,1)} %pad_maximum_fusion.13), channel_id=1, source_target_pairs={{0,16},{1,17},{2,18},{3,19},{4,20},{5,21},{6,22},{7,23},{8,24},{9,... | collective-permute-start | bytes 331784 | tf_op jit(solution)/shard_map/ppermute | solution.py:655
  202.9 8.6 %collective-permute-start.14 = (bf16[216,384]{1,0:T(8,128)(2,1)S(1)}, bf16[216,384]{1,0:T(8,128)(2,1)S(1)}, u32[]{:S(2)}, u32[]{:S(2)}) collective-permute-start(bf16[216,384]{1,0:T(8,128)(2,1)S(1)} %reduce_sum.12), channel_id=1, source_target_pairs={{0,2},{1,3},{2,0},{3,1},{4,6},{5,7},{6,4},{7,5},{8,10},{9,11},{10,... | collective-permute-start | bytes 497672 | tf_op jit(solution)/shard_map/ppermute | solution.py:655
  210.0 5.3 %collective-permute-start.13 = (bf16[208,384]{1,0:T(8,128)(2,1)S(1)}, bf16[208,384]{1,0:T(8,128)(2,1)S(1)}, u32[]{:S(2)}, u32[]{:S(2)}) collective-permute-start(bf16[208,384]{1,0:T(8,128)(2,1)S(1)} %pad_maximum_fusion.11), channel_id=1, source_target_pairs={{0,2},{1,3},{2,0},{3,1},{4,6},{5,7},{6,4},{7,5},{8,10},{9,11},{10,... | collective-permute-start | bytes 479240 | tf_op jit(solution)/shard_map/ppermute | solution.py:655
  215.5 1.8 collective-permute-start.15
  (11 other events, 87.4 us)
Sparse Core Ops, SparseCore 0:
  18.0 57.6 all-gather.5
  77.9 44.4 all-gather.3

commit v11 on v10

--- a/solution.py
+++ b/solution.py
@@ -721,7 +721,6 @@
         ]
     )
     front = pad_rows(front, up_to(front.shape[0], 8))
-    front, late_shard = lax.optimization_barrier((front, late_shard))
     late = lax.all_gather(late_shard, "dp", axis=0)
     ada_shard, _ = lax.optimization_barrier((ada_weight.T, late))
     ada_all = lax.all_gather(ada_shard, "dp", axis=0, tiled=True)

time: 230 us -> 230 us (level)
  waiting for transfers between devices: 48.2 us -> 45.5 us
  starting transfers between devices: 26 us -> 28.5 us
    ppermute x16, waiting for transfers between devices: 43.3 us -> 38.5 us  [swap(): return lax.ppermute(value, AXES, pairs)]
    ppermute x16, starting transfers between devices: 22.3 us -> 24.9 us  [swap(): return lax.ppermute(value, AXES, pairs)]
  transfers between devices with their start and end apart: 19 -> 19, of which waited for: 13 -> 12; matrix products, arithmetic and copies ran while one was open for 6% -> 7% of each run, Pallas kernels for 49% -> 49%
where the time goes in v11:
time: 230 us; the launch traced here: 229 us
  Pallas kernels  115 us (50%)
  waiting for transfers between devices  45.5 us (20%)
  starting transfers between devices  28.5 us (12%)
  between operations  14.8 us (6%)
  other arithmetic  14.4 us (6%)
  local copies, waits for them, and re-layouts  8.71 us (4%)
    pallas_call x3, Pallas kernels, run_kernel(): pl.pallas_call(kernel, grid=(streamed[0].shape[0] // count,), in_specs=[p...  112 us
    ppermute x16, waiting for transfers between devices, swap(): return lax.ppermute(value, AXES, pairs)  38.5 us
    ppermute x16, starting transfers between devices, swap(): return lax.ppermute(value, AXES, pairs)  24.9 us
    all_gather x1, waiting for transfers between devices, body(): late = lax.all_gather(late_shard, 'dp', axis=0)  6.99 us
  transfers between devices with their start and end apart: 19, of which 12 were waited for; matrix products, arithmetic and copies ran while one was open for 7% of the time, Pallas kernels for 49%

profile of v11, /device:TPU:0, one launch (start us, length us, event | category | flops | bytes accessed | tf_op | source)
XLA Modules:
  0.0 228.8 jit_solution(4501997441891510532)
XLA Ops:
  9.6 4.1 %collective-permute-start = (bf16[96,384]{1,0:T(8,128)(2,1)S(1)}, bf16[96,384]{1,0:T(8,128)(2,1)S(1)}, u32[]{:S(2)}, u32[]{:S(2)}) collective-permute-start(bf16[96,384]{1,0:T(8,128)(2,1)S(1)} %fusion.15), channel_id=1, source_target_pairs={{0,16},{1,17},{2,18},{3,19},{4,20},{5,21},{6,22},{7,23},{8,24},{9,... | collective-permute-start | bytes 221192 | tf_op jit(solution)/shard_map/ppermute | solution.py:655
  16.2 1.7 pad_maximum_fusion.4
  20.9 2.4 %collective-permute-done.1 = bf16[2,96,384]{2,1,0:T(8,128)(2,1)S(1)} collective-permute-done((bf16[2,96,384]{2,1,0:T(8,128)(2,1)S(1)}, bf16[2,96,384]{2,1,0:T(8,128)(2,1)S(1)}, u32[]{:S(2)}, u32[]{:S(2)}) %collective-permute-start.1) | collective-permute-done | bytes 147488 | tf_op jit(solution)/shard_map/ppermute | solution.py:655
  23.7 2.3 %collective-permute-start.3 = (f32[2,16,576]{2,1,0:T(8,128)S(1)}, f32[2,16,576]{2,1,0:T(8,128)S(1)}, u32[]{:S(2)}, u32[]{:S(2)}) collective-permute-start(f32[2,16,576]{2,1,0:T(8,128)S(1)} %dynamic-slice_bitcast_fusion), channel_id=1, source_target_pairs={{0,16},{1,17},{2,18},{3,19},{4,20},{5,21},{6,22},{7,23},{8,24},{9,... | collective-permute-start | bytes 221192 | tf_op jit(solution)/shard_map/ppermute | solution.py:655
  26.0 7.3 %collective-permute-done.3 = f32[2,16,576]{2,1,0:T(8,128)S(1)} collective-permute-done((f32[2,16,576]{2,1,0:T(8,128)S(1)}, f32[2,16,576]{2,1,0:T(8,128)S(1)}, u32[]{:S(2)}, u32[]{:S(2)}) %collective-permute-start.3) | collective-permute-done | bytes 73760 | tf_op jit(solution)/shard_map/ppermute | solution.py:655
  33.4 1.7 collective-permute-start.4
  35.1 1.7 collective-permute-start.5
  36.8 4.5 %collective-permute-done.4 = f32[2,16,576]{2,1,0:T(8,128)S(1)} collective-permute-done((f32[2,16,576]{2,1,0:T(8,128)S(1)}, f32[2,16,576]{2,1,0:T(8,128)S(1)}, u32[]{:S(2)}, u32[]{:S(2)}) %collective-permute-start.4) | collective-permute-done | bytes 73760 | tf_op jit(solution)/shard_map/ppermute | solution.py:655
  46.3 2.1 collective-permute-start.7
  49.3 19.3 %shard_map.228 = (bf16[16,256,384]{2,1,0:T(8,128)(2,1)}, bf16[16,1152,256]{2,1,0:T(8,128)(2,1)}, f32[16,8,256]{2,1,0:T(8,128)}, bf16[16,384,256]{2,1,0:T(8,128)(2,1)}, bf16[1152,384]{1,0:T(8,128)(2,1)}) custom-call(s32[1]{0:T(128)} %bitcast.core_ref, bf16[16,256,384]{2,1,0:T(8,128)(2,1)} %tokens_ref.5, f32[16,6,384]{2,1,0:T(8,128)} %broadcast_add_fusion.mod_ref, ...), custom_call_target="tpu_custom_call" | custom-call | flops 5234491392 | bytes 18874368 | tf_op jit(solution)/shard_map/pallas_call | solution.py:612
  68.7 7.0 %all-gather.6.cloned.1.call-done = bf16[3456,384]{1,0:T(8,128)(2,1)} async-done(((bf16[432,384]{1,0:T(8,128)(2,1)}), bf16[3456,384]{1,0:T(8,128)(2,1)}) %all-gather.6.cloned.1.call-update) | async-done | bytes 2654224 | tf_op jit(solution)/shard_map/all_gather | solution.py:724
  76.5 60.0 %shard_map.229 = (bf16[16,256,384]{2,1,0:T(8,128)(2,1)}, f32[16,256,384]{2,1,0:T(8,128)}, bf16[16,384,256]{2,1,0:T(8,128)(2,1)}, f32[16,4,384]{2,1,0:T(4,128)}, ...) custom-call(s32[1]{0:T(128)} %bitcast.core_ref, ...), custom_call_target="tpu_custom_call" | custom-call | flops 32614907904 | bytes 22020096 | tf_op jit(solution)/shard_map/pallas_call | solution.py:612
  136.7 3.3 %collective-permute-done.8 = bf16[8,216,384]{2,1,0:T(8,128)(2,1)S(1)} collective-permute-done((bf16[8,216,384]{2,1,0:T(8,128)(2,1)}, bf16[8,216,384]{2,1,0:T(8,128)(2,1)S(1)}, u32[]{:S(2)}, u32[]{:S(2)}) %collective-permute-start.8) | collective-permute-done | bytes 1327136 | tf_op jit(solution)/shard_map/ppermute | solution.py:655
  140.0 2.8 %add_convert_fusion = bf16[8,216,384]{2,1,0:T(8,128)(2,1)} fusion(bf16[8,216,384]{2,1,0:T(8,128)(2,1)S(1)} %collective-permute-done.8, bf16[8,216,384]{2,1,0:T(8,128)(2,1)} %get-tuple-element.57), kind=kLoop, calls=%fused_computation | loop fusion | flops 2654208 | bytes 3981312 | tf_op jit(solution)/shard_map/convert_element_type | solution.py:845
  142.7 3.6 %all-to-all-start = ((bf16[8,216,384]{2,1,0:T(8,128)(2,1)}), bf16[8,216,384]{2,1,0:T(8,128)(2,1)S(1)}, u32[]{:S(2)}, u32[]{:S(2)}) async-start(bf16[8,216,384]{2,1,0:T(8,128)(2,1)} %add_convert_fusion), calls=%async_computation | async-start | bytes 2654208 | tf_op jit(solution)/shard_map/all_to_all | solution.py:846
  146.4 33.1 %shard_map.230 = (bf16[16,256,384]{2,1,0:T(8,128)(2,1)}, f32[16,2,384]{2,1,0:T(2,128)}, bf16[8,80,384]{2,1,0:T(8,128)(2,1)}, bf16[8,80,384]{2,1,0:T(8,128)(2,1)}, f32[1,1152]{1,0:T(1,128)}) custom-call(s32[1]{0:T(128)} %bitcast.core_ref, bf16[16,1152,256]{2,1,0:T(8,128)(2,1)} %get-tuple-element.53.qkv_ref, f32[16,8,256]{2,1,0:T(8,128)} %get-tuple-element.54.lse_ref, ...), custom_call_target="tpu_custom_call" | custom-call | flops 1 | bytes 1 | tf_op jit(solution)/shard_map/pallas_call | solution.py:612
  183.3 1.9 collective-permute-start.10
  185.2 7.6 %collective-permute-done.10 = bf16[2,2,96,384]{3,2,0,1:T(8,128)(2,1)S(1)} collective-permute-done((bf16[2,2,96,384]{3,2,0,1:T(8,128)(2,1)S(1)}, bf16[2,2,96,384]{3,2,0,1:T(8,128)(2,1)S(1)}, u32[]{:S(2)}, u32[]{:S(2)}) %collective-permute-start.10) | collective-permute-done | bytes 294944 | tf_op jit(solution)/shard_map/ppermute | solution.py:655
  193.0 1.8 collective-permute-start.11
  194.8 4.2 %collective-permute-done.11 = bf16[2,112,384]{2,1,0:T(8,128)(2,1)S(1)} collective-permute-done((bf16[2,112,384]{2,1,0:T(8,128)(2,1)S(1)}, bf16[2,112,384]{2,1,0:T(8,128)(2,1)S(1)}, u32[]{:S(2)}, u32[]{:S(2)}) %collective-permute-start.11) | collective-permute-done | bytes 172064 | tf_op jit(solution)/shard_map/ppermute | solution.py:655
  199.9 2.7 %collective-permute-start.12 = (bf16[144,384]{1,0:T(8,128)(2,1)}, bf16[144,384]{1,0:T(8,128)(2,1)}, u32[]{:S(2)}, u32[]{:S(2)}) collective-permute-start(bf16[144,384]{1,0:T(8,128)(2,1)} %pad_maximum_fusion.13), channel_id=1, source_target_pairs={{0,16},{1,17},{2,18},{3,19},{4,20},{5,21},{6,22},{7,23},{8,24},{9,... | collective-permute-start | bytes 331784 | tf_op jit(solution)/shard_map/ppermute | solution.py:655
  204.4 3.0 %collective-permute-done.12 = bf16[144,384]{1,0:T(8,128)(2,1)} collective-permute-done((bf16[144,384]{1,0:T(8,128)(2,1)}, bf16[144,384]{1,0:T(8,128)(2,1)}, u32[]{:S(2)}, u32[]{:S(2)}) %collective-permute-start.12) | collective-permute-done | bytes 110624 | tf_op jit(solution)/shard_map/ppermute | solution.py:655
  211.5 3.8 %collective-permute-done.13 = bf16[208,384]{1,0:T(8,128)(2,1)S(1)} collective-permute-done((bf16[208,384]{1,0:T(8,128)(2,1)S(1)}, bf16[208,384]{1,0:T(8,128)(2,1)S(1)}, u32[]{:S(2)}, u32[]{:S(2)}) %collective-permute-start.13) | collective-permute-done | bytes 159776 | tf_op jit(solution)/shard_map/ppermute | solution.py:655
  218.1 2.7 %shard_map.231 = (f32[288,384]{1,0:T(8,128)}, f32[1,288]{1,0:T(1,128)}, f32[144,384]{1,0:T(8,128)}, f32[192,384]{1,0:T(8,128)}, f32[48,1536]{1,0:T(8,128)}, /*in...) custom-call(s32[1]{0:T(128)} %bitcast.core_ref, ...), custom_call_target="tpu_custom_call" | custom-call | tf_op jit(solution)/shard_map/pallas_call | solution.py:928
  (151 shorter events, 29.4 us)
Async XLA Ops:
  7.2 68.5 %all-gather.6.cloned.1.call-start = ((), (), s32[]{:S(2)}) async-start(), calls=%async_computation.2 | async-start | bytes 2985984 | tf_op jit(solution)/shard_map/all_gather | solution.py:724
  9.6 8.4 %collective-permute-start = (bf16[96,384]{1,0:T(8,128)(2,1)S(1)}, bf16[96,384]{1,0:T(8,128)(2,1)S(1)}, u32[]{:S(2)}, u32[]{:S(2)}) collective-permute-start(bf16[96,384]{1,0:T(8,128)(2,1)S(1)} %fusion.15), channel_id=1, source_target_pairs={{0,16},{1,17},{2,18},{3,19},{4,20},{5,21},{6,22},{7,23},{8,24},{9,... | collective-permute-start | bytes 221192 | tf_op jit(solution)/shard_map/ppermute | solution.py:655
  13.7 7.1 %collective-permute-start.2 = (bf16[288,384]{1,0:T(8,128)(2,1)}, bf16[288,384]{1,0:T(8,128)(2,1)S(1)}, u32[]{:S(2)}, u32[]{:S(2)}) collective-permute-start(bf16[288,384]{1,0:T(8,128)(2,1)} %bitcast.144), channel_id=1, source_target_pairs={{0,4},{1,5},{2,6},{3,7},{4,0},{5,1},{6,2},{7,3},{8,12},{9,13},{10,... | collective-permute-start | bytes 663560 | tf_op jit(solution)/shard_map/ppermute | solution.py:655
  17.9 118.7 %all-gather.4.cloned.1.call-start = ((), (), s32[]{:S(2)}) async-start(), calls=%async_computation.1 | async-start | bytes 1990656 | tf_op jit(solution)/shard_map/all_gather | solution.py:726
  18.1 5.2 %collective-permute-start.1 = (bf16[2,96,384]{2,1,0:T(8,128)(2,1)S(1)}, bf16[2,96,384]{2,1,0:T(8,128)(2,1)S(1)}, u32[]{:S(2)}, u32[]{:S(2)}) collective-permute-start(bf16[2,96,384]{2,1,0:T(8,128)(2,1)S(1)} %pad_maximum_fusion.12), channel_id=1, source_target_pairs={{0,8},{1,9},{2,10},{3,11},{4,12},{5,13},{6,14},{7,15},{8,0},{9,1},... | collective-permute-start | bytes 442376 | tf_op jit(solution)/shard_map/ppermute | solution.py:655
  23.7 9.7 %collective-permute-start.3 = (f32[2,16,576]{2,1,0:T(8,128)S(1)}, f32[2,16,576]{2,1,0:T(8,128)S(1)}, u32[]{:S(2)}, u32[]{:S(2)}) collective-permute-start(f32[2,16,576]{2,1,0:T(8,128)S(1)} %dynamic-slice_bitcast_fusion), channel_id=1, source_target_pairs={{0,16},{1,17},{2,18},{3,19},{4,20},{5,21},{6,22},{7,23},{8,24},{9,... | collective-permute-start | bytes 221192 | tf_op jit(solution)/shard_map/ppermute | solution.py:655
  33.4 7.9 %collective-permute-start.4 = (f32[2,16,576]{2,1,0:T(8,128)S(1)}, f32[2,16,576]{2,1,0:T(8,128)S(1)}, u32[]{:S(2)}, u32[]{:S(2)}) collective-permute-start(f32[2,16,576]{2,1,0:T(8,128)S(1)} %fusion.10), channel_id=1, source_target_pairs={{0,8},{1,9},{2,10},{3,11},{4,12},{5,13},{6,14},{7,15},{8,0},{9,1},... | collective-permute-start | bytes 221192 | tf_op jit(solution)/shard_map/ppermute | solution.py:655
  35.1 7.6 %collective-permute-start.5 = (bf16[2,2,96,384]{3,2,1,0:T(8,128)(2,1)S(1)}, bf16[2,2,96,384]{3,2,1,0:T(8,128)(2,1)S(1)}, u32[]{:S(2)}, u32[]{:S(2)}) collective-permute-start(bf16[2,2,96,384]{3,2,1,0:T(8,128)(2,1)S(1)} %pad_maximum_fusion.3), channel_id=1, source_target_pairs={{0,4},{1,5},{2,6},{3,7},{4,0},{5,1},{6,2},{7,3},{8,12},{9,13},{10,... | collective-permute-start | bytes 884744 | tf_op jit(solution)/shard_map/ppermute | solution.py:655
  43.8 2.4 %collective-permute-start.6 = (bf16[8,88,384]{2,0,1:T(8,128)(2,1)S(1)}, bf16[8,88,384]{2,0,1:T(8,128)(2,1)S(1)}, u32[]{:S(2)}, u32[]{:S(2)}) collective-permute-start(bf16[8,88,384]{2,0,1:T(8,128)(2,1)S(1)} %slice.82), channel_id=1, source_target_pairs={{0,1},{1,0},{2,3},{3,2},{4,5},{5,4},{6,7},{7,6},{8,9},{9,8},{10,11... | collective-permute-start | bytes 1622024 | tf_op jit(solution)/shard_map/ppermute | solution.py:655
  43.9 24.7 %copy-start.12 = (f32[8,384]{1,0:T(8,128)}, f32[8,384]{1,0:T(8,128)S(1)}, u32[]{:S(2)}) copy-start(f32[8,384]{1,0:T(8,128)S(1)} %fusion.28.biases_ref) | copy-start | bytes 36868
  46.3 22.3 %collective-permute-start.7 = (bf16[2,8,16,384]{3,1,2,0:T(8,128)(2,1)S(1)}, bf16[2,8,16,384]{3,1,2,0:T(8,128)(2,1)S(1)}, u32[]{:S(2)}, u32[]{:S(2)}) collective-permute-start(bf16[2,8,16,384]{3,1,2,0:T(8,128)(2,1)S(1)} %pad_maximum_fusion.6), channel_id=1, source_target_pairs={{0,2},{1,3},{2,0},{3,1},{4,6},{5,7},{6,4},{7,5},{8,10},{9,11},{10,... | collective-permute-start | bytes 589832 | tf_op jit(solution)/shard_map/ppermute | solution.py:655
  136.6 3.3 %collective-permute-start.8 = (bf16[8,216,384]{2,1,0:T(8,128)(2,1)}, bf16[8,216,384]{2,1,0:T(8,128)(2,1)S(1)}, u32[]{:S(2)}, u32[]{:S(2)}) collective-permute-start(bf16[8,216,384]{2,1,0:T(8,128)(2,1)} %get-tuple-element.60), channel_id=1, source_target_pairs={{0,1},{1,0},{2,3},{3,2},{4,5},{5,4},{6,7},{7,6},{8,9},{9,8},{10,11... | collective-permute-start | bytes 3981320 | tf_op jit(solution)/shard_map/ppermute | solution.py:655
  142.7 36.8 %all-to-all-start = ((bf16[8,216,384]{2,1,0:T(8,128)(2,1)}), bf16[8,216,384]{2,1,0:T(8,128)(2,1)S(1)}, u32[]{:S(2)}, u32[]{:S(2)}) async-start(bf16[8,216,384]{2,1,0:T(8,128)(2,1)} %add_convert_fusion), calls=%async_computation | async-start | bytes 2654208 | tf_op jit(solution)/shard_map/all_to_all | solution.py:846
  146.3 33.4 %copy-start.13 = (f32[1,1536]{1,0:T(1,128)S(1)}, f32[1,1536]{1,0:T(1,128)}, u32[]{:S(2)}) copy-start(f32[1,1536]{1,0:T(1,128)} %get-tuple-element.73) | copy-start | bytes 18436
  146.3 33.5 %copy-start.15 = (f32[1,384]{1,0:T(1,128)S(1)}, f32[1,384]{1,0:T(1,128)}, u32[]{:S(2)}) copy-start(f32[1,384]{1,0:T(1,128)} %get-tuple-element.72) | copy-start | bytes 4612
  146.3 33.6 %copy-start.14 = (f32[1,384]{1,0:T(1,128)S(1)}, f32[1,384]{1,0:T(1,128)}, u32[]{:S(2)}) copy-start(f32[1,384]{1,0:T(1,128)} %get-tuple-element.74) | copy-start | bytes 4612
  146.4 34.6 %copy-start.8 = (f32[16,4,384]{2,1,0:T(4,128)S(1)}, f32[16,4,384]{2,1,0:T(4,128)}, u32[]{:S(2)}) copy-start(f32[16,4,384]{2,1,0:T(4,128)} %get-tuple-element.66) | copy-start | bytes 294916
  179.5 2.6 %collective-permute-start.9 = (bf16[8,80,384]{2,1,0:T(8,128)(2,1)}, bf16[8,80,384]{2,1,0:T(8,128)(2,1)S(1)}, u32[]{:S(2)}, u32[]{:S(2)}) collective-permute-start(bf16[8,80,384]{2,1,0:T(8,128)(2,1)} %get-tuple-element.70), channel_id=1, source_target_pairs={{0,1},{1,0},{2,3},{3,2},{4,5},{5,4},{6,7},{7,6},{8,9},{9,8},{10,11... | collective-permute-start | bytes 1474568 | tf_op jit(solution)/shard_map/ppermute | solution.py:655
  183.3 9.5 %collective-permute-start.10 = (bf16[2,2,96,384]{3,2,0,1:T(8,128)(2,1)S(1)}, bf16[2,2,96,384]{3,2,0,1:T(8,128)(2,1)S(1)}, u32[]{:S(2)}, u32[]{:S(2)}) collective-permute-start(bf16[2,2,96,384]{3,2,0,1:T(8,128)(2,1)S(1)} %pad_maximum_fusion.5), channel_id=1, source_target_pairs={{0,4},{1,5},{2,6},{3,7},{4,0},{5,1},{6,2},{7,3},{8,12},{9,13},{10,... | collective-permute-start | bytes 884744 | tf_op jit(solution)/shard_map/ppermute | solution.py:655
  193.0 6.1 %collective-permute-start.11 = (bf16[2,112,384]{2,1,0:T(8,128)(2,1)S(1)}, bf16[2,112,384]{2,1,0:T(8,128)(2,1)S(1)}, u32[]{:S(2)}, u32[]{:S(2)}) collective-permute-start(bf16[2,112,384]{2,1,0:T(8,128)(2,1)S(1)} %pad_maximum_fusion.9), channel_id=1, source_target_pairs={{0,8},{1,9},{2,10},{3,11},{4,12},{5,13},{6,14},{7,15},{8,0},{9,1},... | collective-permute-start | bytes 516104 | tf_op jit(solution)/shard_map/ppermute | solution.py:655
  199.9 7.5 %collective-permute-start.12 = (bf16[144,384]{1,0:T(8,128)(2,1)}, bf16[144,384]{1,0:T(8,128)(2,1)}, u32[]{:S(2)}, u32[]{:S(2)}) collective-permute-start(bf16[144,384]{1,0:T(8,128)(2,1)} %pad_maximum_fusion.13), channel_id=1, source_target_pairs={{0,16},{1,17},{2,18},{3,19},{4,20},{5,21},{6,22},{7,23},{8,24},{9,... | collective-permute-start | bytes 331784 | tf_op jit(solution)/shard_map/ppermute | solution.py:655
  202.8 8.6 %collective-permute-start.14 = (bf16[216,384]{1,0:T(8,128)(2,1)S(1)}, bf16[216,384]{1,0:T(8,128)(2,1)S(1)}, u32[]{:S(2)}, u32[]{:S(2)}) collective-permute-start(bf16[216,384]{1,0:T(8,128)(2,1)S(1)} %reduce_sum.12), channel_id=1, source_target_pairs={{0,2},{1,3},{2,0},{3,1},{4,6},{5,7},{6,4},{7,5},{8,10},{9,11},{10,... | collective-permute-start | bytes 497672 | tf_op jit(solution)/shard_map/ppermute | solution.py:655
  209.9 5.3 %collective-permute-start.13 = (bf16[208,384]{1,0:T(8,128)(2,1)S(1)}, bf16[208,384]{1,0:T(8,128)(2,1)S(1)}, u32[]{:S(2)}, u32[]{:S(2)}) collective-permute-start(bf16[208,384]{1,0:T(8,128)(2,1)S(1)} %pad_maximum_fusion.11), channel_id=1, source_target_pairs={{0,2},{1,3},{2,0},{3,1},{4,6},{5,7},{6,4},{7,5},{8,10},{9,11},{10,... | collective-permute-start | bytes 479240 | tf_op jit(solution)/shard_map/ppermute | solution.py:655
  215.5 1.8 collective-permute-start.15
  (11 other events, 83.7 us)
Sparse Core Ops, SparseCore 0:
  18.0 57.5 all-gather.5
  77.9 44.4 all-gather.3
